TPU v7x, 32 devices: a whole 2x2x4 slice. The times are simulated.
32 devices in a mesh: ctx: 4 (over z), tp: 4 (over x, core), pp: 2 (over y).
Axes of the slice: x: 2, y: 2, z: 4, core: 2. Of those that a mesh axis runs over, the one named last changes fastest.
Arguments:
- queries: bfloat16 [2, 512, 4096], P('pp', 'ctx', 'tp'), may hold values from -0.59765625 to 0.59765625
- key_input: bfloat16 [2, 512, 4096], P('pp', 'ctx', 'tp'), may hold values from -6 to 6
- values: bfloat16 [2, 512, 4096], P('pp', 'ctx', 'tp'), may hold values from -6 to 6
- log_decay: float32 [2, 512, 32], P('pp', 'ctx', 'tp'), may hold values from -1 to 0
- conv_weight: float32 [2, 4, 4096], P('pp', None, 'tp'), may hold values from -3 to 3
- out_grad: bfloat16 [2, 512, 4096], P('pp', 'ctx', 'tp'), may hold values from -6 to 6
Outputs:
- layer_output: bfloat16 [2, 512, 4096], P('pp', 'ctx', 'tp')
- input_grad_next: bfloat16 [2, 512, 4096], P('pp', 'ctx', 'tp')
All inputs are finite; a program needn't handle non-finite values.
Results may differ from a plain program's by a relative error of at most 0.006.
The roundings to bfloat16 on the way count: a program that leaves them out, or rounds other values in their place, can miss the bound.
Values may be sent and summed in bfloat16 or wider, within the bound.
No kernel may reach another device: no remote copies, remote signals or barrier semaphores. Data moves between devices by JAX's collectives and lax.ppermute only.
A program may use at most 64 MiB of HBM per device.

v0:
```python
import jax
import jax.numpy as jnp
from jax import lax
from jax.sharding import PartitionSpec as P


def shifted(block, axis, distance):
    devices = range(lax.axis_size(axis))
    route = [(i - distance, i) for i in devices if i - distance in devices]
    return lax.ppermute(block, axis, route)


def entering(value, axis, combine, identity):
    peers, place = (lax.axis_size(axis), lax.axis_index(axis))
    everything = jax.tree.map(lambda part: lax.all_gather(part, axis), value)
    start = jax.tree.map(
        lambda part, zero: jnp.broadcast_to(jnp.asarray(zero, part.dtype), part.shape),
        value,
        identity,
    )

    def step(k, before):
        reached = k < place
        new = combine(before, jax.tree.map(lambda part: part[k], everything))
        return jax.tree.map(lambda a, b: jnp.where(reached, a, b), new, before)

    return lax.fori_loop(0, peers, step, start)


def carried_in(value, axis, join, neutral):
    count = lax.axis_size(axis)
    place = lax.axis_index(axis)
    ahead = count - 1 - place
    gathered = jax.tree.map(
        lambda a, kind: lax.all_gather(a.astype(kind), axis), value, (jnp.bfloat16, jnp.bfloat16)
    )
    state = jax.tree.map(lambda a, e: jnp.zeros_like(a) + jnp.asarray(e, a.dtype), value, neutral)

    def one(step, state):
        source = count - 1 - step
        return join(
            state,
            jax.tree.map(
                lambda a, own: lax.dynamic_index_in_dim(a, source, 0, False).astype(own.dtype),
                gathered,
                value,
            ),
        )

    return lax.fori_loop(0, ahead, one, state)


def combine(first_part, second_part):
    return (
        first_part[0] + second_part[0],
        jnp.exp(second_part[0])[:, None, None] * first_part[1] + second_part[1],
    )


def decay_table(cum_decay):
    transposed = jnp.swapaxes(cum_decay, 0, 1)
    differ = transposed[:, :, None] - transposed[:, None, :]
    tok_rows = cum_decay.shape[0]
    causal = jnp.arange(tok_rows)[:, None] >= jnp.arange(tok_rows)[None, :]
    return jnp.where(causal, jnp.exp(jnp.where(causal, differ, 0.0)), 0.0)


def per_device(queries, key_input, values, log_decay, conv_weight, out_grad):
    tok_rows = queries.shape[1]
    feat_width = queries.shape[2]
    heads_dev = log_decay.shape[2]
    head_dim = feat_width // heads_dev
    tap_count = conv_weight.shape[1]
    width_all = feat_width * lax.axis_size("tp")
    tap_weights = conv_weight[0]
    head_shape = (tok_rows, heads_dev, head_dim)
    edge_rows = shifted(key_input[0, tok_rows - (tap_count - 1) :], "ctx", 1)
    extended = jnp.concatenate([edge_rows, key_input[0]], 0).astype(jnp.float32)
    conv_sum = jnp.zeros((tok_rows, feat_width), jnp.float32)
    for tap_index in range(tap_count):
        start_row = tap_count - 1 - tap_index
        conv_sum = conv_sum + tap_weights[tap_index] * extended[start_row : start_row + tok_rows]
    smoothed_key_rows = conv_sum.astype(jnp.bfloat16).reshape(head_shape)
    query_tile_block = queries[0].reshape(head_shape)
    value_tile_block = values[0].reshape(head_shape)
    grad_blk = out_grad[0].reshape(head_shape).astype(jnp.float32)
    cum_decay = jnp.cumsum(log_decay[0], axis=0)
    block_total = cum_decay[-1]
    mixing = decay_table(cum_decay)
    scores = jnp.einsum(
        "thk,shk->hts", query_tile_block, smoothed_key_rows, preferred_element_type=jnp.float32
    )
    weights = (scores * mixing).astype(jnp.bfloat16)
    weight_after = jnp.exp(block_total[None, :] - cum_decay)[:, :, None]
    keys_times_decay = (smoothed_key_rows.astype(jnp.float32) * weight_after).astype(jnp.bfloat16)
    block_state = jnp.einsum(
        "pto,ptd->tod", keys_times_decay, value_tile_block, preferred_element_type=jnp.float32
    )
    identity = (
        jnp.zeros((heads_dev,), jnp.float32),
        jnp.zeros((heads_dev, head_dim, head_dim), jnp.float32),
    )
    _, leading_rows = entering((block_total, block_state), "ctx", combine, identity)
    opening_half = leading_rows.astype(jnp.bfloat16)
    growth = jnp.exp(cum_decay)[:, :, None]
    attended = jnp.einsum(
        "hts,shv->thv", weights, value_tile_block, preferred_element_type=jnp.float32
    )
    attended = attended + growth * jnp.einsum(
        "upg,pgn->upn", query_tile_block, opening_half, preferred_element_type=jnp.float32
    )
    squares_local = jnp.sum(attended * attended, axis=(1, 2))
    squares_all = lax.psum(squares_local, "tp")
    root_mean = jnp.sqrt(squares_all / width_all + 1e-06)
    normed = attended / root_mean[:, None, None]
    shift_mean = lax.psum(jnp.sum(grad_blk * normed, axis=(1, 2)), "tp") / width_all
    layer_output = normed.astype(jnp.bfloat16).reshape(1, tok_rows, feat_width)
    gradient_of_attended = (
        (grad_blk - normed * shift_mean[:, None, None]) / root_mean[:, None, None]
    ).astype(jnp.bfloat16)
    queries_times_decay = (query_tile_block.astype(jnp.float32) * growth).astype(jnp.bfloat16)
    block_adjoint = jnp.einsum(
        "ezr,ezs->zrs",
        queries_times_decay,
        gradient_of_attended,
        preferred_element_type=jnp.float32,
    )
    _, state_following = carried_in((block_total, block_adjoint), "ctx", combine, identity)
    trailing_half = state_following.astype(jnp.bfloat16)
    score_grad = (
        jnp.einsum(
            "thv,shv->hts",
            gradient_of_attended,
            value_tile_block,
            preferred_element_type=jnp.float32,
        )
        * mixing
    ).astype(jnp.bfloat16)
    query_grad = jnp.einsum(
        "hts,shk->thk", score_grad, smoothed_key_rows, preferred_element_type=jnp.float32
    )
    query_grad = query_grad + growth * jnp.einsum(
        "csp,sqp->csq", gradient_of_attended, opening_half, preferred_element_type=jnp.float32
    )
    value_grad = jnp.einsum(
        "hts,thv->shv", weights, gradient_of_attended, preferred_element_type=jnp.float32
    )
    value_grad = value_grad + weight_after * jnp.einsum(
        "gnf,nfb->gnb", smoothed_key_rows, trailing_half, preferred_element_type=jnp.float32
    )
    ckey_grad = jnp.einsum(
        "hts,thk->shk", score_grad, query_tile_block, preferred_element_type=jnp.float32
    )
    ckey_grad = ckey_grad + weight_after * jnp.einsum(
        "cmj,mnj->cmn", value_tile_block, trailing_half, preferred_element_type=jnp.float32
    )
    grad_flat = ckey_grad.reshape(tok_rows, feat_width)
    next_rows = shifted(grad_flat[: tap_count - 1], "ctx", -1)
    padded_grad = jnp.concatenate([grad_flat, next_rows], 0)
    input_grad = query_grad.reshape(tok_rows, feat_width) + value_grad.reshape(tok_rows, feat_width)
    for tap_index in range(tap_count):
        input_grad = (
            input_grad + tap_weights[tap_index] * padded_grad[tap_index : tap_index + tok_rows]
        )
    input_send = input_grad.astype(jnp.bfloat16).reshape(1, tok_rows, feat_width)
    input_next = shifted(input_send, "pp", -1)
    return (layer_output, input_next)


def solution(mesh):
    placed = (
        P("pp", "ctx", "tp"),
        P("pp", "ctx", "tp"),
        P("pp", "ctx", "tp"),
        P("pp", "ctx", "tp"),
        P("pp", None, "tp"),
        P("pp", "ctx", "tp"),
    )
    return jax.shard_map(
        per_device,
        mesh=mesh,
        in_specs=placed,
        out_specs=(P("pp", "ctx", "tp"), P("pp", "ctx", "tp")),
        check_vma=False,
    )
```

profile of v0, /device:TPU:0, one launch (start us, length us, event | category | flops | bytes accessed | tf_op | source)
XLA Modules:
  0.0 137.4 jit_solution(8129528889618147594)
XLA Ops:
  7.2 0.0 all-gather.7.cloned.1.call-start
  7.2 0.7 slice_bitcast_fusion
  7.9 4.9 %collective-permute-start = (bf16[3,1024]{1,0:T(4,128)(2,1)S(1)}, bf16[3,1024]{1,0:T(4,128)(2,1)S(1)}, u32[]{:S(2)}, u32[]{:S(2)}) collective-permute-start(bf16[3,1024]{1,0:T(4,128)(2,1)S(1)} %slice_bitcast_fusion), channel_id=1, source_target_pairs={{0,8},{8,16},{16,24},{1,9},{9,17},{17,25},{2,10},{10,18},{18,26},{... | collective-permute-start | bytes 18440 | tf_op jit(solution)/shard_map/ppermute | solution.py:10
  12.9 0.8 copy.78
  13.6 0.2 reduce_window_sum.11
  13.9 0.9 fusion.39
  14.8 1.0 copy.126
  15.8 0.0 collective-permute-done
  15.8 1.0 maximum_convert_fusion
  16.9 0.0 copy-start.4
  16.9 0.0 copy-start.3
  16.9 0.2 fusion.23
  17.1 0.2 copy.74
  17.3 1.0 fusion.26
  18.3 0.0 all-gather.7.cloned.1.call-update
  18.4 0.0 all-gather.9.cloned.1.call-start
  18.4 10.2 %all-gather.2 = f32[4,1,8]{2,1,0:T(1,128)S(1)} all-gather(f32[1,1,8]{2,1,0:T(1,128)S(1)} %get-tuple-element.246), channel_id=1, replica_groups=mesh['ctx'=4,'tp'=4,'pp'=2] {'ctx'}, dimensions={0}, use_global_device_ids=true | all-gather | bytes 160 | tf_op jit(solution)/shard_map/all_gather | solution.py:15
  28.6 0.0 copy-done.4
  28.6 0.2 copy.75
  28.9 0.0 copy-done.3
  28.9 0.2 copy.88
  29.1 0.3 fusion.12
  29.4 0.0 copy-start
  29.4 0.3 convolution_bitcast_fusion
  29.7 35.1 %all-gather.7.cloned.1.call-done = f32[32,128,128]{2,1,0:T(8,128)} async-done(((f32[8,128,128]{2,1,0:T(8,128)}), f32[32,128,128]{2,1,0:T(8,128)}) %all-gather.7.cloned.1.call-update) | async-done | bytes 2097168 | tf_op jit(solution)/shard_map/all_gather | solution.py:15
  64.8 0.0 copy-done
  64.8 4.8 %while.29 = (s32[]{:T(128)}, f32[8,128,128]{2,1,0:T(8,128)S(1)}, s32[]{:T(128)}, f32[4,8]{1,0:T(4,128)S(1)}, f32[4,8,128,128]{3,2,1,0:T(8,128)}, /*index=5*/s32[]{:T(128)}, s32[]{:T(128)}) while((s32[]{:T(128)}, f32[8,128,128]{2,1,0:T(8,128)S(1)}, s32[]{:T(128)}, f32[4,8]{1,0:T(4,128)S(1)}, f32[4,8,128,128]{3,2,1,0:T(8,128)}, ...), condition=%wide.region_2.3_spmd.clone, body=%wide.region_1.2_spmd.clone.sunk | while | flops 524292 | bytes 1573065 | solution.py:27
  64.8 1.2 fusion.55
  66.0 1.2 fusion.55
  67.2 1.2 fusion.55
  68.4 1.2 fusion.55
  69.6 0.4 multiply_reduce_fusion.1
  70.0 6.9 %psum.14 = f32[128]{0:T(128)S(1)} all-reduce(f32[128]{0:T(128)S(1)} %get-tuple-element.251), channel_id=1, replica_groups=mesh['ctx'=4,'tp'=4,'pp'=2] {'tp'}, use_global_device_ids=true, to_apply=%region_4.5 | all-reduce | flops 128 | bytes 1024 | tf_op jit(solution)/shard_map/psum | solution.py:113
  76.9 0.2 multiply_reduce_fusion
  77.0 5.9 %psum.15 = f32[128]{0:T(128)S(1)} all-reduce(f32[128]{0:T(128)S(1)} %multiply_reduce_fusion), channel_id=1, replica_groups=mesh['ctx'=4,'tp'=4,'pp'=2] {'tp'}, use_global_device_ids=true, to_apply=%region_6.7 | all-reduce | flops 128 | bytes 1024 | tf_op jit(solution)/shard_map/psum | solution.py:116
  82.9 0.1 divide_convert_fusion
  83.1 1.0 convolution_convert_fusion
  84.1 0.0 all-gather.9.cloned.1.call-update
  84.1 8.7 %all-gather.3 = bf16[4,1,8]{2,1,0:T(2,128)(2,1)S(1)} all-gather(bf16[1,1,8]{2,1,0:T(2,128)(2,1)S(1)} %convert_bitcast_fusion), channel_id=1, replica_groups=mesh['ctx'=4,'tp'=4,'pp'=2] {'ctx'}, dimensions={0}, use_global_device_ids=true | all-gather | bytes 80 | tf_op jit(solution)/shard_map/all_gather | solution.py:35
  92.8 0.2 fusion.11
  93.0 0.0 copy-start.2
  93.0 0.2 fusion.6
  93.3 16.7 %all-gather.9.cloned.1.call-done = bf16[32,128,128]{2,1,0:T(8,128)(2,1)} async-done(((bf16[8,128,128]{2,1,0:T(8,128)(2,1)}), bf16[32,128,128]{2,1,0:T(8,128)(2,1)}) %all-gather.9.cloned.1.call-update) | async-done | bytes 1048592 | tf_op jit(solution)/shard_map/all_gather | solution.py:35
  110.0 3.5 %while.28 = (s32[]{:T(128)}, f32[8,128,128]{2,1,0:T(8,128)S(1)}, s32[]{:T(128)}, bf16[4,8]{1,0:T(4,128)(2,1)S(1)}, bf16[4,8,128,128]{3,2,1,0:T(8,128)(2,1)}, /*index=5*/s32[]{:T(128)}, s32[]{:T(128)}, s32[]{:T(128)}, s32[]{:T(128)}) while((s32[]{:T(128)}, f32[8,128,128]{2,1,0:T(8,128)S(1)}, s32[]{:T(128)}, bf16[4,8]{1,0:T(4,128)(2,1)S(1)}, ...), condition=%wide.region_8.9_spmd, body=%wide.region_7.8_spmd.sunk | while | flops 393230 | bytes 1310947 | solution.py:50
  110.1 1.1 convert_add_fusion.2
  111.2 1.1 convert_add_fusion.2
  112.4 1.1 convert_add_fusion.2
  113.5 0.0 copy-start.1
  113.5 0.3 fusion.8
  113.8 0.3 fusion.10
  114.1 0.3 copy-done.1
  114.5 0.3 fusion.7
  114.8 0.3 fusion.9
  115.1 0.2 copy.104
  115.3 1.3 collective-permute-start.1
  116.6 1.2 fusion.5
  117.8 0.2 copy.103
  118.0 0.2 copy.102
  118.2 2.7 %collective-permute-done.1 = f32[3,1024]{1,0:T(4,128)S(1)} collective-permute-done((f32[3,1024]{1,0:T(4,128)S(1)}, f32[3,1024]{1,0:T(4,128)S(1)}, u32[]{:S(2)}, u32[]{:S(2)}) %collective-permute-start.1) | collective-permute-done | bytes 12320 | tf_op jit(solution)/shard_map/ppermute | solution.py:10
  120.9 0.3 fusion.29
  121.2 1.3 collective-permute-start.2
  122.5 0.9 copy.106
  123.3 6.5 %collective-permute-done.2 = bf16[1,128,1024]{2,1,0:T(8,128)(2,1)S(1)} collective-permute-done((bf16[1,128,1024]{2,1,0:T(8,128)(2,1)S(1)}, bf16[1,128,1024]{2,1,0:T(8,128)(2,1)S(1)}, u32[]{:S(2)}, u32[]{:S(2)}) %collective-permute-start.2) | collective-permute-done | bytes 262176 | tf_op jit(solution)/shard_map/ppermute | solution.py:10
  129.8 0.7 copy.150
  (20 shorter events, 0.3 us)
Async XLA Ops:
  7.2 57.6 %all-gather.7.cloned.1.call-start = ((), (), s32[]{:S(2)}) async-start(), calls=%async_computation | async-start | bytes 2621440 | tf_op jit(solution)/shard_map/all_gather | solution.py:15
  7.9 7.9 %collective-permute-start = (bf16[3,1024]{1,0:T(4,128)(2,1)S(1)}, bf16[3,1024]{1,0:T(4,128)(2,1)S(1)}, u32[]{:S(2)}, u32[]{:S(2)}) collective-permute-start(bf16[3,1024]{1,0:T(4,128)(2,1)S(1)} %slice_bitcast_fusion), channel_id=1, source_target_pairs={{0,8},{8,16},{16,24},{1,9},{9,17},{17,25},{2,10},{10,18},{18,26},{... | collective-permute-start | bytes 18440 | tf_op jit(solution)/shard_map/ppermute | solution.py:10
  16.9 11.8 %copy-start.4 = (bf16[1,128,1024]{2,1,0:T(8,128)(2,1)S(1)}, bf16[1,128,1024]{2,1,0:T(8,128)(2,1)}, u32[]{:S(2)}) copy-start(bf16[1,128,1024]{2,1,0:T(8,128)(2,1)} %param.10) | copy-start | bytes 786436
  16.9 12.0 %copy-start.3 = (bf16[1,128,1024]{2,1,0:T(8,128)(2,1)S(1)}, bf16[1,128,1024]{2,1,0:T(8,128)(2,1)}, u32[]{:S(2)}) copy-start(bf16[1,128,1024]{2,1,0:T(8,128)(2,1)} %param.15) | copy-start | bytes 786436
  18.4 91.7 %all-gather.9.cloned.1.call-start = ((), (), s32[]{:S(2)}) async-start(), calls=%async_computation.1 | async-start | bytes 1310720 | tf_op jit(solution)/shard_map/all_gather | solution.py:35
  29.4 35.4 %copy-start = (bf16[8,128,128]{1,2,0:T(8,128)(2,1)}, bf16[8,128,128]{1,2,0:T(8,128)(2,1)S(1)}, u32[]{:S(2)}) copy-start(bf16[8,128,128]{1,2,0:T(8,128)(2,1)S(1)} %fusion.12) | copy-start | bytes 786436
  93.0 21.8 %copy-start.2 = (bf16[8,128,128]{1,2,0:T(8,128)(2,1)}, bf16[8,128,128]{1,2,0:T(8,128)(2,1)S(1)}, u32[]{:S(2)}) copy-start(bf16[8,128,128]{1,2,0:T(8,128)(2,1)S(1)} %fusion.11) | copy-start | bytes 786436
  113.5 1.0 copy-start.1
  115.3 5.6 %collective-permute-start.1 = (f32[3,1024]{1,0:T(4,128)S(1)}, f32[3,1024]{1,0:T(4,128)S(1)}, u32[]{:S(2)}, u32[]{:S(2)}) collective-permute-start(f32[3,1024]{1,0:T(4,128)S(1)} %copy.104), channel_id=1, source_target_pairs={{8,0},{16,8},{24,16},{9,1},{17,9},{25,17},{10,2},{18,10},{26,18},{... | collective-permute-start | bytes 36872 | tf_op jit(solution)/shard_map/ppermute | solution.py:10
  121.2 8.6 %collective-permute-start.2 = (bf16[1,128,1024]{2,1,0:T(8,128)(2,1)S(1)}, bf16[1,128,1024]{2,1,0:T(8,128)(2,1)S(1)}, u32[]{:S(2)}, u32[]{:S(2)}) collective-permute-start(bf16[1,128,1024]{2,1,0:T(8,128)(2,1)S(1)} %fusion.29), channel_id=1, source_target_pairs={{1,0},{3,2},{5,4},{7,6},{9,8},{11,10},{13,12},{15,14},{17,16},{19,... | collective-permute-start | bytes 786440 | tf_op jit(solution)/shard_map/ppermute | solution.py:10
Sparse Core Ops, SparseCore 0:
  18.5 46.2 all-gather.6
  84.2 25.7 all-gather.8
where the time goes:
time: 138 us; the launch traced here: 137 us
  waiting for transfers between devices  61.1 us (44%)
  blocking collectives  31.6 us (23%)
  between operations  14.3 us (10%)
  other arithmetic  10.1 us (7%)
  starting transfers between devices  7.58 us (5%)
  local copies, waits for them, and re-layouts  6.67 us (5%)
  matrix products  5.83 us (4%)
    all_gather x1, waiting for transfers between devices, entering(): everything = jax.tree.map(lambda part: lax.all_gather(part, axis), value)  35.1 us
    all_gather x1, waiting for transfers between devices, carried_in(): lax.all_gather(a.astype(kind), axis)  16.7 us
    all_gather x1, blocking collectives, entering(): everything = jax.tree.map(lambda part: lax.all_gather(part, axis), value)  10.2 us
    ppermute x3, waiting for transfers between devices, shifted(): return lax.ppermute(block, axis, route)  9.25 us
    all_gather x1, blocking collectives, carried_in(): lax.all_gather(a.astype(kind), axis)  8.66 us
    ppermute x3, starting transfers between devices, shifted(): return lax.ppermute(block, axis, route)  7.5 us
    psum x1, blocking collectives, per_device(): squares_all = lax.psum(squares_local, 'tp')  6.87 us
    psum x1, blocking collectives, per_device(): lax.psum(jnp.sum(grad_blk * normed, axis=(1, 2)), 'tp') / width_all  5.89 us
  transfers between devices with their start and end apart: 5, of which 4 were waited for; matrix products, arithmetic and copies ran while one was open for 5% of the time, Pallas kernels for 0%

commit v1 on v0

v1 whole, which is shorter than its diff:
```python
import jax
import jax.numpy as jnp
from jax import lax
from jax.experimental import pallas as pl
from jax.experimental.pallas import tpu as pltpu
from jax.sharding import PartitionSpec as P

F32 = jnp.float32
BF16 = jnp.bfloat16
PAIR = 2
EDGE = 16


def call(kernel, outs, *args, scratch=(), flops=0):
    vmem = pl.BlockSpec(memory_space=pltpu.VMEM)
    moved = sum(a.size * a.dtype.itemsize for a in args) + sum(
        s.size * s.dtype.itemsize for s in outs
    )
    return pl.pallas_call(
        kernel,
        out_shape=outs,
        in_specs=[vmem] * len(args),
        out_specs=[vmem] * len(outs),
        scratch_shapes=scratch,
        compiler_params=pltpu.CompilerParams(vmem_limit_bytes=32 * 1024 * 1024),
        cost_estimate=pl.CostEstimate(flops=flops, bytes_accessed=moved, transcendentals=0),
    )(*args)


def shape(dims, dtype):
    return jax.ShapeDtypeStruct(dims, dtype)


def halves(size):
    mine = lax.rem(lax.axis_index("ctx"), PAIR)
    return (
        pl.ds(pl.multiple_of(mine * size, size), size),
        pl.ds(pl.multiple_of((1 - mine) * size, size), size),
    )


def dot(a, b, contract):
    return lax.dot_general(a, b, ((contract[:1], contract[1:]), ((), ())), preferred_element_type=F32)


def split3(x):
    hi = x.astype(BF16)
    rest = x - hi.astype(F32)
    mid = rest.astype(BF16)
    return hi, mid, (rest - mid.astype(F32)).astype(BF16)


def decay_rows(log_decay, mine, heads):
    rows = log_decay[0].T
    return jnp.where(mine == 0, rows[:heads], rows[heads:])


def pack_kernel(q, k, v, g, log_decay, out):
    rows, heads = q.shape[1], log_decay.shape[2] // PAIR
    width = q.shape[2] // PAIR
    _, other = halves(width)
    for i, ref in enumerate((k, v, q, g)):
        out[i * rows : (i + 1) * rows, :] = ref[0, :, other]
    mine = lax.rem(lax.axis_index("ctx"), PAIR)
    decay = decay_rows(log_decay, 1 - mine, heads)
    parts = [
        jnp.concatenate([part[h : h + 1] for h in range(heads)], 1).astype(F32)
        for part in split3(decay)
    ]
    parts.append(jnp.zeros((EDGE - 3, heads * rows), F32))
    out[4 * rows :, :] = jnp.concatenate(parts, 0).astype(BF16)


def join_kernel(
    got, edge, q, k, v, g, log_decay, taps, q2, kc2, v2, g2, cum, state, padded, decays
):
    rows, heads = q.shape[1], log_decay.shape[2] // PAIR
    width = q.shape[2] // PAIR
    dim = width // heads
    own, _ = halves(width)
    here, there = halves(rows)
    mine = lax.rem(lax.axis_index("ctx"), PAIR)
    for i, (ref, out) in enumerate(((v, v2), (q, q2), (g, g2))):
        out[here, :] = ref[0, :, own]
        out[there, :] = got[(i + 1) * rows : (i + 2) * rows, :]
    padded[:EDGE, :] = edge[...].astype(F32)
    start = pl.multiple_of(EDGE + mine * rows, EDGE)
    padded[pl.ds(start, rows), :] = k[0, :, own].astype(F32)
    start = pl.multiple_of(EDGE + (1 - mine) * rows, EDGE)
    padded[pl.ds(start, rows), :] = got[:rows, :].astype(F32)
    total = jnp.zeros((PAIR * rows, width), F32)
    for j in range(taps.shape[1]):
        total = total + taps[0, j : j + 1, own] * padded[EDGE - j : EDGE - j + PAIR * rows, :]
    kc2[...] = total.astype(BF16)

    decays[...] = jnp.zeros_like(decays)
    coded = got[4 * rows :, :].astype(F32)
    row = coded[0:1] + coded[1:2] + coded[2:3]
    decays[:heads, here] = decay_rows(log_decay, mine, heads)
    decays[:heads, there] = jnp.concatenate(
        [row[:, h * rows : (h + 1) * rows] for h in range(heads)], 0
    )
    size = PAIR * rows
    upto = lax.broadcasted_iota(jnp.int32, (size, size), 0) <= lax.broadcasted_iota(
        jnp.int32, (size, size), 1
    )
    upto = upto.astype(F32).astype(BF16)
    cum_rows = sum(dot(part, upto, (1, 0)) for part in split3(decays[...]))
    cum[...] = cum_rows
    cols = cum_rows.T
    after = jnp.exp(cols[size - 1 :, :] - cols)
    for h in range(heads):
        lanes = slice(h * dim, (h + 1) * dim)
        scaled = (kc2[:, lanes].astype(F32) * after[:, h : h + 1]).astype(BF16)
        state[lanes, :] = dot(scaled, v2[:, lanes], (0, 0)).astype(BF16)


def mixing_of(cum_rows, cols, h, size):
    differ = cols[:, h : h + 1] - cum_rows[h : h + 1, :]
    causal = lax.broadcasted_iota(jnp.int32, (size, size), 0) >= lax.broadcasted_iota(
        jnp.int32, (size, size), 1
    )
    return jnp.where(causal, jnp.exp(jnp.where(causal, differ, 0.0)), 0.0)


def local_kernel(q2, kc2, v2, cum, weights, inside):
    size, width = q2.shape
    heads, dim = weights.shape[0], width // weights.shape[0]
    cum_rows = cum[...]
    cols = cum_rows.T
    for h in range(heads):
        lanes = slice(h * dim, (h + 1) * dim)
        scores = dot(q2[:, lanes], kc2[:, lanes], (1, 1))
        w = (scores * mixing_of(cum_rows, cols, h, size)).astype(BF16)
        weights[h] = w
        inside[:, lanes] = dot(w, v2[:, lanes], (1, 0))


def attend_kernel(inside, q2, g2, cum, before, attended, sums):
    size, width = q2.shape
    dim = before.shape[1]
    heads = width // dim
    growth = jnp.exp(cum[...].T)
    squares = jnp.zeros((size, dim), F32)
    products = jnp.zeros((size, dim), F32)
    for h in range(heads):
        lanes = slice(h * dim, (h + 1) * dim)
        a = inside[:, lanes] + growth[:, h : h + 1] * dot(q2[:, lanes], before[lanes, :], (1, 0))
        attended[:, lanes] = a
        squares = squares + a * a
        products = products + a * g2[:, lanes].astype(F32)
    ones = jnp.ones((8, dim), F32)
    line = [
        lax.dot_general(
            ones, x, (((1,), (1,)), ((), ())), precision=lax.Precision.HIGHEST,
            preferred_element_type=F32,
        )[:1]
        for x in (squares, products)
    ]
    sums[...] = jnp.concatenate(line, 0)


def grad_kernel(width_all, n_sums, attended, q2, g2, cum, *refs):
    sums = refs[:n_sums]
    keep, send, grad, adjoint, normed = refs[n_sums:]
    size, width = q2.shape
    dim = adjoint.shape[1]
    heads = width // dim
    total = sum(ref[...] for ref in sums[1:]) + sums[0][...]
    inverse = 1.0 / jnp.sqrt(total[0:1] / width_all + 1e-06)
    shift = total[1:2] / width_all * inverse
    both = jnp.concatenate([inverse, shift, jnp.zeros((6, size), F32)], 0).T
    inverse, shift = both[:, 0:1], both[:, 1:2]
    growth = jnp.exp(cum[...].T)
    for h in range(heads):
        lanes = slice(h * dim, (h + 1) * dim)
        n = attended[:, lanes] * inverse
        normed[:, lanes] = n.astype(BF16)
        d = ((g2[:, lanes].astype(F32) - n * shift) * inverse).astype(BF16)
        grad[:, lanes] = d
        scaled = (q2[:, lanes].astype(F32) * growth[:, h : h + 1]).astype(BF16)
        adjoint[lanes, :] = dot(scaled, d, (0, 0)).astype(BF16)
    here, there = halves(size // PAIR)
    keep[...] = normed[here, :]
    send[...] = normed[there, :]


def inner_grad_kernel(q2, kc2, v2, grad, weights, cum, before, partial, key_grad, first):
    size, width = q2.shape
    dim = before.shape[1]
    heads = width // dim
    cum_rows = cum[...]
    cols = cum_rows.T
    growth = jnp.exp(cols)
    for h in range(heads):
        lanes = slice(h * dim, (h + 1) * dim)
        d = grad[:, lanes]
        scores = dot(d, v2[:, lanes], (1, 1)) * mixing_of(cum_rows, cols, h, size)
        scores = scores.astype(BF16)
        query_grad = dot(scores, kc2[:, lanes], (1, 0)) + growth[:, h : h + 1] * dot(
            d, before[lanes, :], (1, 1)
        )
        key_grad[:, lanes] = dot(scores, q2[:, lanes], (0, 0))
        partial[:, lanes] = query_grad + dot(weights[h], d, (0, 0))
    first[...] = key_grad[: first.shape[0], :]


def outer_grad_kernel(partial, key_grad, follow, kc2, v2, cum, behind, taps, keep, send, padded, done):
    size, width = partial.shape
    dim = behind.shape[1]
    heads = width // dim
    own, _ = halves(width)
    cols = cum[...].T
    after = jnp.exp(cols[size - 1 :, :] - cols)
    padded[size:, :] = follow[...]
    for h in range(heads):
        lanes = slice(h * dim, (h + 1) * dim)
        scale = after[:, h : h + 1]
        padded[:size, lanes] = key_grad[:, lanes] + scale * dot(
            v2[:, lanes], behind[lanes, :], (1, 1)
        )
        done[:, lanes] = partial[:, lanes] + scale * dot(kc2[:, lanes], behind[lanes, :], (1, 0))
    total = done[...]
    for j in range(taps.shape[1]):
        total = total + taps[0, j : j + 1, own] * padded[j : j + size, :]
    done[...] = total
    here, there = halves(size // PAIR)
    keep[...] = done[here, :].astype(BF16)
    send[...] = done[there, :].astype(BF16)


def place_kernel(kept, got, out):
    width = kept.shape[1]
    own, other = halves(width)
    out[0, :, own] = kept[...]
    out[0, :, other] = got[...]


def shifted(block, axis, distance):
    devices = range(lax.axis_size(axis))
    return lax.ppermute(block, axis, [(i - distance, i) for i in devices if i - distance in devices])


def swapped(block):
    return lax.ppermute(block, "ctx", [(i, i ^ 1) for i in range(lax.axis_size("ctx"))])


def to_earlier_section(block, flip):
    blocks, sections = lax.axis_size("ctx"), lax.axis_size("pp")
    route = [
        (c * sections + p, (c ^ flip) * sections + p - 1)
        for c in range(blocks)
        for p in range(1, sections)
    ]
    return lax.ppermute(block, ("ctx", "pp"), route)


def summed_parts(part):
    count = lax.axis_size("tp")
    pair = part + lax.ppermute(part, "tp", [(i, i ^ 1) for i in range(count)])
    parts = [pair]
    for k in range(2, count, 2):
        parts.append(lax.ppermute(pair, "tp", [(i, i ^ k) for i in range(count)]))
    total = sum(parts[1:]) + parts[0]
    return [total, swapped(total)]


def per_device(queries, key_input, values, log_decay, conv_weight, out_grad):
    rows, width = queries.shape[1], queries.shape[2] // PAIR
    heads = log_decay.shape[2] // PAIR
    dim = width // heads
    size = PAIR * rows
    supers = lax.axis_size("ctx") // PAIR
    width_all = queries.shape[2] * lax.axis_size("tp")
    ctx = lax.axis_size("ctx")

    edge = key_input[0, rows - EDGE :]
    near = lax.ppermute(edge[:, :width], "ctx", [(i, i + 1) for i in range(1, ctx - 1, 2)])
    far = lax.ppermute(edge[:, width:], "ctx", [(i, i + 2) for i in range(1, ctx - 2, 2)])
    edge = near + far

    bundle = call(
        pack_kernel,
        [shape((4 * rows + EDGE, width), BF16)],
        queries, key_input, values, out_grad, log_decay,
    )[0]
    got = swapped(bundle)
    q2, kc2, v2, g2, cum, state = call(
        join_kernel,
        [shape((size, width), BF16)] * 4 + [shape((8, size), F32), shape((width, dim), BF16)],
        got, edge, queries, key_input, values, out_grad, log_decay, conv_weight,
        scratch=[pltpu.VMEM((EDGE + size, width), F32), pltpu.VMEM((8, size), F32)],
    )
    carry = jnp.repeat(jnp.exp(cum[:heads, -1]), dim)[:, None]
    before = shifted(state, "ctx", PAIR)
    for _ in range(supers - 2):
        joined = state.astype(F32) + carry * before.astype(F32)
        before = shifted(joined.astype(BF16), "ctx", PAIR)

    weights, inside = call(
        local_kernel,
        [shape((heads, size, size), BF16), shape((size, width), F32)],
        q2, kc2, v2, cum,
        flops=4 * heads * size * size * dim,
    )
    attended, sums = call(
        attend_kernel,
        [shape((size, width), F32), shape((2, size), F32)],
        inside, q2, g2, cum, before,
    )
    parts = summed_parts(sums)
    keep, send, grad, adjoint = call(
        lambda *refs: grad_kernel(width_all, len(parts), *refs),
        [shape((rows, width), BF16)] * 2 + [shape((size, width), BF16), shape((width, dim), BF16)],
        attended, q2, g2, cum, *parts,
        scratch=[pltpu.VMEM((size, width), BF16)],
    )
    behind = shifted(adjoint, "ctx", -PAIR)
    for _ in range(supers - 2):
        joined = adjoint.astype(F32) + carry * behind.astype(F32)
        behind = shifted(joined.astype(BF16), "ctx", -PAIR)

    partial, key_grad, first = call(
        inner_grad_kernel,
        [shape((size, width), F32)] * 2 + [shape((8, width), F32)],
        q2, kc2, v2, grad, weights, cum, before,
        flops=10 * heads * size * size * dim,
    )
    if supers > 2:
        after = jnp.exp(cum[:heads, -1:] - cum[:heads, :8])
        state_part = jnp.einsum(
            "shv,hkv->shk",
            v2[:8].reshape(8, heads, dim),
            behind.reshape(heads, dim, dim),
            preferred_element_type=F32,
        )
        first = first + (after.T[:, :, None] * state_part).reshape(8, width)
    follow = shifted(first, "ctx", -PAIR)
    layer_output = call(
        place_kernel, [shape((1, rows, PAIR * width), BF16)], keep, swapped(send)
    )[0]
    keep, send = call(
        outer_grad_kernel,
        [shape((rows, width), BF16)] * 2,
        partial, key_grad, follow, kc2, v2, cum, behind, conv_weight,
        scratch=[pltpu.VMEM((size + 8, width), F32), pltpu.VMEM((size, width), F32)],
    )
    input_next = call(
        place_kernel,
        [shape((1, rows, PAIR * width), BF16)],
        to_earlier_section(keep, 0), to_earlier_section(send, 1),
    )[0]
    return (layer_output, input_next)


def solution(mesh):
    placed = (
        P("pp", "ctx", "tp"),
        P("pp", "ctx", "tp"),
        P("pp", "ctx", "tp"),
        P("pp", "ctx", "tp"),
        P("pp", None, "tp"),
        P("pp", "ctx", "tp"),
    )
    return jax.shard_map(
        per_device,
        mesh=mesh,
        in_specs=placed,
        out_specs=(P("pp", "ctx", "tp"), P("pp", "ctx", "tp")),
        check_vma=False,
    )
```

time: 138 us -> 61.2 us (0.44)
  waiting for transfers between devices: 61.1 us -> 26.9 us
  blocking collectives: 31.6 us -> 0 us
  starting transfers between devices: 7.58 us -> 21.4 us
  between operations: 14.3 us -> 0.78 us
  other arithmetic: 10.1 us -> 0.02 us
  Pallas kernels: 0 us -> 7.07 us
  matrix products: 5.83 us -> 0 us
  local copies, waits for them, and re-layouts: 6.67 us -> 4.6 us
    all_gather x2 -> x0, waiting for transfers between devices: 51.8 us -> none  [the longest x1 35.1 us: entering(): everything = jax.tree.map(lambda part: lax.all_gather(part, axis), value)]
    all_gather x2 -> x0, blocking collectives: 18.8 us -> none  [the longest x1 10.2 us: entering(): everything = jax.tree.map(lambda part: lax.all_gather(part, axis), value)]
    ppermute x3 -> x12, waiting for transfers between devices: 9.25 us -> 26.9 us  [the longest x3 12.4 us: swapped(): lax.ppermute(block, 'ctx', [(i, i ^ 1) for i in range(lax.axis_size('ctx'...]
    ppermute x3 -> x12, starting transfers between devices: 7.5 us -> 21.4 us  [the longest x3 8.8 us: swapped(): lax.ppermute(block, 'ctx', [(i, i ^ 1) for i in range(lax.axis_size('ctx'...]
    psum x2 -> x0, blocking collectives: 12.8 us -> none  [the longest x1 6.87 us: per_device(): squares_all = lax.psum(squares_local, 'tp')]
    pallas_call x0 -> x9, Pallas kernels: none -> 7.07 us  [call(): pl.pallas_call(kernel, out_shape=outs, in_specs=[vmem] * len(args), out_s...]
    dot_general x12 -> x0, matrix products: 5.83 us -> none  [the longest x1 1.17 us: per_device(): jnp.einsum('hts,shk->thk', score_grad, smoothed_key_rows, preferred_eleme...]
    select_n x4 -> x0, other arithmetic: 4.69 us -> none  [step(): return jax.tree.map(lambda a, b: jnp.where(reached, a, b), new, before)]
  transfers between devices with their start and end apart: 5 -> 12, of which waited for: 4 -> 8; matrix products, arithmetic and copies ran while one was open for 5% -> 0% of each run, Pallas kernels for 0% -> 6%
where the time goes in v1:
time: 61.2 us; the launch traced here: 60.8 us
  waiting for transfers between devices  26.9 us (44%)
  starting transfers between devices  21.4 us (35%)
  Pallas kernels  7.07 us (12%)
  local copies, waits for them, and re-layouts  4.6 us (8%)
  between operations  0.78 us (1%)
    ppermute x3, waiting for transfers between devices, swapped(): lax.ppermute(block, 'ctx', [(i, i ^ 1) for i in range(lax.axis_size('ctx'...  12.4 us
    ppermute x3, starting transfers between devices, swapped(): lax.ppermute(block, 'ctx', [(i, i ^ 1) for i in range(lax.axis_size('ctx'...  8.8 us
    ppermute x3, starting transfers between devices, shifted(): lax.ppermute(block, axis, [(i - distance, i) for i in devices if i - dist...  7.25 us
    pallas_call x9, Pallas kernels, call(): pl.pallas_call(kernel, out_shape=outs, in_specs=[vmem] * len(args), out_s...  7.07 us
    ppermute x2, waiting for transfers between devices, to_earlier_section(): return lax.ppermute(block, ('ctx', 'pp'), route)  6.12 us
    ppermute x3, waiting for transfers between devices, shifted(): lax.ppermute(block, axis, [(i - distance, i) for i in devices if i - dist...  5.06 us
    unnamed x11, local copies, waits for them, and re-layouts  4.59 us
    ppermute x2, starting transfers between devices, to_earlier_section(): return lax.ppermute(block, ('ctx', 'pp'), route)  2.58 us
  transfers between devices with their start and end apart: 12, of which 8 were waited for; matrix products, arithmetic and copies ran while one was open for 0% of the time, Pallas kernels for 6%

profile of v1, /device:TPU:0, one launch (start us, length us, event | category | flops | bytes accessed | tf_op | source)
XLA Modules:
  0.0 60.8 jit_solution(12629948374431269199)
XLA Ops:
  0.6 0.8 %copy.8.log_decay = f32[1,128,8]{2,1,0:T(8,128)S(1)} copy(f32[1,128,8]{1,2,0:T(8,128)} %param.9) | data formatting | bytes 8192 | tf_op args[3]
  1.4 0.0 copy-start
  1.4 0.9 %copy-done = bf16[1,128,1024]{2,1,0:T(8,128)(2,1)S(1)} copy-done((bf16[1,128,1024]{2,1,0:T(8,128)(2,1)S(1)}, bf16[1,128,1024]{2,1,0:T(8,128)(2,1)}, u32[]{:S(2)}) %copy-start) | copy-done | bytes 262168
  2.4 0.0 copy-start.1
  2.4 0.9 %copy-done.1 = bf16[1,128,1024]{2,1,0:T(8,128)(2,1)S(1)} copy-done((bf16[1,128,1024]{2,1,0:T(8,128)(2,1)S(1)}, bf16[1,128,1024]{2,1,0:T(8,128)(2,1)}, u32[]{:S(2)}) %copy-start.1) | copy-done | bytes 262168
  3.3 0.0 copy-start.2
  3.3 0.9 %copy-done.2 = bf16[1,128,1024]{2,1,0:T(8,128)(2,1)S(1)} copy-done((bf16[1,128,1024]{2,1,0:T(8,128)(2,1)S(1)}, bf16[1,128,1024]{2,1,0:T(8,128)(2,1)}, u32[]{:S(2)}) %copy-start.2) | copy-done | bytes 262168
  4.3 0.0 copy-start.3
  4.3 0.9 %copy-done.3 = bf16[1,128,1024]{2,1,0:T(8,128)(2,1)S(1)} copy-done((bf16[1,128,1024]{2,1,0:T(8,128)(2,1)S(1)}, bf16[1,128,1024]{2,1,0:T(8,128)(2,1)}, u32[]{:S(2)}) %copy-start.3) | copy-done | bytes 262168
  5.2 0.1 shard_map.77
  5.3 3.1 %collective-permute-start = (bf16[528,512]{1,0:T(8,128)(2,1)S(1)}, bf16[528,512]{1,0:T(8,128)(2,1)S(1)}, u32[]{:S(2)}, u32[]{:S(2)}) collective-permute-start(bf16[528,512]{1,0:T(8,128)(2,1)S(1)} %shard_map.77), channel_id=1, source_target_pairs={{0,8},{8,0},{16,24},{24,16},{1,9},{9,1},{17,25},{25,17},{2,10},{10... | collective-permute-start | bytes 1622024 | tf_op jit(solution)/shard_map/ppermute | solution.py:245
  8.4 0.7 %collective-permute-start.2 = (bf16[16,512]{1,0:T(8,128)(2,1)S(1)}, bf16[16,512]{1,0:T(8,128)(2,1)S(1)}, u32[]{:S(2)}, u32[]{:S(2)}) collective-permute-start(bf16[16,512]{1,0:T(8,128)(2,1)S(1)} %get-tuple-element.40), channel_id=1, source_target_pairs={{8,24},{9,25},{10,26},{11,27},{12,28},{13,29},{14,30},{15,31}} | collective-permute-start | bytes 49160 | tf_op jit(solution)/shard_map/ppermute | solution.py:279
  9.1 0.0 copy-start.4
  9.1 0.7 %collective-permute-start.1 = (bf16[16,512]{1,0:T(8,128)(2,1)S(1)}, bf16[16,512]{1,0:T(8,128)(2,1)S(1)}, u32[]{:S(2)}, u32[]{:S(2)}) collective-permute-start(bf16[16,512]{1,0:T(8,128)(2,1)S(1)} %get-tuple-element.41), channel_id=1, source_target_pairs={{8,16},{9,17},{10,18},{11,19},{12,20},{13,21},{14,22},{15,23}} | collective-permute-start | bytes 49160 | tf_op jit(solution)/shard_map/ppermute | solution.py:278
  9.7 0.0 collective-permute-done.2
  9.8 0.0 collective-permute-done.1
  9.8 10.9 %collective-permute-done.got = bf16[528,512]{1,0:T(8,128)(2,1)S(1)} collective-permute-done((bf16[528,512]{1,0:T(8,128)(2,1)S(1)}, bf16[528,512]{1,0:T(8,128)(2,1)S(1)}, u32[]{:S(2)}, u32[]{:S(2)}) %collective-permute-start) | collective-permute-done | bytes 540704 | tf_op jit(solution)/shard_map/ppermute | solution.py:245
  20.7 0.0 copy-done.4
  20.7 1.1 %shard_map.78 = (bf16[256,512]{1,0:T(8,128)(2,1)S(1)}, bf16[256,512]{1,0:T(8,128)(2,1)S(1)}, bf16[256,512]{1,0:T(8,128)(2,1)S(1)}, bf16[256,512]{1,0:T(8,128)(2,...) custom-call(bf16[528,512]{1,0:T(8,128)(2,1)S(1)} %collective-permute-done.got, bf16[16,512]{1,0:T(8,128)(2,1)S(1)} %add.9.edge, ...), custom_call_target="tpu_custom_call" | custom-call | bytes 2813952 | tf_op jit(solution)/shard_map/pallas_call | solution.py:19
  21.8 4.7 %collective-permute-start.3 = (bf16[512,128]{1,0:T(8,128)(2,1)S(1)}, bf16[512,128]{1,0:T(8,128)(2,1)S(1)}, u32[]{:S(2)}, u32[]{:S(2)}) collective-permute-start(bf16[512,128]{1,0:T(8,128)(2,1)S(1)} %get-tuple-element.27), channel_id=1, source_target_pairs={{0,16},{8,24},{1,17},{9,25},{2,18},{10,26},{3,19},{11,27},{4,20},{... | collective-permute-start | bytes 393224 | tf_op jit(solution)/shard_map/ppermute | solution.py:241
  26.4 0.8 %shard_map.79 = (bf16[4,256,256]{2,1,0:T(8,128)(2,1)S(1)}, f32[256,512]{1,0:T(8,128)S(1)}) custom-call(bf16[256,512]{1,0:T(8,128)(2,1)S(1)} %get-tuple-element.21.q2.refs_1_, bf16[256,512]{1,0:T(8,128)(2,1)S(1)} %get-tuple-element.22.kc2, bf16[256,512]{1,0:T(8,128)(2,1)S(1)} %get-tuple-element.23.v2, f32[8,256]{1,0:T(8,128)S(1)} %get-tuple-element.24.cum.refs_3_), custom_call_target="tpu_custom_call" | custom-call | flops 134217728 | bytes 1843200 | tf_op jit(solution)/shard_map/pallas_call | solution.py:19
  27.2 1.7 %collective-permute-done.3.before = bf16[512,128]{1,0:T(8,128)(2,1)S(1)} collective-permute-done((bf16[512,128]{1,0:T(8,128)(2,1)S(1)}, bf16[512,128]{1,0:T(8,128)(2,1)S(1)}, u32[]{:S(2)}, u32[]{:S(2)}) %collective-permute-start.3) | collective-permute-done | bytes 131104 | tf_op jit(solution)/shard_map/ppermute | solution.py:241
  29.0 0.7 %shard_map.80 = (f32[256,512]{1,0:T(8,128)S(1)}, f32[2,256]{1,0:T(2,128)S(1)}) custom-call(f32[256,512]{1,0:T(8,128)S(1)} %get-tuple-element.25.inside, bf16[256,512]{1,0:T(8,128)(2,1)S(1)} %get-tuple-element.21.q2.refs_1_, bf16[256,512]{1,0:T(8,128)(2,1)S(1)} %get-tuple-element.26.g2.refs_2_, f32[8,256]{1,0:T(8,128)S(1)} %get-tuple-element.24.cum.refs_3_, ...), custom_call_target="tpu_custom_call" | custom-call | bytes 1714176 | tf_op jit(solution)/shard_map/pallas_call | solution.py:19
  29.7 0.0 collective-permute-start.4
  29.7 1.2 %collective-permute-done.4 = f32[2,256]{1,0:T(2,128)S(1)} collective-permute-done((f32[2,256]{1,0:T(2,128)S(1)}, f32[2,256]{1,0:T(2,128)S(1)}, u32[]{:S(2)}, u32[]{:S(2)}) %collective-permute-start.4) | collective-permute-done | bytes 2080 | tf_op jit(solution)/shard_map/ppermute | solution.py:260
  30.9 1.5 %collective-permute-start.5 = (f32[2,256]{1,0:T(2,128)S(1)}, f32[2,256]{1,0:T(2,128)S(1)}, u32[]{:S(2)}, u32[]{:S(2)}) collective-permute-start(f32[2,256]{1,0:T(2,128)S(1)} %add.10), channel_id=1, source_target_pairs={{0,4},{2,6},{4,0},{6,2},{1,5},{3,7},{5,1},{7,3},{8,12},{10,14},{12... | collective-permute-start | bytes 6152 | tf_op jit(solution)/shard_map/ppermute | solution.py:263
  32.4 2.1 %collective-permute-done.5 = f32[2,256]{1,0:T(2,128)S(1)} collective-permute-done((f32[2,256]{1,0:T(2,128)S(1)}, f32[2,256]{1,0:T(2,128)S(1)}, u32[]{:S(2)}, u32[]{:S(2)}) %collective-permute-start.5) | collective-permute-done | bytes 2080 | tf_op jit(solution)/shard_map/ppermute | solution.py:263
  34.5 3.6 %collective-permute-start.6 = (f32[2,256]{1,0:T(2,128)S(1)}, f32[2,256]{1,0:T(2,128)S(1)}, u32[]{:S(2)}, u32[]{:S(2)}) collective-permute-start(f32[2,256]{1,0:T(2,128)S(1)} %add.11.refs_4_), channel_id=1, source_target_pairs={{0,8},{8,0},{16,24},{24,16},{1,9},{9,1},{17,25},{25,17},{2,10},{10... | collective-permute-start | bytes 6152 | tf_op jit(solution)/shard_map/ppermute | solution.py:245
  38.1 1.6 %collective-permute-done.6.refs_5_ = f32[2,256]{1,0:T(2,128)S(1)} collective-permute-done((f32[2,256]{1,0:T(2,128)S(1)}, f32[2,256]{1,0:T(2,128)S(1)}, u32[]{:S(2)}, u32[]{:S(2)}) %collective-permute-start.6) | collective-permute-done | bytes 2080 | tf_op jit(solution)/shard_map/ppermute | solution.py:245
  39.6 0.8 %shard_map.81 = (bf16[128,512]{1,0:T(8,128)(2,1)S(1)}, bf16[128,512]{1,0:T(8,128)(2,1)S(1)}, bf16[256,512]{1,0:T(8,128)(2,1)S(1)}, bf16[512,128]{1,0:T(8,128)(2,1)S(1)}) custom-call(f32[256,512]{1,0:T(8,128)S(1)} %get-tuple-element.28.refs_0_, bf16[256,512]{1,0:T(8,128)(2,1)S(1)} %get-tuple-element.21.q2.refs_1_, ...), custom_call_target="tpu_custom_call" | custom-call | bytes 1716224 | tf_op jit(solution)/shard_map/pallas_call | solution.py:19
  40.5 1.3 %collective-permute-start.9 = (bf16[512,128]{1,0:T(8,128)(2,1)S(1)}, bf16[512,128]{1,0:T(8,128)(2,1)S(1)}, u32[]{:S(2)}, u32[]{:S(2)}) collective-permute-start(bf16[512,128]{1,0:T(8,128)(2,1)S(1)} %get-tuple-element.37), channel_id=1, source_target_pairs={{16,0},{24,8},{17,1},{25,9},{18,2},{26,10},{19,3},{27,11},{20,4},{... | collective-permute-start | bytes 393224 | tf_op jit(solution)/shard_map/ppermute | solution.py:241
  41.8 1.4 %shard_map.83 = (f32[256,512]{1,0:T(8,128)S(1)}, f32[256,512]{1,0:T(8,128)S(1)}, f32[8,512]{1,0:T(8,128)S(1)}) custom-call(bf16[256,512]{1,0:T(8,128)(2,1)S(1)} %get-tuple-element.21.q2.refs_1_, bf16[256,512]{1,0:T(8,128)(2,1)S(1)} %get-tuple-element.22.kc2, bf16[256,512]{1,0:T(8,128)(2,1)S(1)} %get-tuple-element.23.v2, ...), custom_call_target="tpu_custom_call" | custom-call | flops 335544320 | bytes 2777088 | tf_op jit(solution)/shard_map/pallas_call | solution.py:19
  43.3 1.3 %collective-permute-start.8 = (f32[8,512]{1,0:T(8,128)S(1)}, f32[8,512]{1,0:T(8,128)S(1)}, u32[]{:S(2)}, u32[]{:S(2)}) collective-permute-start(f32[8,512]{1,0:T(8,128)S(1)} %get-tuple-element.36), channel_id=1, source_target_pairs={{16,0},{24,8},{17,1},{25,9},{18,2},{26,10},{19,3},{27,11},{20,4},{... | collective-permute-start | bytes 49160 | tf_op jit(solution)/shard_map/ppermute | solution.py:241
  44.6 2.1 %collective-permute-start.7 = (bf16[128,512]{1,0:T(8,128)(2,1)S(1)}, bf16[128,512]{1,0:T(8,128)(2,1)S(1)}, u32[]{:S(2)}, u32[]{:S(2)}) collective-permute-start(bf16[128,512]{1,0:T(8,128)(2,1)S(1)} %get-tuple-element.31), channel_id=1, source_target_pairs={{0,8},{8,0},{16,24},{24,16},{1,9},{9,1},{17,25},{25,17},{2,10},{10... | collective-permute-start | bytes 393224 | tf_op jit(solution)/shard_map/ppermute | solution.py:245
  46.6 3.3 %collective-permute-done.8.follow = f32[8,512]{1,0:T(8,128)S(1)} collective-permute-done((f32[8,512]{1,0:T(8,128)S(1)}, f32[8,512]{1,0:T(8,128)S(1)}, u32[]{:S(2)}, u32[]{:S(2)}) %collective-permute-start.8) | collective-permute-done | bytes 16416 | tf_op jit(solution)/shard_map/ppermute | solution.py:241
  50.0 0.0 collective-permute-done.9.behind
  50.0 0.7 %shard_map.84 = (bf16[128,512]{1,0:T(8,128)(2,1)S(1)}, bf16[128,512]{1,0:T(8,128)(2,1)S(1)}) custom-call(f32[256,512]{1,0:T(8,128)S(1)} %get-tuple-element.34.partial, f32[256,512]{1,0:T(8,128)S(1)} %get-tuple-element.35.key_grad, f32[8,512]{1,0:T(8,128)S(1)} %collective-permute-done.8.follow, bf16[256,512]{1,0:T(8,128)(2,1)S(1)} %get-tuple-element.22.kc2, ...), custom_call_target="tpu_custom_call" | custom-call | bytes 2007040 | tf_op jit(solution)/shard_map/pallas_call | solution.py:19
  50.6 1.3 %collective-permute-start.10 = (bf16[128,512]{1,0:T(8,128)(2,1)S(1)}, bf16[128,512]{1,0:T(8,128)(2,1)S(1)}, u32[]{:S(2)}, u32[]{:S(2)}) collective-permute-start(bf16[128,512]{1,0:T(8,128)(2,1)S(1)} %get-tuple-element.38), channel_id=1, source_target_pairs={{1,0},{9,8},{17,16},{25,24},{3,2},{11,10},{19,18},{27,26},{5,4},{1... | collective-permute-start | bytes 393224 | tf_op jit(solution)/shard_map/ppermute | solution.py:255
  51.9 1.3 %collective-permute-start.11 = (bf16[128,512]{1,0:T(8,128)(2,1)S(1)}, bf16[128,512]{1,0:T(8,128)(2,1)S(1)}, u32[]{:S(2)}, u32[]{:S(2)}) collective-permute-start(bf16[128,512]{1,0:T(8,128)(2,1)S(1)} %get-tuple-element.39), channel_id=1, source_target_pairs={{1,8},{9,0},{17,24},{25,16},{3,10},{11,2},{19,26},{27,18},{5,12},{... | collective-permute-start | bytes 393224 | tf_op jit(solution)/shard_map/ppermute | solution.py:255
  53.2 0.0 collective-permute-done.7.got
  53.2 0.7 %shard_map.82 = bf16[1,128,1024]{2,1,0:T(8,128)(2,1)} custom-call(bf16[128,512]{1,0:T(8,128)(2,1)S(1)} %get-tuple-element.30.kept, bf16[128,512]{1,0:T(8,128)(2,1)S(1)} %collective-permute-done.7.got), custom_call_target="tpu_custom_call" | custom-call | bytes 524288 | tf_op jit(solution)/shard_map/pallas_call | solution.py:19
  54.0 3.7 %collective-permute-done.10.kept = bf16[128,512]{1,0:T(8,128)(2,1)S(1)} collective-permute-done((bf16[128,512]{1,0:T(8,128)(2,1)S(1)}, bf16[128,512]{1,0:T(8,128)(2,1)S(1)}, u32[]{:S(2)}, u32[]{:S(2)}) %collective-permute-start.10) | collective-permute-done | bytes 131104 | tf_op jit(solution)/shard_map/ppermute | solution.py:255
  57.6 2.5 %collective-permute-done.11.got = bf16[128,512]{1,0:T(8,128)(2,1)S(1)} collective-permute-done((bf16[128,512]{1,0:T(8,128)(2,1)S(1)}, bf16[128,512]{1,0:T(8,128)(2,1)S(1)}, u32[]{:S(2)}, u32[]{:S(2)}) %collective-permute-start.11) | collective-permute-done | bytes 131104 | tf_op jit(solution)/shard_map/ppermute | solution.py:255
  60.1 0.7 %shard_map.85 = bf16[1,128,1024]{2,1,0:T(8,128)(2,1)} custom-call(bf16[128,512]{1,0:T(8,128)(2,1)S(1)} %collective-permute-done.10.kept, bf16[128,512]{1,0:T(8,128)(2,1)S(1)} %collective-permute-done.11.got), custom_call_target="tpu_custom_call" | custom-call | bytes 524288 | tf_op jit(solution)/shard_map/pallas_call | solution.py:19
  (5 shorter events, 0.0 us)
Async XLA Ops:
  1.4 0.9 %copy-start = (bf16[1,128,1024]{2,1,0:T(8,128)(2,1)S(1)}, bf16[1,128,1024]{2,1,0:T(8,128)(2,1)}, u32[]{:S(2)}) copy-start(bf16[1,128,1024]{2,1,0:T(8,128)(2,1)} %k.3) | copy-start | bytes 786436
  2.4 0.9 %copy-start.1 = (bf16[1,128,1024]{2,1,0:T(8,128)(2,1)S(1)}, bf16[1,128,1024]{2,1,0:T(8,128)(2,1)}, u32[]{:S(2)}) copy-start(bf16[1,128,1024]{2,1,0:T(8,128)(2,1)} %q.3) | copy-start | bytes 786436
  3.3 0.9 %copy-start.2 = (bf16[1,128,1024]{2,1,0:T(8,128)(2,1)S(1)}, bf16[1,128,1024]{2,1,0:T(8,128)(2,1)}, u32[]{:S(2)}) copy-start(bf16[1,128,1024]{2,1,0:T(8,128)(2,1)} %v.3) | copy-start | bytes 786436
  4.3 0.9 %copy-start.3 = (bf16[1,128,1024]{2,1,0:T(8,128)(2,1)S(1)}, bf16[1,128,1024]{2,1,0:T(8,128)(2,1)}, u32[]{:S(2)}) copy-start(bf16[1,128,1024]{2,1,0:T(8,128)(2,1)} %g.3) | copy-start | bytes 786436
  5.3 15.4 %collective-permute-start = (bf16[528,512]{1,0:T(8,128)(2,1)S(1)}, bf16[528,512]{1,0:T(8,128)(2,1)S(1)}, u32[]{:S(2)}, u32[]{:S(2)}) collective-permute-start(bf16[528,512]{1,0:T(8,128)(2,1)S(1)} %shard_map.77), channel_id=1, source_target_pairs={{0,8},{8,0},{16,24},{24,16},{1,9},{9,1},{17,25},{25,17},{2,10},{10... | collective-permute-start | bytes 1622024 | tf_op jit(solution)/shard_map/ppermute | solution.py:245
  8.4 1.3 %collective-permute-start.2 = (bf16[16,512]{1,0:T(8,128)(2,1)S(1)}, bf16[16,512]{1,0:T(8,128)(2,1)S(1)}, u32[]{:S(2)}, u32[]{:S(2)}) collective-permute-start(bf16[16,512]{1,0:T(8,128)(2,1)S(1)} %get-tuple-element.40), channel_id=1, source_target_pairs={{8,24},{9,25},{10,26},{11,27},{12,28},{13,29},{14,30},{15,31}} | collective-permute-start | bytes 49160 | tf_op jit(solution)/shard_map/ppermute | solution.py:279
  9.1 11.6 %copy-start.4 = (f32[1,4,1024]{2,1,0:T(4,128)S(1)}, f32[1,4,1024]{2,1,0:T(4,128)}, u32[]{:S(2)}) copy-start(f32[1,4,1024]{2,1,0:T(4,128)} %taps.3) | copy-start | bytes 49156
  9.1 0.7 %collective-permute-start.1 = (bf16[16,512]{1,0:T(8,128)(2,1)S(1)}, bf16[16,512]{1,0:T(8,128)(2,1)S(1)}, u32[]{:S(2)}, u32[]{:S(2)}) collective-permute-start(bf16[16,512]{1,0:T(8,128)(2,1)S(1)} %get-tuple-element.41), channel_id=1, source_target_pairs={{8,16},{9,17},{10,18},{11,19},{12,20},{13,21},{14,22},{15,23}} | collective-permute-start | bytes 49160 | tf_op jit(solution)/shard_map/ppermute | solution.py:278
  21.8 7.2 %collective-permute-start.3 = (bf16[512,128]{1,0:T(8,128)(2,1)S(1)}, bf16[512,128]{1,0:T(8,128)(2,1)S(1)}, u32[]{:S(2)}, u32[]{:S(2)}) collective-permute-start(bf16[512,128]{1,0:T(8,128)(2,1)S(1)} %get-tuple-element.27), channel_id=1, source_target_pairs={{0,16},{8,24},{1,17},{9,25},{2,18},{10,26},{3,19},{11,27},{4,20},{... | collective-permute-start | bytes 393224 | tf_op jit(solution)/shard_map/ppermute | solution.py:241
  29.7 1.2 %collective-permute-start.4 = (f32[2,256]{1,0:T(2,128)S(1)}, f32[2,256]{1,0:T(2,128)S(1)}, u32[]{:S(2)}, u32[]{:S(2)}) collective-permute-start(f32[2,256]{1,0:T(2,128)S(1)} %get-tuple-element.29), channel_id=1, source_target_pairs={{0,2},{2,0},{4,6},{6,4},{1,3},{3,1},{5,7},{7,5},{8,10},{10,8},{12,... | collective-permute-start | bytes 6152 | tf_op jit(solution)/shard_map/ppermute | solution.py:260
  30.9 3.6 %collective-permute-start.5 = (f32[2,256]{1,0:T(2,128)S(1)}, f32[2,256]{1,0:T(2,128)S(1)}, u32[]{:S(2)}, u32[]{:S(2)}) collective-permute-start(f32[2,256]{1,0:T(2,128)S(1)} %add.10), channel_id=1, source_target_pairs={{0,4},{2,6},{4,0},{6,2},{1,5},{3,7},{5,1},{7,3},{8,12},{10,14},{12... | collective-permute-start | bytes 6152 | tf_op jit(solution)/shard_map/ppermute | solution.py:263
  34.5 5.2 %collective-permute-start.6 = (f32[2,256]{1,0:T(2,128)S(1)}, f32[2,256]{1,0:T(2,128)S(1)}, u32[]{:S(2)}, u32[]{:S(2)}) collective-permute-start(f32[2,256]{1,0:T(2,128)S(1)} %add.11.refs_4_), channel_id=1, source_target_pairs={{0,8},{8,0},{16,24},{24,16},{1,9},{9,1},{17,25},{25,17},{2,10},{10... | collective-permute-start | bytes 6152 | tf_op jit(solution)/shard_map/ppermute | solution.py:245
  40.5 9.5 %collective-permute-start.9 = (bf16[512,128]{1,0:T(8,128)(2,1)S(1)}, bf16[512,128]{1,0:T(8,128)(2,1)S(1)}, u32[]{:S(2)}, u32[]{:S(2)}) collective-permute-start(bf16[512,128]{1,0:T(8,128)(2,1)S(1)} %get-tuple-element.37), channel_id=1, source_target_pairs={{16,0},{24,8},{17,1},{25,9},{18,2},{26,10},{19,3},{27,11},{20,4},{... | collective-permute-start | bytes 393224 | tf_op jit(solution)/shard_map/ppermute | solution.py:241
  43.3 6.7 %collective-permute-start.8 = (f32[8,512]{1,0:T(8,128)S(1)}, f32[8,512]{1,0:T(8,128)S(1)}, u32[]{:S(2)}, u32[]{:S(2)}) collective-permute-start(f32[8,512]{1,0:T(8,128)S(1)} %get-tuple-element.36), channel_id=1, source_target_pairs={{16,0},{24,8},{17,1},{25,9},{18,2},{26,10},{19,3},{27,11},{20,4},{... | collective-permute-start | bytes 49160 | tf_op jit(solution)/shard_map/ppermute | solution.py:241
  44.6 8.7 %collective-permute-start.7 = (bf16[128,512]{1,0:T(8,128)(2,1)S(1)}, bf16[128,512]{1,0:T(8,128)(2,1)S(1)}, u32[]{:S(2)}, u32[]{:S(2)}) collective-permute-start(bf16[128,512]{1,0:T(8,128)(2,1)S(1)} %get-tuple-element.31), channel_id=1, source_target_pairs={{0,8},{8,0},{16,24},{24,16},{1,9},{9,1},{17,25},{25,17},{2,10},{10... | collective-permute-start | bytes 393224 | tf_op jit(solution)/shard_map/ppermute | solution.py:245
  50.6 7.0 %collective-permute-start.10 = (bf16[128,512]{1,0:T(8,128)(2,1)S(1)}, bf16[128,512]{1,0:T(8,128)(2,1)S(1)}, u32[]{:S(2)}, u32[]{:S(2)}) collective-permute-start(bf16[128,512]{1,0:T(8,128)(2,1)S(1)} %get-tuple-element.38), channel_id=1, source_target_pairs={{1,0},{9,8},{17,16},{25,24},{3,2},{11,10},{19,18},{27,26},{5,4},{1... | collective-permute-start | bytes 393224 | tf_op jit(solution)/shard_map/ppermute | solution.py:255
  51.9 8.2 %collective-permute-start.11 = (bf16[128,512]{1,0:T(8,128)(2,1)S(1)}, bf16[128,512]{1,0:T(8,128)(2,1)S(1)}, u32[]{:S(2)}, u32[]{:S(2)}) collective-permute-start(bf16[128,512]{1,0:T(8,128)(2,1)S(1)} %get-tuple-element.39), channel_id=1, source_target_pairs={{1,8},{9,0},{17,24},{25,16},{3,10},{11,2},{19,26},{27,18},{5,12},{... | collective-permute-start | bytes 393224 | tf_op jit(solution)/shard_map/ppermute | solution.py:255

commit v2 on v1

v2 whole, which is shorter than its diff:
```python
import jax
import jax.numpy as jnp
from jax import lax
from jax.experimental import pallas as pl
from jax.experimental.pallas import tpu as pltpu
from jax.sharding import PartitionSpec as P

F32 = jnp.float32
BF16 = jnp.bfloat16
PAIR = 2
EDGE = 16


def call(kernel, outs, *args, scratch=(), flops=0, hbm=(), out_hbm=False):
    vmem = pl.BlockSpec(memory_space=pltpu.VMEM)
    moved = sum(a.size * a.dtype.itemsize for a in args) + sum(
        s.size * s.dtype.itemsize for s in outs
    )
    return pl.pallas_call(
        kernel,
        out_shape=outs,
        in_specs=[
            pl.BlockSpec(memory_space=pltpu.HBM) if i in hbm else vmem for i in range(len(args))
        ],
        out_specs=[pl.BlockSpec(memory_space=pltpu.HBM) if out_hbm else vmem] * len(outs),
        scratch_shapes=scratch,
        compiler_params=pltpu.CompilerParams(vmem_limit_bytes=32 * 1024 * 1024),
        cost_estimate=pl.CostEstimate(flops=flops, bytes_accessed=moved, transcendentals=0),
    )(*args)


def shape(dims, dtype):
    return jax.ShapeDtypeStruct(dims, dtype)


def halves(size):
    mine = lax.rem(lax.axis_index("ctx"), PAIR)
    return (
        pl.ds(pl.multiple_of(mine * size, size), size),
        pl.ds(pl.multiple_of((1 - mine) * size, size), size),
    )


def dot(a, b, contract):
    return lax.dot_general(a, b, ((contract[:1], contract[1:]), ((), ())), preferred_element_type=F32)


def split3(x):
    hi = x.astype(BF16)
    rest = x - hi.astype(F32)
    mid = rest.astype(BF16)
    return hi, mid, (rest - mid.astype(F32)).astype(BF16)


def decay_rows(log_decay, mine, heads):
    rows = log_decay[0]
    return jnp.where(mine == 0, rows[:heads], rows[heads:])


def copy_all(pairs, sems):
    copies = [pltpu.make_async_copy(src, to, sems.at[i]) for i, (src, to) in enumerate(pairs)]
    for copy in copies:
        copy.start()
    return copies


def pack_kernel(k, v, log_decay, first, sems):
    rows, heads = k.shape[1], log_decay.shape[1] // PAIR
    _, other = halves(k.shape[2] // PAIR)
    copies = copy_all(
        [(ref.at[0, :, other], first.at[i * rows : (i + 1) * rows, :]) for i, ref in enumerate((k, v))],
        sems,
    )
    mine = lax.rem(lax.axis_index("ctx"), PAIR)
    decay = decay_rows(log_decay, 1 - mine, heads)
    parts = [
        jnp.concatenate([part[h : h + 1] for h in range(heads)], 1).astype(F32)
        for part in split3(decay)
    ]
    parts.append(jnp.zeros((EDGE - 3, heads * rows), F32))
    first[2 * rows :, :] = jnp.concatenate(parts, 0).astype(BF16)
    for copy in copies:
        copy.wait()


def pack_more_kernel(q, k, v, g, _, second, own, sems):
    rows = q.shape[1]
    lanes_own, other = halves(q.shape[2] // PAIR)
    pairs = [
        (ref.at[0, :, other], second.at[i * rows : (i + 1) * rows, :]) for i, ref in enumerate((q, g))
    ]
    pairs += [
        (ref.at[0, :, lanes_own], own.at[i * rows : (i + 1) * rows, :])
        for i, ref in enumerate((k, v, q, g))
    ]
    for copy in copy_all(pairs, sems):
        copy.wait()


def join_kernel(got, near, far, own, log_decay, taps, kc2, v2, cum, state, padded, decays):
    rows, heads = log_decay.shape[2], log_decay.shape[1] // PAIR
    width = own.shape[1]
    dim = width // heads
    size = PAIR * rows
    lanes_own, _ = halves(width)
    here, there = halves(rows)
    mine = lax.rem(lax.axis_index("ctx"), PAIR)
    v2[here, :] = own[rows : 2 * rows, :]
    v2[there, :] = got[rows : 2 * rows, :]
    edge = jnp.where(mine == 0, near[...].astype(F32), far[...].astype(F32))
    padded[:EDGE, :] = jnp.where(lax.axis_index("ctx") < PAIR, 0.0, edge)
    start = pl.multiple_of(EDGE + mine * rows, EDGE)
    padded[pl.ds(start, rows), :] = own[:rows, :].astype(F32)
    start = pl.multiple_of(EDGE + (1 - mine) * rows, EDGE)
    padded[pl.ds(start, rows), :] = got[:rows, :].astype(F32)
    total = jnp.zeros((size, width), F32)
    for j in range(taps.shape[1]):
        total = total + taps[0, j : j + 1, lanes_own] * padded[EDGE - j : EDGE - j + size, :]
    kc2[...] = total.astype(BF16)

    decays[...] = jnp.zeros_like(decays)
    coded = got[2 * rows :, :].astype(F32)
    row = coded[0:1] + coded[1:2] + coded[2:3]
    decays[:heads, here] = decay_rows(log_decay, mine, heads)
    decays[:heads, there] = jnp.concatenate(
        [row[:, h * rows : (h + 1) * rows] for h in range(heads)], 0
    )
    upto = lax.broadcasted_iota(jnp.int32, (size, size), 0) <= lax.broadcasted_iota(
        jnp.int32, (size, size), 1
    )
    upto = upto.astype(F32).astype(BF16)
    cum_rows = sum(dot(part, upto, (1, 0)) for part in split3(decays[...]))
    cum[...] = cum_rows
    cols = cum_rows.T
    after = jnp.exp(cols[size - 1 :, :] - cols)
    for h in range(heads):
        lanes = slice(h * dim, (h + 1) * dim)
        scaled = (kc2[:, lanes].astype(F32) * after[:, h : h + 1]).astype(BF16)
        state[lanes, :] = dot(scaled, v2[:, lanes], (0, 0)).astype(BF16)


def mixing_of(cum_rows, cols, h, size):
    differ = cols[:, h : h + 1] - cum_rows[h : h + 1, :]
    causal = lax.broadcasted_iota(jnp.int32, (size, size), 0) >= lax.broadcasted_iota(
        jnp.int32, (size, size), 1
    )
    return jnp.where(causal, jnp.exp(jnp.where(causal, differ, 0.0)), 0.0)


def local_kernel(got, own, kc2, v2, cum, q2, g2, weights, inside):
    size, width = q2.shape
    heads, dim = weights.shape[0], width // weights.shape[0]
    rows = size // PAIR
    here, there = halves(rows)
    q2[here, :] = own[2 * rows : 3 * rows, :]
    q2[there, :] = got[:rows, :]
    g2[here, :] = own[3 * rows :, :]
    g2[there, :] = got[rows:, :]
    cum_rows = cum[...]
    cols = cum_rows.T
    for h in range(heads):
        lanes = slice(h * dim, (h + 1) * dim)
        scores = dot(q2[:, lanes], kc2[:, lanes], (1, 1))
        w = (scores * mixing_of(cum_rows, cols, h, size)).astype(BF16)
        weights[h] = w
        inside[:, lanes] = dot(w, v2[:, lanes], (1, 0))


def unless(flag, block):
    return jnp.where(flag, jnp.zeros_like(block), block)


def attend_kernel(inside, q2, g2, cum, before, attended, sums):
    size, width = q2.shape
    dim = before.shape[1]
    heads = width // dim
    start = lax.axis_index("ctx") < PAIR
    growth = jnp.exp(cum[...].T)
    squares = jnp.zeros((size, dim), F32)
    products = jnp.zeros((size, dim), F32)
    for h in range(heads):
        lanes = slice(h * dim, (h + 1) * dim)
        carried = dot(q2[:, lanes], unless(start, before[lanes, :]), (1, 0))
        a = inside[:, lanes] + growth[:, h : h + 1] * carried
        attended[:, lanes] = a
        squares = squares + a * a
        products = products + a * g2[:, lanes].astype(F32)
    ones = jnp.ones((8, dim), F32)
    line = [
        lax.dot_general(
            ones, x, (((1,), (1,)), ((), ())), precision=lax.Precision.HIGHEST,
            preferred_element_type=F32,
        )[:1]
        for x in (squares, products)
    ]
    sums[...] = jnp.concatenate(line, 0)


def grad_kernel(width_all, attended, q2, v2, g2, cum, *refs):
    *sums, scales, grad, adjoint = refs
    size, width = q2.shape
    dim = adjoint.shape[1]
    heads = width // dim
    total = sum(ref[...] for ref in sums[1:]) + sums[0][...]
    inverse = 1.0 / jnp.sqrt(total[0:1] / width_all + 1e-06)
    shift = total[1:2] / width_all * inverse
    both = jnp.concatenate([inverse, shift, jnp.zeros((6, size), F32)], 0)
    scales[...] = both
    both = both.T
    inverse, shift = both[:, 0:1], both[:, 1:2]
    cum_rows = cum[...]
    cols = cum_rows.T
    growth = jnp.exp(cols)
    causal = lax.broadcasted_iota(jnp.int32, (EDGE, size), 0) <= lax.broadcasted_iota(
        jnp.int32, (EDGE, size), 1
    )
    heads_rows = []
    for h in range(heads):
        lanes = slice(h * dim, (h + 1) * dim)
        n = attended[:, lanes] * inverse
        d = ((g2[:, lanes].astype(F32) - n * shift) * inverse).astype(BF16)
        grad[:, lanes] = d
        scaled = (q2[:, lanes].astype(F32) * growth[:, h : h + 1]).astype(BF16)
        adjoint[lanes, :] = dot(scaled, d, (0, 0)).astype(BF16)
        differ = cum_rows[h : h + 1, :] - cols[:EDGE, h : h + 1]
        mixing = jnp.where(causal, jnp.exp(jnp.where(causal, differ, 0.0)), 0.0)
        scores = (dot(v2[:EDGE, lanes], d, (1, 1)) * mixing).astype(BF16)
        top = dot(scores, q2[:, lanes], (1, 0))
        heads_rows.append(top[:8])
    adjoint[width:, :] = jnp.concatenate([top[:4] for top in heads_rows], 0).astype(BF16)


def inner_grad_kernel(
    attended, scales, q2, kc2, v2, grad, weights, cum, before,
    keep, send, partial, key_grad, normed,
):
    size, width = q2.shape
    dim = before.shape[1]
    heads = width // dim
    start = lax.axis_index("ctx") < PAIR
    inverse = scales[...].T[:, 0:1]
    cum_rows = cum[...]
    cols = cum_rows.T
    growth = jnp.exp(cols)
    for h in range(heads):
        lanes = slice(h * dim, (h + 1) * dim)
        normed[:, lanes] = (attended[:, lanes] * inverse).astype(BF16)
        d = grad[:, lanes]
        scores = dot(d, v2[:, lanes], (1, 1)) * mixing_of(cum_rows, cols, h, size)
        scores = scores.astype(BF16)
        query_grad = dot(scores, kc2[:, lanes], (1, 0)) + growth[:, h : h + 1] * dot(
            d, unless(start, before[lanes, :]), (1, 1)
        )
        key_grad[:, lanes] = dot(scores, q2[:, lanes], (0, 0))
        partial[:, lanes] = query_grad + dot(weights[h], d, (0, 0))
    here, there = halves(size // PAIR)
    keep[...] = normed[here, :]
    send[...] = normed[there, :]


def outer_grad_kernel(
    last, partial, key_grad, kc2, v2, cum, behind, more, taps, keep, send, padded, done
):
    size, width = partial.shape
    dim = behind.shape[1]
    heads = width // dim
    own, _ = halves(width)
    ends = lax.axis_index("ctx") >= last
    tops = behind[width:, :].astype(F32)
    cols = cum[...].T
    after = jnp.exp(cols[size - 1 :, :] - cols)
    for h in range(heads):
        lanes = slice(h * dim, (h + 1) * dim)
        scale = after[:, h : h + 1]
        state = unless(ends, behind[lanes, :])
        padded[:size, lanes] = key_grad[:, lanes] + scale * dot(v2[:, lanes], state, (1, 1))
        done[:, lanes] = partial[:, lanes] + scale * dot(kc2[:, lanes], state, (1, 0))
        top = jnp.concatenate([tops[4 * h : 4 * h + 4], jnp.zeros((4, dim), F32)], 0)
        padded[size:, lanes] = unless(ends, top) + more[:, lanes]
    total = done[...]
    for j in range(taps.shape[1]):
        total = total + taps[0, j : j + 1, own] * padded[j : j + size, :]
    done[...] = total
    here, there = halves(size // PAIR)
    first = lax.axis_index("pp") == 0
    keep[...] = unless(first, done[here, :]).astype(BF16)
    send[...] = unless(first, done[there, :]).astype(BF16)


def place_kernel(kept, got, out, sems):
    own, other = halves(kept.shape[1])
    for copy in copy_all([(kept, out.at[0, :, own]), (got, out.at[0, :, other])], sems):
        copy.wait()


def placed(kept, got):
    rows, width = kept.shape
    return call(
        place_kernel,
        [shape((1, rows, PAIR * width), BF16)],
        kept, got,
        scratch=[pltpu.SemaphoreType.DMA((2,))],
        out_hbm=True,
    )[0]


def turned(block, axis, distance):
    count = lax.axis_size(axis)
    return lax.ppermute(block, axis, [(i, (i + distance) % count) for i in range(count)])


def swapped(block):
    return lax.ppermute(block, "ctx", [(i, i ^ 1) for i in range(lax.axis_size("ctx"))])


def to_earlier_section(block, flip):
    blocks, sections = lax.axis_size("ctx"), lax.axis_size("pp")
    route = [
        (c * sections + p, (c ^ flip) * sections + (p - 1) % sections)
        for c in range(blocks)
        for p in range(sections)
    ]
    return lax.ppermute(block, ("ctx", "pp"), route)


def summed_parts(part):
    blocks, count = lax.axis_size("ctx"), lax.axis_size("tp")
    pair = part + lax.ppermute(part, "tp", [(i, i ^ 1) for i in range(count)])
    parts = [pair]
    for flip in range(PAIR):
        for k in range(0, count, 2):
            if flip or k:
                route = [
                    (c * count + t, (c ^ flip) * count + (t + k) % count)
                    for c in range(blocks)
                    for t in range(count)
                ]
                parts.append(lax.ppermute(pair, ("ctx", "tp"), route))
    return parts


def per_device(queries, key_input, values, log_decay, conv_weight, out_grad):
    rows, width = queries.shape[1], queries.shape[2] // PAIR
    heads = log_decay.shape[2] // PAIR
    dim = width // heads
    size = PAIR * rows
    blocks = lax.axis_size("ctx")
    supers = blocks // PAIR
    width_all = queries.shape[2] * lax.axis_size("tp")
    log_decay = jnp.swapaxes(log_decay, 1, 2)
    arrays = (queries, key_input, values, out_grad)
    queries, key_input, values, out_grad = (
        pltpu.with_memory_space_constraint(x, pltpu.HBM) for x in arrays
    )

    first = call(
        pack_kernel,
        [shape((2 * rows + EDGE, width), BF16)],
        key_input, values, log_decay,
        scratch=[pltpu.SemaphoreType.DMA((2,))],
        hbm=range(2),
    )[0]
    got = swapped(first)
    edge = arrays[1][0, rows - EDGE :]
    near = lax.ppermute(edge[:, :width], "ctx", [(i, i + 1) for i in range(1, blocks - 1, 2)])
    far = lax.ppermute(edge[:, width:], "ctx", [(i, i + 2) for i in range(1, blocks - 2, 2)])
    second, own = call(
        pack_more_kernel,
        [shape((2 * rows, width), BF16), shape((4 * rows, width), BF16)],
        queries, key_input, values, out_grad, first[2 * rows :],
        scratch=[pltpu.SemaphoreType.DMA((6,))],
        hbm=range(4),
    )
    got_more = swapped(second)
    kc2, v2, cum, state = call(
        join_kernel,
        [shape((size, width), BF16)] * 2 + [shape((8, size), F32), shape((width, dim), BF16)],
        got, near, far, own, log_decay, conv_weight,
        scratch=[pltpu.VMEM((EDGE + size, width), F32), pltpu.VMEM((8, size), F32)],
    )
    carry = jnp.repeat(jnp.exp(cum[:heads, -1]), dim)[:, None]
    pair_index = lax.axis_index("ctx") // PAIR
    before = turned(state, "ctx", PAIR)
    for _ in range(supers - 2):
        earlier = unless(pair_index == 0, before).astype(F32)
        joined = state.astype(F32) + carry * earlier
        before = turned(joined.astype(BF16), "ctx", PAIR)

    q2, g2, weights, inside = call(
        local_kernel,
        [shape((size, width), BF16)] * 2
        + [shape((heads, size, size), BF16), shape((size, width), F32)],
        got_more, own, kc2, v2, cum,
        flops=4 * heads * size * size * dim,
    )
    attended, sums = call(
        attend_kernel,
        [shape((size, width), F32), shape((2, size), F32)],
        inside, q2, g2, cum, before,
    )
    parts = summed_parts(sums)
    scales, grad, adjoint = call(
        lambda *refs: grad_kernel(width_all, *refs),
        [shape((8, size), F32), shape((size, width), BF16),
         shape((width + 4 * heads, dim), BF16)],
        attended, q2, v2, g2, cum, *parts,
    )
    behind = turned(adjoint, "ctx", -PAIR)
    more = jnp.zeros((8, width), F32)
    for step in range(supers - 2):
        later = unless(pair_index == supers - 1, behind[:width]).astype(F32)
        joined = adjoint[:width].astype(F32) + carry * later
        moved = turned(joined.astype(BF16), "ctx", -PAIR)
        behind = jnp.concatenate([moved, behind[width:]], 0)
    if supers > 2:
        after = jnp.exp(cum[:heads, -1:] - cum[:heads, :8])
        state_part = jnp.einsum(
            "shv,hkv->shk",
            v2[:8].reshape(8, heads, dim),
            unless(pair_index == supers - 1, behind[:width]).reshape(heads, dim, dim),
            preferred_element_type=F32,
        )
        more = turned((after.T[:, :, None] * state_part).reshape(8, width), "ctx", -PAIR)
        more = unless(pair_index == supers - 1, more)

    keep, send, partial, key_grad = call(
        inner_grad_kernel,
        [shape((rows, width), BF16)] * 2 + [shape((size, width), F32)] * 2,
        attended, scales, q2, kc2, v2, grad, weights, cum, before,
        scratch=[pltpu.VMEM((size, width), BF16)],
        flops=10 * heads * size * size * dim,
    )
    layer_output = placed(keep, swapped(send))
    keep, send = call(
        lambda *refs: outer_grad_kernel(blocks - PAIR, *refs),
        [shape((rows, width), BF16)] * 2,
        partial, key_grad, kc2, v2, cum, behind, more, conv_weight,
        scratch=[pltpu.VMEM((size + 8, width), F32), pltpu.VMEM((size, width), F32)],
    )
    input_next = placed(to_earlier_section(keep, 0), to_earlier_section(send, 1))
    return (layer_output, input_next)


def solution(mesh):
    placed = (
        P("pp", "ctx", "tp"),
        P("pp", "ctx", "tp"),
        P("pp", "ctx", "tp"),
        P("pp", "ctx", "tp"),
        P("pp", None, "tp"),
        P("pp", "ctx", "tp"),
    )
    return jax.shard_map(
        per_device,
        mesh=mesh,
        in_specs=placed,
        out_specs=(P("pp", "ctx", "tp"), P("pp", "ctx", "tp")),
        check_vma=False,
    )
```

time: 61.2 us -> 50.8 us (0.83)
  waiting for transfers between devices: 26.9 us -> 21.6 us
  starting transfers between devices: 21.4 us -> 17.1 us
  local copies, waits for them, and re-layouts: 4.6 us -> 1.46 us
  Pallas kernels: 7.07 us -> 9.55 us
    ppermute x3, waiting for transfers between devices: 12.4 us -> 5.31 us  [swapped(): lax.ppermute(block, 'ctx', [(i, i ^ 1) for i in range(lax.axis_size('ctx'...]
    ppermute x3, starting transfers between devices: 8.8 us -> 3.27 us  [swapped(): lax.ppermute(block, 'ctx', [(i, i ^ 1) for i in range(lax.axis_size('ctx'...]
    unnamed x11 -> x6, local copies, waits for them, and re-layouts: 4.59 us -> 0.69 us
    ppermute x6 -> x7, waiting for transfers between devices: 7.16 us -> 10.1 us  [the longest x2 7.15 us: turned(): lax.ppermute(block, axis, [(i, (i + distance) % count) for i in range(cou...]
    pallas_call x9 -> x10, Pallas kernels: 7.07 us -> 9.55 us  [call(): pl.pallas_call(kernel, out_shape=outs, in_specs=[pl.BlockSpec(memory_spac...]
    ppermute x6 -> x7, starting transfers between devices: 10.1 us -> 12 us  [the longest x2 7.06 us: turned(): lax.ppermute(block, axis, [(i, (i + distance) % count) for i in range(cou...]
    ppermute x2, waiting for transfers between devices: 6.12 us -> 5.01 us  [to_earlier_section(): return lax.ppermute(block, ('ctx', 'pp'), route)]
    ppermute x2, starting transfers between devices: 2.58 us -> 1.78 us  [to_earlier_section(): return lax.ppermute(block, ('ctx', 'pp'), route)]
  transfers between devices with their start and end apart: 12 -> 13, of which waited for: 8 -> 10; matrix products, arithmetic and copies ran while one was open for 0% -> 2% of each run, Pallas kernels for 6% -> 12%
where the time goes in v2:
time: 50.8 us; the launch traced here: 50.4 us
  waiting for transfers between devices  21.6 us (43%)
  starting transfers between devices  17.1 us (34%)
  Pallas kernels  9.55 us (19%)
  local copies, waits for them, and re-layouts  1.46 us (3%)
  between operations  0.75 us (1%)
    pallas_call x10, Pallas kernels, call(): pl.pallas_call(kernel, out_shape=outs, in_specs=[pl.BlockSpec(memory_spac...  9.55 us
    ppermute x2, waiting for transfers between devices, turned(): lax.ppermute(block, axis, [(i, (i + distance) % count) for i in range(cou...  7.15 us
    ppermute x2, starting transfers between devices, turned(): lax.ppermute(block, axis, [(i, (i + distance) % count) for i in range(cou...  7.06 us
    ppermute x3, waiting for transfers between devices, swapped(): lax.ppermute(block, 'ctx', [(i, i ^ 1) for i in range(lax.axis_size('ctx'...  5.31 us
    ppermute x2, waiting for transfers between devices, to_earlier_section(): return lax.ppermute(block, ('ctx', 'pp'), route)  5.01 us
    ppermute x3, starting transfers between devices, summed_parts(): parts.append(lax.ppermute(pair, ('ctx', 'tp'), route))  3.49 us
    ppermute x3, starting transfers between devices, swapped(): lax.ppermute(block, 'ctx', [(i, i ^ 1) for i in range(lax.axis_size('ctx'...  3.27 us
    ppermute x3, waiting for transfers between devices, summed_parts(): parts.append(lax.ppermute(pair, ('ctx', 'tp'), route))  2.98 us
  transfers between devices with their start and end apart: 13, of which 10 were waited for; matrix products, arithmetic and copies ran while one was open for 2% of the time, Pallas kernels for 12%

profile of v2, /device:TPU:0, one launch (start us, length us, event | category | flops | bytes accessed | tf_op | source)
XLA Modules:
  0.0 50.4 jit_solution(8912120877003368658)
XLA Ops:
  0.6 0.0 copy-start.1
  0.6 0.7 %copy-done.1 = f32[1,128,8]{1,2,0:T(8,128)S(1)} copy-done((f32[1,128,8]{1,2,0:T(8,128)S(1)}, f32[1,128,8]{1,2,0:T(8,128)}, u32[]{:S(2)}) %copy-start.1) | copy-done | bytes 4120
  1.3 1.0 %shard_map.77 = bf16[272,512]{1,0:T(8,128)(2,1)S(1)} custom-call(bf16[1,128,1024]{2,1,0:T(8,128)(2,1)} %k.3, bf16[1,128,1024]{2,1,0:T(8,128)(2,1)} %v.3, f32[1,8,128]{2,1,0:T(8,128)S(1)} %bitcast.3), custom_call_target="tpu_custom_call" | custom-call | bytes 806912 | tf_op jit(solution)/shard_map/pallas_call | solution.py:19
  2.3 3.1 %collective-permute-start.1 = (bf16[272,512]{1,0:T(8,128)(2,1)S(1)}, bf16[272,512]{1,0:T(8,128)(2,1)S(1)}, u32[]{:S(2)}, u32[]{:S(2)}) collective-permute-start(bf16[272,512]{1,0:T(8,128)(2,1)S(1)} %shard_map.77), channel_id=1, source_target_pairs={{0,8},{8,0},{16,24},{24,16},{1,9},{9,1},{17,25},{25,17},{2,10},{10... | collective-permute-start | bytes 835592 | tf_op jit(solution)/shard_map/ppermute | solution.py:313
  5.4 1.3 %shard_map.78 = (bf16[256,512]{1,0:T(8,128)(2,1)S(1)}, bf16[512,512]{1,0:T(8,128)(2,1)S(1)}) custom-call(bf16[1,128,1024]{2,1,0:T(8,128)(2,1)} %q.1, bf16[1,128,1024]{2,1,0:T(8,128)(2,1)} %k.3, bf16[1,128,1024]{2,1,0:T(8,128)(2,1)} %v.3, bf16[1,128,1024]{2,1,0:T(8,128)(2,1)} %g.1, bf16[16,512]{1,0:T(8,128)(2,1)S(1)} %slice.16._), custom_call_target="tpu_custom_call" | custom-call | bytes 1851392 | tf_op jit(solution)/shard_map/pallas_call | solution.py:19
  6.7 0.1 collective-permute-start
  6.8 0.8 %slice_bitcast_fusion = bf16[16,1024]{1,0:T(8,128)(2,1)S(1)} fusion(bf16[1,128,1024]{2,1,0:T(8,128)(2,1)} %k.3), kind=kLoop, calls=%fused_computation | loop fusion | bytes 65536 | tf_op jit(solution)/shard_map/squeeze | solution.py:364
  7.5 0.0 copy-start
  7.5 0.0 copy-start.2
  7.5 0.8 %collective-permute-start.2 = (bf16[16,512]{1,0:T(8,128)(2,1)S(1)}, bf16[16,512]{1,0:T(8,128)(2,1)S(1)}, u32[]{:S(2)}, u32[]{:S(2)}) collective-permute-start(bf16[16,512]{1,0:T(8,128)(2,1)S(1)} %get-tuple-element.45), channel_id=1, source_target_pairs={{8,16},{9,17},{10,18},{11,19},{12,20},{13,21},{14,22},{15,23}} | collective-permute-start | bytes 49160 | tf_op jit(solution)/shard_map/ppermute | solution.py:365
  8.3 0.7 %collective-permute-start.3 = (bf16[16,512]{1,0:T(8,128)(2,1)S(1)}, bf16[16,512]{1,0:T(8,128)(2,1)S(1)}, u32[]{:S(2)}, u32[]{:S(2)}) collective-permute-start(bf16[16,512]{1,0:T(8,128)(2,1)S(1)} %get-tuple-element.44), channel_id=1, source_target_pairs={{8,24},{9,25},{10,26},{11,27},{12,28},{13,29},{14,30},{15,31}} | collective-permute-start | bytes 49160 | tf_op jit(solution)/shard_map/ppermute | solution.py:366
  9.0 0.0 collective-permute-done.2.near
  9.0 0.0 collective-permute-done.3.far
  9.0 3.9 %collective-permute-done.1.got = bf16[272,512]{1,0:T(8,128)(2,1)S(1)} collective-permute-done((bf16[272,512]{1,0:T(8,128)(2,1)S(1)}, bf16[272,512]{1,0:T(8,128)(2,1)S(1)}, u32[]{:S(2)}, u32[]{:S(2)}) %collective-permute-start.1) | collective-permute-done | bytes 278560 | tf_op jit(solution)/shard_map/ppermute | solution.py:313
  12.9 0.0 copy-done
  12.9 0.0 copy-done.2
  12.9 1.1 %shard_map.79 = (bf16[256,512]{1,0:T(8,128)(2,1)S(1)}, bf16[256,512]{1,0:T(8,128)(2,1)S(1)}, f32[8,256]{1,0:T(8,128)S(1)}, bf16[512,128]{1,0:T(8,128)(2,1)S(1)}) custom-call(bf16[272,512]{1,0:T(8,128)(2,1)S(1)} %collective-permute-done.1.got, bf16[16,512]{1,0:T(8,128)(2,1)S(1)} %collective-permute-done.2.near, ...), custom_call_target="tpu_custom_call" | custom-call | bytes 1519616 | tf_op jit(solution)/shard_map/pallas_call | solution.py:19
  14.0 3.7 %collective-permute-start.4 = (bf16[512,128]{1,0:T(8,128)(2,1)S(1)}, bf16[512,128]{1,0:T(8,128)(2,1)S(1)}, u32[]{:S(2)}, u32[]{:S(2)}) collective-permute-start(bf16[512,128]{1,0:T(8,128)(2,1)S(1)} %get-tuple-element.31), channel_id=1, source_target_pairs={{0,16},{8,24},{16,0},{24,8},{1,17},{9,25},{17,1},{25,9},{2,18},{10... | collective-permute-start | bytes 393224 | tf_op jit(solution)/shard_map/ppermute | solution.py:309
  17.6 1.5 %collective-permute-done.got = bf16[256,512]{1,0:T(8,128)(2,1)S(1)} collective-permute-done((bf16[256,512]{1,0:T(8,128)(2,1)S(1)}, bf16[256,512]{1,0:T(8,128)(2,1)S(1)}, u32[]{:S(2)}, u32[]{:S(2)}) %collective-permute-start) | collective-permute-done | bytes 262176 | tf_op jit(solution)/shard_map/ppermute | solution.py:313
  19.1 0.8 %shard_map.80 = (bf16[256,512]{1,0:T(8,128)(2,1)S(1)}, bf16[256,512]{1,0:T(8,128)(2,1)S(1)}, bf16[4,256,256]{2,1,0:T(8,128)(2,1)S(1)}, f32[256,512]{1,0:T(8,128)S(1)}) custom-call(bf16[256,512]{1,0:T(8,128)(2,1)S(1)} %collective-permute-done.got, bf16[512,512]{1,0:T(8,128)(2,1)S(1)} %get-tuple-element.24.own, ...), custom_call_target="tpu_custom_call" | custom-call | flops 134217728 | bytes 2891776 | tf_op jit(solution)/shard_map/pallas_call | solution.py:19
  19.9 3.5 %collective-permute-done.4.before = bf16[512,128]{1,0:T(8,128)(2,1)S(1)} collective-permute-done((bf16[512,128]{1,0:T(8,128)(2,1)S(1)}, bf16[512,128]{1,0:T(8,128)(2,1)S(1)}, u32[]{:S(2)}, u32[]{:S(2)}) %collective-permute-start.4) | collective-permute-done | bytes 131104 | tf_op jit(solution)/shard_map/ppermute | solution.py:309
  23.4 0.7 %shard_map.81 = (f32[256,512]{1,0:T(8,128)S(1)}, f32[2,256]{1,0:T(2,128)S(1)}) custom-call(f32[256,512]{1,0:T(8,128)S(1)} %get-tuple-element.28.inside, bf16[256,512]{1,0:T(8,128)(2,1)S(1)} %get-tuple-element.29.q2.refs_1_, bf16[256,512]{1,0:T(8,128)(2,1)S(1)} %get-tuple-element.30.g2.refs_3_, f32[8,256]{1,0:T(8,128)S(1)} %get-tuple-element.27.cum.refs_4_, ...), custom_call_target="tpu_custom_call" | custom-call | bytes 1714176 | tf_op jit(solution)/shard_map/pallas_call | solution.py:19
  24.1 0.0 collective-permute-start.5
  24.1 1.2 %collective-permute-done.5 = f32[2,256]{1,0:T(2,128)S(1)} collective-permute-done((f32[2,256]{1,0:T(2,128)S(1)}, f32[2,256]{1,0:T(2,128)S(1)}, u32[]{:S(2)}, u32[]{:S(2)}) %collective-permute-start.5) | collective-permute-done | bytes 2080 | tf_op jit(solution)/shard_map/ppermute | solution.py:328
  25.3 1.5 %collective-permute-start.6 = (f32[2,256]{1,0:T(2,128)S(1)}, f32[2,256]{1,0:T(2,128)S(1)}, u32[]{:S(2)}, u32[]{:S(2)}) collective-permute-start(f32[2,256]{1,0:T(2,128)S(1)} %add.3.refs_5_), channel_id=1, source_target_pairs={{0,4},{2,6},{4,0},{6,2},{8,12},{10,14},{12,8},{14,10},{16,20},{18,... | collective-permute-start | bytes 6152 | tf_op jit(solution)/shard_map/ppermute | solution.py:338
  26.8 0.5 collective-permute-start.7
  27.3 1.5 %collective-permute-start.8 = (f32[2,256]{1,0:T(2,128)S(1)}, f32[2,256]{1,0:T(2,128)S(1)}, u32[]{:S(2)}, u32[]{:S(2)}) collective-permute-start(f32[2,256]{1,0:T(2,128)S(1)} %add.3.refs_5_), channel_id=1, source_target_pairs={{0,12},{2,14},{4,8},{6,10},{8,4},{10,6},{12,0},{14,2},{16,28},{18,... | collective-permute-start | bytes 6152 | tf_op jit(solution)/shard_map/ppermute | solution.py:338
  28.8 0.1 collective-permute-done.6.refs_6_
  28.9 1.5 %collective-permute-done.7.refs_7_ = f32[2,256]{1,0:T(2,128)S(1)} collective-permute-done((f32[2,256]{1,0:T(2,128)S(1)}, f32[2,256]{1,0:T(2,128)S(1)}, u32[]{:S(2)}, u32[]{:S(2)}) %collective-permute-start.7) | collective-permute-done | bytes 2080 | tf_op jit(solution)/shard_map/ppermute | solution.py:338
  30.4 1.4 %collective-permute-done.8.refs_8_ = f32[2,256]{1,0:T(2,128)S(1)} collective-permute-done((f32[2,256]{1,0:T(2,128)S(1)}, f32[2,256]{1,0:T(2,128)S(1)}, u32[]{:S(2)}, u32[]{:S(2)}) %collective-permute-start.8) | collective-permute-done | bytes 2080 | tf_op jit(solution)/shard_map/ppermute | solution.py:338
  31.8 1.2 %shard_map.82 = (f32[8,256]{1,0:T(8,128)S(1)}, bf16[256,512]{1,0:T(8,128)(2,1)S(1)}, bf16[528,128]{1,0:T(8,128)(2,1)S(1)}) custom-call(f32[256,512]{1,0:T(8,128)S(1)} %get-tuple-element.32.refs_0_.attended, bf16[256,512]{1,0:T(8,128)(2,1)S(1)} %get-tuple-element.29.q2.refs_1_, bf16[256,512]{1,0:T(8,128)(2,1)S(1)} %get-tuple-element.26.v2.refs_2_.refs_3_, ...), custom_call_target="tpu_custom_call" | custom-call | bytes 1732608 | tf_op jit(solution)/shard_map/pallas_call | solution.py:19
  33.0 3.4 %collective-permute-start.10 = (bf16[528,128]{1,0:T(8,128)(2,1)S(1)}, bf16[528,128]{1,0:T(8,128)(2,1)S(1)}, u32[]{:S(2)}, u32[]{:S(2)}) collective-permute-start(bf16[528,128]{1,0:T(8,128)(2,1)S(1)} %get-tuple-element.41), channel_id=1, source_target_pairs={{0,16},{8,24},{16,0},{24,8},{1,17},{9,25},{17,1},{25,9},{2,18},{10... | collective-permute-start | bytes 405512 | tf_op jit(solution)/shard_map/ppermute | solution.py:309
  36.4 1.5 %shard_map.83 = (bf16[128,512]{1,0:T(8,128)(2,1)S(1)}, bf16[128,512]{1,0:T(8,128)(2,1)S(1)}, f32[256,512]{1,0:T(8,128)S(1)}, f32[256,512]{1,0:T(8,128)S(1)}) custom-call(f32[256,512]{1,0:T(8,128)S(1)} %get-tuple-element.32.refs_0_.attended, f32[8,256]{1,0:T(8,128)S(1)} %get-tuple-element.34.scales, bf16[256,512]{1,0:T(8,128)(2,1)S(1)} %get-tuple-element.29.q2.refs_1_, ...), custom_call_target="tpu_custom_call" | custom-call | flops 335544320 | bytes 3555328 | tf_op jit(solution)/shard_map/pallas_call | solution.py:19
  37.9 0.1 collective-permute-start.9
  37.9 3.6 %collective-permute-done.10.refs_5_ = bf16[528,128]{1,0:T(8,128)(2,1)S(1)} collective-permute-done((bf16[528,128]{1,0:T(8,128)(2,1)S(1)}, bf16[528,128]{1,0:T(8,128)(2,1)S(1)}, u32[]{:S(2)}, u32[]{:S(2)}) %collective-permute-start.10) | collective-permute-done | bytes 135200 | tf_op jit(solution)/shard_map/ppermute | solution.py:309
  41.6 0.6 %shard_map.85 = (bf16[128,512]{1,0:T(8,128)(2,1)S(1)}, bf16[128,512]{1,0:T(8,128)(2,1)S(1)}) custom-call(f32[256,512]{1,0:T(8,128)S(1)} %get-tuple-element.39.refs_0_, f32[256,512]{1,0:T(8,128)S(1)} %get-tuple-element.40.refs_1_, bf16[256,512]{1,0:T(8,128)(2,1)S(1)} %get-tuple-element.25.kc2.refs_2_, ...), custom_call_target="tpu_custom_call" | custom-call | bytes 2011136 | tf_op jit(solution)/shard_map/pallas_call | solution.py:19
  42.2 1.6 %collective-permute-start.11 = (bf16[128,512]{1,0:T(8,128)(2,1)S(1)}, bf16[128,512]{1,0:T(8,128)(2,1)S(1)}, u32[]{:S(2)}, u32[]{:S(2)}) collective-permute-start(bf16[128,512]{1,0:T(8,128)(2,1)S(1)} %get-tuple-element.42), channel_id=1, source_target_pairs={{0,1},{1,0},{8,9},{9,8},{16,17},{17,16},{24,25},{25,24},{2,3},{3,2... | collective-permute-start | bytes 393224 | tf_op jit(solution)/shard_map/ppermute | solution.py:323
  43.8 0.2 collective-permute-start.12
  44.0 0.0 collective-permute-done.9.got
  44.0 0.7 %shard_map.84 = bf16[1,128,1024]{2,1,0:T(8,128)(2,1)} custom-call(bf16[128,512]{1,0:T(8,128)(2,1)S(1)} %get-tuple-element.37.kept, bf16[128,512]{1,0:T(8,128)(2,1)S(1)} %collective-permute-done.9.got), custom_call_target="tpu_custom_call" | custom-call | bytes 524288 | tf_op jit(solution)/shard_map/pallas_call | solution.py:19
  44.7 3.6 %collective-permute-done.11.kept = bf16[128,512]{1,0:T(8,128)(2,1)S(1)} collective-permute-done((bf16[128,512]{1,0:T(8,128)(2,1)S(1)}, bf16[128,512]{1,0:T(8,128)(2,1)S(1)}, u32[]{:S(2)}, u32[]{:S(2)}) %collective-permute-start.11) | collective-permute-done | bytes 131104 | tf_op jit(solution)/shard_map/ppermute | solution.py:323
  48.3 1.4 %collective-permute-done.12.got = bf16[128,512]{1,0:T(8,128)(2,1)S(1)} collective-permute-done((bf16[128,512]{1,0:T(8,128)(2,1)S(1)}, bf16[128,512]{1,0:T(8,128)(2,1)S(1)}, u32[]{:S(2)}, u32[]{:S(2)}) %collective-permute-start.12) | collective-permute-done | bytes 131104 | tf_op jit(solution)/shard_map/ppermute | solution.py:323
  49.7 0.7 %shard_map.86 = bf16[1,128,1024]{2,1,0:T(8,128)(2,1)} custom-call(bf16[128,512]{1,0:T(8,128)(2,1)S(1)} %collective-permute-done.11.kept, bf16[128,512]{1,0:T(8,128)(2,1)S(1)} %collective-permute-done.12.got), custom_call_target="tpu_custom_call" | custom-call | bytes 524288 | tf_op jit(solution)/shard_map/pallas_call | solution.py:19
  (4 shorter events, 0.0 us)
Async XLA Ops:
  0.6 0.7 %copy-start.1 = (f32[1,128,8]{1,2,0:T(8,128)S(1)}, f32[1,128,8]{1,2,0:T(8,128)}, u32[]{:S(2)}) copy-start(f32[1,128,8]{1,2,0:T(8,128)} %param.9) | copy-start | bytes 12292
  2.3 10.6 %collective-permute-start.1 = (bf16[272,512]{1,0:T(8,128)(2,1)S(1)}, bf16[272,512]{1,0:T(8,128)(2,1)S(1)}, u32[]{:S(2)}, u32[]{:S(2)}) collective-permute-start(bf16[272,512]{1,0:T(8,128)(2,1)S(1)} %shard_map.77), channel_id=1, source_target_pairs={{0,8},{8,0},{16,24},{24,16},{1,9},{9,1},{17,25},{25,17},{2,10},{10... | collective-permute-start | bytes 835592 | tf_op jit(solution)/shard_map/ppermute | solution.py:313
  6.7 12.4 %collective-permute-start = (bf16[256,512]{1,0:T(8,128)(2,1)S(1)}, bf16[256,512]{1,0:T(8,128)(2,1)S(1)}, u32[]{:S(2)}, u32[]{:S(2)}) collective-permute-start(bf16[256,512]{1,0:T(8,128)(2,1)S(1)} %get-tuple-element.23), channel_id=1, source_target_pairs={{0,8},{8,0},{16,24},{24,16},{1,9},{9,1},{17,25},{25,17},{2,10},{10... | collective-permute-start | bytes 786440 | tf_op jit(solution)/shard_map/ppermute | solution.py:313
  7.5 5.4 %copy-start = (f32[1,4,1024]{2,1,0:T(4,128)S(1)}, f32[1,4,1024]{2,1,0:T(4,128)}, u32[]{:S(2)}) copy-start(f32[1,4,1024]{2,1,0:T(4,128)} %refs_7_.1) | copy-start | bytes 49156
  7.5 5.4 %copy-start.2 = (f32[1,128,8]{1,2,0:T(8,128)S(1)}, f32[1,128,8]{1,2,0:T(8,128)}, u32[]{:S(2)}) copy-start(f32[1,128,8]{1,2,0:T(8,128)} %param.9) | copy-start | bytes 12292
  7.5 1.5 %collective-permute-start.2 = (bf16[16,512]{1,0:T(8,128)(2,1)S(1)}, bf16[16,512]{1,0:T(8,128)(2,1)S(1)}, u32[]{:S(2)}, u32[]{:S(2)}) collective-permute-start(bf16[16,512]{1,0:T(8,128)(2,1)S(1)} %get-tuple-element.45), channel_id=1, source_target_pairs={{8,16},{9,17},{10,18},{11,19},{12,20},{13,21},{14,22},{15,23}} | collective-permute-start | bytes 49160 | tf_op jit(solution)/shard_map/ppermute | solution.py:365
  8.3 0.7 %collective-permute-start.3 = (bf16[16,512]{1,0:T(8,128)(2,1)S(1)}, bf16[16,512]{1,0:T(8,128)(2,1)S(1)}, u32[]{:S(2)}, u32[]{:S(2)}) collective-permute-start(bf16[16,512]{1,0:T(8,128)(2,1)S(1)} %get-tuple-element.44), channel_id=1, source_target_pairs={{8,24},{9,25},{10,26},{11,27},{12,28},{13,29},{14,30},{15,31}} | collective-permute-start | bytes 49160 | tf_op jit(solution)/shard_map/ppermute | solution.py:366
  14.0 9.4 %collective-permute-start.4 = (bf16[512,128]{1,0:T(8,128)(2,1)S(1)}, bf16[512,128]{1,0:T(8,128)(2,1)S(1)}, u32[]{:S(2)}, u32[]{:S(2)}) collective-permute-start(bf16[512,128]{1,0:T(8,128)(2,1)S(1)} %get-tuple-element.31), channel_id=1, source_target_pairs={{0,16},{8,24},{16,0},{24,8},{1,17},{9,25},{17,1},{25,9},{2,18},{10... | collective-permute-start | bytes 393224 | tf_op jit(solution)/shard_map/ppermute | solution.py:309
  24.1 1.2 %collective-permute-start.5 = (f32[2,256]{1,0:T(2,128)S(1)}, f32[2,256]{1,0:T(2,128)S(1)}, u32[]{:S(2)}, u32[]{:S(2)}) collective-permute-start(f32[2,256]{1,0:T(2,128)S(1)} %get-tuple-element.33), channel_id=1, source_target_pairs={{0,2},{2,0},{4,6},{6,4},{1,3},{3,1},{5,7},{7,5},{8,10},{10,8},{12,... | collective-permute-start | bytes 6152 | tf_op jit(solution)/shard_map/ppermute | solution.py:328
  25.3 3.6 %collective-permute-start.6 = (f32[2,256]{1,0:T(2,128)S(1)}, f32[2,256]{1,0:T(2,128)S(1)}, u32[]{:S(2)}, u32[]{:S(2)}) collective-permute-start(f32[2,256]{1,0:T(2,128)S(1)} %add.3.refs_5_), channel_id=1, source_target_pairs={{0,4},{2,6},{4,0},{6,2},{8,12},{10,14},{12,8},{14,10},{16,20},{18,... | collective-permute-start | bytes 6152 | tf_op jit(solution)/shard_map/ppermute | solution.py:338
  26.8 3.6 %collective-permute-start.7 = (f32[2,256]{1,0:T(2,128)S(1)}, f32[2,256]{1,0:T(2,128)S(1)}, u32[]{:S(2)}, u32[]{:S(2)}) collective-permute-start(f32[2,256]{1,0:T(2,128)S(1)} %add.3.refs_5_), channel_id=1, source_target_pairs={{0,8},{2,10},{4,12},{6,14},{8,0},{10,2},{12,4},{14,6},{16,24},{18,... | collective-permute-start | bytes 6152 | tf_op jit(solution)/shard_map/ppermute | solution.py:338
  27.3 4.5 %collective-permute-start.8 = (f32[2,256]{1,0:T(2,128)S(1)}, f32[2,256]{1,0:T(2,128)S(1)}, u32[]{:S(2)}, u32[]{:S(2)}) collective-permute-start(f32[2,256]{1,0:T(2,128)S(1)} %add.3.refs_5_), channel_id=1, source_target_pairs={{0,12},{2,14},{4,8},{6,10},{8,4},{10,6},{12,0},{14,2},{16,28},{18,... | collective-permute-start | bytes 6152 | tf_op jit(solution)/shard_map/ppermute | solution.py:338
  33.0 8.6 %collective-permute-start.10 = (bf16[528,128]{1,0:T(8,128)(2,1)S(1)}, bf16[528,128]{1,0:T(8,128)(2,1)S(1)}, u32[]{:S(2)}, u32[]{:S(2)}) collective-permute-start(bf16[528,128]{1,0:T(8,128)(2,1)S(1)} %get-tuple-element.41), channel_id=1, source_target_pairs={{0,16},{8,24},{16,0},{24,8},{1,17},{9,25},{17,1},{25,9},{2,18},{10... | collective-permute-start | bytes 405512 | tf_op jit(solution)/shard_map/ppermute | solution.py:309
  37.9 6.1 %collective-permute-start.9 = (bf16[128,512]{1,0:T(8,128)(2,1)S(1)}, bf16[128,512]{1,0:T(8,128)(2,1)S(1)}, u32[]{:S(2)}, u32[]{:S(2)}) collective-permute-start(bf16[128,512]{1,0:T(8,128)(2,1)S(1)} %get-tuple-element.38), channel_id=1, source_target_pairs={{0,8},{8,0},{16,24},{24,16},{1,9},{9,1},{17,25},{25,17},{2,10},{10... | collective-permute-start | bytes 393224 | tf_op jit(solution)/shard_map/ppermute | solution.py:313
  42.2 6.1 %collective-permute-start.11 = (bf16[128,512]{1,0:T(8,128)(2,1)S(1)}, bf16[128,512]{1,0:T(8,128)(2,1)S(1)}, u32[]{:S(2)}, u32[]{:S(2)}) collective-permute-start(bf16[128,512]{1,0:T(8,128)(2,1)S(1)} %get-tuple-element.42), channel_id=1, source_target_pairs={{0,1},{1,0},{8,9},{9,8},{16,17},{17,16},{24,25},{25,24},{2,3},{3,2... | collective-permute-start | bytes 393224 | tf_op jit(solution)/shard_map/ppermute | solution.py:323
  43.8 5.9 %collective-permute-start.12 = (bf16[128,512]{1,0:T(8,128)(2,1)S(1)}, bf16[128,512]{1,0:T(8,128)(2,1)S(1)}, u32[]{:S(2)}, u32[]{:S(2)}) collective-permute-start(bf16[128,512]{1,0:T(8,128)(2,1)S(1)} %get-tuple-element.43), channel_id=1, source_target_pairs={{0,9},{1,8},{8,1},{9,0},{16,25},{17,24},{24,17},{25,16},{2,11},{3,... | collective-permute-start | bytes 393224 | tf_op jit(solution)/shard_map/ppermute | solution.py:323

commit v3 on v2

--- a/solution.py
+++ b/solution.py
@@ -9,9 +9,10 @@
 BF16 = jnp.bfloat16
 PAIR = 2
 EDGE = 16
-
-
-def call(kernel, outs, *args, scratch=(), flops=0, hbm=(), out_hbm=False):
+PARTS = 1
+
+
+def call(kernel, outs, *args, scratch=(), flops=0, hbm=(), out_hbm=False, alias=()):
     vmem = pl.BlockSpec(memory_space=pltpu.VMEM)
     moved = sum(a.size * a.dtype.itemsize for a in args) + sum(
         s.size * s.dtype.itemsize for s in outs
@@ -24,6 +25,7 @@
         ],
         out_specs=[pl.BlockSpec(memory_space=pltpu.HBM) if out_hbm else vmem] * len(outs),
         scratch_shapes=scratch,
+        input_output_aliases=dict(alias),
         compiler_params=pltpu.CompilerParams(vmem_limit_bytes=32 * 1024 * 1024),
         cost_estimate=pl.CostEstimate(flops=flops, bytes_accessed=moved, transcendentals=0),
     )(*args)
@@ -64,22 +66,24 @@
     return copies
 
 
-def pack_kernel(k, v, log_decay, first, sems):
+def pack_kernel(k, v, log_decay, first, decays, sems):
     rows, heads = k.shape[1], log_decay.shape[1] // PAIR
     _, other = halves(k.shape[2] // PAIR)
     copies = copy_all(
-        [(ref.at[0, :, other], first.at[i * rows : (i + 1) * rows, :]) for i, ref in enumerate((k, v))],
+        [(log_decay, decays)]
+        + [(ref.at[0, :, other], first.at[i * rows : (i + 1) * rows, :]) for i, ref in enumerate((k, v))],
         sems,
     )
+    copies[0].wait()
     mine = lax.rem(lax.axis_index("ctx"), PAIR)
-    decay = decay_rows(log_decay, 1 - mine, heads)
+    decay = decay_rows(decays, 1 - mine, heads)
     parts = [
         jnp.concatenate([part[h : h + 1] for h in range(heads)], 1).astype(F32)
         for part in split3(decay)
     ]
     parts.append(jnp.zeros((EDGE - 3, heads * rows), F32))
     first[2 * rows :, :] = jnp.concatenate(parts, 0).astype(BF16)
-    for copy in copies:
+    for copy in copies[1:]:
         copy.wait()
 
 
@@ -97,7 +101,8 @@
         copy.wait()
 
 
-def join_kernel(got, near, far, own, log_decay, taps, kc2, v2, cum, state, padded, decays):
+def join_kernel(got, own, log_decay, taps, *refs):
+    *edges, kc2, v2, cum, state, top, padded, decays = refs
     rows, heads = log_decay.shape[2], log_decay.shape[1] // PAIR
     width = own.shape[1]
     dim = width // heads
@@ -107,8 +112,7 @@
     mine = lax.rem(lax.axis_index("ctx"), PAIR)
     v2[here, :] = own[rows : 2 * rows, :]
     v2[there, :] = got[rows : 2 * rows, :]
-    edge = jnp.where(mine == 0, near[...].astype(F32), far[...].astype(F32))
-    padded[:EDGE, :] = jnp.where(lax.axis_index("ctx") < PAIR, 0.0, edge)
+    padded[:EDGE, :] = edges[0][...].astype(F32) if edges else jnp.zeros((EDGE, width), F32)
     start = pl.multiple_of(EDGE + mine * rows, EDGE)
     padded[pl.ds(start, rows), :] = own[:rows, :].astype(F32)
     start = pl.multiple_of(EDGE + (1 - mine) * rows, EDGE)
@@ -117,6 +121,7 @@
     for j in range(taps.shape[1]):
         total = total + taps[0, j : j + 1, lanes_own] * padded[EDGE - j : EDGE - j + size, :]
     kc2[...] = total.astype(BF16)
+    top[...] = total[:EDGE]
 
     decays[...] = jnp.zeros_like(decays)
     coded = got[2 * rows :, :].astype(F32)
@@ -137,13 +142,16 @@
         lanes = slice(h * dim, (h + 1) * dim)
         scaled = (kc2[:, lanes].astype(F32) * after[:, h : h + 1]).astype(BF16)
         state[lanes, :] = dot(scaled, v2[:, lanes], (0, 0)).astype(BF16)
-
-
-def mixing_of(cum_rows, cols, h, size):
-    differ = cols[:, h : h + 1] - cum_rows[h : h + 1, :]
-    causal = lax.broadcasted_iota(jnp.int32, (size, size), 0) >= lax.broadcasted_iota(
-        jnp.int32, (size, size), 1
-    )
+    last = padded[EDGE + size - 4 : EDGE + size, :]
+    state[width:, :] = jnp.concatenate(
+        [last[:, h * dim : (h + 1) * dim] for h in range(heads)], 0
+    ).astype(BF16)
+
+
+def mixing_of(cum_rows, cols, h, first=0, last=None):
+    differ = cols[:, h : h + 1] - cum_rows[h : h + 1, :last]
+    at = lax.broadcasted_iota(jnp.int32, differ.shape, 1)
+    causal = (lax.broadcasted_iota(jnp.int32, differ.shape, 0) >= at) & (at >= first)
     return jnp.where(causal, jnp.exp(jnp.where(causal, differ, 0.0)), 0.0)
 
 
@@ -161,7 +169,7 @@
     for h in range(heads):
         lanes = slice(h * dim, (h + 1) * dim)
         scores = dot(q2[:, lanes], kc2[:, lanes], (1, 1))
-        w = (scores * mixing_of(cum_rows, cols, h, size)).astype(BF16)
+        w = (scores * mixing_of(cum_rows, cols, h, EDGE)).astype(BF16)
         weights[h] = w
         inside[:, lanes] = dot(w, v2[:, lanes], (1, 0))
 
@@ -170,18 +178,36 @@
     return jnp.where(flag, jnp.zeros_like(block), block)
 
 
-def attend_kernel(inside, q2, g2, cum, before, attended, sums):
+def attend_kernel(
+    kc2, weights, inside, q2, g2, v2, cum, before, top, taps,
+    kc2_whole, weights_whole, attended, sums, lead,
+):
     size, width = q2.shape
     dim = before.shape[1]
     heads = width // dim
     start = lax.axis_index("ctx") < PAIR
-    growth = jnp.exp(cum[...].T)
+    own, _ = halves(width)
+    cum_rows = cum[...]
+    cols = cum_rows.T
+    growth = jnp.exp(cols)
+    tail = unless(start, before[width:, :].astype(F32))
+    lead[...] = jnp.zeros_like(lead)
+    for h in range(heads):
+        lead[4:8, h * dim : (h + 1) * dim] = tail[4 * h : 4 * h + 4]
+    fixed = top[:8, :]
+    for j in range(1, taps.shape[1]):
+        fixed = fixed + taps[0, j : j + 1, own] * lead[8 - j : 16 - j, :]
+    fixed = jnp.concatenate([fixed, top[8:, :]], 0).astype(BF16)
+    kc2_whole[:EDGE, :] = fixed
     squares = jnp.zeros((size, dim), F32)
     products = jnp.zeros((size, dim), F32)
     for h in range(heads):
         lanes = slice(h * dim, (h + 1) * dim)
         carried = dot(q2[:, lanes], unless(start, before[lanes, :]), (1, 0))
-        a = inside[:, lanes] + growth[:, h : h + 1] * carried
+        scores = dot(q2[:, lanes], fixed[:, lanes], (1, 1))
+        w = (scores * mixing_of(cum_rows, cols, h, 0, EDGE)).astype(BF16)
+        weights_whole[h, :, :EDGE] = w
+        a = inside[:, lanes] + dot(w, v2[:EDGE, lanes], (1, 0)) + growth[:, h : h + 1] * carried
         attended[:, lanes] = a
         squares = squares + a * a
         products = products + a * g2[:, lanes].astype(F32)
@@ -197,9 +223,10 @@
 
 
 def grad_kernel(width_all, attended, q2, v2, g2, cum, *refs):
-    *sums, scales, grad, adjoint = refs
+    *sums, scales, grad = refs[:-PARTS]
+    adjoints = refs[-PARTS:]
     size, width = q2.shape
-    dim = adjoint.shape[1]
+    dim = adjoints[0].shape[1]
     heads = width // dim
     total = sum(ref[...] for ref in sums[1:]) + sums[0][...]
     inverse = 1.0 / jnp.sqrt(total[0:1] / width_all + 1e-06)
@@ -221,13 +248,18 @@
         d = ((g2[:, lanes].astype(F32) - n * shift) * inverse).astype(BF16)
         grad[:, lanes] = d
         scaled = (q2[:, lanes].astype(F32) * growth[:, h : h + 1]).astype(BF16)
-        adjoint[lanes, :] = dot(scaled, d, (0, 0)).astype(BF16)
+        part, at = divmod(h, heads // PARTS)
+        adjoints[part][at * dim : (at + 1) * dim, :] = dot(scaled, d, (0, 0)).astype(BF16)
         differ = cum_rows[h : h + 1, :] - cols[:EDGE, h : h + 1]
         mixing = jnp.where(causal, jnp.exp(jnp.where(causal, differ, 0.0)), 0.0)
         scores = (dot(v2[:EDGE, lanes], d, (1, 1)) * mixing).astype(BF16)
         top = dot(scores, q2[:, lanes], (1, 0))
         heads_rows.append(top[:8])
-    adjoint[width:, :] = jnp.concatenate([top[:4] for top in heads_rows], 0).astype(BF16)
+    for i, adjoint in enumerate(adjoints):
+        tops = [top[:4] for top in heads_rows[i * heads // PARTS : (i + 1) * heads // PARTS]]
+        if 4 * len(tops) < EDGE:
+            tops.append(jnp.zeros((EDGE - 4 * len(tops), dim), F32))
+        adjoint[width // PARTS :, :] = jnp.concatenate(tops, 0).astype(BF16)
 
 
 def inner_grad_kernel(
@@ -246,7 +278,7 @@
         lanes = slice(h * dim, (h + 1) * dim)
         normed[:, lanes] = (attended[:, lanes] * inverse).astype(BF16)
         d = grad[:, lanes]
-        scores = dot(d, v2[:, lanes], (1, 1)) * mixing_of(cum_rows, cols, h, size)
+        scores = dot(d, v2[:, lanes], (1, 1)) * mixing_of(cum_rows, cols, h)
         scores = scores.astype(BF16)
         query_grad = dot(scores, kc2[:, lanes], (1, 0)) + growth[:, h : h + 1] * dot(
             d, unless(start, before[lanes, :]), (1, 1)
@@ -259,24 +291,28 @@
 
 
 def outer_grad_kernel(
-    last, partial, key_grad, kc2, v2, cum, behind, more, taps, keep, send, padded, done
+    last, part, partial, key_grad, kc2, v2, cum, behind, more, taps, keep, send, padded, done
 ):
     size, width = partial.shape
     dim = behind.shape[1]
-    heads = width // dim
-    own, _ = halves(width)
+    heads = width // dim // PARTS
+    chunk = width // PARTS
+    mine = lax.rem(lax.axis_index("ctx"), PAIR)
+    own = pl.ds(pl.multiple_of(mine * width + part * chunk, chunk), chunk)
     ends = lax.axis_index("ctx") >= last
-    tops = behind[width:, :].astype(F32)
+    tops = unless(ends, behind[chunk:, :].astype(F32))
     cols = cum[...].T
     after = jnp.exp(cols[size - 1 :, :] - cols)
     for h in range(heads):
-        lanes = slice(h * dim, (h + 1) * dim)
-        scale = after[:, h : h + 1]
-        state = unless(ends, behind[lanes, :])
-        padded[:size, lanes] = key_grad[:, lanes] + scale * dot(v2[:, lanes], state, (1, 1))
-        done[:, lanes] = partial[:, lanes] + scale * dot(kc2[:, lanes], state, (1, 0))
+        at = part * heads + h
+        lanes = slice(at * dim, (at + 1) * dim)
+        here = slice(h * dim, (h + 1) * dim)
+        scale = after[:, at : at + 1]
+        state = unless(ends, behind[here, :])
+        padded[:size, here] = key_grad[:, lanes] + scale * dot(v2[:, lanes], state, (1, 1))
+        done[:, here] = partial[:, lanes] + scale * dot(kc2[:, lanes], state, (1, 0))
         top = jnp.concatenate([tops[4 * h : 4 * h + 4], jnp.zeros((4, dim), F32)], 0)
-        padded[size:, lanes] = unless(ends, top) + more[:, lanes]
+        padded[size:, here] = top + more[:, lanes]
     total = done[...]
     for j in range(taps.shape[1]):
         total = total + taps[0, j : j + 1, own] * padded[j : j + size, :]
@@ -287,19 +323,28 @@
     send[...] = unless(first, done[there, :]).astype(BF16)
 
 
-def place_kernel(kept, got, out, sems):
-    own, other = halves(kept.shape[1])
-    for copy in copy_all([(kept, out.at[0, :, own]), (got, out.at[0, :, other])], sems):
+def place_kernel(*refs):
+    *pieces, out, sems = refs
+    kept, got = pieces[: len(pieces) // 2], pieces[len(pieces) // 2 :]
+    width = kept[0].shape[1]
+    mine = lax.rem(lax.axis_index("ctx"), PAIR)
+    pairs = []
+    for half, parts in ((mine, kept), (1 - mine, got)):
+        for i, part in enumerate(parts):
+            start = pl.multiple_of((half * len(parts) + i) * width, width)
+            pairs.append((part, out.at[0, :, pl.ds(start, width)]))
+    for copy in copy_all(pairs, sems):
         copy.wait()
 
 
 def placed(kept, got):
-    rows, width = kept.shape
+    pieces = kept + got
+    rows = kept[0].shape[0]
     return call(
         place_kernel,
-        [shape((1, rows, PAIR * width), BF16)],
-        kept, got,
-        scratch=[pltpu.SemaphoreType.DMA((2,))],
+        [shape((1, rows, sum(piece.shape[1] for piece in pieces)), BF16)],
+        *pieces,
+        scratch=[pltpu.SemaphoreType.DMA((len(pieces),))],
         out_hbm=True,
     )[0]
 
@@ -348,22 +393,25 @@
     supers = blocks // PAIR
     width_all = queries.shape[2] * lax.axis_size("tp")
     log_decay = jnp.swapaxes(log_decay, 1, 2)
-    arrays = (queries, key_input, values, out_grad)
-    queries, key_input, values, out_grad = (
+    arrays = (queries, key_input, values, out_grad, log_decay)
+    queries, key_input, values, out_grad, decays = (
         pltpu.with_memory_space_constraint(x, pltpu.HBM) for x in arrays
     )
 
     first = call(
         pack_kernel,
         [shape((2 * rows + EDGE, width), BF16)],
-        key_input, values, log_decay,
-        scratch=[pltpu.SemaphoreType.DMA((2,))],
-        hbm=range(2),
+        key_input, values, decays,
+        scratch=[pltpu.VMEM(log_decay.shape, F32), pltpu.SemaphoreType.DMA((3,))],
+        hbm=range(3),
     )[0]
     got = swapped(first)
-    edge = arrays[1][0, rows - EDGE :]
-    near = lax.ppermute(edge[:, :width], "ctx", [(i, i + 1) for i in range(1, blocks - 1, 2)])
-    far = lax.ppermute(edge[:, width:], "ctx", [(i, i + 2) for i in range(1, blocks - 2, 2)])
+    edges = ()
+    if supers > 2:
+        edge = arrays[1][0, rows - EDGE :]
+        near = lax.ppermute(edge[:, :width], "ctx", [(i, i + 1) for i in range(1, blocks - 1, 2)])
+        far = lax.ppermute(edge[:, width:], "ctx", [(i, i + 2) for i in range(1, blocks - 2, 2)])
+        edges = (near + far,)
     second, own = call(
         pack_more_kernel,
         [shape((2 * rows, width), BF16), shape((4 * rows, width), BF16)],
@@ -372,19 +420,21 @@
         hbm=range(4),
     )
     got_more = swapped(second)
-    kc2, v2, cum, state = call(
+    kc2, v2, cum, state, top = call(
         join_kernel,
-        [shape((size, width), BF16)] * 2 + [shape((8, size), F32), shape((width, dim), BF16)],
-        got, near, far, own, log_decay, conv_weight,
+        [shape((size, width), BF16)] * 2
+        + [shape((8, size), F32), shape((width + 4 * heads, dim), BF16), shape((EDGE, width), F32)],
+        got, own, log_decay, conv_weight, *edges,
         scratch=[pltpu.VMEM((EDGE + size, width), F32), pltpu.VMEM((8, size), F32)],
     )
     carry = jnp.repeat(jnp.exp(cum[:heads, -1]), dim)[:, None]
     pair_index = lax.axis_index("ctx") // PAIR
     before = turned(state, "ctx", PAIR)
     for _ in range(supers - 2):
-        earlier = unless(pair_index == 0, before).astype(F32)
-        joined = state.astype(F32) + carry * earlier
-        before = turned(joined.astype(BF16), "ctx", PAIR)
+        earlier = unless(pair_index == 0, before[:width]).astype(F32)
+        joined = state[:width].astype(F32) + carry * earlier
+        moved = turned(joined.astype(BF16), "ctx", PAIR)
+        before = jnp.concatenate([moved, before[width:]], 0)
 
     q2, g2, weights, inside = call(
         local_kernel,
@@ -393,35 +443,44 @@
         got_more, own, kc2, v2, cum,
         flops=4 * heads * size * size * dim,
     )
-    attended, sums = call(
+    kc2, weights, attended, sums = call(
         attend_kernel,
-        [shape((size, width), F32), shape((2, size), F32)],
-        inside, q2, g2, cum, before,
+        [shape(kc2.shape, BF16), shape(weights.shape, BF16),
+         shape((size, width), F32), shape((2, size), F32)],
+        kc2, weights, inside, q2, g2, v2, cum, before, top, conv_weight,
+        scratch=[pltpu.VMEM((EDGE, width), F32)],
+        alias=((0, 0), (1, 1)),
     )
     parts = summed_parts(sums)
-    scales, grad, adjoint = call(
+    chunk = width // PARTS
+    scales, grad, *adjoints = call(
         lambda *refs: grad_kernel(width_all, *refs),
-        [shape((8, size), F32), shape((size, width), BF16),
-         shape((width + 4 * heads, dim), BF16)],
+        [shape((8, size), F32), shape((size, width), BF16)]
+        + [shape((chunk + EDGE, dim), BF16)] * PARTS,
         attended, q2, v2, g2, cum, *parts,
     )
-    behind = turned(adjoint, "ctx", -PAIR)
+    last_pair = pair_index == supers - 1
+    behind = []
+    for i, adjoint in enumerate(adjoints):
+        moved = turned(adjoint, "ctx", -PAIR)
+        for _ in range(supers - 2):
+            later = unless(last_pair, moved[:chunk]).astype(F32)
+            joined = adjoint[:chunk].astype(F32) + carry[i * chunk : (i + 1) * chunk] * later
+            state = turned(joined.astype(BF16), "ctx", -PAIR)
+            moved = jnp.concatenate([state, moved[chunk:]], 0)
+        behind.append(moved)
     more = jnp.zeros((8, width), F32)
-    for step in range(supers - 2):
-        later = unless(pair_index == supers - 1, behind[:width]).astype(F32)
-        joined = adjoint[:width].astype(F32) + carry * later
-        moved = turned(joined.astype(BF16), "ctx", -PAIR)
-        behind = jnp.concatenate([moved, behind[width:]], 0)
     if supers > 2:
         after = jnp.exp(cum[:heads, -1:] - cum[:heads, :8])
+        states = jnp.concatenate([part[:chunk] for part in behind], 0)
         state_part = jnp.einsum(
             "shv,hkv->shk",
             v2[:8].reshape(8, heads, dim),
-            unless(pair_index == supers - 1, behind[:width]).reshape(heads, dim, dim),
+            unless(last_pair, states).reshape(heads, dim, dim),
             preferred_element_type=F32,
         )
         more = turned((after.T[:, :, None] * state_part).reshape(8, width), "ctx", -PAIR)
-        more = unless(pair_index == supers - 1, more)
+        more = unless(last_pair, more)
 
     keep, send, partial, key_grad = call(
         inner_grad_kernel,
@@ -430,15 +489,18 @@
         scratch=[pltpu.VMEM((size, width), BF16)],
         flops=10 * heads * size * size * dim,
     )
-    layer_output = placed(keep, swapped(send))
-    keep, send = call(
-        lambda *refs: outer_grad_kernel(blocks - PAIR, *refs),
-        [shape((rows, width), BF16)] * 2,
-        partial, key_grad, kc2, v2, cum, behind, more, conv_weight,
-        scratch=[pltpu.VMEM((size + 8, width), F32), pltpu.VMEM((size, width), F32)],
-    )
-    input_next = placed(to_earlier_section(keep, 0), to_earlier_section(send, 1))
-    return (layer_output, input_next)
+    layer_output = placed([keep], [swapped(send)])
+    kept, got = [], []
+    for i in range(PARTS):
+        keep, send = call(
+            lambda *refs, i=i: outer_grad_kernel(blocks - PAIR, i, *refs),
+            [shape((rows, chunk), BF16)] * 2,
+            partial, key_grad, kc2, v2, cum, behind[i], more, conv_weight,
+            scratch=[pltpu.VMEM((size + 8, chunk), F32), pltpu.VMEM((size, chunk), F32)],
+        )
+        kept.append(to_earlier_section(keep, 0))
+        got.append(to_earlier_section(send, 1))
+    return (layer_output, placed(kept, got))
 
 
 def solution(mesh):

time: 50.8 us -> 49 us (0.965)
  starting transfers between devices: 17.1 us -> 14.5 us
  waiting for transfers between devices: 21.6 us -> 23.5 us
  local copies, waits for them, and re-layouts: 1.46 us -> 0.01 us
  Pallas kernels: 9.55 us -> 10.1 us
    ppermute x3, waiting for transfers between devices: 5.31 us -> 8.62 us  [swapped(): lax.ppermute(block, 'ctx', [(i, i ^ 1) for i in range(lax.axis_size('ctx'...]
    ppermute x2 -> x0, starting transfers between devices: 1.46 us -> none  [the longest x1 0.79 us: per_device(): lax.ppermute(edge[:, :width], 'ctx', [(i, i + 1) for i in range(1, blocks...]
    ppermute x2, starting transfers between devices: 7.06 us -> 5.84 us  [turned(): lax.ppermute(block, axis, [(i, (i + distance) % count) for i in range(cou...]
    ppermute x2, waiting for transfers between devices: 7.15 us -> 6.09 us  [turned(): lax.ppermute(block, axis, [(i, (i + distance) % count) for i in range(cou...]
    squeeze x1 -> x0, local copies, waits for them, and re-layouts: 0.76 us -> none  [per_device(): edge = arrays[1][0, rows - EDGE:]]
    unnamed x6 -> x4, local copies, waits for them, and re-layouts: 0.69 us -> 0.01 us
    pallas_call x10, Pallas kernels: 9.55 us -> 10.1 us  [call(): pl.pallas_call(kernel, out_shape=outs, in_specs=[pl.BlockSpec(memory_spac...]
  transfers between devices with their start and end apart: 13 -> 11, of which waited for: 10 -> 10; matrix products, arithmetic and copies ran while one was open for 2% -> 0% of each run, Pallas kernels for 12% -> 12%
where the time goes in v3:
time: 49 us; the launch traced here: 48.8 us
  waiting for transfers between devices  23.5 us (48%)
  starting transfers between devices  14.5 us (30%)
  Pallas kernels  10.1 us (21%)
  between operations  0.7 us (1%)
    pallas_call x10, Pallas kernels, call(): pl.pallas_call(kernel, out_shape=outs, in_specs=[pl.BlockSpec(memory_spac...  10.1 us
    ppermute x3, waiting for transfers between devices, swapped(): lax.ppermute(block, 'ctx', [(i, i ^ 1) for i in range(lax.axis_size('ctx'...  8.62 us
    ppermute x2, waiting for transfers between devices, turned(): lax.ppermute(block, axis, [(i, (i + distance) % count) for i in range(cou...  6.09 us
    ppermute x2, starting transfers between devices, turned(): lax.ppermute(block, axis, [(i, (i + distance) % count) for i in range(cou...  5.84 us
    ppermute x2, waiting for transfers between devices, to_earlier_section(): return lax.ppermute(block, ('ctx', 'pp'), route)  4.68 us
    ppermute x3, starting transfers between devices, summed_parts(): parts.append(lax.ppermute(pair, ('ctx', 'tp'), route))  3.49 us
    ppermute x3, starting transfers between devices, swapped(): lax.ppermute(block, 'ctx', [(i, i ^ 1) for i in range(lax.axis_size('ctx'...  3.27 us
    ppermute x3, waiting for transfers between devices, summed_parts(): parts.append(lax.ppermute(pair, ('ctx', 'tp'), route))  2.91 us
  transfers between devices with their start and end apart: 11, of which 10 were waited for; matrix products, arithmetic and copies ran while one was open for 0% of the time, Pallas kernels for 12%

profile of v3, /device:TPU:0, one launch (start us, length us, event | category | flops | bytes accessed | tf_op | source)
XLA Modules:
  0.0 48.8 jit_solution(8184989547698760041)
XLA Ops:
  0.6 1.0 %shard_map.77 = bf16[272,512]{1,0:T(8,128)(2,1)S(1)} custom-call(bf16[1,128,1024]{2,1,0:T(8,128)(2,1)} %k.3, bf16[1,128,1024]{2,1,0:T(8,128)(2,1)} %v.3, f32[1,8,128]{2,1,0:T(8,128)} %bitcast.1), custom_call_target="tpu_custom_call" | custom-call | bytes 806912 | tf_op jit(solution)/shard_map/pallas_call | solution.py:20
  1.6 3.1 %collective-permute-start = (bf16[272,512]{1,0:T(8,128)(2,1)S(1)}, bf16[272,512]{1,0:T(8,128)(2,1)S(1)}, u32[]{:S(2)}, u32[]{:S(2)}) collective-permute-start(bf16[272,512]{1,0:T(8,128)(2,1)S(1)} %shard_map.77), channel_id=1, source_target_pairs={{0,8},{8,0},{16,24},{24,16},{1,9},{9,1},{17,25},{25,17},{2,10},{10... | collective-permute-start | bytes 835592 | tf_op jit(solution)/shard_map/ppermute | solution.py:358
  4.7 0.0 copy-start
  4.7 0.0 copy-start.1
  4.7 1.3 %shard_map.78 = (bf16[256,512]{1,0:T(8,128)(2,1)S(1)}, bf16[512,512]{1,0:T(8,128)(2,1)S(1)}) custom-call(bf16[1,128,1024]{2,1,0:T(8,128)(2,1)} %q.1, bf16[1,128,1024]{2,1,0:T(8,128)(2,1)} %k.3, bf16[1,128,1024]{2,1,0:T(8,128)(2,1)} %v.3, bf16[1,128,1024]{2,1,0:T(8,128)(2,1)} %g.1, bf16[16,512]{1,0:T(8,128)(2,1)S(1)} %slice.4._), custom_call_target="tpu_custom_call" | custom-call | bytes 1851392 | tf_op jit(solution)/shard_map/pallas_call | solution.py:20
  6.0 0.1 collective-permute-start.1
  6.1 6.1 %collective-permute-done.got = bf16[272,512]{1,0:T(8,128)(2,1)S(1)} collective-permute-done((bf16[272,512]{1,0:T(8,128)(2,1)S(1)}, bf16[272,512]{1,0:T(8,128)(2,1)S(1)}, u32[]{:S(2)}, u32[]{:S(2)}) %collective-permute-start) | collective-permute-done | bytes 278560 | tf_op jit(solution)/shard_map/ppermute | solution.py:358
  12.2 0.0 copy-done
  12.2 0.0 copy-done.1
  12.2 1.1 %shard_map.79 = (bf16[256,512]{1,0:T(8,128)(2,1)S(1)}, bf16[256,512]{1,0:T(8,128)(2,1)S(1)}, f32[8,256]{1,0:T(8,128)S(1)}, bf16[528,128]{1,0:T(8,128)(2,1)S(1)}, f32[16,512]{1,0:T(8,128)S(1)}) custom-call(bf16[272,512]{1,0:T(8,128)(2,1)S(1)} %collective-permute-done.got, bf16[512,512]{1,0:T(8,128)(2,1)S(1)} %get-tuple-element.26.own, ...), custom_call_target="tpu_custom_call" | custom-call | bytes 1523712 | tf_op jit(solution)/shard_map/pallas_call | solution.py:20
  13.3 3.1 %collective-permute-start.2 = (bf16[528,128]{1,0:T(8,128)(2,1)S(1)}, bf16[528,128]{1,0:T(8,128)(2,1)S(1)}, u32[]{:S(2)}, u32[]{:S(2)}) collective-permute-start(bf16[528,128]{1,0:T(8,128)(2,1)S(1)} %get-tuple-element.35), channel_id=1, source_target_pairs={{0,16},{8,24},{16,0},{24,8},{1,17},{9,25},{17,1},{25,9},{2,18},{10... | collective-permute-start | bytes 405512 | tf_op jit(solution)/shard_map/ppermute | solution.py:354
  16.5 2.5 %collective-permute-done.1.got = bf16[256,512]{1,0:T(8,128)(2,1)S(1)} collective-permute-done((bf16[256,512]{1,0:T(8,128)(2,1)S(1)}, bf16[256,512]{1,0:T(8,128)(2,1)S(1)}, u32[]{:S(2)}, u32[]{:S(2)}) %collective-permute-start.1) | collective-permute-done | bytes 262176 | tf_op jit(solution)/shard_map/ppermute | solution.py:358
  19.0 0.8 %shard_map.80 = (bf16[256,512]{1,0:T(8,128)(2,1)S(1)}, bf16[256,512]{1,0:T(8,128)(2,1)S(1)}, bf16[4,256,256]{2,1,0:T(8,128)(2,1)S(1)}, f32[256,512]{1,0:T(8,128)S(1)}) custom-call(bf16[256,512]{1,0:T(8,128)(2,1)S(1)} %collective-permute-done.1.got, bf16[512,512]{1,0:T(8,128)(2,1)S(1)} %get-tuple-element.26.own, bf16[256,512]{1,0:T(8,128)(2,1)S(1)} %get-tuple-element.27.kc2, ...), custom_call_target="tpu_custom_call" | custom-call | flops 134217728 | bytes 2891776 | tf_op jit(solution)/shard_map/pallas_call | solution.py:20
  19.8 2.6 %collective-permute-done.2.before = bf16[528,128]{1,0:T(8,128)(2,1)S(1)} collective-permute-done((bf16[528,128]{1,0:T(8,128)(2,1)S(1)}, bf16[528,128]{1,0:T(8,128)(2,1)S(1)}, u32[]{:S(2)}, u32[]{:S(2)}) %collective-permute-start.2) | collective-permute-done | bytes 135200 | tf_op jit(solution)/shard_map/ppermute | solution.py:354
  22.3 1.2 %shard_map.81 = (bf16[256,512]{1,0:T(8,128)(2,1)S(1)}, bf16[4,256,256]{2,1,0:T(8,128)(2,1)S(1)}, f32[256,512]{1,0:T(8,128)S(1)}, f32[2,256]{1,0:T(2,128)S(1)}) custom-call(bf16[256,512]{1,0:T(8,128)(2,1)S(1)} %get-tuple-element.27.kc2, bf16[4,256,256]{2,1,0:T(8,128)(2,1)S(1)} %get-tuple-element.31.weights, ...), custom_call_target="tpu_custom_call", output_to_operand_aliasing={{0}: (0, {}), {1}: (1, {})} | custom-call | bytes 3602432 | tf_op jit(solution)/shard_map/pallas_call | solution.py:20
  23.5 0.0 collective-permute-start.3
  23.5 1.2 %collective-permute-done.3 = f32[2,256]{1,0:T(2,128)S(1)} collective-permute-done((f32[2,256]{1,0:T(2,128)S(1)}, f32[2,256]{1,0:T(2,128)S(1)}, u32[]{:S(2)}, u32[]{:S(2)}) %collective-permute-start.3) | collective-permute-done | bytes 2080 | tf_op jit(solution)/shard_map/ppermute | solution.py:373
  24.7 1.7 %collective-permute-start.4 = (f32[2,256]{1,0:T(2,128)S(1)}, f32[2,256]{1,0:T(2,128)S(1)}, u32[]{:S(2)}, u32[]{:S(2)}) collective-permute-start(f32[2,256]{1,0:T(2,128)S(1)} %add.3.refs_5_), channel_id=1, source_target_pairs={{0,4},{2,6},{4,0},{6,2},{8,12},{10,14},{12,8},{14,10},{16,20},{18,... | collective-permute-start | bytes 6152 | tf_op jit(solution)/shard_map/ppermute | solution.py:383
  26.4 0.2 collective-permute-start.5
  26.6 1.6 %collective-permute-start.6 = (f32[2,256]{1,0:T(2,128)S(1)}, f32[2,256]{1,0:T(2,128)S(1)}, u32[]{:S(2)}, u32[]{:S(2)}) collective-permute-start(f32[2,256]{1,0:T(2,128)S(1)} %add.3.refs_5_), channel_id=1, source_target_pairs={{0,12},{2,14},{4,8},{6,10},{8,4},{10,6},{12,0},{14,2},{16,28},{18,... | collective-permute-start | bytes 6152 | tf_op jit(solution)/shard_map/ppermute | solution.py:383
  28.2 0.1 collective-permute-done.4.refs_6_
  28.3 1.7 %collective-permute-done.5.refs_7_ = f32[2,256]{1,0:T(2,128)S(1)} collective-permute-done((f32[2,256]{1,0:T(2,128)S(1)}, f32[2,256]{1,0:T(2,128)S(1)}, u32[]{:S(2)}, u32[]{:S(2)}) %collective-permute-start.5) | collective-permute-done | bytes 2080 | tf_op jit(solution)/shard_map/ppermute | solution.py:383
  30.0 1.1 %collective-permute-done.6.refs_8_ = f32[2,256]{1,0:T(2,128)S(1)} collective-permute-done((f32[2,256]{1,0:T(2,128)S(1)}, f32[2,256]{1,0:T(2,128)S(1)}, u32[]{:S(2)}, u32[]{:S(2)}) %collective-permute-start.6) | collective-permute-done | bytes 2080 | tf_op jit(solution)/shard_map/ppermute | solution.py:383
  31.1 1.2 %shard_map.82 = (f32[8,256]{1,0:T(8,128)S(1)}, bf16[256,512]{1,0:T(8,128)(2,1)S(1)}, bf16[528,128]{1,0:T(8,128)(2,1)S(1)}) custom-call(f32[256,512]{1,0:T(8,128)S(1)} %get-tuple-element.37.refs_0_.attended, bf16[256,512]{1,0:T(8,128)(2,1)S(1)} %get-tuple-element.33.q2.refs_1_, bf16[256,512]{1,0:T(8,128)(2,1)S(1)} %get-tuple-element.29.v2.refs_2_.refs_3_, ...), custom_call_target="tpu_custom_call" | custom-call | bytes 1732608 | tf_op jit(solution)/shard_map/pallas_call | solution.py:20
  32.3 2.7 %collective-permute-start.8 = (bf16[528,128]{1,0:T(8,128)(2,1)S(1)}, bf16[528,128]{1,0:T(8,128)(2,1)S(1)}, u32[]{:S(2)}, u32[]{:S(2)}) collective-permute-start(bf16[528,128]{1,0:T(8,128)(2,1)S(1)} %get-tuple-element.47), channel_id=1, source_target_pairs={{0,16},{8,24},{16,0},{24,8},{1,17},{9,25},{17,1},{25,9},{2,18},{10... | collective-permute-start | bytes 405512 | tf_op jit(solution)/shard_map/ppermute | solution.py:354
  35.0 1.5 %shard_map.83 = (bf16[128,512]{1,0:T(8,128)(2,1)S(1)}, bf16[128,512]{1,0:T(8,128)(2,1)S(1)}, f32[256,512]{1,0:T(8,128)S(1)}, f32[256,512]{1,0:T(8,128)S(1)}) custom-call(f32[256,512]{1,0:T(8,128)S(1)} %get-tuple-element.37.refs_0_.attended, f32[8,256]{1,0:T(8,128)S(1)} %get-tuple-element.39.scales, bf16[256,512]{1,0:T(8,128)(2,1)S(1)} %get-tuple-element.33.q2.refs_1_, ...), custom_call_target="tpu_custom_call" | custom-call | flops 335544320 | bytes 3559424 | tf_op jit(solution)/shard_map/pallas_call | solution.py:20
  36.5 0.1 collective-permute-start.7
  36.6 3.5 %collective-permute-done.8.refs_5_ = bf16[528,128]{1,0:T(8,128)(2,1)S(1)} collective-permute-done((bf16[528,128]{1,0:T(8,128)(2,1)S(1)}, bf16[528,128]{1,0:T(8,128)(2,1)S(1)}, u32[]{:S(2)}, u32[]{:S(2)}) %collective-permute-start.8) | collective-permute-done | bytes 135200 | tf_op jit(solution)/shard_map/ppermute | solution.py:354
  40.1 0.6 %shard_map.85 = (bf16[128,512]{1,0:T(8,128)(2,1)S(1)}, bf16[128,512]{1,0:T(8,128)(2,1)S(1)}) custom-call(f32[256,512]{1,0:T(8,128)S(1)} %get-tuple-element.45.refs_0_, f32[256,512]{1,0:T(8,128)S(1)} %get-tuple-element.46.refs_1_, bf16[256,512]{1,0:T(8,128)(2,1)S(1)} %get-tuple-element.40.kc2.refs_2_, ...), custom_call_target="tpu_custom_call" | custom-call | bytes 2011136 | tf_op jit(solution)/shard_map/pallas_call | solution.py:20
  40.8 1.4 %collective-permute-start.10 = (bf16[128,512]{1,0:T(8,128)(2,1)S(1)}, bf16[128,512]{1,0:T(8,128)(2,1)S(1)}, u32[]{:S(2)}, u32[]{:S(2)}) collective-permute-start(bf16[128,512]{1,0:T(8,128)(2,1)S(1)} %get-tuple-element.49), channel_id=1, source_target_pairs={{0,9},{1,8},{8,1},{9,0},{16,25},{17,24},{24,17},{25,16},{2,11},{3,... | collective-permute-start | bytes 393224 | tf_op jit(solution)/shard_map/ppermute | solution.py:368
  42.2 0.5 %collective-permute-start.9 = (bf16[128,512]{1,0:T(8,128)(2,1)S(1)}, bf16[128,512]{1,0:T(8,128)(2,1)S(1)}, u32[]{:S(2)}, u32[]{:S(2)}) collective-permute-start(bf16[128,512]{1,0:T(8,128)(2,1)S(1)} %get-tuple-element.48), channel_id=1, source_target_pairs={{0,1},{1,0},{8,9},{9,8},{16,17},{17,16},{24,25},{25,24},{2,3},{3,2... | collective-permute-start | bytes 393224 | tf_op jit(solution)/shard_map/ppermute | solution.py:368
  42.7 0.0 collective-permute-done.7.refs_1_
  42.7 0.7 %shard_map.84 = bf16[1,128,1024]{2,1,0:T(8,128)(2,1)} custom-call(bf16[128,512]{1,0:T(8,128)(2,1)S(1)} %get-tuple-element.43.refs_0_, bf16[128,512]{1,0:T(8,128)(2,1)S(1)} %collective-permute-done.7.refs_1_), custom_call_target="tpu_custom_call" | custom-call | bytes 524288 | tf_op jit(solution)/shard_map/pallas_call | solution.py:20
  43.4 3.4 %collective-permute-done.10.refs_1_ = bf16[128,512]{1,0:T(8,128)(2,1)S(1)} collective-permute-done((bf16[128,512]{1,0:T(8,128)(2,1)S(1)}, bf16[128,512]{1,0:T(8,128)(2,1)S(1)}, u32[]{:S(2)}, u32[]{:S(2)}) %collective-permute-start.10) | collective-permute-done | bytes 131104 | tf_op jit(solution)/shard_map/ppermute | solution.py:368
  46.8 1.3 %collective-permute-done.9.refs_0_ = bf16[128,512]{1,0:T(8,128)(2,1)S(1)} collective-permute-done((bf16[128,512]{1,0:T(8,128)(2,1)S(1)}, bf16[128,512]{1,0:T(8,128)(2,1)S(1)}, u32[]{:S(2)}, u32[]{:S(2)}) %collective-permute-start.9) | collective-permute-done | bytes 131104 | tf_op jit(solution)/shard_map/ppermute | solution.py:368
  48.1 0.7 %shard_map.86 = bf16[1,128,1024]{2,1,0:T(8,128)(2,1)} custom-call(bf16[128,512]{1,0:T(8,128)(2,1)S(1)} %collective-permute-done.9.refs_0_, bf16[128,512]{1,0:T(8,128)(2,1)S(1)} %collective-permute-done.10.refs_1_), custom_call_target="tpu_custom_call" | custom-call | bytes 524288 | tf_op jit(solution)/shard_map/pallas_call | solution.py:20
  (3 shorter events, 0.0 us)
Async XLA Ops:
  1.6 10.6 %collective-permute-start = (bf16[272,512]{1,0:T(8,128)(2,1)S(1)}, bf16[272,512]{1,0:T(8,128)(2,1)S(1)}, u32[]{:S(2)}, u32[]{:S(2)}) collective-permute-start(bf16[272,512]{1,0:T(8,128)(2,1)S(1)} %shard_map.77), channel_id=1, source_target_pairs={{0,8},{8,0},{16,24},{24,16},{1,9},{9,1},{17,25},{25,17},{2,10},{10... | collective-permute-start | bytes 835592 | tf_op jit(solution)/shard_map/ppermute | solution.py:358
  4.7 7.5 %copy-start = (f32[1,4,1024]{2,1,0:T(4,128)S(1)}, f32[1,4,1024]{2,1,0:T(4,128)}, u32[]{:S(2)}) copy-start(f32[1,4,1024]{2,1,0:T(4,128)} %refs_7_.1) | copy-start | bytes 49156
  4.7 7.5 %copy-start.1 = (f32[1,128,8]{1,2,0:T(8,128)S(1)}, f32[1,128,8]{1,2,0:T(8,128)}, u32[]{:S(2)}) copy-start(f32[1,128,8]{1,2,0:T(8,128)} %param.9) | copy-start | bytes 12292
  6.0 13.0 %collective-permute-start.1 = (bf16[256,512]{1,0:T(8,128)(2,1)S(1)}, bf16[256,512]{1,0:T(8,128)(2,1)S(1)}, u32[]{:S(2)}, u32[]{:S(2)}) collective-permute-start(bf16[256,512]{1,0:T(8,128)(2,1)S(1)} %get-tuple-element.28), channel_id=1, source_target_pairs={{0,8},{8,0},{16,24},{24,16},{1,9},{9,1},{17,25},{25,17},{2,10},{10... | collective-permute-start | bytes 786440 | tf_op jit(solution)/shard_map/ppermute | solution.py:358
  13.3 9.0 %collective-permute-start.2 = (bf16[528,128]{1,0:T(8,128)(2,1)S(1)}, bf16[528,128]{1,0:T(8,128)(2,1)S(1)}, u32[]{:S(2)}, u32[]{:S(2)}) collective-permute-start(bf16[528,128]{1,0:T(8,128)(2,1)S(1)} %get-tuple-element.35), channel_id=1, source_target_pairs={{0,16},{8,24},{16,0},{24,8},{1,17},{9,25},{17,1},{25,9},{2,18},{10... | collective-permute-start | bytes 405512 | tf_op jit(solution)/shard_map/ppermute | solution.py:354
  23.5 1.2 %collective-permute-start.3 = (f32[2,256]{1,0:T(2,128)S(1)}, f32[2,256]{1,0:T(2,128)S(1)}, u32[]{:S(2)}, u32[]{:S(2)}) collective-permute-start(f32[2,256]{1,0:T(2,128)S(1)} %get-tuple-element.38), channel_id=1, source_target_pairs={{0,2},{2,0},{4,6},{6,4},{1,3},{3,1},{5,7},{7,5},{8,10},{10,8},{12,... | collective-permute-start | bytes 6152 | tf_op jit(solution)/shard_map/ppermute | solution.py:373
  24.7 3.6 %collective-permute-start.4 = (f32[2,256]{1,0:T(2,128)S(1)}, f32[2,256]{1,0:T(2,128)S(1)}, u32[]{:S(2)}, u32[]{:S(2)}) collective-permute-start(f32[2,256]{1,0:T(2,128)S(1)} %add.3.refs_5_), channel_id=1, source_target_pairs={{0,4},{2,6},{4,0},{6,2},{8,12},{10,14},{12,8},{14,10},{16,20},{18,... | collective-permute-start | bytes 6152 | tf_op jit(solution)/shard_map/ppermute | solution.py:383
  26.4 3.6 %collective-permute-start.5 = (f32[2,256]{1,0:T(2,128)S(1)}, f32[2,256]{1,0:T(2,128)S(1)}, u32[]{:S(2)}, u32[]{:S(2)}) collective-permute-start(f32[2,256]{1,0:T(2,128)S(1)} %add.3.refs_5_), channel_id=1, source_target_pairs={{0,8},{2,10},{4,12},{6,14},{8,0},{10,2},{12,4},{14,6},{16,24},{18,... | collective-permute-start | bytes 6152 | tf_op jit(solution)/shard_map/ppermute | solution.py:383
  26.6 4.5 %collective-permute-start.6 = (f32[2,256]{1,0:T(2,128)S(1)}, f32[2,256]{1,0:T(2,128)S(1)}, u32[]{:S(2)}, u32[]{:S(2)}) collective-permute-start(f32[2,256]{1,0:T(2,128)S(1)} %add.3.refs_5_), channel_id=1, source_target_pairs={{0,12},{2,14},{4,8},{6,10},{8,4},{10,6},{12,0},{14,2},{16,28},{18,... | collective-permute-start | bytes 6152 | tf_op jit(solution)/shard_map/ppermute | solution.py:383
  32.3 7.8 %collective-permute-start.8 = (bf16[528,128]{1,0:T(8,128)(2,1)S(1)}, bf16[528,128]{1,0:T(8,128)(2,1)S(1)}, u32[]{:S(2)}, u32[]{:S(2)}) collective-permute-start(bf16[528,128]{1,0:T(8,128)(2,1)S(1)} %get-tuple-element.47), channel_id=1, source_target_pairs={{0,16},{8,24},{16,0},{24,8},{1,17},{9,25},{17,1},{25,9},{2,18},{10... | collective-permute-start | bytes 405512 | tf_op jit(solution)/shard_map/ppermute | solution.py:354
  36.5 6.1 %collective-permute-start.7 = (bf16[128,512]{1,0:T(8,128)(2,1)S(1)}, bf16[128,512]{1,0:T(8,128)(2,1)S(1)}, u32[]{:S(2)}, u32[]{:S(2)}) collective-permute-start(bf16[128,512]{1,0:T(8,128)(2,1)S(1)} %get-tuple-element.44), channel_id=1, source_target_pairs={{0,8},{8,0},{16,24},{24,16},{1,9},{9,1},{17,25},{25,17},{2,10},{10... | collective-permute-start | bytes 393224 | tf_op jit(solution)/shard_map/ppermute | solution.py:358
  40.8 6.0 %collective-permute-start.10 = (bf16[128,512]{1,0:T(8,128)(2,1)S(1)}, bf16[128,512]{1,0:T(8,128)(2,1)S(1)}, u32[]{:S(2)}, u32[]{:S(2)}) collective-permute-start(bf16[128,512]{1,0:T(8,128)(2,1)S(1)} %get-tuple-element.49), channel_id=1, source_target_pairs={{0,9},{1,8},{8,1},{9,0},{16,25},{17,24},{24,17},{25,16},{2,11},{3,... | collective-permute-start | bytes 393224 | tf_op jit(solution)/shard_map/ppermute | solution.py:368
  42.2 5.9 %collective-permute-start.9 = (bf16[128,512]{1,0:T(8,128)(2,1)S(1)}, bf16[128,512]{1,0:T(8,128)(2,1)S(1)}, u32[]{:S(2)}, u32[]{:S(2)}) collective-permute-start(bf16[128,512]{1,0:T(8,128)(2,1)S(1)} %get-tuple-element.48), channel_id=1, source_target_pairs={{0,1},{1,0},{8,9},{9,8},{16,17},{17,16},{24,25},{25,24},{2,3},{3,2... | collective-permute-start | bytes 393224 | tf_op jit(solution)/shard_map/ppermute | solution.py:368

commit v4 on v3

v4 whole, which is shorter than its diff:
```python
import jax
import jax.numpy as jnp
from jax import lax
from jax.experimental import pallas as pl
from jax.experimental.pallas import tpu as pltpu
from jax.sharding import PartitionSpec as P

F32 = jnp.float32
BF16 = jnp.bfloat16
PAIR = 2
EDGE = 16
LEAD = 4
STEPS = 2
PARTS = 1


def call(kernel, outs, *args, scratch=(), flops=0, hbm=(), out_hbm=False, alias=()):
    vmem = pl.BlockSpec(memory_space=pltpu.VMEM)
    moved = sum(a.size * a.dtype.itemsize for a in args) + sum(
        s.size * s.dtype.itemsize for s in outs
    )
    return pl.pallas_call(
        kernel,
        out_shape=outs,
        in_specs=[
            pl.BlockSpec(memory_space=pltpu.HBM) if i in hbm else vmem for i in range(len(args))
        ],
        out_specs=[pl.BlockSpec(memory_space=pltpu.HBM) if out_hbm else vmem] * len(outs),
        scratch_shapes=scratch,
        input_output_aliases=dict(alias),
        compiler_params=pltpu.CompilerParams(vmem_limit_bytes=32 * 1024 * 1024),
        cost_estimate=pl.CostEstimate(flops=flops, bytes_accessed=moved, transcendentals=0),
    )(*args)


def shape(dims, dtype):
    return jax.ShapeDtypeStruct(dims, dtype)


def halves(size):
    mine = lax.rem(lax.axis_index("ctx"), PAIR)
    return (
        pl.ds(pl.multiple_of(mine * size, size), size),
        pl.ds(pl.multiple_of((1 - mine) * size, size), size),
    )


def dot(a, b, contract):
    return lax.dot_general(a, b, ((contract[:1], contract[1:]), ((), ())), preferred_element_type=F32)


def split3(x):
    hi = x.astype(BF16)
    rest = x - hi.astype(F32)
    mid = rest.astype(BF16)
    return hi, mid, (rest - mid.astype(F32)).astype(BF16)


def half_rows(rows, mine, heads):
    return jnp.where(mine == 0, rows[:heads], rows[heads:])


def copy_all(pairs, sems):
    copies = [pltpu.make_async_copy(src, to, sems.at[i]) for i, (src, to) in enumerate(pairs)]
    for copy in copies:
        copy.start()
    return copies


def step_lanes(width, chunk, step, mine):
    return pl.ds(pl.multiple_of(mine * width + step * chunk, chunk), chunk)


def pack_kernel(k, v, log_decay, *refs):
    *outs, cum, decays, sems = refs
    first = outs[0]
    rows, heads = k.shape[1], log_decay.shape[1] // PAIR
    mine = lax.rem(lax.axis_index("ctx"), PAIR)
    chunk = first.shape[1]
    pairs = [(log_decay, decays)]
    for step, out in enumerate(outs):
        other = step_lanes(k.shape[2] // PAIR, chunk, step, 1 - mine)
        for i, ref in enumerate((k, v)):
            pairs.append((ref.at[0, :, other], out.at[i * rows : (i + 1) * rows, :]))
    copies = copy_all(pairs, sems)
    copies[0].wait()
    upto = lax.broadcasted_iota(jnp.int32, (rows, rows), 0) <= lax.broadcasted_iota(
        jnp.int32, (rows, rows), 1
    )
    upto = upto.astype(F32).astype(BF16)
    sums = sum(dot(part, upto, (1, 0)) for part in split3(decays[0]))
    cum[...] = sums
    line = chunk // rows
    parts = [
        jnp.concatenate([part[h : h + 1] for h in range(at, at + line)], 1).astype(F32)
        for part in split3(half_rows(sums, 1 - mine, heads))
        for at in range(0, heads, line)
    ]
    parts.append(jnp.zeros((EDGE - len(parts), chunk), F32))
    first[2 * rows :, :] = jnp.concatenate(parts, 0).astype(BF16)
    for copy in copies[1:]:
        copy.wait()


def pack_more_kernel(q, k, v, g, _, second, third, own, sems):
    rows = q.shape[1]
    lanes_own, other = halves(q.shape[2] // PAIR)
    pairs = [(q.at[0, :, other], second), (g.at[0, :, other], third)]
    pairs += [
        (ref.at[0, :, lanes_own], own.at[i * rows : (i + 1) * rows, :])
        for i, ref in enumerate((k, v, q, g))
    ]
    for copy in copy_all(pairs, sems):
        copy.wait()


def join_step(step, got, own, taps, edges, cum_rows, kc2, v2, top, state, padded):
    size, width = kc2.shape
    rows, chunk = size // PAIR, got.shape[1]
    dim = state.shape[1]
    heads = chunk // dim
    here, there = halves(rows)
    mine = lax.rem(lax.axis_index("ctx"), PAIR)
    lanes = slice(step * chunk, (step + 1) * chunk)
    v2[here, lanes] = own[rows : 2 * rows, lanes]
    v2[there, lanes] = got[rows : 2 * rows, :]
    padded[:EDGE, :] = edges[0][:, lanes].astype(F32) if edges else jnp.zeros((EDGE, chunk), F32)
    start = pl.multiple_of(EDGE + mine * rows, EDGE)
    padded[pl.ds(start, rows), :] = own[:rows, lanes].astype(F32)
    start = pl.multiple_of(EDGE + (1 - mine) * rows, EDGE)
    padded[pl.ds(start, rows), :] = got[:rows, :].astype(F32)
    total = jnp.zeros((size, chunk), F32)
    taps_at = step_lanes(width, chunk, step, mine)
    for j in range(taps.shape[1]):
        total = total + taps[0, j : j + 1, taps_at] * padded[EDGE - j : EDGE - j + size, :]
    keys = total.astype(BF16)
    kc2[:, lanes] = keys
    top[:, lanes] = total[:EDGE]
    cols = cum_rows.T
    after = jnp.exp(cols[size - 1 :, :] - cols)
    keys = keys.astype(F32)
    for h in range(heads):
        at = step * heads + h
        scaled = (keys[:, h * dim : (h + 1) * dim] * after[:, at : at + 1]).astype(BF16)
        sums = dot(scaled, v2[:, at * dim : (at + 1) * dim], (0, 0))
        state[h * dim : (h + 1) * dim, :] = sums.astype(BF16)
    last = padded[EDGE + size - LEAD : EDGE + size, :]
    last = [last[:, h * dim : (h + 1) * dim] for h in range(heads)]
    if LEAD * heads < EDGE:
        last.append(jnp.zeros((EDGE - LEAD * heads, dim), F32))
    state[chunk:, :] = jnp.concatenate(last, 0).astype(BF16)


def join_kernel(got, own, own_cum, taps, *refs):
    *edges, kc2, v2, top, state, cum, padded = refs
    rows, heads = own_cum.shape[1], own_cum.shape[0] // PAIR
    mine = lax.rem(lax.axis_index("ctx"), PAIR)
    coded = got[2 * rows :, :].astype(F32)
    lines = heads * rows // coded.shape[1]
    row = coded[:lines] + coded[lines : 2 * lines] + coded[2 * lines : 3 * lines]
    per_line = heads // lines
    other_rows = jnp.concatenate(
        [
            row[h // per_line : h // per_line + 1, h % per_line * rows : (h % per_line + 1) * rows]
            for h in range(heads)
        ],
        0,
    )
    own_rows = half_rows(own_cum[...], mine, heads)
    front = jnp.where(mine == 0, own_rows, other_rows)
    back = jnp.where(mine == 0, other_rows, own_rows) + front[:, rows - 1 :]
    cum_rows = jnp.concatenate([front, back], 1)
    cum_rows = jnp.concatenate([cum_rows, jnp.zeros((8 - heads, PAIR * rows), F32)], 0)
    cum[...] = cum_rows
    join_step(0, got, own, taps, edges, cum_rows, kc2, v2, top, state, padded)


def join_next_kernel(step, _kc2, _v2, _top, got, own, cum, taps, *refs):
    *edges, kc2, v2, top, state, padded = refs
    join_step(step, got, own, taps, edges, cum[...], kc2, v2, top, state, padded)


def mixing_of(cum_rows, cols, h, first=0):
    differ = cols[:, h : h + 1] - cum_rows[h : h + 1, :]
    at = lax.broadcasted_iota(jnp.int32, differ.shape, 1)
    causal = (lax.broadcasted_iota(jnp.int32, differ.shape, 0) >= at) & (at >= first)
    return jnp.where(causal, jnp.exp(jnp.where(causal, differ, 0.0)), 0.0)


def lead_mixing_of(cum_rows, cols, heads):
    wide = (cols.shape[0], heads * LEAD)
    lane = lax.broadcasted_iota(jnp.int32, wide, 1)
    late = jnp.zeros(wide, F32)
    for h in range(heads):
        late = jnp.where(lane // LEAD == h, cols[:, h : h + 1], late)
    early = jnp.concatenate([cum_rows[h : h + 1, :LEAD] for h in range(heads)], 1)
    causal = lax.broadcasted_iota(jnp.int32, wide, 0) >= lane % LEAD
    return jnp.where(causal, jnp.exp(jnp.where(causal, late - early, 0.0)), 0.0)


def block_diagonal(rows, dim, heads, first=0):
    wide = jnp.concatenate([rows] * heads, 0)
    head = lax.broadcasted_iota(jnp.int32, wide.shape, 0) // LEAD
    lane = lax.broadcasted_iota(jnp.int32, wide.shape, 1) // dim + first
    return jnp.where(head == lane, wide, 0.0).astype(BF16)


def local_kernel(got, got_g, own, kc2, v2, cum, q2, g2, weights, inside, lead_mixing, lead_values):
    size, width = q2.shape
    heads, dim = weights.shape[0], width // weights.shape[0]
    rows = size // PAIR
    here, there = halves(rows)
    q2[here, :] = own[2 * rows : 3 * rows, :]
    q2[there, :] = got[...]
    g2[here, :] = own[3 * rows :, :]
    g2[there, :] = got_g[...]
    cum_rows = cum[...]
    cols = cum_rows.T
    lead_mixing[...] = lead_mixing_of(cum_rows, cols, heads)
    lead_values[...] = block_diagonal(v2[:EDGE, :].astype(F32)[:LEAD], dim, heads)
    for h in range(heads):
        lanes = slice(h * dim, (h + 1) * dim)
        scores = dot(q2[:, lanes], kc2[:, lanes], (1, 1))
        w = (scores * mixing_of(cum_rows, cols, h, LEAD)).astype(BF16)
        weights[h] = w
        inside[:, lanes] = dot(w, v2[:, lanes], (1, 0))


def unless(flag, block):
    return jnp.where(flag, jnp.zeros_like(block), block)


def attend_kernel(step, *refs):
    kc2, inside, q2, g2, cum, top, taps, lead_mixing, lead_values, before, *refs = refs
    *carried, kc2_whole, attended, lead_weights, out, reach = refs
    size, width = q2.shape
    dim = before.shape[1]
    heads = width // dim
    chunk = width // STEPS
    lanes = slice(step * chunk, (step + 1) * chunk)
    mine = lax.rem(lax.axis_index("ctx"), PAIR)
    start = lax.axis_index("ctx") < PAIR
    tail = unless(start, before[chunk:, :].astype(F32))
    reach[...] = jnp.zeros_like(reach)
    for h in range(chunk // dim):
        reach[LEAD : 2 * LEAD, h * dim : (h + 1) * dim] = tail[LEAD * h : LEAD * (h + 1)]
    fixed = top[: 2 * LEAD, lanes]
    taps_at = step_lanes(width, chunk, step, mine)
    for j in range(1, taps.shape[1]):
        fixed = fixed + taps[0, j : j + 1, taps_at] * reach[2 * LEAD - j : 4 * LEAD - j, :]
    rows = jnp.concatenate([fixed, top[2 * LEAD :, lanes]], 0)
    kc2_whole[:EDGE, lanes] = rows.astype(BF16)
    lead_keys = block_diagonal(fixed[:LEAD], dim, heads, step * chunk // dim)
    lead = (dot(q2[:, lanes], lead_keys, (1, 1)) * lead_mixing[...]).astype(BF16)
    lead_weights[...] = lead
    growth = jnp.exp(cum[...].T)
    squares = carried[0][0] if carried else jnp.zeros((size, dim), F32)
    products = carried[0][1] if carried else jnp.zeros((size, dim), F32)
    for h in range(chunk // dim):
        at = step * chunk // dim + h
        here = slice(at * dim, (at + 1) * dim)
        state = unless(start, before[h * dim : (h + 1) * dim, :])
        a = inside[:, here] + dot(lead, lead_values[:, here], (1, 0))
        a = a + growth[:, at : at + 1] * dot(q2[:, here], state, (1, 0))
        attended[:, here] = a
        squares = squares + a * a
        products = products + a * g2[:, here].astype(F32)
    if step < STEPS - 1:
        out[0] = squares
        out[1] = products
        return
    ones = jnp.ones((8, dim), BF16)
    both = jnp.concatenate([squares, products], 0)
    line = sum(dot(ones, part, (1, 1)) for part in split3(both))[:1]
    out[...] = jnp.concatenate([line[:, :size], line[:, size:]], 0)


def grad_kernel(width_all, attended, q2, lead_mixing, lead_values, g2, cum, *refs):
    *sums, scales, grad = refs[:-PARTS]
    adjoints = refs[-PARTS:]
    size, width = q2.shape
    dim = adjoints[0].shape[1]
    heads = width // dim
    total = sum(ref[...] for ref in sums[1:]) + sums[0][...]
    inverse = 1.0 / jnp.sqrt(total[0:1] / width_all + 1e-06)
    shift = total[1:2] / width_all * inverse
    both = jnp.concatenate([inverse, shift, jnp.zeros((6, size), F32)], 0)
    scales[...] = both
    both = both.T
    inverse, shift = both[:, 0:1], both[:, 1:2]
    growth = jnp.exp(cum[...].T)
    for h in range(heads):
        lanes = slice(h * dim, (h + 1) * dim)
        n = attended[:, lanes] * inverse
        d = ((g2[:, lanes].astype(F32) - n * shift) * inverse).astype(BF16)
        grad[:, lanes] = d
        scaled = (q2[:, lanes].astype(F32) * growth[:, h : h + 1]).astype(BF16)
        part, at = divmod(h, heads // PARTS)
        adjoints[part][at * dim : (at + 1) * dim, :] = dot(scaled, d, (0, 0)).astype(BF16)
    scores = (dot(grad[...], lead_values[...], (1, 1)) * lead_mixing[...]).astype(BF16)
    tops = dot(scores, q2[...], (0, 0))
    per_part = heads // PARTS
    for i, adjoint in enumerate(adjoints):
        rows = [
            tops[LEAD * h : LEAD * (h + 1), h * dim : (h + 1) * dim]
            for h in range(i * per_part, (i + 1) * per_part)
        ]
        if LEAD * per_part < EDGE:
            rows.append(jnp.zeros((EDGE - LEAD * per_part, dim), F32))
        adjoint[width // PARTS :, :] = jnp.concatenate(rows, 0).astype(BF16)


def inner_grad_kernel(
    attended, scales, q2, kc2, v2, grad, weights, cum, *refs
):
    before, lead_weights = refs[:STEPS], refs[STEPS : 2 * STEPS]
    keep, send, partial, key_grad, normed = refs[2 * STEPS :]
    size, width = q2.shape
    dim = before[0].shape[1]
    heads = width // dim
    per_step = heads // STEPS
    start = lax.axis_index("ctx") < PAIR
    inverse = scales[...].T[:, 0:1]
    cum_rows = cum[...]
    cols = cum_rows.T
    growth = jnp.exp(cols)
    for h in range(heads):
        lanes = slice(h * dim, (h + 1) * dim)
        normed[:, lanes] = (attended[:, lanes] * inverse).astype(BF16)
        d = grad[:, lanes]
        scores = dot(d, v2[:, lanes], (1, 1)) * mixing_of(cum_rows, cols, h)
        scores = scores.astype(BF16)
        step, at = divmod(h, per_step)
        state = unless(start, before[step][at * dim : (at + 1) * dim, :])
        query_grad = dot(scores, kc2[:, lanes], (1, 0)) + growth[:, h : h + 1] * dot(
            d, state, (1, 1)
        )
        key_grad[:, lanes] = dot(scores, q2[:, lanes], (0, 0))
        partial[:, lanes] = query_grad + dot(weights[h], d, (0, 0))
    lead = sum(ref[...].astype(F32) for ref in lead_weights).astype(BF16)
    lead = dot(lead, grad[...], (0, 0))
    for h in range(heads):
        lanes = slice(h * dim, (h + 1) * dim)
        partial[:LEAD, lanes] = partial[:LEAD, lanes] + lead[LEAD * h : LEAD * (h + 1), lanes]
    here, there = halves(size // PAIR)
    keep[...] = normed[here, :]
    send[...] = normed[there, :]


def outer_grad_kernel(
    last, part, partial, key_grad, kc2, v2, cum, behind, more, taps, keep, send, padded, done
):
    size, width = partial.shape
    dim = behind.shape[1]
    heads = width // dim // PARTS
    chunk = width // PARTS
    mine = lax.rem(lax.axis_index("ctx"), PAIR)
    own = pl.ds(pl.multiple_of(mine * width + part * chunk, chunk), chunk)
    ends = lax.axis_index("ctx") >= last
    tops = unless(ends, behind[chunk:, :].astype(F32))
    cols = cum[...].T
    after = jnp.exp(cols[size - 1 :, :] - cols)
    for h in range(heads):
        at = part * heads + h
        lanes = slice(at * dim, (at + 1) * dim)
        here = slice(h * dim, (h + 1) * dim)
        scale = after[:, at : at + 1]
        state = unless(ends, behind[here, :])
        padded[:size, here] = key_grad[:, lanes] + scale * dot(v2[:, lanes], state, (1, 1))
        done[:, here] = partial[:, lanes] + scale * dot(kc2[:, lanes], state, (1, 0))
        top = jnp.concatenate([tops[4 * h : 4 * h + 4], jnp.zeros((4, dim), F32)], 0)
        padded[size:, here] = top + more[:, lanes]
    total = done[...]
    for j in range(taps.shape[1]):
        total = total + taps[0, j : j + 1, own] * padded[j : j + size, :]
    done[...] = total
    here, there = halves(size // PAIR)
    first = lax.axis_index("pp") == 0
    keep[...] = unless(first, done[here, :]).astype(BF16)
    send[...] = unless(first, done[there, :]).astype(BF16)


def place_kernel(*refs):
    *pieces, out, sems = refs
    kept, got = pieces[: len(pieces) // 2], pieces[len(pieces) // 2 :]
    width = kept[0].shape[1]
    mine = lax.rem(lax.axis_index("ctx"), PAIR)
    pairs = []
    for half, parts in ((mine, kept), (1 - mine, got)):
        for i, part in enumerate(parts):
            start = pl.multiple_of((half * len(parts) + i) * width, width)
            pairs.append((part, out.at[0, :, pl.ds(start, width)]))
    for copy in copy_all(pairs, sems):
        copy.wait()


def placed(kept, got):
    pieces = kept + got
    rows = kept[0].shape[0]
    return call(
        place_kernel,
        [shape((1, rows, sum(piece.shape[1] for piece in pieces)), BF16)],
        *pieces,
        scratch=[pltpu.SemaphoreType.DMA((len(pieces),))],
        out_hbm=True,
    )[0]


def turned(block, axis, distance):
    count = lax.axis_size(axis)
    return lax.ppermute(block, axis, [(i, (i + distance) % count) for i in range(count)])


def swapped(block):
    return lax.ppermute(block, "ctx", [(i, i ^ 1) for i in range(lax.axis_size("ctx"))])


def to_earlier_section(block, flip):
    blocks, sections = lax.axis_size("ctx"), lax.axis_size("pp")
    route = [
        (c * sections + p, (c ^ flip) * sections + (p - 1) % sections)
        for c in range(blocks)
        for p in range(sections)
    ]
    return lax.ppermute(block, ("ctx", "pp"), route)


def summed_parts(part):
    blocks, count = lax.axis_size("ctx"), lax.axis_size("tp")
    pair = part + lax.ppermute(part, "tp", [(i, i ^ 1) for i in range(count)])
    parts = [pair]
    ways = [(flip, k) for k in range(2, count, 2) for flip in range(PAIR)] + [(1, 0)]
    for flip, k in ways:
        route = [
            (c * count + t, (c ^ flip) * count + (t + k) % count)
            for c in range(blocks)
            for t in range(count)
        ]
        parts.append(lax.ppermute(pair, ("ctx", "tp"), route))
    return parts


def per_device(queries, key_input, values, log_decay, conv_weight, out_grad):
    rows, width = queries.shape[1], queries.shape[2] // PAIR
    heads = log_decay.shape[2] // PAIR
    dim = width // heads
    size = PAIR * rows
    blocks = lax.axis_size("ctx")
    supers = blocks // PAIR
    width_all = queries.shape[2] * lax.axis_size("tp")
    log_decay = jnp.swapaxes(log_decay, 1, 2)
    arrays = (queries, key_input, values, out_grad, log_decay)
    queries, key_input, values, out_grad, decays = (
        pltpu.with_memory_space_constraint(x, pltpu.HBM) for x in arrays
    )

    step_width = width // STEPS
    *packed, own_cum = call(
        pack_kernel,
        [shape((2 * rows + EDGE, step_width), BF16)]
        + [shape((2 * rows, step_width), BF16)] * (STEPS - 1)
        + [shape((PAIR * heads, rows), F32)],
        key_input, values, decays,
        scratch=[pltpu.VMEM(log_decay.shape, F32), pltpu.SemaphoreType.DMA((1 + 2 * STEPS,))],
        hbm=range(3),
    )
    got = [swapped(part) for part in packed]
    edges = ()
    if supers > 2:
        edge = arrays[1][0, rows - EDGE :]
        near = lax.ppermute(edge[:, :width], "ctx", [(i, i + 1) for i in range(1, blocks - 1, 2)])
        far = lax.ppermute(edge[:, width:], "ctx", [(i, i + 2) for i in range(1, blocks - 2, 2)])
        edges = (near + far,)
    second, third, own = call(
        pack_more_kernel,
        [shape((rows, width), BF16)] * 2 + [shape((4 * rows, width), BF16)],
        queries, key_input, values, out_grad, packed[0][2 * rows :],
        scratch=[pltpu.SemaphoreType.DMA((6,))],
        hbm=range(4),
    )
    got_q, got_g = swapped(second), swapped(third)
    joined = [
        shape((size, width), BF16), shape((size, width), BF16), shape((EDGE, width), F32),
        shape((step_width + EDGE, dim), BF16),
    ]
    room = [pltpu.VMEM((EDGE + size, step_width), F32)]
    kc2, v2, top, state, cum = call(
        join_kernel,
        joined + [shape((8, size), F32)],
        got[0], own, own_cum, conv_weight, *edges,
        scratch=room,
    )
    states = [state]
    for step in range(1, STEPS):
        kc2, v2, top, state = call(
            lambda *refs, step=step: join_next_kernel(step, *refs),
            joined,
            kc2, v2, top, got[step], own, cum, conv_weight, *edges,
            scratch=room,
            alias=((0, 0), (1, 1), (2, 2)),
        )
        states.append(state)
    carry = jnp.repeat(jnp.exp(cum[:heads, -1]), dim)[:, None]
    pair_index = lax.axis_index("ctx") // PAIR
    before = []
    for step, state in enumerate(states):
        moved = turned(state, "ctx", PAIR)
        for _ in range(supers - 2):
            earlier = unless(pair_index == 0, moved[:step_width]).astype(F32)
            earlier = carry[step * step_width : (step + 1) * step_width] * earlier
            earlier = (state[:step_width].astype(F32) + earlier).astype(BF16)
            moved = jnp.concatenate([turned(earlier, "ctx", PAIR), moved[step_width:]], 0)
        before.append(moved)

    q2, g2, weights, inside, lead_mixing, lead_values = call(
        local_kernel,
        [shape((size, width), BF16)] * 2
        + [shape((heads, size, size), BF16), shape((size, width), F32)]
        + [shape((size, LEAD * heads), F32), shape((LEAD * heads, width), BF16)],
        got_q, got_g, own, kc2, v2, cum,
        flops=4 * heads * size * size * dim,
    )
    lead_weights, carried = [], []
    for step in range(STEPS):
        last = step == STEPS - 1
        kc2, inside, lead, sums = call(
            lambda *refs, step=step: attend_kernel(step, *refs),
            [shape(kc2.shape, BF16), shape((size, width), F32), shape((size, LEAD * heads), BF16),
             shape((2, size) if last else (2, size, dim), F32)],
            kc2, inside, q2, g2, cum, top, conv_weight, lead_mixing, lead_values,
            before[step], *carried,
            scratch=[pltpu.VMEM((4 * LEAD, step_width), F32)],
            alias=((0, 0), (1, 1)),
        )
        lead_weights.append(lead)
        carried = [sums]
    attended = inside
    parts = summed_parts(sums)
    chunk = width // PARTS
    scales, grad, *adjoints = call(
        lambda *refs: grad_kernel(width_all, *refs),
        [shape((8, size), F32), shape((size, width), BF16)]
        + [shape((chunk + EDGE, dim), BF16)] * PARTS,
        attended, q2, lead_mixing, lead_values, g2, cum, *parts,
    )
    last_pair = pair_index == supers - 1
    behind = []
    for i, adjoint in enumerate(adjoints):
        moved = turned(adjoint, "ctx", -PAIR)
        for _ in range(supers - 2):
            later = unless(last_pair, moved[:chunk]).astype(F32)
            joined = adjoint[:chunk].astype(F32) + carry[i * chunk : (i + 1) * chunk] * later
            state = turned(joined.astype(BF16), "ctx", -PAIR)
            moved = jnp.concatenate([state, moved[chunk:]], 0)
        behind.append(moved)
    more = jnp.zeros((8, width), F32)
    if supers > 2:
        after = jnp.exp(cum[:heads, -1:] - cum[:heads, :8])
        states = jnp.concatenate([part[:chunk] for part in behind], 0)
        state_part = jnp.einsum(
            "shv,hkv->shk",
            v2[:8].reshape(8, heads, dim),
            unless(last_pair, states).reshape(heads, dim, dim),
            preferred_element_type=F32,
        )
        more = turned((after.T[:, :, None] * state_part).reshape(8, width), "ctx", -PAIR)
        more = unless(last_pair, more)

    keep, send, partial, key_grad = call(
        inner_grad_kernel,
        [shape((rows, width), BF16)] * 2 + [shape((size, width), F32)] * 2,
        attended, scales, q2, kc2, v2, grad, weights, cum, *before, *lead_weights,
        scratch=[pltpu.VMEM((size, width), BF16)],
        flops=10 * heads * size * size * dim,
    )
    layer_output = placed([keep], [swapped(send)])
    kept, got = [], []
    for i in range(PARTS):
        keep, send = call(
            lambda *refs, i=i: outer_grad_kernel(blocks - PAIR, i, *refs),
            [shape((rows, chunk), BF16)] * 2,
            partial, key_grad, kc2, v2, cum, behind[i], more, conv_weight,
            scratch=[pltpu.VMEM((size + 8, chunk), F32), pltpu.VMEM((size, chunk), F32)],
        )
        kept.append(to_earlier_section(keep, 0))
        got.append(to_earlier_section(send, 1))
    return (layer_output, placed(kept, got))


def solution(mesh):
    placed = (
        P("pp", "ctx", "tp"),
        P("pp", "ctx", "tp"),
        P("pp", "ctx", "tp"),
        P("pp", "ctx", "tp"),
        P("pp", None, "tp"),
        P("pp", "ctx", "tp"),
    )
    return jax.shard_map(
        per_device,
        mesh=mesh,
        in_specs=placed,
        out_specs=(P("pp", "ctx", "tp"), P("pp", "ctx", "tp")),
        check_vma=False,
    )
```

time: 49 us -> 47.3 us (0.965)
  waiting for transfers between devices: 23.5 us -> 16.9 us
  starting transfers between devices: 14.5 us -> 19.4 us
    ppermute x3 -> x5, waiting for transfers between devices: 8.62 us -> 5.12 us  [swapped(): lax.ppermute(block, 'ctx', [(i, i ^ 1) for i in range(lax.axis_size('ctx'...]
    ppermute x2 -> x3, waiting for transfers between devices: 6.09 us -> 2.92 us  [turned(): lax.ppermute(block, axis, [(i, (i + distance) % count) for i in range(cou...]
    ppermute x3 -> x5, starting transfers between devices: 3.27 us -> 6.26 us  [swapped(): lax.ppermute(block, 'ctx', [(i, i ^ 1) for i in range(lax.axis_size('ctx'...]
    ppermute x2 -> x3, starting transfers between devices: 5.84 us -> 7.64 us  [turned(): lax.ppermute(block, axis, [(i, (i + distance) % count) for i in range(cou...]
    pallas_call x10 -> x12, Pallas kernels: 10.1 us -> 10.1 us  [call(): pl.pallas_call(kernel, out_shape=outs, in_specs=[pl.BlockSpec(memory_spac...]
  transfers between devices with their start and end apart: 11 -> 14, of which waited for: 10 -> 10; matrix products, arithmetic and copies ran while one was open for 0% -> 0% of each run, Pallas kernels for 12% -> 14%
where the time goes in v4:
time: 47.3 us; the launch traced here: 47.1 us
  starting transfers between devices  19.4 us (41%)
  waiting for transfers between devices  16.9 us (36%)
  Pallas kernels  10.1 us (21%)
  between operations  0.73 us (2%)
    pallas_call x12, Pallas kernels, call(): pl.pallas_call(kernel, out_shape=outs, in_specs=[pl.BlockSpec(memory_spac...  10.1 us
    ppermute x3, starting transfers between devices, turned(): lax.ppermute(block, axis, [(i, (i + distance) % count) for i in range(cou...  7.64 us
    ppermute x5, starting transfers between devices, swapped(): lax.ppermute(block, 'ctx', [(i, i ^ 1) for i in range(lax.axis_size('ctx'...  6.26 us
    ppermute x5, waiting for transfers between devices, swapped(): lax.ppermute(block, 'ctx', [(i, i ^ 1) for i in range(lax.axis_size('ctx'...  5.12 us
    ppermute x2, waiting for transfers between devices, to_earlier_section(): return lax.ppermute(block, ('ctx', 'pp'), route)  4.7 us
    ppermute x3, starting transfers between devices, summed_parts(): parts.append(lax.ppermute(pair, ('ctx', 'tp'), route))  3.49 us
    ppermute x3, waiting for transfers between devices, summed_parts(): parts.append(lax.ppermute(pair, ('ctx', 'tp'), route))  2.94 us
    ppermute x3, waiting for transfers between devices, turned(): lax.ppermute(block, axis, [(i, (i + distance) % count) for i in range(cou...  2.92 us
  transfers between devices with their start and end apart: 14, of which 10 were waited for; matrix products, arithmetic and copies ran while one was open for 0% of the time, Pallas kernels for 14%

profile of v4, /device:TPU:0, one launch (start us, length us, event | category | flops | bytes accessed | tf_op | source)
XLA Modules:
  0.0 47.1 jit_solution(14528784542186635368)
XLA Ops:
  0.6 1.0 %shard_map.77 = (bf16[272,256]{1,0:T(8,128)(2,1)S(1)}, bf16[256,256]{1,0:T(8,128)(2,1)S(1)}, f32[8,128]{1,0:T(8,128)S(1)}) custom-call(bf16[1,128,1024]{2,1,0:T(8,128)(2,1)} %k.3, bf16[1,128,1024]{2,1,0:T(8,128)(2,1)} %v.3, f32[1,8,128]{2,1,0:T(8,128)} %bitcast.1), custom_call_target="tpu_custom_call" | custom-call | bytes 802816 | tf_op jit(solution)/shard_map/pallas_call | solution.py:22
  1.6 3.1 %collective-permute-start = (bf16[272,256]{1,0:T(8,128)(2,1)S(1)}, bf16[272,256]{1,0:T(8,128)(2,1)S(1)}, u32[]{:S(2)}, u32[]{:S(2)}) collective-permute-start(bf16[272,256]{1,0:T(8,128)(2,1)S(1)} %get-tuple-element.40), channel_id=1, source_target_pairs={{0,8},{8,0},{16,24},{24,16},{1,9},{9,1},{17,25},{25,17},{2,10},{10... | collective-permute-start | bytes 417800 | tf_op jit(solution)/shard_map/ppermute | solution.py:415
  4.7 0.1 collective-permute-start.1
  4.8 0.0 copy-start
  4.8 1.3 %shard_map.78 = (bf16[128,512]{1,0:T(8,128)(2,1)S(1)}, bf16[128,512]{1,0:T(8,128)(2,1)S(1)}, bf16[512,512]{1,0:T(8,128)(2,1)S(1)}) custom-call(bf16[1,128,1024]{2,1,0:T(8,128)(2,1)} %q.1, bf16[1,128,1024]{2,1,0:T(8,128)(2,1)} %k.3, bf16[1,128,1024]{2,1,0:T(8,128)(2,1)} %v.3, bf16[1,128,1024]{2,1,0:T(8,128)(2,1)} %g.1, bf16[16,256]{1,0:T(8,128)(2,1)S(1)} %slice.3._), custom_call_target="tpu_custom_call" | custom-call | bytes 1843200 | tf_op jit(solution)/shard_map/pallas_call | solution.py:22
  6.1 2.0 %collective-permute-start.2 = (bf16[128,512]{1,0:T(8,128)(2,1)S(1)}, bf16[128,512]{1,0:T(8,128)(2,1)S(1)}, u32[]{:S(2)}, u32[]{:S(2)}) collective-permute-start(bf16[128,512]{1,0:T(8,128)(2,1)S(1)} %get-tuple-element.49), channel_id=1, source_target_pairs={{0,8},{8,0},{16,24},{24,16},{1,9},{9,1},{17,25},{25,17},{2,10},{10... | collective-permute-start | bytes 393224 | tf_op jit(solution)/shard_map/ppermute | solution.py:415
  8.1 0.1 collective-permute-start.3
  8.2 1.1 %collective-permute-done.got = bf16[272,256]{1,0:T(8,128)(2,1)S(1)} collective-permute-done((bf16[272,256]{1,0:T(8,128)(2,1)S(1)}, bf16[272,256]{1,0:T(8,128)(2,1)S(1)}, u32[]{:S(2)}, u32[]{:S(2)}) %collective-permute-start) | collective-permute-done | bytes 139296 | tf_op jit(solution)/shard_map/ppermute | solution.py:415
  9.2 0.0 copy-done
  9.2 0.6 %shard_map.79 = (bf16[256,512]{1,0:T(8,128)(2,1)S(1)}, bf16[256,512]{1,0:T(8,128)(2,1)S(1)}, f32[16,512]{1,0:T(8,128)S(1)}, bf16[272,128]{1,0:T(8,128)(2,1)S(1)}, f32[8,256]{1,0:T(8,128)S(1)}) custom-call(bf16[272,256]{1,0:T(8,128)(2,1)S(1)} %collective-permute-done.got, bf16[512,512]{1,0:T(8,128)(2,1)S(1)} %get-tuple-element.41.own.refs_4_, ...), custom_call_target="tpu_custom_call" | custom-call | bytes 1318912 | tf_op jit(solution)/shard_map/pallas_call | solution.py:22
  9.9 3.1 %collective-permute-start.4 = (bf16[272,128]{1,0:T(8,128)(2,1)S(1)}, bf16[272,128]{1,0:T(8,128)(2,1)S(1)}, u32[]{:S(2)}, u32[]{:S(2)}) collective-permute-start(bf16[272,128]{1,0:T(8,128)(2,1)S(1)} %get-tuple-element.58), channel_id=1, source_target_pairs={{0,16},{8,24},{16,0},{24,8},{1,17},{9,25},{17,1},{25,9},{2,18},{10... | collective-permute-start | bytes 208904 | tf_op jit(solution)/shard_map/ppermute | solution.py:411
  13.0 0.0 collective-permute-done.1.refs_3_
  13.0 0.6 %shard_map.80 = (bf16[256,512]{1,0:T(8,128)(2,1)S(1)}, bf16[256,512]{1,0:T(8,128)(2,1)S(1)}, f32[16,512]{1,0:T(8,128)S(1)}, bf16[272,128]{1,0:T(8,128)(2,1)S(1)}) custom-call(bf16[256,512]{1,0:T(8,128)(2,1)S(1)} %get-tuple-element.43.refs_0_, ...), custom_call_target="tpu_custom_call", output_to_operand_aliasing={{0}: (0, {}), {1}: (1, {}), {2}: (2, {})} | custom-call | bytes 1863680 | tf_op jit(solution)/shard_map/pallas_call | solution.py:22
  13.6 2.2 %collective-permute-start.5 = (bf16[272,128]{1,0:T(8,128)(2,1)S(1)}, bf16[272,128]{1,0:T(8,128)(2,1)S(1)}, u32[]{:S(2)}, u32[]{:S(2)}) collective-permute-start(bf16[272,128]{1,0:T(8,128)(2,1)S(1)} %get-tuple-element.61), channel_id=1, source_target_pairs={{0,16},{8,24},{16,0},{24,8},{1,17},{9,25},{17,1},{25,9},{2,18},{10... | collective-permute-start | bytes 208904 | tf_op jit(solution)/shard_map/ppermute | solution.py:411
  15.7 1.3 %collective-permute-done.2.got = bf16[128,512]{1,0:T(8,128)(2,1)S(1)} collective-permute-done((bf16[128,512]{1,0:T(8,128)(2,1)S(1)}, bf16[128,512]{1,0:T(8,128)(2,1)S(1)}, u32[]{:S(2)}, u32[]{:S(2)}) %collective-permute-start.2) | collective-permute-done | bytes 131104 | tf_op jit(solution)/shard_map/ppermute | solution.py:415
  17.1 2.7 %collective-permute-done.3.got_g = bf16[128,512]{1,0:T(8,128)(2,1)S(1)} collective-permute-done((bf16[128,512]{1,0:T(8,128)(2,1)S(1)}, bf16[128,512]{1,0:T(8,128)(2,1)S(1)}, u32[]{:S(2)}, u32[]{:S(2)}) %collective-permute-start.3) | collective-permute-done | bytes 131104 | tf_op jit(solution)/shard_map/ppermute | solution.py:415
  19.8 0.8 %shard_map.81 = (bf16[256,512]{1,0:T(8,128)(2,1)S(1)}, bf16[256,512]{1,0:T(8,128)(2,1)S(1)}, bf16[4,256,256]{2,1,0:T(8,128)(2,1)S(1)}, f32[256,512]{1,0:T(8,128)...) custom-call(bf16[128,512]{1,0:T(8,128)(2,1)S(1)} %collective-permute-done.2.got, ...), custom_call_target="tpu_custom_call" | custom-call | flops 134217728 | bytes 2924544 | tf_op jit(solution)/shard_map/pallas_call | solution.py:22
  20.6 0.0 collective-permute-done.4.refs_9_.refs_0_
  20.6 0.6 %shard_map.82 = (bf16[256,512]{1,0:T(8,128)(2,1)S(1)}, f32[256,512]{1,0:T(8,128)S(1)}, bf16[256,16]{1,0:T(8,128)(2,1)S(1)}, f32[2,256,128]{2,1,0:T(8,128)S(1)}) custom-call(bf16[256,512]{1,0:T(8,128)(2,1)S(1)} %get-tuple-element.48.kc2.refs_0_, f32[256,512]{1,0:T(8,128)S(1)} %get-tuple-element.52.refs_1_, ...), custom_call_target="tpu_custom_call", output_to_operand_aliasing={{0}: (0, {}), {1}: (1, {})} | custom-call | bytes 2527232 | tf_op jit(solution)/shard_map/pallas_call | solution.py:22
  21.2 0.0 collective-permute-done.5.refs_9_.refs_1_
  21.2 0.7 %shard_map.83 = (bf16[256,512]{1,0:T(8,128)(2,1)S(1)}, f32[256,512]{1,0:T(8,128)S(1)}, bf16[256,16]{1,0:T(8,128)(2,1)S(1)}, f32[2,256]{1,0:T(2,128)S(1)}) custom-call(bf16[256,512]{1,0:T(8,128)(2,1)S(1)} %get-tuple-element.59.refs_0_, f32[256,512]{1,0:T(8,128)S(1)} %get-tuple-element.60.refs_1_, ...), custom_call_target="tpu_custom_call", output_to_operand_aliasing={{0}: (0, {}), {1}: (1, {})} | custom-call | bytes 2529280 | tf_op jit(solution)/shard_map/pallas_call | solution.py:22
  21.9 0.0 collective-permute-start.6
  21.9 1.2 %collective-permute-done.6 = f32[2,256]{1,0:T(2,128)S(1)} collective-permute-done((f32[2,256]{1,0:T(2,128)S(1)}, f32[2,256]{1,0:T(2,128)S(1)}, u32[]{:S(2)}, u32[]{:S(2)}) %collective-permute-start.6) | collective-permute-done | bytes 2080 | tf_op jit(solution)/shard_map/ppermute | solution.py:430
  23.1 1.7 %collective-permute-start.7 = (f32[2,256]{1,0:T(2,128)S(1)}, f32[2,256]{1,0:T(2,128)S(1)}, u32[]{:S(2)}, u32[]{:S(2)}) collective-permute-start(f32[2,256]{1,0:T(2,128)S(1)} %add.3.refs_6_), channel_id=1, source_target_pairs={{0,4},{2,6},{4,0},{6,2},{8,12},{10,14},{12,8},{14,10},{16,20},{18,... | collective-permute-start | bytes 6152 | tf_op jit(solution)/shard_map/ppermute | solution.py:439
  24.7 1.2 %collective-permute-start.8 = (f32[2,256]{1,0:T(2,128)S(1)}, f32[2,256]{1,0:T(2,128)S(1)}, u32[]{:S(2)}, u32[]{:S(2)}) collective-permute-start(f32[2,256]{1,0:T(2,128)S(1)} %add.3.refs_6_), channel_id=1, source_target_pairs={{0,12},{2,14},{4,8},{6,10},{8,4},{10,6},{12,0},{14,2},{16,28},{18,... | collective-permute-start | bytes 6152 | tf_op jit(solution)/shard_map/ppermute | solution.py:439
  25.9 0.6 %collective-permute-start.9 = (f32[2,256]{1,0:T(2,128)S(1)}, f32[2,256]{1,0:T(2,128)S(1)}, u32[]{:S(2)}, u32[]{:S(2)}) collective-permute-start(f32[2,256]{1,0:T(2,128)S(1)} %add.3.refs_6_), channel_id=1, source_target_pairs={{0,8},{2,10},{4,12},{6,14},{8,0},{10,2},{12,4},{14,6},{16,24},{18,... | collective-permute-start | bytes 6152 | tf_op jit(solution)/shard_map/ppermute | solution.py:439
  26.6 0.1 collective-permute-done.7.refs_7_
  26.6 2.6 %collective-permute-done.8.refs_8_ = f32[2,256]{1,0:T(2,128)S(1)} collective-permute-done((f32[2,256]{1,0:T(2,128)S(1)}, f32[2,256]{1,0:T(2,128)S(1)}, u32[]{:S(2)}, u32[]{:S(2)}) %collective-permute-start.8) | collective-permute-done | bytes 2080 | tf_op jit(solution)/shard_map/ppermute | solution.py:439
  29.2 0.3 collective-permute-done.9.refs_9_
  29.5 1.0 %shard_map.84 = (f32[8,256]{1,0:T(8,128)S(1)}, bf16[256,512]{1,0:T(8,128)(2,1)S(1)}, bf16[528,128]{1,0:T(8,128)(2,1)S(1)}) custom-call(f32[256,512]{1,0:T(8,128)S(1)} %get-tuple-element.63.refs_0_.attended, bf16[256,512]{1,0:T(8,128)(2,1)S(1)} %get-tuple-element.53.refs_2_.refs_1_.q2, f32[256,16]{1,0:T(8,128)S(1)} %get-tuple-element.56.refs_7_.refs_2_, ...), custom_call_target="tpu_custom_call" | custom-call | bytes 1503232 | tf_op jit(solution)/shard_map/pallas_call | solution.py:22
  30.5 2.3 %collective-permute-start.11 = (bf16[528,128]{1,0:T(8,128)(2,1)S(1)}, bf16[528,128]{1,0:T(8,128)(2,1)S(1)}, u32[]{:S(2)}, u32[]{:S(2)}) collective-permute-start(bf16[528,128]{1,0:T(8,128)(2,1)S(1)} %get-tuple-element.75), channel_id=1, source_target_pairs={{0,16},{8,24},{16,0},{24,8},{1,17},{9,25},{17,1},{25,9},{2,18},{10... | collective-permute-start | bytes 405512 | tf_op jit(solution)/shard_map/ppermute | solution.py:411
  32.8 1.5 %shard_map.85 = (bf16[128,512]{1,0:T(8,128)(2,1)S(1)}, bf16[128,512]{1,0:T(8,128)(2,1)S(1)}, f32[256,512]{1,0:T(8,128)S(1)}, f32[256,512]{1,0:T(8,128)S(1)}) custom-call(f32[256,512]{1,0:T(8,128)S(1)} %get-tuple-element.63.refs_0_.attended, f32[8,256]{1,0:T(8,128)S(1)} %get-tuple-element.65.scales, ...), custom_call_target="tpu_custom_call" | custom-call | flops 335544320 | bytes 3579904 | tf_op jit(solution)/shard_map/pallas_call | solution.py:22
  34.4 1.0 %collective-permute-start.10 = (bf16[128,512]{1,0:T(8,128)(2,1)S(1)}, bf16[128,512]{1,0:T(8,128)(2,1)S(1)}, u32[]{:S(2)}, u32[]{:S(2)}) collective-permute-start(bf16[128,512]{1,0:T(8,128)(2,1)S(1)} %get-tuple-element.72), channel_id=1, source_target_pairs={{0,8},{8,0},{16,24},{24,16},{1,9},{9,1},{17,25},{25,17},{2,10},{10... | collective-permute-start | bytes 393224 | tf_op jit(solution)/shard_map/ppermute | solution.py:415
  35.4 2.9 %collective-permute-done.11.refs_5_ = bf16[528,128]{1,0:T(8,128)(2,1)S(1)} collective-permute-done((bf16[528,128]{1,0:T(8,128)(2,1)S(1)}, bf16[528,128]{1,0:T(8,128)(2,1)S(1)}, u32[]{:S(2)}, u32[]{:S(2)}) %collective-permute-start.11) | collective-permute-done | bytes 135200 | tf_op jit(solution)/shard_map/ppermute | solution.py:411
  38.3 0.6 %shard_map.87 = (bf16[128,512]{1,0:T(8,128)(2,1)S(1)}, bf16[128,512]{1,0:T(8,128)(2,1)S(1)}) custom-call(f32[256,512]{1,0:T(8,128)S(1)} %get-tuple-element.73.refs_0_, f32[256,512]{1,0:T(8,128)S(1)} %get-tuple-element.74.refs_1_, bf16[256,512]{1,0:T(8,128)(2,1)S(1)} %get-tuple-element.66.kc2.refs_2_, bf16[256,512]{1,0:T(8,128)(2,1)S(1)} %get-tuple-element.51.v2.refs_3_, ...), custom_call_target="tpu_custom_call" | custom-call | bytes 2011136 | tf_op jit(solution)/shard_map/pallas_call | solution.py:22
  38.9 1.6 %collective-permute-start.12 = (bf16[128,512]{1,0:T(8,128)(2,1)S(1)}, bf16[128,512]{1,0:T(8,128)(2,1)S(1)}, u32[]{:S(2)}, u32[]{:S(2)}) collective-permute-start(bf16[128,512]{1,0:T(8,128)(2,1)S(1)} %get-tuple-element.76), channel_id=1, source_target_pairs={{0,1},{1,0},{8,9},{9,8},{16,17},{17,16},{24,25},{25,24},{2,3},{3,2... | collective-permute-start | bytes 393224 | tf_op jit(solution)/shard_map/ppermute | solution.py:425
  40.5 0.4 collective-permute-start.13
  41.0 0.0 collective-permute-done.10.refs_1_
  41.0 0.7 %shard_map.86 = bf16[1,128,1024]{2,1,0:T(8,128)(2,1)} custom-call(bf16[128,512]{1,0:T(8,128)(2,1)S(1)} %get-tuple-element.71.refs_0_, bf16[128,512]{1,0:T(8,128)(2,1)S(1)} %collective-permute-done.10.refs_1_), custom_call_target="tpu_custom_call" | custom-call | bytes 524288 | tf_op jit(solution)/shard_map/pallas_call | solution.py:22
  41.7 2.7 %collective-permute-done.12.refs_0_ = bf16[128,512]{1,0:T(8,128)(2,1)S(1)} collective-permute-done((bf16[128,512]{1,0:T(8,128)(2,1)S(1)}, bf16[128,512]{1,0:T(8,128)(2,1)S(1)}, u32[]{:S(2)}, u32[]{:S(2)}) %collective-permute-start.12) | collective-permute-done | bytes 131104 | tf_op jit(solution)/shard_map/ppermute | solution.py:425
  44.4 2.0 %collective-permute-done.13.refs_1_ = bf16[128,512]{1,0:T(8,128)(2,1)S(1)} collective-permute-done((bf16[128,512]{1,0:T(8,128)(2,1)S(1)}, bf16[128,512]{1,0:T(8,128)(2,1)S(1)}, u32[]{:S(2)}, u32[]{:S(2)}) %collective-permute-start.13) | collective-permute-done | bytes 131104 | tf_op jit(solution)/shard_map/ppermute | solution.py:425
  46.4 0.7 %shard_map.88 = bf16[1,128,1024]{2,1,0:T(8,128)(2,1)} custom-call(bf16[128,512]{1,0:T(8,128)(2,1)S(1)} %collective-permute-done.12.refs_0_, bf16[128,512]{1,0:T(8,128)(2,1)S(1)} %collective-permute-done.13.refs_1_), custom_call_target="tpu_custom_call" | custom-call | bytes 524288 | tf_op jit(solution)/shard_map/pallas_call | solution.py:22
  (3 shorter events, 0.0 us)
Async XLA Ops:
  1.6 7.6 %collective-permute-start = (bf16[272,256]{1,0:T(8,128)(2,1)S(1)}, bf16[272,256]{1,0:T(8,128)(2,1)S(1)}, u32[]{:S(2)}, u32[]{:S(2)}) collective-permute-start(bf16[272,256]{1,0:T(8,128)(2,1)S(1)} %get-tuple-element.40), channel_id=1, source_target_pairs={{0,8},{8,0},{16,24},{24,16},{1,9},{9,1},{17,25},{25,17},{2,10},{10... | collective-permute-start | bytes 417800 | tf_op jit(solution)/shard_map/ppermute | solution.py:415
  4.7 8.3 %collective-permute-start.1 = (bf16[256,256]{1,0:T(8,128)(2,1)S(1)}, bf16[256,256]{1,0:T(8,128)(2,1)S(1)}, u32[]{:S(2)}, u32[]{:S(2)}) collective-permute-start(bf16[256,256]{1,0:T(8,128)(2,1)S(1)} %get-tuple-element.46), channel_id=1, source_target_pairs={{0,8},{8,0},{16,24},{24,16},{1,9},{9,1},{17,25},{25,17},{2,10},{10... | collective-permute-start | bytes 393224 | tf_op jit(solution)/shard_map/ppermute | solution.py:415
  4.8 4.4 %copy-start = (f32[1,4,1024]{2,1,0:T(4,128)S(1)}, f32[1,4,1024]{2,1,0:T(4,128)}, u32[]{:S(2)}) copy-start(f32[1,4,1024]{2,1,0:T(4,128)} %refs_7_.1) | copy-start | bytes 49156
  6.1 11.0 %collective-permute-start.2 = (bf16[128,512]{1,0:T(8,128)(2,1)S(1)}, bf16[128,512]{1,0:T(8,128)(2,1)S(1)}, u32[]{:S(2)}, u32[]{:S(2)}) collective-permute-start(bf16[128,512]{1,0:T(8,128)(2,1)S(1)} %get-tuple-element.49), channel_id=1, source_target_pairs={{0,8},{8,0},{16,24},{24,16},{1,9},{9,1},{17,25},{25,17},{2,10},{10... | collective-permute-start | bytes 393224 | tf_op jit(solution)/shard_map/ppermute | solution.py:415
  8.1 11.7 %collective-permute-start.3 = (bf16[128,512]{1,0:T(8,128)(2,1)S(1)}, bf16[128,512]{1,0:T(8,128)(2,1)S(1)}, u32[]{:S(2)}, u32[]{:S(2)}) collective-permute-start(bf16[128,512]{1,0:T(8,128)(2,1)S(1)} %get-tuple-element.50), channel_id=1, source_target_pairs={{0,8},{8,0},{16,24},{24,16},{1,9},{9,1},{17,25},{25,17},{2,10},{10... | collective-permute-start | bytes 393224 | tf_op jit(solution)/shard_map/ppermute | solution.py:415
  9.9 10.7 %collective-permute-start.4 = (bf16[272,128]{1,0:T(8,128)(2,1)S(1)}, bf16[272,128]{1,0:T(8,128)(2,1)S(1)}, u32[]{:S(2)}, u32[]{:S(2)}) collective-permute-start(bf16[272,128]{1,0:T(8,128)(2,1)S(1)} %get-tuple-element.58), channel_id=1, source_target_pairs={{0,16},{8,24},{16,0},{24,8},{1,17},{9,25},{17,1},{25,9},{2,18},{10... | collective-permute-start | bytes 208904 | tf_op jit(solution)/shard_map/ppermute | solution.py:411
  13.6 7.6 %collective-permute-start.5 = (bf16[272,128]{1,0:T(8,128)(2,1)S(1)}, bf16[272,128]{1,0:T(8,128)(2,1)S(1)}, u32[]{:S(2)}, u32[]{:S(2)}) collective-permute-start(bf16[272,128]{1,0:T(8,128)(2,1)S(1)} %get-tuple-element.61), channel_id=1, source_target_pairs={{0,16},{8,24},{16,0},{24,8},{1,17},{9,25},{17,1},{25,9},{2,18},{10... | collective-permute-start | bytes 208904 | tf_op jit(solution)/shard_map/ppermute | solution.py:411
  21.9 1.2 %collective-permute-start.6 = (f32[2,256]{1,0:T(2,128)S(1)}, f32[2,256]{1,0:T(2,128)S(1)}, u32[]{:S(2)}, u32[]{:S(2)}) collective-permute-start(f32[2,256]{1,0:T(2,128)S(1)} %get-tuple-element.64), channel_id=1, source_target_pairs={{0,2},{2,0},{4,6},{6,4},{1,3},{3,1},{5,7},{7,5},{8,10},{10,8},{12,... | collective-permute-start | bytes 6152 | tf_op jit(solution)/shard_map/ppermute | solution.py:430
  23.1 3.6 %collective-permute-start.7 = (f32[2,256]{1,0:T(2,128)S(1)}, f32[2,256]{1,0:T(2,128)S(1)}, u32[]{:S(2)}, u32[]{:S(2)}) collective-permute-start(f32[2,256]{1,0:T(2,128)S(1)} %add.3.refs_6_), channel_id=1, source_target_pairs={{0,4},{2,6},{4,0},{6,2},{8,12},{10,14},{12,8},{14,10},{16,20},{18,... | collective-permute-start | bytes 6152 | tf_op jit(solution)/shard_map/ppermute | solution.py:439
  24.7 4.5 %collective-permute-start.8 = (f32[2,256]{1,0:T(2,128)S(1)}, f32[2,256]{1,0:T(2,128)S(1)}, u32[]{:S(2)}, u32[]{:S(2)}) collective-permute-start(f32[2,256]{1,0:T(2,128)S(1)} %add.3.refs_6_), channel_id=1, source_target_pairs={{0,12},{2,14},{4,8},{6,10},{8,4},{10,6},{12,0},{14,2},{16,28},{18,... | collective-permute-start | bytes 6152 | tf_op jit(solution)/shard_map/ppermute | solution.py:439
  25.9 3.6 %collective-permute-start.9 = (f32[2,256]{1,0:T(2,128)S(1)}, f32[2,256]{1,0:T(2,128)S(1)}, u32[]{:S(2)}, u32[]{:S(2)}) collective-permute-start(f32[2,256]{1,0:T(2,128)S(1)} %add.3.refs_6_), channel_id=1, source_target_pairs={{0,8},{2,10},{4,12},{6,14},{8,0},{10,2},{12,4},{14,6},{16,24},{18,... | collective-permute-start | bytes 6152 | tf_op jit(solution)/shard_map/ppermute | solution.py:439
  30.5 7.8 %collective-permute-start.11 = (bf16[528,128]{1,0:T(8,128)(2,1)S(1)}, bf16[528,128]{1,0:T(8,128)(2,1)S(1)}, u32[]{:S(2)}, u32[]{:S(2)}) collective-permute-start(bf16[528,128]{1,0:T(8,128)(2,1)S(1)} %get-tuple-element.75), channel_id=1, source_target_pairs={{0,16},{8,24},{16,0},{24,8},{1,17},{9,25},{17,1},{25,9},{2,18},{10... | collective-permute-start | bytes 405512 | tf_op jit(solution)/shard_map/ppermute | solution.py:411
  34.4 6.6 %collective-permute-start.10 = (bf16[128,512]{1,0:T(8,128)(2,1)S(1)}, bf16[128,512]{1,0:T(8,128)(2,1)S(1)}, u32[]{:S(2)}, u32[]{:S(2)}) collective-permute-start(bf16[128,512]{1,0:T(8,128)(2,1)S(1)} %get-tuple-element.72), channel_id=1, source_target_pairs={{0,8},{8,0},{16,24},{24,16},{1,9},{9,1},{17,25},{25,17},{2,10},{10... | collective-permute-start | bytes 393224 | tf_op jit(solution)/shard_map/ppermute | solution.py:415
  38.9 5.5 %collective-permute-start.12 = (bf16[128,512]{1,0:T(8,128)(2,1)S(1)}, bf16[128,512]{1,0:T(8,128)(2,1)S(1)}, u32[]{:S(2)}, u32[]{:S(2)}) collective-permute-start(bf16[128,512]{1,0:T(8,128)(2,1)S(1)} %get-tuple-element.76), channel_id=1, source_target_pairs={{0,1},{1,0},{8,9},{9,8},{16,17},{17,16},{24,25},{25,24},{2,3},{3,2... | collective-permute-start | bytes 393224 | tf_op jit(solution)/shard_map/ppermute | solution.py:425
  40.5 5.9 %collective-permute-start.13 = (bf16[128,512]{1,0:T(8,128)(2,1)S(1)}, bf16[128,512]{1,0:T(8,128)(2,1)S(1)}, u32[]{:S(2)}, u32[]{:S(2)}) collective-permute-start(bf16[128,512]{1,0:T(8,128)(2,1)S(1)} %get-tuple-element.77), channel_id=1, source_target_pairs={{0,9},{1,8},{8,1},{9,0},{16,25},{17,24},{24,17},{25,16},{2,11},{3,... | collective-permute-start | bytes 393224 | tf_op jit(solution)/shard_map/ppermute | solution.py:425

commit v5 on v4

--- a/solution.py
+++ b/solution.py
@@ -114,7 +114,7 @@
         copy.wait()
 
 
-def join_step(step, got, own, taps, edges, cum_rows, kc2, v2, top, state, padded):
+def join_step(step, got, own, taps, edges, cum_rows, kc2, v2, top, ks2, state, padded):
     size, width = kc2.shape
     rows, chunk = size // PAIR, got.shape[1]
     dim = state.shape[1]
@@ -142,6 +142,7 @@
     for h in range(heads):
         at = step * heads + h
         scaled = (keys[:, h * dim : (h + 1) * dim] * after[:, at : at + 1]).astype(BF16)
+        ks2[:, at * dim : (at + 1) * dim] = scaled
         sums = dot(scaled, v2[:, at * dim : (at + 1) * dim], (0, 0))
         state[h * dim : (h + 1) * dim, :] = sums.astype(BF16)
     last = padded[EDGE + size - LEAD : EDGE + size, :]
@@ -152,7 +153,7 @@
 
 
 def join_kernel(got, own, own_cum, taps, *refs):
-    *edges, kc2, v2, top, state, cum, padded = refs
+    *edges, kc2, v2, top, ks2, state, cum, padded = refs
     rows, heads = own_cum.shape[1], own_cum.shape[0] // PAIR
     mine = lax.rem(lax.axis_index("ctx"), PAIR)
     coded = got[2 * rows :, :].astype(F32)
@@ -172,12 +173,12 @@
     cum_rows = jnp.concatenate([front, back], 1)
     cum_rows = jnp.concatenate([cum_rows, jnp.zeros((8 - heads, PAIR * rows), F32)], 0)
     cum[...] = cum_rows
-    join_step(0, got, own, taps, edges, cum_rows, kc2, v2, top, state, padded)
-
-
-def join_next_kernel(step, _kc2, _v2, _top, got, own, cum, taps, *refs):
-    *edges, kc2, v2, top, state, padded = refs
-    join_step(step, got, own, taps, edges, cum[...], kc2, v2, top, state, padded)
+    join_step(0, got, own, taps, edges, cum_rows, kc2, v2, top, ks2, state, padded)
+
+
+def join_next_kernel(step, _kc2, _v2, _top, _ks2, got, own, cum, taps, *refs):
+    *edges, kc2, v2, top, ks2, state, padded = refs
+    join_step(step, got, own, taps, edges, cum[...], kc2, v2, top, ks2, state, padded)
 
 
 def mixing_of(cum_rows, cols, h, first=0):
@@ -205,21 +206,21 @@
     return jnp.where(head == lane, wide, 0.0).astype(BF16)
 
 
-def local_kernel(got, got_g, own, kc2, v2, cum, q2, g2, weights, inside, lead_mixing, lead_values):
+def local_kernel(got, own, kc2, v2, cum, q2, qs2, weights, inside, lead_mixing, lead_values):
     size, width = q2.shape
     heads, dim = weights.shape[0], width // weights.shape[0]
     rows = size // PAIR
     here, there = halves(rows)
     q2[here, :] = own[2 * rows : 3 * rows, :]
     q2[there, :] = got[...]
-    g2[here, :] = own[3 * rows :, :]
-    g2[there, :] = got_g[...]
     cum_rows = cum[...]
     cols = cum_rows.T
+    growth = jnp.exp(cols)
     lead_mixing[...] = lead_mixing_of(cum_rows, cols, heads)
     lead_values[...] = block_diagonal(v2[:EDGE, :].astype(F32)[:LEAD], dim, heads)
     for h in range(heads):
         lanes = slice(h * dim, (h + 1) * dim)
+        qs2[:, lanes] = (q2[:, lanes].astype(F32) * growth[:, h : h + 1]).astype(BF16)
         scores = dot(q2[:, lanes], kc2[:, lanes], (1, 1))
         w = (scores * mixing_of(cum_rows, cols, h, LEAD)).astype(BF16)
         weights[h] = w
@@ -231,8 +232,8 @@
 
 
 def attend_kernel(step, *refs):
-    kc2, inside, q2, g2, cum, top, taps, lead_mixing, lead_values, before, *refs = refs
-    *carried, kc2_whole, attended, lead_weights, out, reach = refs
+    kc2, inside, q2, qs2, top, taps, lead_mixing, lead_values, before, *refs = refs
+    kc2_whole, attended, lead_weights, reach = refs
     size, width = q2.shape
     dim = before.shape[1]
     heads = width // dim
@@ -253,29 +254,33 @@
     lead_keys = block_diagonal(fixed[:LEAD], dim, heads, step * chunk // dim)
     lead = (dot(q2[:, lanes], lead_keys, (1, 1)) * lead_mixing[...]).astype(BF16)
     lead_weights[...] = lead
-    growth = jnp.exp(cum[...].T)
-    squares = carried[0][0] if carried else jnp.zeros((size, dim), F32)
-    products = carried[0][1] if carried else jnp.zeros((size, dim), F32)
     for h in range(chunk // dim):
         at = step * chunk // dim + h
         here = slice(at * dim, (at + 1) * dim)
         state = unless(start, before[h * dim : (h + 1) * dim, :])
         a = inside[:, here] + dot(lead, lead_values[:, here], (1, 0))
-        a = a + growth[:, at : at + 1] * dot(q2[:, here], state, (1, 0))
-        attended[:, here] = a
+        attended[:, here] = a + dot(qs2[:, here], state, (1, 0))
+
+
+def sums_kernel(dim, attended, own, got, g2, sums):
+    size, width = attended.shape
+    rows = size // PAIR
+    here, there = halves(rows)
+    g2[here, :] = own[3 * rows :, :]
+    g2[there, :] = got[...]
+    squares = jnp.zeros((size, dim), F32)
+    products = jnp.zeros((size, dim), F32)
+    for at in range(0, width, dim):
+        a = attended[:, at : at + dim]
         squares = squares + a * a
-        products = products + a * g2[:, here].astype(F32)
-    if step < STEPS - 1:
-        out[0] = squares
-        out[1] = products
-        return
+        products = products + a * g2[:, at : at + dim].astype(F32)
     ones = jnp.ones((8, dim), BF16)
     both = jnp.concatenate([squares, products], 0)
     line = sum(dot(ones, part, (1, 1)) for part in split3(both))[:1]
-    out[...] = jnp.concatenate([line[:, :size], line[:, size:]], 0)
-
-
-def grad_kernel(width_all, attended, q2, lead_mixing, lead_values, g2, cum, *refs):
+    sums[...] = jnp.concatenate([line[:, :size], line[:, size:]], 0)
+
+
+def grad_kernel(width_all, attended, q2, qs2, lead_mixing, lead_values, g2, *refs):
     *sums, scales, grad = refs[:-PARTS]
     adjoints = refs[-PARTS:]
     size, width = q2.shape
@@ -284,19 +289,16 @@
     total = sum(ref[...] for ref in sums[1:]) + sums[0][...]
     inverse = 1.0 / jnp.sqrt(total[0:1] / width_all + 1e-06)
     shift = total[1:2] / width_all * inverse
-    both = jnp.concatenate([inverse, shift, jnp.zeros((6, size), F32)], 0)
+    both = jnp.concatenate([inverse, shift * inverse * inverse, jnp.zeros((6, size), F32)], 0)
     scales[...] = both
     both = both.T
-    inverse, shift = both[:, 0:1], both[:, 1:2]
-    growth = jnp.exp(cum[...].T)
+    inverse, pull = both[:, 0:1], both[:, 1:2]
     for h in range(heads):
         lanes = slice(h * dim, (h + 1) * dim)
-        n = attended[:, lanes] * inverse
-        d = ((g2[:, lanes].astype(F32) - n * shift) * inverse).astype(BF16)
+        d = (g2[:, lanes].astype(F32) * inverse - attended[:, lanes] * pull).astype(BF16)
         grad[:, lanes] = d
-        scaled = (q2[:, lanes].astype(F32) * growth[:, h : h + 1]).astype(BF16)
         part, at = divmod(h, heads // PARTS)
-        adjoints[part][at * dim : (at + 1) * dim, :] = dot(scaled, d, (0, 0)).astype(BF16)
+        adjoints[part][at * dim : (at + 1) * dim, :] = dot(qs2[:, lanes], d, (0, 0)).astype(BF16)
     scores = (dot(grad[...], lead_values[...], (1, 1)) * lead_mixing[...]).astype(BF16)
     tops = dot(scores, q2[...], (0, 0))
     per_part = heads // PARTS
@@ -314,7 +316,7 @@
     attended, scales, q2, kc2, v2, grad, weights, cum, *refs
 ):
     before, lead_weights = refs[:STEPS], refs[STEPS : 2 * STEPS]
-    keep, send, partial, key_grad, normed = refs[2 * STEPS :]
+    keep, send, partial, key_grad, vs2, normed = refs[2 * STEPS :]
     size, width = q2.shape
     dim = before[0].shape[1]
     heads = width // dim
@@ -324,8 +326,10 @@
     cum_rows = cum[...]
     cols = cum_rows.T
     growth = jnp.exp(cols)
+    after = jnp.exp(cols[size - 1 :, :] - cols)
     for h in range(heads):
         lanes = slice(h * dim, (h + 1) * dim)
+        vs2[:, lanes] = (v2[:, lanes].astype(F32) * after[:, h : h + 1]).astype(BF16)
         normed[:, lanes] = (attended[:, lanes] * inverse).astype(BF16)
         d = grad[:, lanes]
         scores = dot(d, v2[:, lanes], (1, 1)) * mixing_of(cum_rows, cols, h)
@@ -348,7 +352,7 @@
 
 
 def outer_grad_kernel(
-    last, part, partial, key_grad, kc2, v2, cum, behind, more, taps, keep, send, padded, done
+    last, part, partial, key_grad, ks2, vs2, behind, more, taps, keep, send, padded, done
 ):
     size, width = partial.shape
     dim = behind.shape[1]
@@ -358,16 +362,13 @@
     own = pl.ds(pl.multiple_of(mine * width + part * chunk, chunk), chunk)
     ends = lax.axis_index("ctx") >= last
     tops = unless(ends, behind[chunk:, :].astype(F32))
-    cols = cum[...].T
-    after = jnp.exp(cols[size - 1 :, :] - cols)
     for h in range(heads):
         at = part * heads + h
         lanes = slice(at * dim, (at + 1) * dim)
         here = slice(h * dim, (h + 1) * dim)
-        scale = after[:, at : at + 1]
         state = unless(ends, behind[here, :])
-        padded[:size, here] = key_grad[:, lanes] + scale * dot(v2[:, lanes], state, (1, 1))
-        done[:, here] = partial[:, lanes] + scale * dot(kc2[:, lanes], state, (1, 0))
+        padded[:size, here] = key_grad[:, lanes] + dot(vs2[:, lanes], state, (1, 1))
+        done[:, here] = partial[:, lanes] + dot(ks2[:, lanes], state, (1, 0))
         top = jnp.concatenate([tops[4 * h : 4 * h + 4], jnp.zeros((4, dim), F32)], 0)
         padded[size:, here] = top + more[:, lanes]
     total = done[...]
@@ -382,7 +383,7 @@
 
 def place_kernel(*refs):
     *pieces, out, sems = refs
-    kept, got = pieces[: len(pieces) // 2], pieces[len(pieces) // 2 :]
+    got, kept = pieces[: len(pieces) // 2], pieces[len(pieces) // 2 :]
     width = kept[0].shape[1]
     mine = lax.rem(lax.axis_index("ctx"), PAIR)
     pairs = []
@@ -395,7 +396,7 @@
 
 
 def placed(kept, got):
-    pieces = kept + got
+    pieces = got + kept
     rows = kept[0].shape[0]
     return call(
         place_kernel,
@@ -481,10 +482,10 @@
     got_q, got_g = swapped(second), swapped(third)
     joined = [
         shape((size, width), BF16), shape((size, width), BF16), shape((EDGE, width), F32),
-        shape((step_width + EDGE, dim), BF16),
+        shape((size, width), BF16), shape((step_width + EDGE, dim), BF16),
     ]
     room = [pltpu.VMEM((EDGE + size, step_width), F32)]
-    kc2, v2, top, state, cum = call(
+    kc2, v2, top, ks2, state, cum = call(
         join_kernel,
         joined + [shape((8, size), F32)],
         got[0], own, own_cum, conv_weight, *edges,
@@ -492,12 +493,12 @@
     )
     states = [state]
     for step in range(1, STEPS):
-        kc2, v2, top, state = call(
+        kc2, v2, top, ks2, state = call(
             lambda *refs, step=step: join_next_kernel(step, *refs),
             joined,
-            kc2, v2, top, got[step], own, cum, conv_weight, *edges,
+            kc2, v2, top, ks2, got[step], own, cum, conv_weight, *edges,
             scratch=room,
-            alias=((0, 0), (1, 1), (2, 2)),
+            alias=((0, 0), (1, 1), (2, 2), (3, 3)),
         )
         states.append(state)
     carry = jnp.repeat(jnp.exp(cum[:heads, -1]), dim)[:, None]
@@ -512,36 +513,37 @@
             moved = jnp.concatenate([turned(earlier, "ctx", PAIR), moved[step_width:]], 0)
         before.append(moved)
 
-    q2, g2, weights, inside, lead_mixing, lead_values = call(
+    q2, qs2, weights, inside, lead_mixing, lead_values = call(
         local_kernel,
         [shape((size, width), BF16)] * 2
         + [shape((heads, size, size), BF16), shape((size, width), F32)]
         + [shape((size, LEAD * heads), F32), shape((LEAD * heads, width), BF16)],
-        got_q, got_g, own, kc2, v2, cum,
+        got_q, own, kc2, v2, cum,
         flops=4 * heads * size * size * dim,
     )
-    lead_weights, carried = [], []
+    lead_weights = []
     for step in range(STEPS):
-        last = step == STEPS - 1
-        kc2, inside, lead, sums = call(
+        kc2, inside, lead = call(
             lambda *refs, step=step: attend_kernel(step, *refs),
-            [shape(kc2.shape, BF16), shape((size, width), F32), shape((size, LEAD * heads), BF16),
-             shape((2, size) if last else (2, size, dim), F32)],
-            kc2, inside, q2, g2, cum, top, conv_weight, lead_mixing, lead_values,
-            before[step], *carried,
+            [shape(kc2.shape, BF16), shape((size, width), F32), shape((size, LEAD * heads), BF16)],
+            kc2, inside, q2, qs2, top, conv_weight, lead_mixing, lead_values, before[step],
             scratch=[pltpu.VMEM((4 * LEAD, step_width), F32)],
             alias=((0, 0), (1, 1)),
         )
         lead_weights.append(lead)
-        carried = [sums]
     attended = inside
+    g2, sums = call(
+        lambda *refs: sums_kernel(dim, *refs),
+        [shape((size, width), BF16), shape((2, size), F32)],
+        attended, own, got_g,
+    )
     parts = summed_parts(sums)
     chunk = width // PARTS
     scales, grad, *adjoints = call(
         lambda *refs: grad_kernel(width_all, *refs),
         [shape((8, size), F32), shape((size, width), BF16)]
         + [shape((chunk + EDGE, dim), BF16)] * PARTS,
-        attended, q2, lead_mixing, lead_values, g2, cum, *parts,
+        attended, q2, qs2, lead_mixing, lead_values, g2, *parts,
     )
     last_pair = pair_index == supers - 1
     behind = []
@@ -566,9 +568,11 @@
         more = turned((after.T[:, :, None] * state_part).reshape(8, width), "ctx", -PAIR)
         more = unless(last_pair, more)
 
-    keep, send, partial, key_grad = call(
+    keep, send, partial, key_grad, vs2 = call(
         inner_grad_kernel,
-        [shape((rows, width), BF16)] * 2 + [shape((size, width), F32)] * 2,
+        [shape((rows, width), BF16)] * 2
+        + [shape((size, width), F32)] * 2
+        + [shape((size, width), BF16)],
         attended, scales, q2, kc2, v2, grad, weights, cum, *before, *lead_weights,
         scratch=[pltpu.VMEM((size, width), BF16)],
         flops=10 * heads * size * size * dim,
@@ -579,11 +583,11 @@
         keep, send = call(
             lambda *refs, i=i: outer_grad_kernel(blocks - PAIR, i, *refs),
             [shape((rows, chunk), BF16)] * 2,
-            partial, key_grad, kc2, v2, cum, behind[i], more, conv_weight,
+            partial, key_grad, ks2, vs2, behind[i], more, conv_weight,
             scratch=[pltpu.VMEM((size + 8, chunk), F32), pltpu.VMEM((size, chunk), F32)],
         )
+        got.append(to_earlier_section(send, 1))
         kept.append(to_earlier_section(keep, 0))
-        got.append(to_earlier_section(send, 1))
     return (layer_output, placed(kept, got))
 
 

time: 47.3 us -> 46.9 us (level)
  starting transfers between devices: 19.4 us -> 20.2 us
  waiting for transfers between devices: 16.9 us -> 16.1 us
    ppermute x5, waiting for transfers between devices: 5.12 us -> 2.39 us  [swapped(): lax.ppermute(block, 'ctx', [(i, i ^ 1) for i in range(lax.axis_size('ctx'...]
    ppermute x3, waiting for transfers between devices: 2.92 us -> 4.41 us  [turned(): lax.ppermute(block, axis, [(i, (i + distance) % count) for i in range(cou...]
    ppermute x3, starting transfers between devices: 3.49 us -> 4.43 us  [summed_parts(): parts.append(lax.ppermute(pair, ('ctx', 'tp'), route))]
    ppermute x3, waiting for transfers between devices: 2.94 us -> 3.55 us  [summed_parts(): parts.append(lax.ppermute(pair, ('ctx', 'tp'), route))]
    pallas_call x12 -> x13, Pallas kernels: 10.1 us -> 9.64 us  [call(): pl.pallas_call(kernel, out_shape=outs, in_specs=[pl.BlockSpec(memory_spac...]
  transfers between devices with their start and end apart: 14 -> 14, of which waited for: 10 -> 10; matrix products, arithmetic and copies ran while one was open for 0% -> 0% of each run, Pallas kernels for 14% -> 15%
where the time goes in v5:
time: 46.9 us; the launch traced here: 46.7 us
  starting transfers between devices  20.2 us (43%)
  waiting for transfers between devices  16.1 us (34%)
  Pallas kernels  9.64 us (21%)
  between operations  0.73 us (2%)
    pallas_call x13, Pallas kernels, call(): pl.pallas_call(kernel, out_shape=outs, in_specs=[pl.BlockSpec(memory_spac...  9.64 us
    ppermute x3, starting transfers between devices, turned(): lax.ppermute(block, axis, [(i, (i + distance) % count) for i in range(cou...  7.43 us
    ppermute x5, starting transfers between devices, swapped(): lax.ppermute(block, 'ctx', [(i, i ^ 1) for i in range(lax.axis_size('ctx'...  6.26 us
    ppermute x2, waiting for transfers between devices, to_earlier_section(): return lax.ppermute(block, ('ctx', 'pp'), route)  4.58 us
    ppermute x3, starting transfers between devices, summed_parts(): parts.append(lax.ppermute(pair, ('ctx', 'tp'), route))  4.43 us
    ppermute x3, waiting for transfers between devices, turned(): lax.ppermute(block, axis, [(i, (i + distance) % count) for i in range(cou...  4.41 us
    ppermute x3, waiting for transfers between devices, summed_parts(): parts.append(lax.ppermute(pair, ('ctx', 'tp'), route))  3.55 us
    ppermute x5, waiting for transfers between devices, swapped(): lax.ppermute(block, 'ctx', [(i, i ^ 1) for i in range(lax.axis_size('ctx'...  2.39 us
  transfers between devices with their start and end apart: 14, of which 10 were waited for; matrix products, arithmetic and copies ran while one was open for 0% of the time, Pallas kernels for 15%

profile of v5, /device:TPU:0, one launch (start us, length us, event | category | flops | bytes accessed | tf_op | source)
XLA Modules:
  0.0 46.7 jit_solution(16164308138667887955)
XLA Ops:
  0.6 1.0 %shard_map.77 = (bf16[272,256]{1,0:T(8,128)(2,1)S(1)}, bf16[256,256]{1,0:T(8,128)(2,1)S(1)}, f32[8,128]{1,0:T(8,128)S(1)}) custom-call(bf16[1,128,1024]{2,1,0:T(8,128)(2,1)} %k.3, bf16[1,128,1024]{2,1,0:T(8,128)(2,1)} %v.3, f32[1,8,128]{2,1,0:T(8,128)} %bitcast.1), custom_call_target="tpu_custom_call" | custom-call | bytes 802816 | tf_op jit(solution)/shard_map/pallas_call | solution.py:22
  1.6 3.1 %collective-permute-start = (bf16[272,256]{1,0:T(8,128)(2,1)S(1)}, bf16[272,256]{1,0:T(8,128)(2,1)S(1)}, u32[]{:S(2)}, u32[]{:S(2)}) collective-permute-start(bf16[272,256]{1,0:T(8,128)(2,1)S(1)} %get-tuple-element.43), channel_id=1, source_target_pairs={{0,8},{8,0},{16,24},{24,16},{1,9},{9,1},{17,25},{25,17},{2,10},{10... | collective-permute-start | bytes 417800 | tf_op jit(solution)/shard_map/ppermute | solution.py:416
  4.7 0.1 collective-permute-start.1
  4.8 0.0 copy-start
  4.8 1.3 %shard_map.78 = (bf16[128,512]{1,0:T(8,128)(2,1)S(1)}, bf16[128,512]{1,0:T(8,128)(2,1)S(1)}, bf16[512,512]{1,0:T(8,128)(2,1)S(1)}) custom-call(bf16[1,128,1024]{2,1,0:T(8,128)(2,1)} %q.1, bf16[1,128,1024]{2,1,0:T(8,128)(2,1)} %k.3, bf16[1,128,1024]{2,1,0:T(8,128)(2,1)} %v.3, bf16[1,128,1024]{2,1,0:T(8,128)(2,1)} %g.1, bf16[16,256]{1,0:T(8,128)(2,1)S(1)} %slice.3._), custom_call_target="tpu_custom_call" | custom-call | bytes 1843200 | tf_op jit(solution)/shard_map/pallas_call | solution.py:22
  6.1 2.0 %collective-permute-start.2 = (bf16[128,512]{1,0:T(8,128)(2,1)S(1)}, bf16[128,512]{1,0:T(8,128)(2,1)S(1)}, u32[]{:S(2)}, u32[]{:S(2)}) collective-permute-start(bf16[128,512]{1,0:T(8,128)(2,1)S(1)} %get-tuple-element.53), channel_id=1, source_target_pairs={{0,8},{8,0},{16,24},{24,16},{1,9},{9,1},{17,25},{25,17},{2,10},{10... | collective-permute-start | bytes 393224 | tf_op jit(solution)/shard_map/ppermute | solution.py:416
  8.1 0.1 collective-permute-start.5
  8.2 1.1 %collective-permute-done.got = bf16[272,256]{1,0:T(8,128)(2,1)S(1)} collective-permute-done((bf16[272,256]{1,0:T(8,128)(2,1)S(1)}, bf16[272,256]{1,0:T(8,128)(2,1)S(1)}, u32[]{:S(2)}, u32[]{:S(2)}) %collective-permute-start) | collective-permute-done | bytes 139296 | tf_op jit(solution)/shard_map/ppermute | solution.py:416
  9.2 0.0 copy-done
  9.2 0.6 %shard_map.79 = (bf16[256,512]{1,0:T(8,128)(2,1)S(1)}, bf16[256,512]{1,0:T(8,128)(2,1)S(1)}, f32[16,512]{1,0:T(8,128)S(1)}, bf16[256,512]{1,0:T(8,128)(2,1)S(1)}...) custom-call(bf16[272,256]{1,0:T(8,128)(2,1)S(1)} %collective-permute-done.got, ...), custom_call_target="tpu_custom_call" | custom-call | bytes 1581056 | tf_op jit(solution)/shard_map/pallas_call | solution.py:22
  9.9 3.1 %collective-permute-start.3 = (bf16[272,128]{1,0:T(8,128)(2,1)S(1)}, bf16[272,128]{1,0:T(8,128)(2,1)S(1)}, u32[]{:S(2)}, u32[]{:S(2)}) collective-permute-start(bf16[272,128]{1,0:T(8,128)(2,1)S(1)} %get-tuple-element.61), channel_id=1, source_target_pairs={{0,16},{8,24},{16,0},{24,8},{1,17},{9,25},{17,1},{25,9},{2,18},{10... | collective-permute-start | bytes 208904 | tf_op jit(solution)/shard_map/ppermute | solution.py:412
  13.0 0.0 collective-permute-done.1.refs_4_
  13.0 0.6 %shard_map.80 = (bf16[256,512]{1,0:T(8,128)(2,1)S(1)}, bf16[256,512]{1,0:T(8,128)(2,1)S(1)}, f32[16,512]{1,0:T(8,128)S(1)}, bf16[256,512]{1,0:T(8,128)(2,1)S(1)}, bf16[272,128]{1,0:T(8,128)(2,1)S(1)}) custom-call(bf16[256,512]{1,0:T(8,128)(2,1)S(1)} %get-tuple-element.46.refs_0_, ...), custom_call_target="tpu_custom_call", output_to_operand_aliasing={{0}: (0, {}), {1}: (1, {}), {2}: (2, {}), {3}: (3, {})} | custom-call | bytes 2387968 | tf_op jit(solution)/shard_map/pallas_call | solution.py:22
  13.6 2.1 %collective-permute-start.4 = (bf16[272,128]{1,0:T(8,128)(2,1)S(1)}, bf16[272,128]{1,0:T(8,128)(2,1)S(1)}, u32[]{:S(2)}, u32[]{:S(2)}) collective-permute-start(bf16[272,128]{1,0:T(8,128)(2,1)S(1)} %get-tuple-element.64), channel_id=1, source_target_pairs={{0,16},{8,24},{16,0},{24,8},{1,17},{9,25},{17,1},{25,9},{2,18},{10... | collective-permute-start | bytes 208904 | tf_op jit(solution)/shard_map/ppermute | solution.py:412
  15.8 1.3 %collective-permute-done.2.got = bf16[128,512]{1,0:T(8,128)(2,1)S(1)} collective-permute-done((bf16[128,512]{1,0:T(8,128)(2,1)S(1)}, bf16[128,512]{1,0:T(8,128)(2,1)S(1)}, u32[]{:S(2)}, u32[]{:S(2)}) %collective-permute-start.2) | collective-permute-done | bytes 131104 | tf_op jit(solution)/shard_map/ppermute | solution.py:416
  17.1 0.7 %shard_map.81 = (bf16[256,512]{1,0:T(8,128)(2,1)S(1)}, bf16[256,512]{1,0:T(8,128)(2,1)S(1)}, bf16[4,256,256]{2,1,0:T(8,128)(2,1)S(1)}, f32[256,512]{1,0:T(8,128)...) custom-call(bf16[128,512]{1,0:T(8,128)(2,1)S(1)} %collective-permute-done.2.got, ...), custom_call_target="tpu_custom_call" | custom-call | flops 134217728 | bytes 2793472 | tf_op jit(solution)/shard_map/pallas_call | solution.py:22
  17.8 0.5 %collective-permute-done.3.refs_8_.refs_0_ = bf16[272,128]{1,0:T(8,128)(2,1)S(1)} collective-permute-done((bf16[272,128]{1,0:T(8,128)(2,1)S(1)}, bf16[272,128]{1,0:T(8,128)(2,1)S(1)}, u32[]{:S(2)}, u32[]{:S(2)}) %collective-permute-start.3) | collective-permute-done | bytes 69664 | tf_op jit(solution)/shard_map/ppermute | solution.py:412
  18.3 0.4 shard_map.82
  18.7 0.9 %collective-permute-done.4.refs_8_.refs_1_ = bf16[272,128]{1,0:T(8,128)(2,1)S(1)} collective-permute-done((bf16[272,128]{1,0:T(8,128)(2,1)S(1)}, bf16[272,128]{1,0:T(8,128)(2,1)S(1)}, u32[]{:S(2)}, u32[]{:S(2)}) %collective-permute-start.4) | collective-permute-done | bytes 69664 | tf_op jit(solution)/shard_map/ppermute | solution.py:412
  19.6 0.4 shard_map.83
  20.0 0.0 collective-permute-done.5.refs_2_
  20.0 0.2 shard_map.84
  20.3 0.0 collective-permute-start.6
  20.3 1.2 %collective-permute-done.6 = f32[2,256]{1,0:T(2,128)S(1)} collective-permute-done((f32[2,256]{1,0:T(2,128)S(1)}, f32[2,256]{1,0:T(2,128)S(1)}, u32[]{:S(2)}, u32[]{:S(2)}) %collective-permute-start.6) | collective-permute-done | bytes 2080 | tf_op jit(solution)/shard_map/ppermute | solution.py:431
  21.5 1.7 %collective-permute-start.7 = (f32[2,256]{1,0:T(2,128)S(1)}, f32[2,256]{1,0:T(2,128)S(1)}, u32[]{:S(2)}, u32[]{:S(2)}) collective-permute-start(f32[2,256]{1,0:T(2,128)S(1)} %add.3.refs_6_), channel_id=1, source_target_pairs={{0,4},{2,6},{4,0},{6,2},{8,12},{10,14},{12,8},{14,10},{16,20},{18,... | collective-permute-start | bytes 6152 | tf_op jit(solution)/shard_map/ppermute | solution.py:440
  23.3 2.7 %collective-permute-start.8 = (f32[2,256]{1,0:T(2,128)S(1)}, f32[2,256]{1,0:T(2,128)S(1)}, u32[]{:S(2)}, u32[]{:S(2)}) collective-permute-start(f32[2,256]{1,0:T(2,128)S(1)} %add.3.refs_6_), channel_id=1, source_target_pairs={{0,12},{2,14},{4,8},{6,10},{8,4},{10,6},{12,0},{14,2},{16,28},{18,... | collective-permute-start | bytes 6152 | tf_op jit(solution)/shard_map/ppermute | solution.py:440
  25.9 0.0 collective-permute-start.9
  26.0 0.0 collective-permute-done.7.refs_7_
  26.0 1.8 %collective-permute-done.8.refs_8_ = f32[2,256]{1,0:T(2,128)S(1)} collective-permute-done((f32[2,256]{1,0:T(2,128)S(1)}, f32[2,256]{1,0:T(2,128)S(1)}, u32[]{:S(2)}, u32[]{:S(2)}) %collective-permute-start.8) | collective-permute-done | bytes 2080 | tf_op jit(solution)/shard_map/ppermute | solution.py:440
  27.7 1.8 %collective-permute-done.9.refs_9_ = f32[2,256]{1,0:T(2,128)S(1)} collective-permute-done((f32[2,256]{1,0:T(2,128)S(1)}, f32[2,256]{1,0:T(2,128)S(1)}, u32[]{:S(2)}, u32[]{:S(2)}) %collective-permute-start.9) | collective-permute-done | bytes 2080 | tf_op jit(solution)/shard_map/ppermute | solution.py:440
  29.5 0.8 %shard_map.85 = (f32[8,256]{1,0:T(8,128)S(1)}, bf16[256,512]{1,0:T(8,128)(2,1)S(1)}, bf16[528,128]{1,0:T(8,128)(2,1)S(1)}) custom-call(f32[256,512]{1,0:T(8,128)S(1)} %get-tuple-element.65.refs_0_.attended, bf16[256,512]{1,0:T(8,128)(2,1)S(1)} %get-tuple-element.56.refs_2_.refs_1_.q2, bf16[256,512]{1,0:T(8,128)(2,1)S(1)} %get-tuple-element.57.refs_3_.refs_2_, ...), custom_call_target="tpu_custom_call" | custom-call | bytes 1757184 | tf_op jit(solution)/shard_map/pallas_call | solution.py:22
  30.3 2.1 %collective-permute-start.11 = (bf16[528,128]{1,0:T(8,128)(2,1)S(1)}, bf16[528,128]{1,0:T(8,128)(2,1)S(1)}, u32[]{:S(2)}, u32[]{:S(2)}) collective-permute-start(bf16[528,128]{1,0:T(8,128)(2,1)S(1)} %get-tuple-element.81), channel_id=1, source_target_pairs={{0,16},{8,24},{16,0},{24,8},{1,17},{9,25},{17,1},{25,9},{2,18},{10... | collective-permute-start | bytes 405512 | tf_op jit(solution)/shard_map/ppermute | solution.py:412
  32.4 1.6 %shard_map.86 = (bf16[128,512]{1,0:T(8,128)(2,1)S(1)}, bf16[128,512]{1,0:T(8,128)(2,1)S(1)}, f32[256,512]{1,0:T(8,128)S(1)}, f32[256,512]{1,0:T(8,128)S(1)}, bf16[256,512]{1,0:T(8,128)(2,1)S(1)}) custom-call(f32[256,512]{1,0:T(8,128)S(1)} %get-tuple-element.65.refs_0_.attended, f32[8,256]{1,0:T(8,128)S(1)} %get-tuple-element.69.scales, ...), custom_call_target="tpu_custom_call" | custom-call | flops 335544320 | bytes 3842048 | tf_op jit(solution)/shard_map/pallas_call | solution.py:22
  34.1 1.0 %collective-permute-start.10 = (bf16[128,512]{1,0:T(8,128)(2,1)S(1)}, bf16[128,512]{1,0:T(8,128)(2,1)S(1)}, u32[]{:S(2)}, u32[]{:S(2)}) collective-permute-start(bf16[128,512]{1,0:T(8,128)(2,1)S(1)} %get-tuple-element.75), channel_id=1, source_target_pairs={{0,8},{8,0},{16,24},{24,16},{1,9},{9,1},{17,25},{25,17},{2,10},{10... | collective-permute-start | bytes 393224 | tf_op jit(solution)/shard_map/ppermute | solution.py:416
  35.1 3.0 %collective-permute-done.11.refs_4_ = bf16[528,128]{1,0:T(8,128)(2,1)S(1)} collective-permute-done((bf16[528,128]{1,0:T(8,128)(2,1)S(1)}, bf16[528,128]{1,0:T(8,128)(2,1)S(1)}, u32[]{:S(2)}, u32[]{:S(2)}) %collective-permute-start.11) | collective-permute-done | bytes 135200 | tf_op jit(solution)/shard_map/ppermute | solution.py:412
  38.1 0.5 %shard_map.88 = (bf16[128,512]{1,0:T(8,128)(2,1)S(1)}, bf16[128,512]{1,0:T(8,128)(2,1)S(1)}) custom-call(f32[256,512]{1,0:T(8,128)S(1)} %get-tuple-element.77.refs_0_, f32[256,512]{1,0:T(8,128)S(1)} %get-tuple-element.78.refs_1_, bf16[256,512]{1,0:T(8,128)(2,1)S(1)} %get-tuple-element.79.refs_2_, bf16[256,512]{1,0:T(8,128)(2,1)S(1)} %get-tuple-element.80.refs_3_, ...), custom_call_target="tpu_custom_call" | custom-call | bytes 2002944 | tf_op jit(solution)/shard_map/pallas_call | solution.py:22
  38.6 1.5 %collective-permute-start.12 = (bf16[128,512]{1,0:T(8,128)(2,1)S(1)}, bf16[128,512]{1,0:T(8,128)(2,1)S(1)}, u32[]{:S(2)}, u32[]{:S(2)}) collective-permute-start(bf16[128,512]{1,0:T(8,128)(2,1)S(1)} %get-tuple-element.82), channel_id=1, source_target_pairs={{0,9},{1,8},{8,1},{9,0},{16,25},{17,24},{24,17},{25,16},{2,11},{3,... | collective-permute-start | bytes 393224 | tf_op jit(solution)/shard_map/ppermute | solution.py:426
  40.1 0.5 %collective-permute-start.13 = (bf16[128,512]{1,0:T(8,128)(2,1)S(1)}, bf16[128,512]{1,0:T(8,128)(2,1)S(1)}, u32[]{:S(2)}, u32[]{:S(2)}) collective-permute-start(bf16[128,512]{1,0:T(8,128)(2,1)S(1)} %get-tuple-element.83), channel_id=1, source_target_pairs={{0,1},{1,0},{8,9},{9,8},{16,17},{17,16},{24,25},{25,24},{2,3},{3,2... | collective-permute-start | bytes 393224 | tf_op jit(solution)/shard_map/ppermute | solution.py:426
  40.7 0.0 collective-permute-done.10.refs_0_
  40.7 0.7 %shard_map.87 = bf16[1,128,1024]{2,1,0:T(8,128)(2,1)} custom-call(bf16[128,512]{1,0:T(8,128)(2,1)S(1)} %collective-permute-done.10.refs_0_, bf16[128,512]{1,0:T(8,128)(2,1)S(1)} %get-tuple-element.76.refs_1_), custom_call_target="tpu_custom_call" | custom-call | bytes 524288 | tf_op jit(solution)/shard_map/pallas_call | solution.py:22
  41.4 3.3 %collective-permute-done.12.refs_0_ = bf16[128,512]{1,0:T(8,128)(2,1)S(1)} collective-permute-done((bf16[128,512]{1,0:T(8,128)(2,1)S(1)}, bf16[128,512]{1,0:T(8,128)(2,1)S(1)}, u32[]{:S(2)}, u32[]{:S(2)}) %collective-permute-start.12) | collective-permute-done | bytes 131104 | tf_op jit(solution)/shard_map/ppermute | solution.py:426
  44.6 1.3 %collective-permute-done.13.refs_1_ = bf16[128,512]{1,0:T(8,128)(2,1)S(1)} collective-permute-done((bf16[128,512]{1,0:T(8,128)(2,1)S(1)}, bf16[128,512]{1,0:T(8,128)(2,1)S(1)}, u32[]{:S(2)}, u32[]{:S(2)}) %collective-permute-start.13) | collective-permute-done | bytes 131104 | tf_op jit(solution)/shard_map/ppermute | solution.py:426
  46.0 0.7 %shard_map.89 = bf16[1,128,1024]{2,1,0:T(8,128)(2,1)} custom-call(bf16[128,512]{1,0:T(8,128)(2,1)S(1)} %collective-permute-done.12.refs_0_, bf16[128,512]{1,0:T(8,128)(2,1)S(1)} %collective-permute-done.13.refs_1_), custom_call_target="tpu_custom_call" | custom-call | bytes 524288 | tf_op jit(solution)/shard_map/pallas_call | solution.py:22
  (3 shorter events, 0.0 us)
Async XLA Ops:
  1.6 7.6 %collective-permute-start = (bf16[272,256]{1,0:T(8,128)(2,1)S(1)}, bf16[272,256]{1,0:T(8,128)(2,1)S(1)}, u32[]{:S(2)}, u32[]{:S(2)}) collective-permute-start(bf16[272,256]{1,0:T(8,128)(2,1)S(1)} %get-tuple-element.43), channel_id=1, source_target_pairs={{0,8},{8,0},{16,24},{24,16},{1,9},{9,1},{17,25},{25,17},{2,10},{10... | collective-permute-start | bytes 417800 | tf_op jit(solution)/shard_map/ppermute | solution.py:416
  4.7 8.3 %collective-permute-start.1 = (bf16[256,256]{1,0:T(8,128)(2,1)S(1)}, bf16[256,256]{1,0:T(8,128)(2,1)S(1)}, u32[]{:S(2)}, u32[]{:S(2)}) collective-permute-start(bf16[256,256]{1,0:T(8,128)(2,1)S(1)} %get-tuple-element.50), channel_id=1, source_target_pairs={{0,8},{8,0},{16,24},{24,16},{1,9},{9,1},{17,25},{25,17},{2,10},{10... | collective-permute-start | bytes 393224 | tf_op jit(solution)/shard_map/ppermute | solution.py:416
  4.8 4.4 %copy-start = (f32[1,4,1024]{2,1,0:T(4,128)S(1)}, f32[1,4,1024]{2,1,0:T(4,128)}, u32[]{:S(2)}) copy-start(f32[1,4,1024]{2,1,0:T(4,128)} %refs_6_.1) | copy-start | bytes 49156
  6.1 11.0 %collective-permute-start.2 = (bf16[128,512]{1,0:T(8,128)(2,1)S(1)}, bf16[128,512]{1,0:T(8,128)(2,1)S(1)}, u32[]{:S(2)}, u32[]{:S(2)}) collective-permute-start(bf16[128,512]{1,0:T(8,128)(2,1)S(1)} %get-tuple-element.53), channel_id=1, source_target_pairs={{0,8},{8,0},{16,24},{24,16},{1,9},{9,1},{17,25},{25,17},{2,10},{10... | collective-permute-start | bytes 393224 | tf_op jit(solution)/shard_map/ppermute | solution.py:416
  8.1 12.0 %collective-permute-start.5 = (bf16[128,512]{1,0:T(8,128)(2,1)S(1)}, bf16[128,512]{1,0:T(8,128)(2,1)S(1)}, u32[]{:S(2)}, u32[]{:S(2)}) collective-permute-start(bf16[128,512]{1,0:T(8,128)(2,1)S(1)} %get-tuple-element.66), channel_id=1, source_target_pairs={{0,8},{8,0},{16,24},{24,16},{1,9},{9,1},{17,25},{25,17},{2,10},{10... | collective-permute-start | bytes 393224 | tf_op jit(solution)/shard_map/ppermute | solution.py:416
  9.9 8.4 %collective-permute-start.3 = (bf16[272,128]{1,0:T(8,128)(2,1)S(1)}, bf16[272,128]{1,0:T(8,128)(2,1)S(1)}, u32[]{:S(2)}, u32[]{:S(2)}) collective-permute-start(bf16[272,128]{1,0:T(8,128)(2,1)S(1)} %get-tuple-element.61), channel_id=1, source_target_pairs={{0,16},{8,24},{16,0},{24,8},{1,17},{9,25},{17,1},{25,9},{2,18},{10... | collective-permute-start | bytes 208904 | tf_op jit(solution)/shard_map/ppermute | solution.py:412
  13.6 6.0 %collective-permute-start.4 = (bf16[272,128]{1,0:T(8,128)(2,1)S(1)}, bf16[272,128]{1,0:T(8,128)(2,1)S(1)}, u32[]{:S(2)}, u32[]{:S(2)}) collective-permute-start(bf16[272,128]{1,0:T(8,128)(2,1)S(1)} %get-tuple-element.64), channel_id=1, source_target_pairs={{0,16},{8,24},{16,0},{24,8},{1,17},{9,25},{17,1},{25,9},{2,18},{10... | collective-permute-start | bytes 208904 | tf_op jit(solution)/shard_map/ppermute | solution.py:412
  20.3 1.2 %collective-permute-start.6 = (f32[2,256]{1,0:T(2,128)S(1)}, f32[2,256]{1,0:T(2,128)S(1)}, u32[]{:S(2)}, u32[]{:S(2)}) collective-permute-start(f32[2,256]{1,0:T(2,128)S(1)} %get-tuple-element.68), channel_id=1, source_target_pairs={{0,2},{2,0},{4,6},{6,4},{1,3},{3,1},{5,7},{7,5},{8,10},{10,8},{12,... | collective-permute-start | bytes 6152 | tf_op jit(solution)/shard_map/ppermute | solution.py:431
  21.5 4.4 %collective-permute-start.7 = (f32[2,256]{1,0:T(2,128)S(1)}, f32[2,256]{1,0:T(2,128)S(1)}, u32[]{:S(2)}, u32[]{:S(2)}) collective-permute-start(f32[2,256]{1,0:T(2,128)S(1)} %add.3.refs_6_), channel_id=1, source_target_pairs={{0,4},{2,6},{4,0},{6,2},{8,12},{10,14},{12,8},{14,10},{16,20},{18,... | collective-permute-start | bytes 6152 | tf_op jit(solution)/shard_map/ppermute | solution.py:440
  23.3 4.5 %collective-permute-start.8 = (f32[2,256]{1,0:T(2,128)S(1)}, f32[2,256]{1,0:T(2,128)S(1)}, u32[]{:S(2)}, u32[]{:S(2)}) collective-permute-start(f32[2,256]{1,0:T(2,128)S(1)} %add.3.refs_6_), channel_id=1, source_target_pairs={{0,12},{2,14},{4,8},{6,10},{8,4},{10,6},{12,0},{14,2},{16,28},{18,... | collective-permute-start | bytes 6152 | tf_op jit(solution)/shard_map/ppermute | solution.py:440
  25.9 3.6 %collective-permute-start.9 = (f32[2,256]{1,0:T(2,128)S(1)}, f32[2,256]{1,0:T(2,128)S(1)}, u32[]{:S(2)}, u32[]{:S(2)}) collective-permute-start(f32[2,256]{1,0:T(2,128)S(1)} %add.3.refs_6_), channel_id=1, source_target_pairs={{0,8},{2,10},{4,12},{6,14},{8,0},{10,2},{12,4},{14,6},{16,24},{18,... | collective-permute-start | bytes 6152 | tf_op jit(solution)/shard_map/ppermute | solution.py:440
  30.3 7.8 %collective-permute-start.11 = (bf16[528,128]{1,0:T(8,128)(2,1)S(1)}, bf16[528,128]{1,0:T(8,128)(2,1)S(1)}, u32[]{:S(2)}, u32[]{:S(2)}) collective-permute-start(bf16[528,128]{1,0:T(8,128)(2,1)S(1)} %get-tuple-element.81), channel_id=1, source_target_pairs={{0,16},{8,24},{16,0},{24,8},{1,17},{9,25},{17,1},{25,9},{2,18},{10... | collective-permute-start | bytes 405512 | tf_op jit(solution)/shard_map/ppermute | solution.py:412
  34.1 6.6 %collective-permute-start.10 = (bf16[128,512]{1,0:T(8,128)(2,1)S(1)}, bf16[128,512]{1,0:T(8,128)(2,1)S(1)}, u32[]{:S(2)}, u32[]{:S(2)}) collective-permute-start(bf16[128,512]{1,0:T(8,128)(2,1)S(1)} %get-tuple-element.75), channel_id=1, source_target_pairs={{0,8},{8,0},{16,24},{24,16},{1,9},{9,1},{17,25},{25,17},{2,10},{10... | collective-permute-start | bytes 393224 | tf_op jit(solution)/shard_map/ppermute | solution.py:416
  38.6 6.0 %collective-permute-start.12 = (bf16[128,512]{1,0:T(8,128)(2,1)S(1)}, bf16[128,512]{1,0:T(8,128)(2,1)S(1)}, u32[]{:S(2)}, u32[]{:S(2)}) collective-permute-start(bf16[128,512]{1,0:T(8,128)(2,1)S(1)} %get-tuple-element.82), channel_id=1, source_target_pairs={{0,9},{1,8},{8,1},{9,0},{16,25},{17,24},{24,17},{25,16},{2,11},{3,... | collective-permute-start | bytes 393224 | tf_op jit(solution)/shard_map/ppermute | solution.py:426
  40.1 5.8 %collective-permute-start.13 = (bf16[128,512]{1,0:T(8,128)(2,1)S(1)}, bf16[128,512]{1,0:T(8,128)(2,1)S(1)}, u32[]{:S(2)}, u32[]{:S(2)}) collective-permute-start(bf16[128,512]{1,0:T(8,128)(2,1)S(1)} %get-tuple-element.83), channel_id=1, source_target_pairs={{0,1},{1,0},{8,9},{9,8},{16,17},{17,16},{24,25},{25,24},{2,3},{3,2... | collective-permute-start | bytes 393224 | tf_op jit(solution)/shard_map/ppermute | solution.py:426

commit v6 on v5

--- a/solution.py
+++ b/solution.py
@@ -383,7 +383,7 @@
 
 def place_kernel(*refs):
     *pieces, out, sems = refs
-    got, kept = pieces[: len(pieces) // 2], pieces[len(pieces) // 2 :]
+    kept, got = pieces[: len(pieces) // 2], pieces[len(pieces) // 2 :]
     width = kept[0].shape[1]
     mine = lax.rem(lax.axis_index("ctx"), PAIR)
     pairs = []
@@ -396,7 +396,7 @@
 
 
 def placed(kept, got):
-    pieces = got + kept
+    pieces = kept + got
     rows = kept[0].shape[0]
     return call(
         place_kernel,
@@ -428,16 +428,24 @@
 
 def summed_parts(part):
     blocks, count = lax.axis_size("ctx"), lax.axis_size("tp")
-    pair = part + lax.ppermute(part, "tp", [(i, i ^ 1) for i in range(count)])
-    parts = [pair]
-    ways = [(flip, k) for k in range(2, count, 2) for flip in range(PAIR)] + [(1, 0)]
-    for flip, k in ways:
+
+    def neighbour(block):
+        return lax.ppermute(block, "tp", [(i, i ^ 1) for i in range(count)])
+
+    def fetched(block, *ways):
         route = [
-            (c * count + t, (c ^ flip) * count + (t + k) % count)
+            (c * count + t, (c ^ ways[t % len(ways)][0]) * count + (t + ways[t % len(ways)][1]) % count)
             for c in range(blocks)
             for t in range(count)
         ]
-        parts.append(lax.ppermute(pair, ("ctx", "tp"), route))
+        return lax.ppermute(block, ("ctx", "tp"), route)
+
+    pair = part + neighbour(part)
+    ways = [(1, 0)] + [(flip, k) for k in range(2, count, 2) for flip in (0, 1)]
+    shared = [fetched(pair, *ways[i : i + 2]) for i in range(0, len(ways) - 1, 2)]
+    parts = [pair, fetched(pair, ways[-1])]
+    for block in shared:
+        parts += [block, neighbour(block)]
     return parts
 
 
@@ -586,8 +594,8 @@
             partial, key_grad, ks2, vs2, behind[i], more, conv_weight,
             scratch=[pltpu.VMEM((size + 8, chunk), F32), pltpu.VMEM((size, chunk), F32)],
         )
+        kept.append(to_earlier_section(keep, 0))
         got.append(to_earlier_section(send, 1))
-        kept.append(to_earlier_section(keep, 0))
     return (layer_output, placed(kept, got))
 
 

time: 46.9 us -> 46.4 us (0.989)
  starting transfers between devices: 20.2 us -> 18.6 us
  waiting for transfers between devices: 16.1 us -> 17.2 us
    ppermute x5, starting transfers between devices: 6.26 us -> 5.58 us  [swapped(): lax.ppermute(block, 'ctx', [(i, i ^ 1) for i in range(lax.axis_size('ctx'...]
    ppermute x3, waiting for transfers between devices: 4.41 us -> 5.07 us  [turned(): lax.ppermute(block, axis, [(i, (i + distance) % count) for i in range(cou...]
    ppermute x4, starting transfers between devices: 4.45 us -> 3.89 us  [the longest x2 3.86 us: fetched(): return lax.ppermute(block, ('ctx', 'tp'), route)]
where the time goes in v6:
time: 46.4 us; the launch traced here: 46.2 us
  starting transfers between devices  18.6 us (40%)
  waiting for transfers between devices  17.2 us (37%)
  Pallas kernels  9.64 us (21%)
  between operations  0.73 us (2%)
    pallas_call x13, Pallas kernels, call(): pl.pallas_call(kernel, out_shape=outs, in_specs=[pl.BlockSpec(memory_spac...  9.64 us
    ppermute x3, starting transfers between devices, turned(): lax.ppermute(block, axis, [(i, (i + distance) % count) for i in range(cou...  7.43 us
    ppermute x5, starting transfers between devices, swapped(): lax.ppermute(block, 'ctx', [(i, i ^ 1) for i in range(lax.axis_size('ctx'...  5.58 us
    ppermute x3, waiting for transfers between devices, turned(): lax.ppermute(block, axis, [(i, (i + distance) % count) for i in range(cou...  5.07 us
    ppermute x2, waiting for transfers between devices, to_earlier_section(): return lax.ppermute(block, ('ctx', 'pp'), route)  5.01 us
    ppermute x2, starting transfers between devices, fetched(): return lax.ppermute(block, ('ctx', 'tp'), route)  3.86 us
    ppermute x2, waiting for transfers between devices, fetched(): return lax.ppermute(block, ('ctx', 'tp'), route)  3.55 us
    ppermute x5, waiting for transfers between devices, swapped(): lax.ppermute(block, 'ctx', [(i, i ^ 1) for i in range(lax.axis_size('ctx'...  2.39 us
  transfers between devices with their start and end apart: 14, of which 10 were waited for; matrix products, arithmetic and copies ran while one was open for 0% of the time, Pallas kernels for 15%

profile of v6, /device:TPU:0, one launch (start us, length us, event | category | flops | bytes accessed | tf_op | source)
XLA Modules:
  0.0 46.2 jit_solution(11877941206310922365)
XLA Ops:
  0.6 1.0 %shard_map.77 = (bf16[272,256]{1,0:T(8,128)(2,1)S(1)}, bf16[256,256]{1,0:T(8,128)(2,1)S(1)}, f32[8,128]{1,0:T(8,128)S(1)}) custom-call(bf16[1,128,1024]{2,1,0:T(8,128)(2,1)} %k.3, bf16[1,128,1024]{2,1,0:T(8,128)(2,1)} %v.3, f32[1,8,128]{2,1,0:T(8,128)} %bitcast.1), custom_call_target="tpu_custom_call" | custom-call | bytes 802816 | tf_op jit(solution)/shard_map/pallas_call | solution.py:22
  1.6 3.1 %collective-permute-start = (bf16[272,256]{1,0:T(8,128)(2,1)S(1)}, bf16[272,256]{1,0:T(8,128)(2,1)S(1)}, u32[]{:S(2)}, u32[]{:S(2)}) collective-permute-start(bf16[272,256]{1,0:T(8,128)(2,1)S(1)} %get-tuple-element.43), channel_id=1, source_target_pairs={{0,8},{8,0},{16,24},{24,16},{1,9},{9,1},{17,25},{25,17},{2,10},{10... | collective-permute-start | bytes 417800 | tf_op jit(solution)/shard_map/ppermute | solution.py:416
  4.7 0.1 collective-permute-start.1
  4.8 0.0 copy-start
  4.8 1.3 %shard_map.78 = (bf16[128,512]{1,0:T(8,128)(2,1)S(1)}, bf16[128,512]{1,0:T(8,128)(2,1)S(1)}, bf16[512,512]{1,0:T(8,128)(2,1)S(1)}) custom-call(bf16[1,128,1024]{2,1,0:T(8,128)(2,1)} %q.1, bf16[1,128,1024]{2,1,0:T(8,128)(2,1)} %k.3, bf16[1,128,1024]{2,1,0:T(8,128)(2,1)} %v.3, bf16[1,128,1024]{2,1,0:T(8,128)(2,1)} %g.1, bf16[16,256]{1,0:T(8,128)(2,1)S(1)} %slice.3._), custom_call_target="tpu_custom_call" | custom-call | bytes 1843200 | tf_op jit(solution)/shard_map/pallas_call | solution.py:22
  6.1 2.0 %collective-permute-start.2 = (bf16[128,512]{1,0:T(8,128)(2,1)S(1)}, bf16[128,512]{1,0:T(8,128)(2,1)S(1)}, u32[]{:S(2)}, u32[]{:S(2)}) collective-permute-start(bf16[128,512]{1,0:T(8,128)(2,1)S(1)} %get-tuple-element.53), channel_id=1, source_target_pairs={{0,8},{8,0},{16,24},{24,16},{1,9},{9,1},{17,25},{25,17},{2,10},{10... | collective-permute-start | bytes 393224 | tf_op jit(solution)/shard_map/ppermute | solution.py:416
  8.1 0.1 collective-permute-start.5
  8.2 1.1 %collective-permute-done.got = bf16[272,256]{1,0:T(8,128)(2,1)S(1)} collective-permute-done((bf16[272,256]{1,0:T(8,128)(2,1)S(1)}, bf16[272,256]{1,0:T(8,128)(2,1)S(1)}, u32[]{:S(2)}, u32[]{:S(2)}) %collective-permute-start) | collective-permute-done | bytes 139296 | tf_op jit(solution)/shard_map/ppermute | solution.py:416
  9.2 0.0 copy-done
  9.2 0.6 %shard_map.79 = (bf16[256,512]{1,0:T(8,128)(2,1)S(1)}, bf16[256,512]{1,0:T(8,128)(2,1)S(1)}, f32[16,512]{1,0:T(8,128)S(1)}, bf16[256,512]{1,0:T(8,128)(2,1)S(1)}...) custom-call(bf16[272,256]{1,0:T(8,128)(2,1)S(1)} %collective-permute-done.got, ...), custom_call_target="tpu_custom_call" | custom-call | bytes 1581056 | tf_op jit(solution)/shard_map/pallas_call | solution.py:22
  9.9 3.1 %collective-permute-start.3 = (bf16[272,128]{1,0:T(8,128)(2,1)S(1)}, bf16[272,128]{1,0:T(8,128)(2,1)S(1)}, u32[]{:S(2)}, u32[]{:S(2)}) collective-permute-start(bf16[272,128]{1,0:T(8,128)(2,1)S(1)} %get-tuple-element.61), channel_id=1, source_target_pairs={{0,16},{8,24},{16,0},{24,8},{1,17},{9,25},{17,1},{25,9},{2,18},{10... | collective-permute-start | bytes 208904 | tf_op jit(solution)/shard_map/ppermute | solution.py:412
  13.0 0.0 collective-permute-done.1.refs_4_
  13.0 0.6 %shard_map.80 = (bf16[256,512]{1,0:T(8,128)(2,1)S(1)}, bf16[256,512]{1,0:T(8,128)(2,1)S(1)}, f32[16,512]{1,0:T(8,128)S(1)}, bf16[256,512]{1,0:T(8,128)(2,1)S(1)}, bf16[272,128]{1,0:T(8,128)(2,1)S(1)}) custom-call(bf16[256,512]{1,0:T(8,128)(2,1)S(1)} %get-tuple-element.46.refs_0_, ...), custom_call_target="tpu_custom_call", output_to_operand_aliasing={{0}: (0, {}), {1}: (1, {}), {2}: (2, {}), {3}: (3, {})} | custom-call | bytes 2387968 | tf_op jit(solution)/shard_map/pallas_call | solution.py:22
  13.6 2.1 %collective-permute-start.4 = (bf16[272,128]{1,0:T(8,128)(2,1)S(1)}, bf16[272,128]{1,0:T(8,128)(2,1)S(1)}, u32[]{:S(2)}, u32[]{:S(2)}) collective-permute-start(bf16[272,128]{1,0:T(8,128)(2,1)S(1)} %get-tuple-element.64), channel_id=1, source_target_pairs={{0,16},{8,24},{16,0},{24,8},{1,17},{9,25},{17,1},{25,9},{2,18},{10... | collective-permute-start | bytes 208904 | tf_op jit(solution)/shard_map/ppermute | solution.py:412
  15.8 1.3 %collective-permute-done.2.got = bf16[128,512]{1,0:T(8,128)(2,1)S(1)} collective-permute-done((bf16[128,512]{1,0:T(8,128)(2,1)S(1)}, bf16[128,512]{1,0:T(8,128)(2,1)S(1)}, u32[]{:S(2)}, u32[]{:S(2)}) %collective-permute-start.2) | collective-permute-done | bytes 131104 | tf_op jit(solution)/shard_map/ppermute | solution.py:416
  17.1 0.7 %shard_map.81 = (bf16[256,512]{1,0:T(8,128)(2,1)S(1)}, bf16[256,512]{1,0:T(8,128)(2,1)S(1)}, bf16[4,256,256]{2,1,0:T(8,128)(2,1)S(1)}, f32[256,512]{1,0:T(8,128)...) custom-call(bf16[128,512]{1,0:T(8,128)(2,1)S(1)} %collective-permute-done.2.got, ...), custom_call_target="tpu_custom_call" | custom-call | flops 134217728 | bytes 2793472 | tf_op jit(solution)/shard_map/pallas_call | solution.py:22
  17.8 0.5 %collective-permute-done.3.refs_8_.refs_0_ = bf16[272,128]{1,0:T(8,128)(2,1)S(1)} collective-permute-done((bf16[272,128]{1,0:T(8,128)(2,1)S(1)}, bf16[272,128]{1,0:T(8,128)(2,1)S(1)}, u32[]{:S(2)}, u32[]{:S(2)}) %collective-permute-start.3) | collective-permute-done | bytes 69664 | tf_op jit(solution)/shard_map/ppermute | solution.py:412
  18.3 0.4 shard_map.82
  18.7 0.9 %collective-permute-done.4.refs_8_.refs_1_ = bf16[272,128]{1,0:T(8,128)(2,1)S(1)} collective-permute-done((bf16[272,128]{1,0:T(8,128)(2,1)S(1)}, bf16[272,128]{1,0:T(8,128)(2,1)S(1)}, u32[]{:S(2)}, u32[]{:S(2)}) %collective-permute-start.4) | collective-permute-done | bytes 69664 | tf_op jit(solution)/shard_map/ppermute | solution.py:412
  19.6 0.4 shard_map.83
  20.0 0.0 collective-permute-done.5.refs_2_
  20.0 0.2 shard_map.84
  20.3 0.0 collective-permute-start.6
  20.3 1.2 %collective-permute-done.6 = f32[2,256]{1,0:T(2,128)S(1)} collective-permute-done((f32[2,256]{1,0:T(2,128)S(1)}, f32[2,256]{1,0:T(2,128)S(1)}, u32[]{:S(2)}, u32[]{:S(2)}) %collective-permute-start.6) | collective-permute-done | bytes 2080 | tf_op jit(solution)/shard_map/ppermute | solution.py:433
  21.5 2.9 %collective-permute-start.8 = (f32[2,256]{1,0:T(2,128)S(1)}, f32[2,256]{1,0:T(2,128)S(1)}, u32[]{:S(2)}, u32[]{:S(2)}) collective-permute-start(f32[2,256]{1,0:T(2,128)S(1)} %add.3.refs_6_), channel_id=1, source_target_pairs={{0,8},{2,6},{4,12},{6,2},{8,0},{10,14},{12,4},{14,10},{16,24},{18,... | collective-permute-start | bytes 6152 | tf_op jit(solution)/shard_map/ppermute | solution.py:441
  24.5 0.9 %collective-permute-start.7 = (f32[2,256]{1,0:T(2,128)S(1)}, f32[2,256]{1,0:T(2,128)S(1)}, u32[]{:S(2)}, u32[]{:S(2)}) collective-permute-start(f32[2,256]{1,0:T(2,128)S(1)} %add.3.refs_6_), channel_id=1, source_target_pairs={{0,12},{2,14},{4,8},{6,10},{8,4},{10,6},{12,0},{14,2},{16,28},{18,... | collective-permute-start | bytes 6152 | tf_op jit(solution)/shard_map/ppermute | solution.py:441
  25.4 0.6 %collective-permute-done.8.refs_8_ = f32[2,256]{1,0:T(2,128)S(1)} collective-permute-done((f32[2,256]{1,0:T(2,128)S(1)}, f32[2,256]{1,0:T(2,128)S(1)}, u32[]{:S(2)}, u32[]{:S(2)}) %collective-permute-start.8) | collective-permute-done | bytes 2080 | tf_op jit(solution)/shard_map/ppermute | solution.py:441
  26.0 0.0 collective-permute-start.9
  26.0 2.9 %collective-permute-done.7.refs_7_ = f32[2,256]{1,0:T(2,128)S(1)} collective-permute-done((f32[2,256]{1,0:T(2,128)S(1)}, f32[2,256]{1,0:T(2,128)S(1)}, u32[]{:S(2)}, u32[]{:S(2)}) %collective-permute-start.7) | collective-permute-done | bytes 2080 | tf_op jit(solution)/shard_map/ppermute | solution.py:441
  28.9 0.0 collective-permute-done.9.refs_9_
  28.9 0.8 %shard_map.85 = (f32[8,256]{1,0:T(8,128)S(1)}, bf16[256,512]{1,0:T(8,128)(2,1)S(1)}, bf16[528,128]{1,0:T(8,128)(2,1)S(1)}) custom-call(f32[256,512]{1,0:T(8,128)S(1)} %get-tuple-element.65.refs_0_.attended, bf16[256,512]{1,0:T(8,128)(2,1)S(1)} %get-tuple-element.56.refs_2_.refs_1_.q2, bf16[256,512]{1,0:T(8,128)(2,1)S(1)} %get-tuple-element.57.refs_3_.refs_2_, ...), custom_call_target="tpu_custom_call" | custom-call | bytes 1757184 | tf_op jit(solution)/shard_map/pallas_call | solution.py:22
  29.7 2.1 %collective-permute-start.11 = (bf16[528,128]{1,0:T(8,128)(2,1)S(1)}, bf16[528,128]{1,0:T(8,128)(2,1)S(1)}, u32[]{:S(2)}, u32[]{:S(2)}) collective-permute-start(bf16[528,128]{1,0:T(8,128)(2,1)S(1)} %get-tuple-element.81), channel_id=1, source_target_pairs={{0,16},{8,24},{16,0},{24,8},{1,17},{9,25},{17,1},{25,9},{2,18},{10... | collective-permute-start | bytes 405512 | tf_op jit(solution)/shard_map/ppermute | solution.py:412
  31.9 1.6 %shard_map.86 = (bf16[128,512]{1,0:T(8,128)(2,1)S(1)}, bf16[128,512]{1,0:T(8,128)(2,1)S(1)}, f32[256,512]{1,0:T(8,128)S(1)}, f32[256,512]{1,0:T(8,128)S(1)}, bf16[256,512]{1,0:T(8,128)(2,1)S(1)}) custom-call(f32[256,512]{1,0:T(8,128)S(1)} %get-tuple-element.65.refs_0_.attended, f32[8,256]{1,0:T(8,128)S(1)} %get-tuple-element.69.scales, ...), custom_call_target="tpu_custom_call" | custom-call | flops 335544320 | bytes 3842048 | tf_op jit(solution)/shard_map/pallas_call | solution.py:22
  33.5 0.3 collective-permute-start.10
  33.8 3.7 %collective-permute-done.11.refs_4_ = bf16[528,128]{1,0:T(8,128)(2,1)S(1)} collective-permute-done((bf16[528,128]{1,0:T(8,128)(2,1)S(1)}, bf16[528,128]{1,0:T(8,128)(2,1)S(1)}, u32[]{:S(2)}, u32[]{:S(2)}) %collective-permute-start.11) | collective-permute-done | bytes 135200 | tf_op jit(solution)/shard_map/ppermute | solution.py:412
  37.5 0.5 %shard_map.88 = (bf16[128,512]{1,0:T(8,128)(2,1)S(1)}, bf16[128,512]{1,0:T(8,128)(2,1)S(1)}) custom-call(f32[256,512]{1,0:T(8,128)S(1)} %get-tuple-element.77.refs_0_, f32[256,512]{1,0:T(8,128)S(1)} %get-tuple-element.78.refs_1_, bf16[256,512]{1,0:T(8,128)(2,1)S(1)} %get-tuple-element.79.refs_2_, bf16[256,512]{1,0:T(8,128)(2,1)S(1)} %get-tuple-element.80.refs_3_, ...), custom_call_target="tpu_custom_call" | custom-call | bytes 2002944 | tf_op jit(solution)/shard_map/pallas_call | solution.py:22
  38.1 1.6 %collective-permute-start.12 = (bf16[128,512]{1,0:T(8,128)(2,1)S(1)}, bf16[128,512]{1,0:T(8,128)(2,1)S(1)}, u32[]{:S(2)}, u32[]{:S(2)}) collective-permute-start(bf16[128,512]{1,0:T(8,128)(2,1)S(1)} %get-tuple-element.82), channel_id=1, source_target_pairs={{0,1},{1,0},{8,9},{9,8},{16,17},{17,16},{24,25},{25,24},{2,3},{3,2... | collective-permute-start | bytes 393224 | tf_op jit(solution)/shard_map/ppermute | solution.py:426
  39.6 0.1 collective-permute-start.13
  39.8 0.0 collective-permute-done.10.refs_1_
  39.8 0.7 %shard_map.87 = bf16[1,128,1024]{2,1,0:T(8,128)(2,1)} custom-call(bf16[128,512]{1,0:T(8,128)(2,1)S(1)} %get-tuple-element.75.refs_0_, bf16[128,512]{1,0:T(8,128)(2,1)S(1)} %collective-permute-done.10.refs_1_), custom_call_target="tpu_custom_call" | custom-call | bytes 524288 | tf_op jit(solution)/shard_map/pallas_call | solution.py:22
  40.5 2.6 %collective-permute-done.12.refs_0_ = bf16[128,512]{1,0:T(8,128)(2,1)S(1)} collective-permute-done((bf16[128,512]{1,0:T(8,128)(2,1)S(1)}, bf16[128,512]{1,0:T(8,128)(2,1)S(1)}, u32[]{:S(2)}, u32[]{:S(2)}) %collective-permute-start.12) | collective-permute-done | bytes 131104 | tf_op jit(solution)/shard_map/ppermute | solution.py:426
  43.1 2.4 %collective-permute-done.13.refs_1_ = bf16[128,512]{1,0:T(8,128)(2,1)S(1)} collective-permute-done((bf16[128,512]{1,0:T(8,128)(2,1)S(1)}, bf16[128,512]{1,0:T(8,128)(2,1)S(1)}, u32[]{:S(2)}, u32[]{:S(2)}) %collective-permute-start.13) | collective-permute-done | bytes 131104 | tf_op jit(solution)/shard_map/ppermute | solution.py:426
  45.5 0.7 %shard_map.89 = bf16[1,128,1024]{2,1,0:T(8,128)(2,1)} custom-call(bf16[128,512]{1,0:T(8,128)(2,1)S(1)} %collective-permute-done.12.refs_0_, bf16[128,512]{1,0:T(8,128)(2,1)S(1)} %collective-permute-done.13.refs_1_), custom_call_target="tpu_custom_call" | custom-call | bytes 524288 | tf_op jit(solution)/shard_map/pallas_call | solution.py:22
  (3 shorter events, 0.0 us)
Async XLA Ops:
  1.6 7.6 %collective-permute-start = (bf16[272,256]{1,0:T(8,128)(2,1)S(1)}, bf16[272,256]{1,0:T(8,128)(2,1)S(1)}, u32[]{:S(2)}, u32[]{:S(2)}) collective-permute-start(bf16[272,256]{1,0:T(8,128)(2,1)S(1)} %get-tuple-element.43), channel_id=1, source_target_pairs={{0,8},{8,0},{16,24},{24,16},{1,9},{9,1},{17,25},{25,17},{2,10},{10... | collective-permute-start | bytes 417800 | tf_op jit(solution)/shard_map/ppermute | solution.py:416
  4.7 8.3 %collective-permute-start.1 = (bf16[256,256]{1,0:T(8,128)(2,1)S(1)}, bf16[256,256]{1,0:T(8,128)(2,1)S(1)}, u32[]{:S(2)}, u32[]{:S(2)}) collective-permute-start(bf16[256,256]{1,0:T(8,128)(2,1)S(1)} %get-tuple-element.50), channel_id=1, source_target_pairs={{0,8},{8,0},{16,24},{24,16},{1,9},{9,1},{17,25},{25,17},{2,10},{10... | collective-permute-start | bytes 393224 | tf_op jit(solution)/shard_map/ppermute | solution.py:416
  4.8 4.4 %copy-start = (f32[1,4,1024]{2,1,0:T(4,128)S(1)}, f32[1,4,1024]{2,1,0:T(4,128)}, u32[]{:S(2)}) copy-start(f32[1,4,1024]{2,1,0:T(4,128)} %refs_6_.1) | copy-start | bytes 49156
  6.1 11.0 %collective-permute-start.2 = (bf16[128,512]{1,0:T(8,128)(2,1)S(1)}, bf16[128,512]{1,0:T(8,128)(2,1)S(1)}, u32[]{:S(2)}, u32[]{:S(2)}) collective-permute-start(bf16[128,512]{1,0:T(8,128)(2,1)S(1)} %get-tuple-element.53), channel_id=1, source_target_pairs={{0,8},{8,0},{16,24},{24,16},{1,9},{9,1},{17,25},{25,17},{2,10},{10... | collective-permute-start | bytes 393224 | tf_op jit(solution)/shard_map/ppermute | solution.py:416
  8.1 12.0 %collective-permute-start.5 = (bf16[128,512]{1,0:T(8,128)(2,1)S(1)}, bf16[128,512]{1,0:T(8,128)(2,1)S(1)}, u32[]{:S(2)}, u32[]{:S(2)}) collective-permute-start(bf16[128,512]{1,0:T(8,128)(2,1)S(1)} %get-tuple-element.66), channel_id=1, source_target_pairs={{0,8},{8,0},{16,24},{24,16},{1,9},{9,1},{17,25},{25,17},{2,10},{10... | collective-permute-start | bytes 393224 | tf_op jit(solution)/shard_map/ppermute | solution.py:416
  9.9 8.4 %collective-permute-start.3 = (bf16[272,128]{1,0:T(8,128)(2,1)S(1)}, bf16[272,128]{1,0:T(8,128)(2,1)S(1)}, u32[]{:S(2)}, u32[]{:S(2)}) collective-permute-start(bf16[272,128]{1,0:T(8,128)(2,1)S(1)} %get-tuple-element.61), channel_id=1, source_target_pairs={{0,16},{8,24},{16,0},{24,8},{1,17},{9,25},{17,1},{25,9},{2,18},{10... | collective-permute-start | bytes 208904 | tf_op jit(solution)/shard_map/ppermute | solution.py:412
  13.6 6.0 %collective-permute-start.4 = (bf16[272,128]{1,0:T(8,128)(2,1)S(1)}, bf16[272,128]{1,0:T(8,128)(2,1)S(1)}, u32[]{:S(2)}, u32[]{:S(2)}) collective-permute-start(bf16[272,128]{1,0:T(8,128)(2,1)S(1)} %get-tuple-element.64), channel_id=1, source_target_pairs={{0,16},{8,24},{16,0},{24,8},{1,17},{9,25},{17,1},{25,9},{2,18},{10... | collective-permute-start | bytes 208904 | tf_op jit(solution)/shard_map/ppermute | solution.py:412
  20.3 1.2 %collective-permute-start.6 = (f32[2,256]{1,0:T(2,128)S(1)}, f32[2,256]{1,0:T(2,128)S(1)}, u32[]{:S(2)}, u32[]{:S(2)}) collective-permute-start(f32[2,256]{1,0:T(2,128)S(1)} %get-tuple-element.68), channel_id=1, source_target_pairs={{0,2},{2,0},{4,6},{6,4},{1,3},{3,1},{5,7},{7,5},{8,10},{10,8},{12,... | collective-permute-start | bytes 6152 | tf_op jit(solution)/shard_map/ppermute | solution.py:433
  21.5 4.5 %collective-permute-start.8 = (f32[2,256]{1,0:T(2,128)S(1)}, f32[2,256]{1,0:T(2,128)S(1)}, u32[]{:S(2)}, u32[]{:S(2)}) collective-permute-start(f32[2,256]{1,0:T(2,128)S(1)} %add.3.refs_6_), channel_id=1, source_target_pairs={{0,8},{2,6},{4,12},{6,2},{8,0},{10,14},{12,4},{14,10},{16,24},{18,... | collective-permute-start | bytes 6152 | tf_op jit(solution)/shard_map/ppermute | solution.py:441
  24.5 4.5 %collective-permute-start.7 = (f32[2,256]{1,0:T(2,128)S(1)}, f32[2,256]{1,0:T(2,128)S(1)}, u32[]{:S(2)}, u32[]{:S(2)}) collective-permute-start(f32[2,256]{1,0:T(2,128)S(1)} %add.3.refs_6_), channel_id=1, source_target_pairs={{0,12},{2,14},{4,8},{6,10},{8,4},{10,6},{12,0},{14,2},{16,28},{18,... | collective-permute-start | bytes 6152 | tf_op jit(solution)/shard_map/ppermute | solution.py:441
  26.0 2.9 %collective-permute-start.9 = (f32[2,256]{1,0:T(2,128)S(1)}, f32[2,256]{1,0:T(2,128)S(1)}, u32[]{:S(2)}, u32[]{:S(2)}) collective-permute-start(f32[2,256]{1,0:T(2,128)S(1)} %collective-permute-done.8.refs_8_), channel_id=1, source_target_pairs={{0,2},{2,0},{4,6},{6,4},{1,3},{3,1},{5,7},{7,5},{8,10},{10,8},{12,... | collective-permute-start | bytes 6152 | tf_op jit(solution)/shard_map/ppermute | solution.py:433
  29.7 7.8 %collective-permute-start.11 = (bf16[528,128]{1,0:T(8,128)(2,1)S(1)}, bf16[528,128]{1,0:T(8,128)(2,1)S(1)}, u32[]{:S(2)}, u32[]{:S(2)}) collective-permute-start(bf16[528,128]{1,0:T(8,128)(2,1)S(1)} %get-tuple-element.81), channel_id=1, source_target_pairs={{0,16},{8,24},{16,0},{24,8},{1,17},{9,25},{17,1},{25,9},{2,18},{10... | collective-permute-start | bytes 405512 | tf_op jit(solution)/shard_map/ppermute | solution.py:412
  33.5 6.3 %collective-permute-start.10 = (bf16[128,512]{1,0:T(8,128)(2,1)S(1)}, bf16[128,512]{1,0:T(8,128)(2,1)S(1)}, u32[]{:S(2)}, u32[]{:S(2)}) collective-permute-start(bf16[128,512]{1,0:T(8,128)(2,1)S(1)} %get-tuple-element.76), channel_id=1, source_target_pairs={{0,8},{8,0},{16,24},{24,16},{1,9},{9,1},{17,25},{25,17},{2,10},{10... | collective-permute-start | bytes 393224 | tf_op jit(solution)/shard_map/ppermute | solution.py:416
  38.1 5.1 %collective-permute-start.12 = (bf16[128,512]{1,0:T(8,128)(2,1)S(1)}, bf16[128,512]{1,0:T(8,128)(2,1)S(1)}, u32[]{:S(2)}, u32[]{:S(2)}) collective-permute-start(bf16[128,512]{1,0:T(8,128)(2,1)S(1)} %get-tuple-element.82), channel_id=1, source_target_pairs={{0,1},{1,0},{8,9},{9,8},{16,17},{17,16},{24,25},{25,24},{2,3},{3,2... | collective-permute-start | bytes 393224 | tf_op jit(solution)/shard_map/ppermute | solution.py:426
  39.6 5.9 %collective-permute-start.13 = (bf16[128,512]{1,0:T(8,128)(2,1)S(1)}, bf16[128,512]{1,0:T(8,128)(2,1)S(1)}, u32[]{:S(2)}, u32[]{:S(2)}) collective-permute-start(bf16[128,512]{1,0:T(8,128)(2,1)S(1)} %get-tuple-element.83), channel_id=1, source_target_pairs={{0,9},{1,8},{8,1},{9,0},{16,25},{17,24},{24,17},{25,16},{2,11},{3,... | collective-permute-start | bytes 393224 | tf_op jit(solution)/shard_map/ppermute | solution.py:426

commit v7 on v6

--- a/solution.py
+++ b/solution.py
@@ -442,8 +442,8 @@
 
     pair = part + neighbour(part)
     ways = [(1, 0)] + [(flip, k) for k in range(2, count, 2) for flip in (0, 1)]
+    parts = [pair, fetched(pair, ways[-1])]
     shared = [fetched(pair, *ways[i : i + 2]) for i in range(0, len(ways) - 1, 2)]
-    parts = [pair, fetched(pair, ways[-1])]
     for block in shared:
         parts += [block, neighbour(block)]
     return parts
@@ -585,7 +585,7 @@
         scratch=[pltpu.VMEM((size, width), BF16)],
         flops=10 * heads * size * size * dim,
     )
-    layer_output = placed([keep], [swapped(send)])
+    out_keep, out_send = keep, send
     kept, got = [], []
     for i in range(PARTS):
         keep, send = call(
@@ -596,7 +596,8 @@
         )
         kept.append(to_earlier_section(keep, 0))
         got.append(to_earlier_section(send, 1))
-    return (layer_output, placed(kept, got))
+    input_next = placed(kept, got)
+    return (placed([out_keep], [swapped(out_send)]), input_next)
 
 
 def solution(mesh):

time: 46.4 us -> 46.4 us (level)
  no operation moved by 1% of the time
where the time goes in v7:
time: 46.4 us; the launch traced here: 46.2 us
  starting transfers between devices  18.6 us (40%)
  waiting for transfers between devices  17.2 us (37%)
  Pallas kernels  9.64 us (21%)
  between operations  0.73 us (2%)
    pallas_call x13, Pallas kernels, call(): pl.pallas_call(kernel, out_shape=outs, in_specs=[pl.BlockSpec(memory_spac...  9.64 us
    ppermute x3, starting transfers between devices, turned(): lax.ppermute(block, axis, [(i, (i + distance) % count) for i in range(cou...  7.43 us
    ppermute x5, starting transfers between devices, swapped(): lax.ppermute(block, 'ctx', [(i, i ^ 1) for i in range(lax.axis_size('ctx'...  5.58 us
    ppermute x3, waiting for transfers between devices, turned(): lax.ppermute(block, axis, [(i, (i + distance) % count) for i in range(cou...  5.07 us
    ppermute x2, waiting for transfers between devices, to_earlier_section(): return lax.ppermute(block, ('ctx', 'pp'), route)  5.01 us
    ppermute x2, starting transfers between devices, fetched(): return lax.ppermute(block, ('ctx', 'tp'), route)  3.86 us
    ppermute x2, waiting for transfers between devices, fetched(): return lax.ppermute(block, ('ctx', 'tp'), route)  3.55 us
    ppermute x5, waiting for transfers between devices, swapped(): lax.ppermute(block, 'ctx', [(i, i ^ 1) for i in range(lax.axis_size('ctx'...  2.39 us
  transfers between devices with their start and end apart: 14, of which 10 were waited for; matrix products, arithmetic and copies ran while one was open for 0% of the time, Pallas kernels for 15%

profile of v7, /device:TPU:0, one launch (start us, length us, event | category | flops | bytes accessed | tf_op | source)
XLA Modules:
  0.0 46.2 jit_solution(11877941206310922365)
XLA Ops:
  0.6 1.0 %shard_map.77 = (bf16[272,256]{1,0:T(8,128)(2,1)S(1)}, bf16[256,256]{1,0:T(8,128)(2,1)S(1)}, f32[8,128]{1,0:T(8,128)S(1)}) custom-call(bf16[1,128,1024]{2,1,0:T(8,128)(2,1)} %k.3, bf16[1,128,1024]{2,1,0:T(8,128)(2,1)} %v.3, f32[1,8,128]{2,1,0:T(8,128)} %bitcast.1), custom_call_target="tpu_custom_call" | custom-call | bytes 802816 | tf_op jit(solution)/shard_map/pallas_call | solution.py:22
  1.6 3.1 %collective-permute-start = (bf16[272,256]{1,0:T(8,128)(2,1)S(1)}, bf16[272,256]{1,0:T(8,128)(2,1)S(1)}, u32[]{:S(2)}, u32[]{:S(2)}) collective-permute-start(bf16[272,256]{1,0:T(8,128)(2,1)S(1)} %get-tuple-element.43), channel_id=1, source_target_pairs={{0,8},{8,0},{16,24},{24,16},{1,9},{9,1},{17,25},{25,17},{2,10},{10... | collective-permute-start | bytes 417800 | tf_op jit(solution)/shard_map/ppermute | solution.py:416
  4.7 0.1 collective-permute-start.1
  4.8 0.0 copy-start
  4.8 1.3 %shard_map.78 = (bf16[128,512]{1,0:T(8,128)(2,1)S(1)}, bf16[128,512]{1,0:T(8,128)(2,1)S(1)}, bf16[512,512]{1,0:T(8,128)(2,1)S(1)}) custom-call(bf16[1,128,1024]{2,1,0:T(8,128)(2,1)} %q.1, bf16[1,128,1024]{2,1,0:T(8,128)(2,1)} %k.3, bf16[1,128,1024]{2,1,0:T(8,128)(2,1)} %v.3, bf16[1,128,1024]{2,1,0:T(8,128)(2,1)} %g.1, bf16[16,256]{1,0:T(8,128)(2,1)S(1)} %slice.3._), custom_call_target="tpu_custom_call" | custom-call | bytes 1843200 | tf_op jit(solution)/shard_map/pallas_call | solution.py:22
  6.1 2.0 %collective-permute-start.2 = (bf16[128,512]{1,0:T(8,128)(2,1)S(1)}, bf16[128,512]{1,0:T(8,128)(2,1)S(1)}, u32[]{:S(2)}, u32[]{:S(2)}) collective-permute-start(bf16[128,512]{1,0:T(8,128)(2,1)S(1)} %get-tuple-element.53), channel_id=1, source_target_pairs={{0,8},{8,0},{16,24},{24,16},{1,9},{9,1},{17,25},{25,17},{2,10},{10... | collective-permute-start | bytes 393224 | tf_op jit(solution)/shard_map/ppermute | solution.py:416
  8.1 0.1 collective-permute-start.5
  8.2 1.1 %collective-permute-done.got = bf16[272,256]{1,0:T(8,128)(2,1)S(1)} collective-permute-done((bf16[272,256]{1,0:T(8,128)(2,1)S(1)}, bf16[272,256]{1,0:T(8,128)(2,1)S(1)}, u32[]{:S(2)}, u32[]{:S(2)}) %collective-permute-start) | collective-permute-done | bytes 139296 | tf_op jit(solution)/shard_map/ppermute | solution.py:416
  9.2 0.0 copy-done
  9.2 0.6 %shard_map.79 = (bf16[256,512]{1,0:T(8,128)(2,1)S(1)}, bf16[256,512]{1,0:T(8,128)(2,1)S(1)}, f32[16,512]{1,0:T(8,128)S(1)}, bf16[256,512]{1,0:T(8,128)(2,1)S(1)}...) custom-call(bf16[272,256]{1,0:T(8,128)(2,1)S(1)} %collective-permute-done.got, ...), custom_call_target="tpu_custom_call" | custom-call | bytes 1581056 | tf_op jit(solution)/shard_map/pallas_call | solution.py:22
  9.9 3.1 %collective-permute-start.3 = (bf16[272,128]{1,0:T(8,128)(2,1)S(1)}, bf16[272,128]{1,0:T(8,128)(2,1)S(1)}, u32[]{:S(2)}, u32[]{:S(2)}) collective-permute-start(bf16[272,128]{1,0:T(8,128)(2,1)S(1)} %get-tuple-element.61), channel_id=1, source_target_pairs={{0,16},{8,24},{16,0},{24,8},{1,17},{9,25},{17,1},{25,9},{2,18},{10... | collective-permute-start | bytes 208904 | tf_op jit(solution)/shard_map/ppermute | solution.py:412
  13.0 0.0 collective-permute-done.1.refs_4_
  13.0 0.6 %shard_map.80 = (bf16[256,512]{1,0:T(8,128)(2,1)S(1)}, bf16[256,512]{1,0:T(8,128)(2,1)S(1)}, f32[16,512]{1,0:T(8,128)S(1)}, bf16[256,512]{1,0:T(8,128)(2,1)S(1)}, bf16[272,128]{1,0:T(8,128)(2,1)S(1)}) custom-call(bf16[256,512]{1,0:T(8,128)(2,1)S(1)} %get-tuple-element.46.refs_0_, ...), custom_call_target="tpu_custom_call", output_to_operand_aliasing={{0}: (0, {}), {1}: (1, {}), {2}: (2, {}), {3}: (3, {})} | custom-call | bytes 2387968 | tf_op jit(solution)/shard_map/pallas_call | solution.py:22
  13.6 2.1 %collective-permute-start.4 = (bf16[272,128]{1,0:T(8,128)(2,1)S(1)}, bf16[272,128]{1,0:T(8,128)(2,1)S(1)}, u32[]{:S(2)}, u32[]{:S(2)}) collective-permute-start(bf16[272,128]{1,0:T(8,128)(2,1)S(1)} %get-tuple-element.64), channel_id=1, source_target_pairs={{0,16},{8,24},{16,0},{24,8},{1,17},{9,25},{17,1},{25,9},{2,18},{10... | collective-permute-start | bytes 208904 | tf_op jit(solution)/shard_map/ppermute | solution.py:412
  15.8 1.3 %collective-permute-done.2.got = bf16[128,512]{1,0:T(8,128)(2,1)S(1)} collective-permute-done((bf16[128,512]{1,0:T(8,128)(2,1)S(1)}, bf16[128,512]{1,0:T(8,128)(2,1)S(1)}, u32[]{:S(2)}, u32[]{:S(2)}) %collective-permute-start.2) | collective-permute-done | bytes 131104 | tf_op jit(solution)/shard_map/ppermute | solution.py:416
  17.1 0.7 %shard_map.81 = (bf16[256,512]{1,0:T(8,128)(2,1)S(1)}, bf16[256,512]{1,0:T(8,128)(2,1)S(1)}, bf16[4,256,256]{2,1,0:T(8,128)(2,1)S(1)}, f32[256,512]{1,0:T(8,128)...) custom-call(bf16[128,512]{1,0:T(8,128)(2,1)S(1)} %collective-permute-done.2.got, ...), custom_call_target="tpu_custom_call" | custom-call | flops 134217728 | bytes 2793472 | tf_op jit(solution)/shard_map/pallas_call | solution.py:22
  17.8 0.5 %collective-permute-done.3.refs_8_.refs_0_ = bf16[272,128]{1,0:T(8,128)(2,1)S(1)} collective-permute-done((bf16[272,128]{1,0:T(8,128)(2,1)S(1)}, bf16[272,128]{1,0:T(8,128)(2,1)S(1)}, u32[]{:S(2)}, u32[]{:S(2)}) %collective-permute-start.3) | collective-permute-done | bytes 69664 | tf_op jit(solution)/shard_map/ppermute | solution.py:412
  18.3 0.4 shard_map.82
  18.7 0.9 %collective-permute-done.4.refs_8_.refs_1_ = bf16[272,128]{1,0:T(8,128)(2,1)S(1)} collective-permute-done((bf16[272,128]{1,0:T(8,128)(2,1)S(1)}, bf16[272,128]{1,0:T(8,128)(2,1)S(1)}, u32[]{:S(2)}, u32[]{:S(2)}) %collective-permute-start.4) | collective-permute-done | bytes 69664 | tf_op jit(solution)/shard_map/ppermute | solution.py:412
  19.6 0.4 shard_map.83
  20.0 0.0 collective-permute-done.5.refs_2_
  20.0 0.2 shard_map.84
  20.3 0.0 collective-permute-start.6
  20.3 1.2 %collective-permute-done.6 = f32[2,256]{1,0:T(2,128)S(1)} collective-permute-done((f32[2,256]{1,0:T(2,128)S(1)}, f32[2,256]{1,0:T(2,128)S(1)}, u32[]{:S(2)}, u32[]{:S(2)}) %collective-permute-start.6) | collective-permute-done | bytes 2080 | tf_op jit(solution)/shard_map/ppermute | solution.py:433
  21.5 2.9 %collective-permute-start.8 = (f32[2,256]{1,0:T(2,128)S(1)}, f32[2,256]{1,0:T(2,128)S(1)}, u32[]{:S(2)}, u32[]{:S(2)}) collective-permute-start(f32[2,256]{1,0:T(2,128)S(1)} %add.3.refs_6_), channel_id=1, source_target_pairs={{0,8},{2,6},{4,12},{6,2},{8,0},{10,14},{12,4},{14,10},{16,24},{18,... | collective-permute-start | bytes 6152 | tf_op jit(solution)/shard_map/ppermute | solution.py:441
  24.5 0.9 %collective-permute-start.7 = (f32[2,256]{1,0:T(2,128)S(1)}, f32[2,256]{1,0:T(2,128)S(1)}, u32[]{:S(2)}, u32[]{:S(2)}) collective-permute-start(f32[2,256]{1,0:T(2,128)S(1)} %add.3.refs_6_), channel_id=1, source_target_pairs={{0,12},{2,14},{4,8},{6,10},{8,4},{10,6},{12,0},{14,2},{16,28},{18,... | collective-permute-start | bytes 6152 | tf_op jit(solution)/shard_map/ppermute | solution.py:441
  25.4 0.6 %collective-permute-done.8.refs_8_ = f32[2,256]{1,0:T(2,128)S(1)} collective-permute-done((f32[2,256]{1,0:T(2,128)S(1)}, f32[2,256]{1,0:T(2,128)S(1)}, u32[]{:S(2)}, u32[]{:S(2)}) %collective-permute-start.8) | collective-permute-done | bytes 2080 | tf_op jit(solution)/shard_map/ppermute | solution.py:441
  26.0 0.0 collective-permute-start.9
  26.0 2.9 %collective-permute-done.7.refs_7_ = f32[2,256]{1,0:T(2,128)S(1)} collective-permute-done((f32[2,256]{1,0:T(2,128)S(1)}, f32[2,256]{1,0:T(2,128)S(1)}, u32[]{:S(2)}, u32[]{:S(2)}) %collective-permute-start.7) | collective-permute-done | bytes 2080 | tf_op jit(solution)/shard_map/ppermute | solution.py:441
  28.9 0.0 collective-permute-done.9.refs_9_
  28.9 0.8 %shard_map.85 = (f32[8,256]{1,0:T(8,128)S(1)}, bf16[256,512]{1,0:T(8,128)(2,1)S(1)}, bf16[528,128]{1,0:T(8,128)(2,1)S(1)}) custom-call(f32[256,512]{1,0:T(8,128)S(1)} %get-tuple-element.65.refs_0_.attended, bf16[256,512]{1,0:T(8,128)(2,1)S(1)} %get-tuple-element.56.refs_2_.refs_1_.q2, bf16[256,512]{1,0:T(8,128)(2,1)S(1)} %get-tuple-element.57.refs_3_.refs_2_, ...), custom_call_target="tpu_custom_call" | custom-call | bytes 1757184 | tf_op jit(solution)/shard_map/pallas_call | solution.py:22
  29.7 2.1 %collective-permute-start.11 = (bf16[528,128]{1,0:T(8,128)(2,1)S(1)}, bf16[528,128]{1,0:T(8,128)(2,1)S(1)}, u32[]{:S(2)}, u32[]{:S(2)}) collective-permute-start(bf16[528,128]{1,0:T(8,128)(2,1)S(1)} %get-tuple-element.81), channel_id=1, source_target_pairs={{0,16},{8,24},{16,0},{24,8},{1,17},{9,25},{17,1},{25,9},{2,18},{10... | collective-permute-start | bytes 405512 | tf_op jit(solution)/shard_map/ppermute | solution.py:412
  31.9 1.6 %shard_map.86 = (bf16[128,512]{1,0:T(8,128)(2,1)S(1)}, bf16[128,512]{1,0:T(8,128)(2,1)S(1)}, f32[256,512]{1,0:T(8,128)S(1)}, f32[256,512]{1,0:T(8,128)S(1)}, bf16[256,512]{1,0:T(8,128)(2,1)S(1)}) custom-call(f32[256,512]{1,0:T(8,128)S(1)} %get-tuple-element.65.refs_0_.attended, f32[8,256]{1,0:T(8,128)S(1)} %get-tuple-element.69.scales, ...), custom_call_target="tpu_custom_call" | custom-call | flops 335544320 | bytes 3842048 | tf_op jit(solution)/shard_map/pallas_call | solution.py:22
  33.5 0.3 collective-permute-start.10
  33.8 3.7 %collective-permute-done.11.refs_4_ = bf16[528,128]{1,0:T(8,128)(2,1)S(1)} collective-permute-done((bf16[528,128]{1,0:T(8,128)(2,1)S(1)}, bf16[528,128]{1,0:T(8,128)(2,1)S(1)}, u32[]{:S(2)}, u32[]{:S(2)}) %collective-permute-start.11) | collective-permute-done | bytes 135200 | tf_op jit(solution)/shard_map/ppermute | solution.py:412
  37.5 0.5 %shard_map.88 = (bf16[128,512]{1,0:T(8,128)(2,1)S(1)}, bf16[128,512]{1,0:T(8,128)(2,1)S(1)}) custom-call(f32[256,512]{1,0:T(8,128)S(1)} %get-tuple-element.77.refs_0_, f32[256,512]{1,0:T(8,128)S(1)} %get-tuple-element.78.refs_1_, bf16[256,512]{1,0:T(8,128)(2,1)S(1)} %get-tuple-element.79.refs_2_, bf16[256,512]{1,0:T(8,128)(2,1)S(1)} %get-tuple-element.80.refs_3_, ...), custom_call_target="tpu_custom_call" | custom-call | bytes 2002944 | tf_op jit(solution)/shard_map/pallas_call | solution.py:22
  38.1 1.6 %collective-permute-start.12 = (bf16[128,512]{1,0:T(8,128)(2,1)S(1)}, bf16[128,512]{1,0:T(8,128)(2,1)S(1)}, u32[]{:S(2)}, u32[]{:S(2)}) collective-permute-start(bf16[128,512]{1,0:T(8,128)(2,1)S(1)} %get-tuple-element.82), channel_id=1, source_target_pairs={{0,1},{1,0},{8,9},{9,8},{16,17},{17,16},{24,25},{25,24},{2,3},{3,2... | collective-permute-start | bytes 393224 | tf_op jit(solution)/shard_map/ppermute | solution.py:426
  39.6 0.1 collective-permute-start.13
  39.8 0.0 collective-permute-done.10.refs_1_
  39.8 0.7 %shard_map.87 = bf16[1,128,1024]{2,1,0:T(8,128)(2,1)} custom-call(bf16[128,512]{1,0:T(8,128)(2,1)S(1)} %get-tuple-element.75.refs_0_, bf16[128,512]{1,0:T(8,128)(2,1)S(1)} %collective-permute-done.10.refs_1_), custom_call_target="tpu_custom_call" | custom-call | bytes 524288 | tf_op jit(solution)/shard_map/pallas_call | solution.py:22
  40.5 2.6 %collective-permute-done.12.refs_0_ = bf16[128,512]{1,0:T(8,128)(2,1)S(1)} collective-permute-done((bf16[128,512]{1,0:T(8,128)(2,1)S(1)}, bf16[128,512]{1,0:T(8,128)(2,1)S(1)}, u32[]{:S(2)}, u32[]{:S(2)}) %collective-permute-start.12) | collective-permute-done | bytes 131104 | tf_op jit(solution)/shard_map/ppermute | solution.py:426
  43.1 2.4 %collective-permute-done.13.refs_1_ = bf16[128,512]{1,0:T(8,128)(2,1)S(1)} collective-permute-done((bf16[128,512]{1,0:T(8,128)(2,1)S(1)}, bf16[128,512]{1,0:T(8,128)(2,1)S(1)}, u32[]{:S(2)}, u32[]{:S(2)}) %collective-permute-start.13) | collective-permute-done | bytes 131104 | tf_op jit(solution)/shard_map/ppermute | solution.py:426
  45.5 0.7 %shard_map.89 = bf16[1,128,1024]{2,1,0:T(8,128)(2,1)} custom-call(bf16[128,512]{1,0:T(8,128)(2,1)S(1)} %collective-permute-done.12.refs_0_, bf16[128,512]{1,0:T(8,128)(2,1)S(1)} %collective-permute-done.13.refs_1_), custom_call_target="tpu_custom_call" | custom-call | bytes 524288 | tf_op jit(solution)/shard_map/pallas_call | solution.py:22
  (3 shorter events, 0.0 us)
Async XLA Ops:
  1.6 7.6 %collective-permute-start = (bf16[272,256]{1,0:T(8,128)(2,1)S(1)}, bf16[272,256]{1,0:T(8,128)(2,1)S(1)}, u32[]{:S(2)}, u32[]{:S(2)}) collective-permute-start(bf16[272,256]{1,0:T(8,128)(2,1)S(1)} %get-tuple-element.43), channel_id=1, source_target_pairs={{0,8},{8,0},{16,24},{24,16},{1,9},{9,1},{17,25},{25,17},{2,10},{10... | collective-permute-start | bytes 417800 | tf_op jit(solution)/shard_map/ppermute | solution.py:416
  4.7 8.3 %collective-permute-start.1 = (bf16[256,256]{1,0:T(8,128)(2,1)S(1)}, bf16[256,256]{1,0:T(8,128)(2,1)S(1)}, u32[]{:S(2)}, u32[]{:S(2)}) collective-permute-start(bf16[256,256]{1,0:T(8,128)(2,1)S(1)} %get-tuple-element.50), channel_id=1, source_target_pairs={{0,8},{8,0},{16,24},{24,16},{1,9},{9,1},{17,25},{25,17},{2,10},{10... | collective-permute-start | bytes 393224 | tf_op jit(solution)/shard_map/ppermute | solution.py:416
  4.8 4.4 %copy-start = (f32[1,4,1024]{2,1,0:T(4,128)S(1)}, f32[1,4,1024]{2,1,0:T(4,128)}, u32[]{:S(2)}) copy-start(f32[1,4,1024]{2,1,0:T(4,128)} %refs_6_.1) | copy-start | bytes 49156
  6.1 11.0 %collective-permute-start.2 = (bf16[128,512]{1,0:T(8,128)(2,1)S(1)}, bf16[128,512]{1,0:T(8,128)(2,1)S(1)}, u32[]{:S(2)}, u32[]{:S(2)}) collective-permute-start(bf16[128,512]{1,0:T(8,128)(2,1)S(1)} %get-tuple-element.53), channel_id=1, source_target_pairs={{0,8},{8,0},{16,24},{24,16},{1,9},{9,1},{17,25},{25,17},{2,10},{10... | collective-permute-start | bytes 393224 | tf_op jit(solution)/shard_map/ppermute | solution.py:416
  8.1 12.0 %collective-permute-start.5 = (bf16[128,512]{1,0:T(8,128)(2,1)S(1)}, bf16[128,512]{1,0:T(8,128)(2,1)S(1)}, u32[]{:S(2)}, u32[]{:S(2)}) collective-permute-start(bf16[128,512]{1,0:T(8,128)(2,1)S(1)} %get-tuple-element.66), channel_id=1, source_target_pairs={{0,8},{8,0},{16,24},{24,16},{1,9},{9,1},{17,25},{25,17},{2,10},{10... | collective-permute-start | bytes 393224 | tf_op jit(solution)/shard_map/ppermute | solution.py:416
  9.9 8.4 %collective-permute-start.3 = (bf16[272,128]{1,0:T(8,128)(2,1)S(1)}, bf16[272,128]{1,0:T(8,128)(2,1)S(1)}, u32[]{:S(2)}, u32[]{:S(2)}) collective-permute-start(bf16[272,128]{1,0:T(8,128)(2,1)S(1)} %get-tuple-element.61), channel_id=1, source_target_pairs={{0,16},{8,24},{16,0},{24,8},{1,17},{9,25},{17,1},{25,9},{2,18},{10... | collective-permute-start | bytes 208904 | tf_op jit(solution)/shard_map/ppermute | solution.py:412
  13.6 6.0 %collective-permute-start.4 = (bf16[272,128]{1,0:T(8,128)(2,1)S(1)}, bf16[272,128]{1,0:T(8,128)(2,1)S(1)}, u32[]{:S(2)}, u32[]{:S(2)}) collective-permute-start(bf16[272,128]{1,0:T(8,128)(2,1)S(1)} %get-tuple-element.64), channel_id=1, source_target_pairs={{0,16},{8,24},{16,0},{24,8},{1,17},{9,25},{17,1},{25,9},{2,18},{10... | collective-permute-start | bytes 208904 | tf_op jit(solution)/shard_map/ppermute | solution.py:412
  20.3 1.2 %collective-permute-start.6 = (f32[2,256]{1,0:T(2,128)S(1)}, f32[2,256]{1,0:T(2,128)S(1)}, u32[]{:S(2)}, u32[]{:S(2)}) collective-permute-start(f32[2,256]{1,0:T(2,128)S(1)} %get-tuple-element.68), channel_id=1, source_target_pairs={{0,2},{2,0},{4,6},{6,4},{1,3},{3,1},{5,7},{7,5},{8,10},{10,8},{12,... | collective-permute-start | bytes 6152 | tf_op jit(solution)/shard_map/ppermute | solution.py:433
  21.5 4.5 %collective-permute-start.8 = (f32[2,256]{1,0:T(2,128)S(1)}, f32[2,256]{1,0:T(2,128)S(1)}, u32[]{:S(2)}, u32[]{:S(2)}) collective-permute-start(f32[2,256]{1,0:T(2,128)S(1)} %add.3.refs_6_), channel_id=1, source_target_pairs={{0,8},{2,6},{4,12},{6,2},{8,0},{10,14},{12,4},{14,10},{16,24},{18,... | collective-permute-start | bytes 6152 | tf_op jit(solution)/shard_map/ppermute | solution.py:441
  24.5 4.5 %collective-permute-start.7 = (f32[2,256]{1,0:T(2,128)S(1)}, f32[2,256]{1,0:T(2,128)S(1)}, u32[]{:S(2)}, u32[]{:S(2)}) collective-permute-start(f32[2,256]{1,0:T(2,128)S(1)} %add.3.refs_6_), channel_id=1, source_target_pairs={{0,12},{2,14},{4,8},{6,10},{8,4},{10,6},{12,0},{14,2},{16,28},{18,... | collective-permute-start | bytes 6152 | tf_op jit(solution)/shard_map/ppermute | solution.py:441
  26.0 2.9 %collective-permute-start.9 = (f32[2,256]{1,0:T(2,128)S(1)}, f32[2,256]{1,0:T(2,128)S(1)}, u32[]{:S(2)}, u32[]{:S(2)}) collective-permute-start(f32[2,256]{1,0:T(2,128)S(1)} %collective-permute-done.8.refs_8_), channel_id=1, source_target_pairs={{0,2},{2,0},{4,6},{6,4},{1,3},{3,1},{5,7},{7,5},{8,10},{10,8},{12,... | collective-permute-start | bytes 6152 | tf_op jit(solution)/shard_map/ppermute | solution.py:433
  29.7 7.8 %collective-permute-start.11 = (bf16[528,128]{1,0:T(8,128)(2,1)S(1)}, bf16[528,128]{1,0:T(8,128)(2,1)S(1)}, u32[]{:S(2)}, u32[]{:S(2)}) collective-permute-start(bf16[528,128]{1,0:T(8,128)(2,1)S(1)} %get-tuple-element.81), channel_id=1, source_target_pairs={{0,16},{8,24},{16,0},{24,8},{1,17},{9,25},{17,1},{25,9},{2,18},{10... | collective-permute-start | bytes 405512 | tf_op jit(solution)/shard_map/ppermute | solution.py:412
  33.5 6.3 %collective-permute-start.10 = (bf16[128,512]{1,0:T(8,128)(2,1)S(1)}, bf16[128,512]{1,0:T(8,128)(2,1)S(1)}, u32[]{:S(2)}, u32[]{:S(2)}) collective-permute-start(bf16[128,512]{1,0:T(8,128)(2,1)S(1)} %get-tuple-element.76), channel_id=1, source_target_pairs={{0,8},{8,0},{16,24},{24,16},{1,9},{9,1},{17,25},{25,17},{2,10},{10... | collective-permute-start | bytes 393224 | tf_op jit(solution)/shard_map/ppermute | solution.py:416
  38.1 5.1 %collective-permute-start.12 = (bf16[128,512]{1,0:T(8,128)(2,1)S(1)}, bf16[128,512]{1,0:T(8,128)(2,1)S(1)}, u32[]{:S(2)}, u32[]{:S(2)}) collective-permute-start(bf16[128,512]{1,0:T(8,128)(2,1)S(1)} %get-tuple-element.82), channel_id=1, source_target_pairs={{0,1},{1,0},{8,9},{9,8},{16,17},{17,16},{24,25},{25,24},{2,3},{3,2... | collective-permute-start | bytes 393224 | tf_op jit(solution)/shard_map/ppermute | solution.py:426
  39.6 5.9 %collective-permute-start.13 = (bf16[128,512]{1,0:T(8,128)(2,1)S(1)}, bf16[128,512]{1,0:T(8,128)(2,1)S(1)}, u32[]{:S(2)}, u32[]{:S(2)}) collective-permute-start(bf16[128,512]{1,0:T(8,128)(2,1)S(1)} %get-tuple-element.83), channel_id=1, source_target_pairs={{0,9},{1,8},{8,1},{9,0},{16,25},{17,24},{24,17},{25,16},{2,11},{3,... | collective-permute-start | bytes 393224 | tf_op jit(solution)/shard_map/ppermute | solution.py:426

commit v8 on v6

--- a/solution.py
+++ b/solution.py
@@ -381,30 +381,35 @@
     send[...] = unless(first, done[there, :]).astype(BF16)
 
 
-def place_kernel(*refs):
-    *pieces, out, sems = refs
-    kept, got = pieces[: len(pieces) // 2], pieces[len(pieces) // 2 :]
-    width = kept[0].shape[1]
+def place_kernel(count, *refs):
+    pieces, outs, sems = refs[: -1 - count], refs[-1 - count : -1], refs[-1]
+    each = len(pieces) // count
     mine = lax.rem(lax.axis_index("ctx"), PAIR)
     pairs = []
-    for half, parts in ((mine, kept), (1 - mine, got)):
-        for i, part in enumerate(parts):
-            start = pl.multiple_of((half * len(parts) + i) * width, width)
+    for i, out in enumerate(outs):
+        parts = pieces[i * each : (i + 1) * each]
+        width = parts[0].shape[1]
+        for j, part in enumerate(parts):
+            half = mine if j < each // 2 else 1 - mine
+            start = pl.multiple_of((half * (each // 2) + j % (each // 2)) * width, width)
             pairs.append((part, out.at[0, :, pl.ds(start, width)]))
     for copy in copy_all(pairs, sems):
         copy.wait()
 
 
-def placed(kept, got):
-    pieces = kept + got
-    rows = kept[0].shape[0]
+def placed(*results):
+    pieces = [piece for kept, got in results for piece in kept + got]
+    rows = pieces[0].shape[0]
     return call(
-        place_kernel,
-        [shape((1, rows, sum(piece.shape[1] for piece in pieces)), BF16)],
+        lambda *refs: place_kernel(len(results), *refs),
+        [
+            shape((1, rows, sum(piece.shape[1] for piece in kept + got)), BF16)
+            for kept, got in results
+        ],
         *pieces,
         scratch=[pltpu.SemaphoreType.DMA((len(pieces),))],
         out_hbm=True,
-    )[0]
+    )
 
 
 def turned(block, axis, distance):
@@ -585,7 +590,7 @@
         scratch=[pltpu.VMEM((size, width), BF16)],
         flops=10 * heads * size * size * dim,
     )
-    layer_output = placed([keep], [swapped(send)])
+    out_keep, out_got = keep, swapped(send)
     kept, got = [], []
     for i in range(PARTS):
         keep, send = call(
@@ -596,7 +601,7 @@
         )
         kept.append(to_earlier_section(keep, 0))
         got.append(to_earlier_section(send, 1))
-    return (layer_output, placed(kept, got))
+    return tuple(placed(([out_keep], [out_got]), (kept, got)))
 
 
 def solution(mesh):

time: 46.4 us -> 46.5 us (level)
  waiting for transfers between devices: 17.2 us -> 17.9 us
  Pallas kernels: 9.64 us -> 9.03 us
    ppermute x2, waiting for transfers between devices: 5.01 us -> 5.73 us  [to_earlier_section(): return lax.ppermute(block, ('ctx', 'pp'), route)]
    pallas_call x13 -> x12, Pallas kernels: 9.64 us -> 9.03 us  [call(): pl.pallas_call(kernel, out_shape=outs, in_specs=[pl.BlockSpec(memory_spac...]
  transfers between devices with their start and end apart: 14 -> 14, of which waited for: 10 -> 10; matrix products, arithmetic and copies ran while one was open for 0% -> 0% of each run, Pallas kernels for 15% -> 13%
where the time goes in v8:
time: 46.5 us; the launch traced here: 46.3 us
  starting transfers between devices  18.6 us (40%)
  waiting for transfers between devices  17.9 us (38%)
  Pallas kernels  9.03 us (19%)
  between operations  0.73 us (2%)
    pallas_call x12, Pallas kernels, call(): pl.pallas_call(kernel, out_shape=outs, in_specs=[pl.BlockSpec(memory_spac...  9.03 us
    ppermute x3, starting transfers between devices, turned(): lax.ppermute(block, axis, [(i, (i + distance) % count) for i in range(cou...  7.43 us
    ppermute x2, waiting for transfers between devices, to_earlier_section(): return lax.ppermute(block, ('ctx', 'pp'), route)  5.73 us
    ppermute x5, starting transfers between devices, swapped(): lax.ppermute(block, 'ctx', [(i, i ^ 1) for i in range(lax.axis_size('ctx'...  5.58 us
    ppermute x3, waiting for transfers between devices, turned(): lax.ppermute(block, axis, [(i, (i + distance) % count) for i in range(cou...  5.07 us
    ppermute x2, starting transfers between devices, fetched(): return lax.ppermute(block, ('ctx', 'tp'), route)  3.86 us
    ppermute x2, waiting for transfers between devices, fetched(): return lax.ppermute(block, ('ctx', 'tp'), route)  3.55 us
    ppermute x5, waiting for transfers between devices, swapped(): lax.ppermute(block, 'ctx', [(i, i ^ 1) for i in range(lax.axis_size('ctx'...  2.39 us
  transfers between devices with their start and end apart: 14, of which 10 were waited for; matrix products, arithmetic and copies ran while one was open for 0% of the time, Pallas kernels for 13%

profile of v8, /device:TPU:0, one launch (start us, length us, event | category | flops | bytes accessed | tf_op | source)
XLA Modules:
  0.0 46.3 jit_solution(6677766649021608123)
XLA Ops:
  0.6 1.0 %shard_map.77 = (bf16[272,256]{1,0:T(8,128)(2,1)S(1)}, bf16[256,256]{1,0:T(8,128)(2,1)S(1)}, f32[8,128]{1,0:T(8,128)S(1)}) custom-call(bf16[1,128,1024]{2,1,0:T(8,128)(2,1)} %k.3, bf16[1,128,1024]{2,1,0:T(8,128)(2,1)} %v.3, f32[1,8,128]{2,1,0:T(8,128)} %bitcast.1), custom_call_target="tpu_custom_call" | custom-call | bytes 802816 | tf_op jit(solution)/shard_map/pallas_call | solution.py:22
  1.6 3.1 %collective-permute-start = (bf16[272,256]{1,0:T(8,128)(2,1)S(1)}, bf16[272,256]{1,0:T(8,128)(2,1)S(1)}, u32[]{:S(2)}, u32[]{:S(2)}) collective-permute-start(bf16[272,256]{1,0:T(8,128)(2,1)S(1)} %get-tuple-element.43), channel_id=1, source_target_pairs={{0,8},{8,0},{16,24},{24,16},{1,9},{9,1},{17,25},{25,17},{2,10},{10... | collective-permute-start | bytes 417800 | tf_op jit(solution)/shard_map/ppermute | solution.py:421
  4.7 0.1 collective-permute-start.1
  4.8 0.0 copy-start
  4.8 1.3 %shard_map.78 = (bf16[128,512]{1,0:T(8,128)(2,1)S(1)}, bf16[128,512]{1,0:T(8,128)(2,1)S(1)}, bf16[512,512]{1,0:T(8,128)(2,1)S(1)}) custom-call(bf16[1,128,1024]{2,1,0:T(8,128)(2,1)} %q.1, bf16[1,128,1024]{2,1,0:T(8,128)(2,1)} %k.3, bf16[1,128,1024]{2,1,0:T(8,128)(2,1)} %v.3, bf16[1,128,1024]{2,1,0:T(8,128)(2,1)} %g.1, bf16[16,256]{1,0:T(8,128)(2,1)S(1)} %slice.3._), custom_call_target="tpu_custom_call" | custom-call | bytes 1843200 | tf_op jit(solution)/shard_map/pallas_call | solution.py:22
  6.1 2.0 %collective-permute-start.2 = (bf16[128,512]{1,0:T(8,128)(2,1)S(1)}, bf16[128,512]{1,0:T(8,128)(2,1)S(1)}, u32[]{:S(2)}, u32[]{:S(2)}) collective-permute-start(bf16[128,512]{1,0:T(8,128)(2,1)S(1)} %get-tuple-element.53), channel_id=1, source_target_pairs={{0,8},{8,0},{16,24},{24,16},{1,9},{9,1},{17,25},{25,17},{2,10},{10... | collective-permute-start | bytes 393224 | tf_op jit(solution)/shard_map/ppermute | solution.py:421
  8.1 0.1 collective-permute-start.5
  8.2 1.1 %collective-permute-done.got = bf16[272,256]{1,0:T(8,128)(2,1)S(1)} collective-permute-done((bf16[272,256]{1,0:T(8,128)(2,1)S(1)}, bf16[272,256]{1,0:T(8,128)(2,1)S(1)}, u32[]{:S(2)}, u32[]{:S(2)}) %collective-permute-start) | collective-permute-done | bytes 139296 | tf_op jit(solution)/shard_map/ppermute | solution.py:421
  9.2 0.0 copy-done
  9.2 0.6 %shard_map.79 = (bf16[256,512]{1,0:T(8,128)(2,1)S(1)}, bf16[256,512]{1,0:T(8,128)(2,1)S(1)}, f32[16,512]{1,0:T(8,128)S(1)}, bf16[256,512]{1,0:T(8,128)(2,1)S(1)}...) custom-call(bf16[272,256]{1,0:T(8,128)(2,1)S(1)} %collective-permute-done.got, ...), custom_call_target="tpu_custom_call" | custom-call | bytes 1581056 | tf_op jit(solution)/shard_map/pallas_call | solution.py:22
  9.9 3.1 %collective-permute-start.3 = (bf16[272,128]{1,0:T(8,128)(2,1)S(1)}, bf16[272,128]{1,0:T(8,128)(2,1)S(1)}, u32[]{:S(2)}, u32[]{:S(2)}) collective-permute-start(bf16[272,128]{1,0:T(8,128)(2,1)S(1)} %get-tuple-element.61), channel_id=1, source_target_pairs={{0,16},{8,24},{16,0},{24,8},{1,17},{9,25},{17,1},{25,9},{2,18},{10... | collective-permute-start | bytes 208904 | tf_op jit(solution)/shard_map/ppermute | solution.py:417
  13.0 0.0 collective-permute-done.1.refs_4_
  13.0 0.6 %shard_map.80 = (bf16[256,512]{1,0:T(8,128)(2,1)S(1)}, bf16[256,512]{1,0:T(8,128)(2,1)S(1)}, f32[16,512]{1,0:T(8,128)S(1)}, bf16[256,512]{1,0:T(8,128)(2,1)S(1)}, bf16[272,128]{1,0:T(8,128)(2,1)S(1)}) custom-call(bf16[256,512]{1,0:T(8,128)(2,1)S(1)} %get-tuple-element.46.refs_0_, ...), custom_call_target="tpu_custom_call", output_to_operand_aliasing={{0}: (0, {}), {1}: (1, {}), {2}: (2, {}), {3}: (3, {})} | custom-call | bytes 2387968 | tf_op jit(solution)/shard_map/pallas_call | solution.py:22
  13.6 2.1 %collective-permute-start.4 = (bf16[272,128]{1,0:T(8,128)(2,1)S(1)}, bf16[272,128]{1,0:T(8,128)(2,1)S(1)}, u32[]{:S(2)}, u32[]{:S(2)}) collective-permute-start(bf16[272,128]{1,0:T(8,128)(2,1)S(1)} %get-tuple-element.64), channel_id=1, source_target_pairs={{0,16},{8,24},{16,0},{24,8},{1,17},{9,25},{17,1},{25,9},{2,18},{10... | collective-permute-start | bytes 208904 | tf_op jit(solution)/shard_map/ppermute | solution.py:417
  15.8 1.3 %collective-permute-done.2.got = bf16[128,512]{1,0:T(8,128)(2,1)S(1)} collective-permute-done((bf16[128,512]{1,0:T(8,128)(2,1)S(1)}, bf16[128,512]{1,0:T(8,128)(2,1)S(1)}, u32[]{:S(2)}, u32[]{:S(2)}) %collective-permute-start.2) | collective-permute-done | bytes 131104 | tf_op jit(solution)/shard_map/ppermute | solution.py:421
  17.1 0.7 %shard_map.81 = (bf16[256,512]{1,0:T(8,128)(2,1)S(1)}, bf16[256,512]{1,0:T(8,128)(2,1)S(1)}, bf16[4,256,256]{2,1,0:T(8,128)(2,1)S(1)}, f32[256,512]{1,0:T(8,128)...) custom-call(bf16[128,512]{1,0:T(8,128)(2,1)S(1)} %collective-permute-done.2.got, ...), custom_call_target="tpu_custom_call" | custom-call | flops 134217728 | bytes 2793472 | tf_op jit(solution)/shard_map/pallas_call | solution.py:22
  17.8 0.5 %collective-permute-done.3.refs_8_.refs_0_ = bf16[272,128]{1,0:T(8,128)(2,1)S(1)} collective-permute-done((bf16[272,128]{1,0:T(8,128)(2,1)S(1)}, bf16[272,128]{1,0:T(8,128)(2,1)S(1)}, u32[]{:S(2)}, u32[]{:S(2)}) %collective-permute-start.3) | collective-permute-done | bytes 69664 | tf_op jit(solution)/shard_map/ppermute | solution.py:417
  18.3 0.4 shard_map.82
  18.7 0.9 %collective-permute-done.4.refs_8_.refs_1_ = bf16[272,128]{1,0:T(8,128)(2,1)S(1)} collective-permute-done((bf16[272,128]{1,0:T(8,128)(2,1)S(1)}, bf16[272,128]{1,0:T(8,128)(2,1)S(1)}, u32[]{:S(2)}, u32[]{:S(2)}) %collective-permute-start.4) | collective-permute-done | bytes 69664 | tf_op jit(solution)/shard_map/ppermute | solution.py:417
  19.6 0.4 shard_map.83
  20.0 0.0 collective-permute-done.5.refs_2_
  20.0 0.2 shard_map.84
  20.3 0.0 collective-permute-start.6
  20.3 1.2 %collective-permute-done.6 = f32[2,256]{1,0:T(2,128)S(1)} collective-permute-done((f32[2,256]{1,0:T(2,128)S(1)}, f32[2,256]{1,0:T(2,128)S(1)}, u32[]{:S(2)}, u32[]{:S(2)}) %collective-permute-start.6) | collective-permute-done | bytes 2080 | tf_op jit(solution)/shard_map/ppermute | solution.py:438
  21.5 2.9 %collective-permute-start.8 = (f32[2,256]{1,0:T(2,128)S(1)}, f32[2,256]{1,0:T(2,128)S(1)}, u32[]{:S(2)}, u32[]{:S(2)}) collective-permute-start(f32[2,256]{1,0:T(2,128)S(1)} %add.3.refs_6_), channel_id=1, source_target_pairs={{0,8},{2,6},{4,12},{6,2},{8,0},{10,14},{12,4},{14,10},{16,24},{18,... | collective-permute-start | bytes 6152 | tf_op jit(solution)/shard_map/ppermute | solution.py:446
  24.5 0.9 %collective-permute-start.7 = (f32[2,256]{1,0:T(2,128)S(1)}, f32[2,256]{1,0:T(2,128)S(1)}, u32[]{:S(2)}, u32[]{:S(2)}) collective-permute-start(f32[2,256]{1,0:T(2,128)S(1)} %add.3.refs_6_), channel_id=1, source_target_pairs={{0,12},{2,14},{4,8},{6,10},{8,4},{10,6},{12,0},{14,2},{16,28},{18,... | collective-permute-start | bytes 6152 | tf_op jit(solution)/shard_map/ppermute | solution.py:446
  25.4 0.6 %collective-permute-done.8.refs_8_ = f32[2,256]{1,0:T(2,128)S(1)} collective-permute-done((f32[2,256]{1,0:T(2,128)S(1)}, f32[2,256]{1,0:T(2,128)S(1)}, u32[]{:S(2)}, u32[]{:S(2)}) %collective-permute-start.8) | collective-permute-done | bytes 2080 | tf_op jit(solution)/shard_map/ppermute | solution.py:446
  26.0 0.0 collective-permute-start.9
  26.0 2.9 %collective-permute-done.7.refs_7_ = f32[2,256]{1,0:T(2,128)S(1)} collective-permute-done((f32[2,256]{1,0:T(2,128)S(1)}, f32[2,256]{1,0:T(2,128)S(1)}, u32[]{:S(2)}, u32[]{:S(2)}) %collective-permute-start.7) | collective-permute-done | bytes 2080 | tf_op jit(solution)/shard_map/ppermute | solution.py:446
  28.9 0.0 collective-permute-done.9.refs_9_
  28.9 0.8 %shard_map.85 = (f32[8,256]{1,0:T(8,128)S(1)}, bf16[256,512]{1,0:T(8,128)(2,1)S(1)}, bf16[528,128]{1,0:T(8,128)(2,1)S(1)}) custom-call(f32[256,512]{1,0:T(8,128)S(1)} %get-tuple-element.65.refs_0_.attended, bf16[256,512]{1,0:T(8,128)(2,1)S(1)} %get-tuple-element.56.refs_2_.refs_1_.q2, bf16[256,512]{1,0:T(8,128)(2,1)S(1)} %get-tuple-element.57.refs_3_.refs_2_, ...), custom_call_target="tpu_custom_call" | custom-call | bytes 1757184 | tf_op jit(solution)/shard_map/pallas_call | solution.py:22
  29.7 2.1 %collective-permute-start.11 = (bf16[528,128]{1,0:T(8,128)(2,1)S(1)}, bf16[528,128]{1,0:T(8,128)(2,1)S(1)}, u32[]{:S(2)}, u32[]{:S(2)}) collective-permute-start(bf16[528,128]{1,0:T(8,128)(2,1)S(1)} %get-tuple-element.81), channel_id=1, source_target_pairs={{0,16},{8,24},{16,0},{24,8},{1,17},{9,25},{17,1},{25,9},{2,18},{10... | collective-permute-start | bytes 405512 | tf_op jit(solution)/shard_map/ppermute | solution.py:417
  31.9 1.6 %shard_map.86 = (bf16[128,512]{1,0:T(8,128)(2,1)S(1)}, bf16[128,512]{1,0:T(8,128)(2,1)S(1)}, f32[256,512]{1,0:T(8,128)S(1)}, f32[256,512]{1,0:T(8,128)S(1)}, bf16[256,512]{1,0:T(8,128)(2,1)S(1)}) custom-call(f32[256,512]{1,0:T(8,128)S(1)} %get-tuple-element.65.refs_0_.attended, f32[8,256]{1,0:T(8,128)S(1)} %get-tuple-element.69.scales, ...), custom_call_target="tpu_custom_call" | custom-call | flops 335544320 | bytes 3842048 | tf_op jit(solution)/shard_map/pallas_call | solution.py:22
  33.5 0.3 collective-permute-start.10
  33.8 3.7 %collective-permute-done.11.refs_4_ = bf16[528,128]{1,0:T(8,128)(2,1)S(1)} collective-permute-done((bf16[528,128]{1,0:T(8,128)(2,1)S(1)}, bf16[528,128]{1,0:T(8,128)(2,1)S(1)}, u32[]{:S(2)}, u32[]{:S(2)}) %collective-permute-start.11) | collective-permute-done | bytes 135200 | tf_op jit(solution)/shard_map/ppermute | solution.py:417
  37.5 0.5 %shard_map.87 = (bf16[128,512]{1,0:T(8,128)(2,1)S(1)}, bf16[128,512]{1,0:T(8,128)(2,1)S(1)}) custom-call(f32[256,512]{1,0:T(8,128)S(1)} %get-tuple-element.77.refs_0_, f32[256,512]{1,0:T(8,128)S(1)} %get-tuple-element.78.refs_1_, bf16[256,512]{1,0:T(8,128)(2,1)S(1)} %get-tuple-element.79.refs_2_, bf16[256,512]{1,0:T(8,128)(2,1)S(1)} %get-tuple-element.80.refs_3_, ...), custom_call_target="tpu_custom_call" | custom-call | bytes 2002944 | tf_op jit(solution)/shard_map/pallas_call | solution.py:22
  38.1 1.6 %collective-permute-start.12 = (bf16[128,512]{1,0:T(8,128)(2,1)S(1)}, bf16[128,512]{1,0:T(8,128)(2,1)S(1)}, u32[]{:S(2)}, u32[]{:S(2)}) collective-permute-start(bf16[128,512]{1,0:T(8,128)(2,1)S(1)} %get-tuple-element.82), channel_id=1, source_target_pairs={{0,1},{1,0},{8,9},{9,8},{16,17},{17,16},{24,25},{25,24},{2,3},{3,2... | collective-permute-start | bytes 393224 | tf_op jit(solution)/shard_map/ppermute | solution.py:431
  39.6 0.1 collective-permute-start.13
  39.8 0.0 collective-permute-done.10.refs_1_
  39.8 3.4 %collective-permute-done.12.refs_2_ = bf16[128,512]{1,0:T(8,128)(2,1)S(1)} collective-permute-done((bf16[128,512]{1,0:T(8,128)(2,1)S(1)}, bf16[128,512]{1,0:T(8,128)(2,1)S(1)}, u32[]{:S(2)}, u32[]{:S(2)}) %collective-permute-start.12) | collective-permute-done | bytes 131104 | tf_op jit(solution)/shard_map/ppermute | solution.py:431
  43.1 2.4 %collective-permute-done.13.refs_3_ = bf16[128,512]{1,0:T(8,128)(2,1)S(1)} collective-permute-done((bf16[128,512]{1,0:T(8,128)(2,1)S(1)}, bf16[128,512]{1,0:T(8,128)(2,1)S(1)}, u32[]{:S(2)}, u32[]{:S(2)}) %collective-permute-start.13) | collective-permute-done | bytes 131104 | tf_op jit(solution)/shard_map/ppermute | solution.py:431
  45.5 0.8 %shard_map.88 = (bf16[1,128,1024]{2,1,0:T(8,128)(2,1)}, bf16[1,128,1024]{2,1,0:T(8,128)(2,1)}) custom-call(bf16[128,512]{1,0:T(8,128)(2,1)S(1)} %get-tuple-element.75.refs_0_, bf16[128,512]{1,0:T(8,128)(2,1)S(1)} %collective-permute-done.10.refs_1_, bf16[128,512]{1,0:T(8,128)(2,1)S(1)} %collective-permute-done.12.refs_2_, ...), custom_call_target="tpu_custom_call" | custom-call | bytes 1048576 | tf_op jit(solution)/shard_map/pallas_call | solution.py:22
  (3 shorter events, 0.0 us)
Async XLA Ops:
  1.6 7.6 %collective-permute-start = (bf16[272,256]{1,0:T(8,128)(2,1)S(1)}, bf16[272,256]{1,0:T(8,128)(2,1)S(1)}, u32[]{:S(2)}, u32[]{:S(2)}) collective-permute-start(bf16[272,256]{1,0:T(8,128)(2,1)S(1)} %get-tuple-element.43), channel_id=1, source_target_pairs={{0,8},{8,0},{16,24},{24,16},{1,9},{9,1},{17,25},{25,17},{2,10},{10... | collective-permute-start | bytes 417800 | tf_op jit(solution)/shard_map/ppermute | solution.py:421
  4.7 8.3 %collective-permute-start.1 = (bf16[256,256]{1,0:T(8,128)(2,1)S(1)}, bf16[256,256]{1,0:T(8,128)(2,1)S(1)}, u32[]{:S(2)}, u32[]{:S(2)}) collective-permute-start(bf16[256,256]{1,0:T(8,128)(2,1)S(1)} %get-tuple-element.50), channel_id=1, source_target_pairs={{0,8},{8,0},{16,24},{24,16},{1,9},{9,1},{17,25},{25,17},{2,10},{10... | collective-permute-start | bytes 393224 | tf_op jit(solution)/shard_map/ppermute | solution.py:421
  4.8 4.4 %copy-start = (f32[1,4,1024]{2,1,0:T(4,128)S(1)}, f32[1,4,1024]{2,1,0:T(4,128)}, u32[]{:S(2)}) copy-start(f32[1,4,1024]{2,1,0:T(4,128)} %refs_6_.1) | copy-start | bytes 49156
  6.1 11.0 %collective-permute-start.2 = (bf16[128,512]{1,0:T(8,128)(2,1)S(1)}, bf16[128,512]{1,0:T(8,128)(2,1)S(1)}, u32[]{:S(2)}, u32[]{:S(2)}) collective-permute-start(bf16[128,512]{1,0:T(8,128)(2,1)S(1)} %get-tuple-element.53), channel_id=1, source_target_pairs={{0,8},{8,0},{16,24},{24,16},{1,9},{9,1},{17,25},{25,17},{2,10},{10... | collective-permute-start | bytes 393224 | tf_op jit(solution)/shard_map/ppermute | solution.py:421
  8.1 12.0 %collective-permute-start.5 = (bf16[128,512]{1,0:T(8,128)(2,1)S(1)}, bf16[128,512]{1,0:T(8,128)(2,1)S(1)}, u32[]{:S(2)}, u32[]{:S(2)}) collective-permute-start(bf16[128,512]{1,0:T(8,128)(2,1)S(1)} %get-tuple-element.66), channel_id=1, source_target_pairs={{0,8},{8,0},{16,24},{24,16},{1,9},{9,1},{17,25},{25,17},{2,10},{10... | collective-permute-start | bytes 393224 | tf_op jit(solution)/shard_map/ppermute | solution.py:421
  9.9 8.4 %collective-permute-start.3 = (bf16[272,128]{1,0:T(8,128)(2,1)S(1)}, bf16[272,128]{1,0:T(8,128)(2,1)S(1)}, u32[]{:S(2)}, u32[]{:S(2)}) collective-permute-start(bf16[272,128]{1,0:T(8,128)(2,1)S(1)} %get-tuple-element.61), channel_id=1, source_target_pairs={{0,16},{8,24},{16,0},{24,8},{1,17},{9,25},{17,1},{25,9},{2,18},{10... | collective-permute-start | bytes 208904 | tf_op jit(solution)/shard_map/ppermute | solution.py:417
  13.6 6.0 %collective-permute-start.4 = (bf16[272,128]{1,0:T(8,128)(2,1)S(1)}, bf16[272,128]{1,0:T(8,128)(2,1)S(1)}, u32[]{:S(2)}, u32[]{:S(2)}) collective-permute-start(bf16[272,128]{1,0:T(8,128)(2,1)S(1)} %get-tuple-element.64), channel_id=1, source_target_pairs={{0,16},{8,24},{16,0},{24,8},{1,17},{9,25},{17,1},{25,9},{2,18},{10... | collective-permute-start | bytes 208904 | tf_op jit(solution)/shard_map/ppermute | solution.py:417
  20.3 1.2 %collective-permute-start.6 = (f32[2,256]{1,0:T(2,128)S(1)}, f32[2,256]{1,0:T(2,128)S(1)}, u32[]{:S(2)}, u32[]{:S(2)}) collective-permute-start(f32[2,256]{1,0:T(2,128)S(1)} %get-tuple-element.68), channel_id=1, source_target_pairs={{0,2},{2,0},{4,6},{6,4},{1,3},{3,1},{5,7},{7,5},{8,10},{10,8},{12,... | collective-permute-start | bytes 6152 | tf_op jit(solution)/shard_map/ppermute | solution.py:438
  21.5 4.5 %collective-permute-start.8 = (f32[2,256]{1,0:T(2,128)S(1)}, f32[2,256]{1,0:T(2,128)S(1)}, u32[]{:S(2)}, u32[]{:S(2)}) collective-permute-start(f32[2,256]{1,0:T(2,128)S(1)} %add.3.refs_6_), channel_id=1, source_target_pairs={{0,8},{2,6},{4,12},{6,2},{8,0},{10,14},{12,4},{14,10},{16,24},{18,... | collective-permute-start | bytes 6152 | tf_op jit(solution)/shard_map/ppermute | solution.py:446
  24.5 4.5 %collective-permute-start.7 = (f32[2,256]{1,0:T(2,128)S(1)}, f32[2,256]{1,0:T(2,128)S(1)}, u32[]{:S(2)}, u32[]{:S(2)}) collective-permute-start(f32[2,256]{1,0:T(2,128)S(1)} %add.3.refs_6_), channel_id=1, source_target_pairs={{0,12},{2,14},{4,8},{6,10},{8,4},{10,6},{12,0},{14,2},{16,28},{18,... | collective-permute-start | bytes 6152 | tf_op jit(solution)/shard_map/ppermute | solution.py:446
  26.0 2.9 %collective-permute-start.9 = (f32[2,256]{1,0:T(2,128)S(1)}, f32[2,256]{1,0:T(2,128)S(1)}, u32[]{:S(2)}, u32[]{:S(2)}) collective-permute-start(f32[2,256]{1,0:T(2,128)S(1)} %collective-permute-done.8.refs_8_), channel_id=1, source_target_pairs={{0,2},{2,0},{4,6},{6,4},{1,3},{3,1},{5,7},{7,5},{8,10},{10,8},{12,... | collective-permute-start | bytes 6152 | tf_op jit(solution)/shard_map/ppermute | solution.py:438
  29.7 7.8 %collective-permute-start.11 = (bf16[528,128]{1,0:T(8,128)(2,1)S(1)}, bf16[528,128]{1,0:T(8,128)(2,1)S(1)}, u32[]{:S(2)}, u32[]{:S(2)}) collective-permute-start(bf16[528,128]{1,0:T(8,128)(2,1)S(1)} %get-tuple-element.81), channel_id=1, source_target_pairs={{0,16},{8,24},{16,0},{24,8},{1,17},{9,25},{17,1},{25,9},{2,18},{10... | collective-permute-start | bytes 405512 | tf_op jit(solution)/shard_map/ppermute | solution.py:417
  33.5 6.3 %collective-permute-start.10 = (bf16[128,512]{1,0:T(8,128)(2,1)S(1)}, bf16[128,512]{1,0:T(8,128)(2,1)S(1)}, u32[]{:S(2)}, u32[]{:S(2)}) collective-permute-start(bf16[128,512]{1,0:T(8,128)(2,1)S(1)} %get-tuple-element.76), channel_id=1, source_target_pairs={{0,8},{8,0},{16,24},{24,16},{1,9},{9,1},{17,25},{25,17},{2,10},{10... | collective-permute-start | bytes 393224 | tf_op jit(solution)/shard_map/ppermute | solution.py:421
  38.1 5.1 %collective-permute-start.12 = (bf16[128,512]{1,0:T(8,128)(2,1)S(1)}, bf16[128,512]{1,0:T(8,128)(2,1)S(1)}, u32[]{:S(2)}, u32[]{:S(2)}) collective-permute-start(bf16[128,512]{1,0:T(8,128)(2,1)S(1)} %get-tuple-element.82), channel_id=1, source_target_pairs={{0,1},{1,0},{8,9},{9,8},{16,17},{17,16},{24,25},{25,24},{2,3},{3,2... | collective-permute-start | bytes 393224 | tf_op jit(solution)/shard_map/ppermute | solution.py:431
  39.6 5.9 %collective-permute-start.13 = (bf16[128,512]{1,0:T(8,128)(2,1)S(1)}, bf16[128,512]{1,0:T(8,128)(2,1)S(1)}, u32[]{:S(2)}, u32[]{:S(2)}) collective-permute-start(bf16[128,512]{1,0:T(8,128)(2,1)S(1)} %get-tuple-element.83), channel_id=1, source_target_pairs={{0,9},{1,8},{8,1},{9,0},{16,25},{17,24},{24,17},{25,16},{2,11},{3,... | collective-permute-start | bytes 393224 | tf_op jit(solution)/shard_map/ppermute | solution.py:431

commit v9 on v6

--- a/solution.py
+++ b/solution.py
@@ -206,7 +206,9 @@
     return jnp.where(head == lane, wide, 0.0).astype(BF16)
 
 
-def local_kernel(got, own, kc2, v2, cum, q2, qs2, weights, inside, lead_mixing, lead_values):
+def local_kernel(
+    got, own, kc2, v2, cum, q2, qs2, qst, weights, inside, lead_mixing, lead_mixing_t, lead_values
+):
     size, width = q2.shape
     heads, dim = weights.shape[0], width // weights.shape[0]
     rows = size // PAIR
@@ -216,11 +218,16 @@
     cum_rows = cum[...]
     cols = cum_rows.T
     growth = jnp.exp(cols)
-    lead_mixing[...] = lead_mixing_of(cum_rows, cols, heads)
+    lead = lead_mixing_of(cum_rows, cols, heads)
+    lead_mixing[...] = lead
+    wide = jnp.concatenate([lead, jnp.zeros((size, dim - LEAD * heads), F32)], 1)
+    lead_mixing_t[...] = wide.T[: LEAD * heads]
     lead_values[...] = block_diagonal(v2[:EDGE, :].astype(F32)[:LEAD], dim, heads)
     for h in range(heads):
         lanes = slice(h * dim, (h + 1) * dim)
-        qs2[:, lanes] = (q2[:, lanes].astype(F32) * growth[:, h : h + 1]).astype(BF16)
+        scaled = q2[:, lanes].astype(F32) * growth[:, h : h + 1]
+        qs2[:, lanes] = scaled.astype(BF16)
+        qst[lanes, :] = scaled.T.astype(BF16)
         scores = dot(q2[:, lanes], kc2[:, lanes], (1, 1))
         w = (scores * mixing_of(cum_rows, cols, h, LEAD)).astype(BF16)
         weights[h] = w
@@ -280,7 +287,7 @@
     sums[...] = jnp.concatenate([line[:, :size], line[:, size:]], 0)
 
 
-def grad_kernel(width_all, attended, q2, qs2, lead_mixing, lead_values, g2, *refs):
+def grad_kernel(width_all, attended, q2, qst, lead_mixing_t, lead_values, g2, *refs):
     *sums, scales, grad = refs[:-PARTS]
     adjoints = refs[-PARTS:]
     size, width = q2.shape
@@ -298,9 +305,9 @@
         d = (g2[:, lanes].astype(F32) * inverse - attended[:, lanes] * pull).astype(BF16)
         grad[:, lanes] = d
         part, at = divmod(h, heads // PARTS)
-        adjoints[part][at * dim : (at + 1) * dim, :] = dot(qs2[:, lanes], d, (0, 0)).astype(BF16)
-    scores = (dot(grad[...], lead_values[...], (1, 1)) * lead_mixing[...]).astype(BF16)
-    tops = dot(scores, q2[...], (0, 0))
+        adjoints[part][at * dim : (at + 1) * dim, :] = dot(qst[lanes, :], d, (1, 0)).astype(BF16)
+    scores = (dot(lead_values[...], grad[...], (1, 1)) * lead_mixing_t[...]).astype(BF16)
+    tops = dot(scores, q2[...], (1, 0))
     per_part = heads // PARTS
     for i, adjoint in enumerate(adjoints):
         rows = [
@@ -521,11 +528,13 @@
             moved = jnp.concatenate([turned(earlier, "ctx", PAIR), moved[step_width:]], 0)
         before.append(moved)
 
-    q2, qs2, weights, inside, lead_mixing, lead_values = call(
+    q2, qs2, qst, weights, inside, lead_mixing, lead_mixing_t, lead_values = call(
         local_kernel,
         [shape((size, width), BF16)] * 2
+        + [shape((width, size), BF16)]
         + [shape((heads, size, size), BF16), shape((size, width), F32)]
-        + [shape((size, LEAD * heads), F32), shape((LEAD * heads, width), BF16)],
+        + [shape((size, LEAD * heads), F32), shape((LEAD * heads, size), F32)]
+        + [shape((LEAD * heads, width), BF16)],
         got_q, own, kc2, v2, cum,
         flops=4 * heads * size * size * dim,
     )
@@ -551,7 +560,7 @@
         lambda *refs: grad_kernel(width_all, *refs),
         [shape((8, size), F32), shape((size, width), BF16)]
         + [shape((chunk + EDGE, dim), BF16)] * PARTS,
-        attended, q2, qs2, lead_mixing, lead_values, g2, *parts,
+        attended, q2, qst, lead_mixing_t, lead_values, g2, *parts,
     )
     last_pair = pair_index == supers - 1
     behind = []

time: 46.4 us -> 46.4 us (level)
  no operation moved by 1% of the time
where the time goes in v9:
time: 46.4 us; the launch traced here: 46.2 us
  starting transfers between devices  18.6 us (40%)
  waiting for transfers between devices  17.2 us (37%)
  Pallas kernels  9.59 us (21%)
  between operations  0.73 us (2%)
    pallas_call x13, Pallas kernels, call(): pl.pallas_call(kernel, out_shape=outs, in_specs=[pl.BlockSpec(memory_spac...  9.59 us
    ppermute x3, starting transfers between devices, turned(): lax.ppermute(block, axis, [(i, (i + distance) % count) for i in range(cou...  7.43 us
    ppermute x5, starting transfers between devices, swapped(): lax.ppermute(block, 'ctx', [(i, i ^ 1) for i in range(lax.axis_size('ctx'...  5.58 us
    ppermute x3, waiting for transfers between devices, turned(): lax.ppermute(block, axis, [(i, (i + distance) % count) for i in range(cou...  5.08 us
    ppermute x2, waiting for transfers between devices, to_earlier_section(): return lax.ppermute(block, ('ctx', 'pp'), route)  5.01 us
    ppermute x2, starting transfers between devices, fetched(): return lax.ppermute(block, ('ctx', 'tp'), route)  3.86 us
    ppermute x2, waiting for transfers between devices, fetched(): return lax.ppermute(block, ('ctx', 'tp'), route)  3.55 us
    ppermute x5, waiting for transfers between devices, swapped(): lax.ppermute(block, 'ctx', [(i, i ^ 1) for i in range(lax.axis_size('ctx'...  2.39 us
  transfers between devices with their start and end apart: 14, of which 10 were waited for; matrix products, arithmetic and copies ran while one was open for 0% of the time, Pallas kernels for 15%

profile of v9, /device:TPU:0, one launch (start us, length us, event | category | flops | bytes accessed | tf_op | source)
XLA Modules:
  0.0 46.2 jit_solution(14024444754167546152)
XLA Ops:
  0.6 1.0 %shard_map.77 = (bf16[272,256]{1,0:T(8,128)(2,1)S(1)}, bf16[256,256]{1,0:T(8,128)(2,1)S(1)}, f32[8,128]{1,0:T(8,128)S(1)}) custom-call(bf16[1,128,1024]{2,1,0:T(8,128)(2,1)} %k.3, bf16[1,128,1024]{2,1,0:T(8,128)(2,1)} %v.3, f32[1,8,128]{2,1,0:T(8,128)} %bitcast.1), custom_call_target="tpu_custom_call" | custom-call | bytes 802816 | tf_op jit(solution)/shard_map/pallas_call | solution.py:22
  1.6 3.1 %collective-permute-start = (bf16[272,256]{1,0:T(8,128)(2,1)S(1)}, bf16[272,256]{1,0:T(8,128)(2,1)S(1)}, u32[]{:S(2)}, u32[]{:S(2)}) collective-permute-start(bf16[272,256]{1,0:T(8,128)(2,1)S(1)} %get-tuple-element.45), channel_id=1, source_target_pairs={{0,8},{8,0},{16,24},{24,16},{1,9},{9,1},{17,25},{25,17},{2,10},{10... | collective-permute-start | bytes 417800 | tf_op jit(solution)/shard_map/ppermute | solution.py:423
  4.7 0.1 collective-permute-start.1
  4.8 0.0 copy-start
  4.8 1.3 %shard_map.78 = (bf16[128,512]{1,0:T(8,128)(2,1)S(1)}, bf16[128,512]{1,0:T(8,128)(2,1)S(1)}, bf16[512,512]{1,0:T(8,128)(2,1)S(1)}) custom-call(bf16[1,128,1024]{2,1,0:T(8,128)(2,1)} %q.1, bf16[1,128,1024]{2,1,0:T(8,128)(2,1)} %k.3, bf16[1,128,1024]{2,1,0:T(8,128)(2,1)} %v.3, bf16[1,128,1024]{2,1,0:T(8,128)(2,1)} %g.1, bf16[16,256]{1,0:T(8,128)(2,1)S(1)} %slice.3._), custom_call_target="tpu_custom_call" | custom-call | bytes 1843200 | tf_op jit(solution)/shard_map/pallas_call | solution.py:22
  6.1 2.0 %collective-permute-start.2 = (bf16[128,512]{1,0:T(8,128)(2,1)S(1)}, bf16[128,512]{1,0:T(8,128)(2,1)S(1)}, u32[]{:S(2)}, u32[]{:S(2)}) collective-permute-start(bf16[128,512]{1,0:T(8,128)(2,1)S(1)} %get-tuple-element.55), channel_id=1, source_target_pairs={{0,8},{8,0},{16,24},{24,16},{1,9},{9,1},{17,25},{25,17},{2,10},{10... | collective-permute-start | bytes 393224 | tf_op jit(solution)/shard_map/ppermute | solution.py:423
  8.1 0.1 collective-permute-start.5
  8.2 1.1 %collective-permute-done.got = bf16[272,256]{1,0:T(8,128)(2,1)S(1)} collective-permute-done((bf16[272,256]{1,0:T(8,128)(2,1)S(1)}, bf16[272,256]{1,0:T(8,128)(2,1)S(1)}, u32[]{:S(2)}, u32[]{:S(2)}) %collective-permute-start) | collective-permute-done | bytes 139296 | tf_op jit(solution)/shard_map/ppermute | solution.py:423
  9.2 0.0 copy-done
  9.2 0.6 %shard_map.79 = (bf16[256,512]{1,0:T(8,128)(2,1)S(1)}, bf16[256,512]{1,0:T(8,128)(2,1)S(1)}, f32[16,512]{1,0:T(8,128)S(1)}, bf16[256,512]{1,0:T(8,128)(2,1)S(1)}...) custom-call(bf16[272,256]{1,0:T(8,128)(2,1)S(1)} %collective-permute-done.got, ...), custom_call_target="tpu_custom_call" | custom-call | bytes 1581056 | tf_op jit(solution)/shard_map/pallas_call | solution.py:22
  9.9 3.1 %collective-permute-start.3 = (bf16[272,128]{1,0:T(8,128)(2,1)S(1)}, bf16[272,128]{1,0:T(8,128)(2,1)S(1)}, u32[]{:S(2)}, u32[]{:S(2)}) collective-permute-start(bf16[272,128]{1,0:T(8,128)(2,1)S(1)} %get-tuple-element.63), channel_id=1, source_target_pairs={{0,16},{8,24},{16,0},{24,8},{1,17},{9,25},{17,1},{25,9},{2,18},{10... | collective-permute-start | bytes 208904 | tf_op jit(solution)/shard_map/ppermute | solution.py:419
  13.0 0.0 collective-permute-done.1.refs_4_
  13.0 0.6 %shard_map.80 = (bf16[256,512]{1,0:T(8,128)(2,1)S(1)}, bf16[256,512]{1,0:T(8,128)(2,1)S(1)}, f32[16,512]{1,0:T(8,128)S(1)}, bf16[256,512]{1,0:T(8,128)(2,1)S(1)}, bf16[272,128]{1,0:T(8,128)(2,1)S(1)}) custom-call(bf16[256,512]{1,0:T(8,128)(2,1)S(1)} %get-tuple-element.48.refs_0_, ...), custom_call_target="tpu_custom_call", output_to_operand_aliasing={{0}: (0, {}), {1}: (1, {}), {2}: (2, {}), {3}: (3, {})} | custom-call | bytes 2387968 | tf_op jit(solution)/shard_map/pallas_call | solution.py:22
  13.6 2.2 %collective-permute-start.4 = (bf16[272,128]{1,0:T(8,128)(2,1)S(1)}, bf16[272,128]{1,0:T(8,128)(2,1)S(1)}, u32[]{:S(2)}, u32[]{:S(2)}) collective-permute-start(bf16[272,128]{1,0:T(8,128)(2,1)S(1)} %get-tuple-element.66), channel_id=1, source_target_pairs={{0,16},{8,24},{16,0},{24,8},{1,17},{9,25},{17,1},{25,9},{2,18},{10... | collective-permute-start | bytes 208904 | tf_op jit(solution)/shard_map/ppermute | solution.py:419
  15.8 1.3 %collective-permute-done.2.got = bf16[128,512]{1,0:T(8,128)(2,1)S(1)} collective-permute-done((bf16[128,512]{1,0:T(8,128)(2,1)S(1)}, bf16[128,512]{1,0:T(8,128)(2,1)S(1)}, u32[]{:S(2)}, u32[]{:S(2)}) %collective-permute-start.2) | collective-permute-done | bytes 131104 | tf_op jit(solution)/shard_map/ppermute | solution.py:423
  17.1 0.7 %shard_map.81 = (bf16[256,512]{1,0:T(8,128)(2,1)S(1)}, bf16[256,512]{1,0:T(8,128)(2,1)S(1)}, bf16[512,256]{1,0:T(8,128)(2,1)S(1)}, bf16[4,256,256]{2,1,0:T(8,128...) custom-call(bf16[128,512]{1,0:T(8,128)(2,1)S(1)} %collective-permute, ...), custom_call_target="tpu_custom_call" | custom-call | flops 134217728 | bytes 3072000 | tf_op jit(solution)/shard_map/pallas_call | solution.py:22
  17.8 0.5 %collective-permute-done.3.refs_8_.refs_0_ = bf16[272,128]{1,0:T(8,128)(2,1)S(1)} collective-permute-done((bf16[272,128]{1,0:T(8,128)(2,1)S(1)}, bf16[272,128]{1,0:T(8,128)(2,1)S(1)}, u32[]{:S(2)}, u32[]{:S(2)}) %collective-permute-start.3) | collective-permute-done | bytes 69664 | tf_op jit(solution)/shard_map/ppermute | solution.py:419
  18.3 0.4 shard_map.82
  18.7 0.9 %collective-permute-done.4.refs_8_.refs_1_ = bf16[272,128]{1,0:T(8,128)(2,1)S(1)} collective-permute-done((bf16[272,128]{1,0:T(8,128)(2,1)S(1)}, bf16[272,128]{1,0:T(8,128)(2,1)S(1)}, u32[]{:S(2)}, u32[]{:S(2)}) %collective-permute-start.4) | collective-permute-done | bytes 69664 | tf_op jit(solution)/shard_map/ppermute | solution.py:419
  19.6 0.4 shard_map.83
  20.0 0.0 collective-permute-done.5.refs_2_
  20.0 0.2 shard_map.84
  20.3 0.0 collective-permute-start.6
  20.3 1.2 %collective-permute-done.6 = f32[2,256]{1,0:T(2,128)S(1)} collective-permute-done((f32[2,256]{1,0:T(2,128)S(1)}, f32[2,256]{1,0:T(2,128)S(1)}, u32[]{:S(2)}, u32[]{:S(2)}) %collective-permute-start.6) | collective-permute-done | bytes 2080 | tf_op jit(solution)/shard_map/ppermute | solution.py:440
  21.5 2.9 %collective-permute-start.8 = (f32[2,256]{1,0:T(2,128)S(1)}, f32[2,256]{1,0:T(2,128)S(1)}, u32[]{:S(2)}, u32[]{:S(2)}) collective-permute-start(f32[2,256]{1,0:T(2,128)S(1)} %add.3.refs_6_), channel_id=1, source_target_pairs={{0,8},{2,6},{4,12},{6,2},{8,0},{10,14},{12,4},{14,10},{16,24},{18,... | collective-permute-start | bytes 6152 | tf_op jit(solution)/shard_map/ppermute | solution.py:448
  24.5 0.9 %collective-permute-start.7 = (f32[2,256]{1,0:T(2,128)S(1)}, f32[2,256]{1,0:T(2,128)S(1)}, u32[]{:S(2)}, u32[]{:S(2)}) collective-permute-start(f32[2,256]{1,0:T(2,128)S(1)} %add.3.refs_6_), channel_id=1, source_target_pairs={{0,12},{2,14},{4,8},{6,10},{8,4},{10,6},{12,0},{14,2},{16,28},{18,... | collective-permute-start | bytes 6152 | tf_op jit(solution)/shard_map/ppermute | solution.py:448
  25.4 0.6 %collective-permute-done.8.refs_8_ = f32[2,256]{1,0:T(2,128)S(1)} collective-permute-done((f32[2,256]{1,0:T(2,128)S(1)}, f32[2,256]{1,0:T(2,128)S(1)}, u32[]{:S(2)}, u32[]{:S(2)}) %collective-permute-start.8) | collective-permute-done | bytes 2080 | tf_op jit(solution)/shard_map/ppermute | solution.py:448
  26.0 0.0 collective-permute-start.9
  26.0 2.9 %collective-permute-done.7.refs_7_ = f32[2,256]{1,0:T(2,128)S(1)} collective-permute-done((f32[2,256]{1,0:T(2,128)S(1)}, f32[2,256]{1,0:T(2,128)S(1)}, u32[]{:S(2)}, u32[]{:S(2)}) %collective-permute-start.7) | collective-permute-done | bytes 2080 | tf_op jit(solution)/shard_map/ppermute | solution.py:448
  28.9 0.0 collective-permute-done.9.refs_9_
  28.9 0.7 %shard_map.85 = (f32[8,256]{1,0:T(8,128)S(1)}, bf16[256,512]{1,0:T(8,128)(2,1)S(1)}, bf16[528,128]{1,0:T(8,128)(2,1)S(1)}) custom-call(f32[256,512]{1,0:T(8,128)S(1)} %get-tuple-element.67.refs_0_.attended, bf16[256,512]{1,0:T(8,128)(2,1)S(1)} %get-tuple-element.58.refs_2_.refs_1_.q2, bf16[512,256]{1,0:T(8,128)(2,1)S(1)} %get-tuple-element.68.refs_2_, ...), custom_call_target="tpu_custom_call" | custom-call | bytes 1757184 | tf_op jit(solution)/shard_map/pallas_call | solution.py:22
  29.7 2.1 %collective-permute-start.11 = (bf16[528,128]{1,0:T(8,128)(2,1)S(1)}, bf16[528,128]{1,0:T(8,128)(2,1)S(1)}, u32[]{:S(2)}, u32[]{:S(2)}) collective-permute-start(bf16[528,128]{1,0:T(8,128)(2,1)S(1)} %get-tuple-element.85), channel_id=1, source_target_pairs={{0,16},{8,24},{16,0},{24,8},{1,17},{9,25},{17,1},{25,9},{2,18},{10... | collective-permute-start | bytes 405512 | tf_op jit(solution)/shard_map/ppermute | solution.py:419
  31.8 1.6 %shard_map.86 = (bf16[128,512]{1,0:T(8,128)(2,1)S(1)}, bf16[128,512]{1,0:T(8,128)(2,1)S(1)}, f32[256,512]{1,0:T(8,128)S(1)}, f32[256,512]{1,0:T(8,128)S(1)}, bf16[256,512]{1,0:T(8,128)(2,1)S(1)}) custom-call(f32[256,512]{1,0:T(8,128)S(1)} %get-tuple-element.67.refs_0_.attended, f32[8,256]{1,0:T(8,128)S(1)} %get-tuple-element.73.scales, ...), custom_call_target="tpu_custom_call" | custom-call | flops 335544320 | bytes 3842048 | tf_op jit(solution)/shard_map/pallas_call | solution.py:22
  33.5 0.3 collective-permute-start.10
  33.8 3.7 %collective-permute-done.11.refs_4_ = bf16[528,128]{1,0:T(8,128)(2,1)S(1)} collective-permute-done((bf16[528,128]{1,0:T(8,128)(2,1)S(1)}, bf16[528,128]{1,0:T(8,128)(2,1)S(1)}, u32[]{:S(2)}, u32[]{:S(2)}) %collective-permute-start.11) | collective-permute-done | bytes 135200 | tf_op jit(solution)/shard_map/ppermute | solution.py:419
  37.5 0.5 %shard_map.88 = (bf16[128,512]{1,0:T(8,128)(2,1)S(1)}, bf16[128,512]{1,0:T(8,128)(2,1)S(1)}) custom-call(f32[256,512]{1,0:T(8,128)S(1)} %get-tuple-element.81.refs_0_, f32[256,512]{1,0:T(8,128)S(1)} %get-tuple-element.82.refs_1_, bf16[256,512]{1,0:T(8,128)(2,1)S(1)} %get-tuple-element.83.refs_2_, bf16[256,512]{1,0:T(8,128)(2,1)S(1)} %get-tuple-element.84.refs_3_, ...), custom_call_target="tpu_custom_call" | custom-call | bytes 2002944 | tf_op jit(solution)/shard_map/pallas_call | solution.py:22
  38.0 1.6 %collective-permute-start.12 = (bf16[128,512]{1,0:T(8,128)(2,1)S(1)}, bf16[128,512]{1,0:T(8,128)(2,1)S(1)}, u32[]{:S(2)}, u32[]{:S(2)}) collective-permute-start(bf16[128,512]{1,0:T(8,128)(2,1)S(1)} %get-tuple-element.86), channel_id=1, source_target_pairs={{0,1},{1,0},{8,9},{9,8},{16,17},{17,16},{24,25},{25,24},{2,3},{3,2... | collective-permute-start | bytes 393224 | tf_op jit(solution)/shard_map/ppermute | solution.py:433
  39.6 0.1 collective-permute-start.13
  39.7 0.0 collective-permute-done.10.refs_1_
  39.7 0.7 %shard_map.87 = bf16[1,128,1024]{2,1,0:T(8,128)(2,1)} custom-call(bf16[128,512]{1,0:T(8,128)(2,1)S(1)} %get-tuple-element.79.refs_0_, bf16[128,512]{1,0:T(8,128)(2,1)S(1)} %collective-permute-done.10.refs_1_), custom_call_target="tpu_custom_call" | custom-call | bytes 524288 | tf_op jit(solution)/shard_map/pallas_call | solution.py:22
  40.4 2.6 %collective-permute-done.12.refs_0_ = bf16[128,512]{1,0:T(8,128)(2,1)S(1)} collective-permute-done((bf16[128,512]{1,0:T(8,128)(2,1)S(1)}, bf16[128,512]{1,0:T(8,128)(2,1)S(1)}, u32[]{:S(2)}, u32[]{:S(2)}) %collective-permute-start.12) | collective-permute-done | bytes 131104 | tf_op jit(solution)/shard_map/ppermute | solution.py:433
  43.1 2.4 %collective-permute-done.13.refs_1_ = bf16[128,512]{1,0:T(8,128)(2,1)S(1)} collective-permute-done((bf16[128,512]{1,0:T(8,128)(2,1)S(1)}, bf16[128,512]{1,0:T(8,128)(2,1)S(1)}, u32[]{:S(2)}, u32[]{:S(2)}) %collective-permute-start.13) | collective-permute-done | bytes 131104 | tf_op jit(solution)/shard_map/ppermute | solution.py:433
  45.5 0.7 %shard_map.89 = bf16[1,128,1024]{2,1,0:T(8,128)(2,1)} custom-call(bf16[128,512]{1,0:T(8,128)(2,1)S(1)} %collective-permute-done.12.refs_0_, bf16[128,512]{1,0:T(8,128)(2,1)S(1)} %collective-permute-done.13.refs_1_), custom_call_target="tpu_custom_call" | custom-call | bytes 524288 | tf_op jit(solution)/shard_map/pallas_call | solution.py:22
  (3 shorter events, 0.0 us)
Async XLA Ops:
  1.6 7.6 %collective-permute-start = (bf16[272,256]{1,0:T(8,128)(2,1)S(1)}, bf16[272,256]{1,0:T(8,128)(2,1)S(1)}, u32[]{:S(2)}, u32[]{:S(2)}) collective-permute-start(bf16[272,256]{1,0:T(8,128)(2,1)S(1)} %get-tuple-element.45), channel_id=1, source_target_pairs={{0,8},{8,0},{16,24},{24,16},{1,9},{9,1},{17,25},{25,17},{2,10},{10... | collective-permute-start | bytes 417800 | tf_op jit(solution)/shard_map/ppermute | solution.py:423
  4.7 8.3 %collective-permute-start.1 = (bf16[256,256]{1,0:T(8,128)(2,1)S(1)}, bf16[256,256]{1,0:T(8,128)(2,1)S(1)}, u32[]{:S(2)}, u32[]{:S(2)}) collective-permute-start(bf16[256,256]{1,0:T(8,128)(2,1)S(1)} %get-tuple-element.52), channel_id=1, source_target_pairs={{0,8},{8,0},{16,24},{24,16},{1,9},{9,1},{17,25},{25,17},{2,10},{10... | collective-permute-start | bytes 393224 | tf_op jit(solution)/shard_map/ppermute | solution.py:423
  4.8 4.4 %copy-start = (f32[1,4,1024]{2,1,0:T(4,128)S(1)}, f32[1,4,1024]{2,1,0:T(4,128)}, u32[]{:S(2)}) copy-start(f32[1,4,1024]{2,1,0:T(4,128)} %refs_6_.1) | copy-start | bytes 49156
  6.1 11.0 %collective-permute-start.2 = (bf16[128,512]{1,0:T(8,128)(2,1)S(1)}, bf16[128,512]{1,0:T(8,128)(2,1)S(1)}, u32[]{:S(2)}, u32[]{:S(2)}) collective-permute-start(bf16[128,512]{1,0:T(8,128)(2,1)S(1)} %get-tuple-element.55), channel_id=1, source_target_pairs={{0,8},{8,0},{16,24},{24,16},{1,9},{9,1},{17,25},{25,17},{2,10},{10... | collective-permute-start | bytes 393224 | tf_op jit(solution)/shard_map/ppermute | solution.py:423
  8.1 12.0 %collective-permute-start.5 = (bf16[128,512]{1,0:T(8,128)(2,1)S(1)}, bf16[128,512]{1,0:T(8,128)(2,1)S(1)}, u32[]{:S(2)}, u32[]{:S(2)}) collective-permute-start(bf16[128,512]{1,0:T(8,128)(2,1)S(1)} %get-tuple-element.70), channel_id=1, source_target_pairs={{0,8},{8,0},{16,24},{24,16},{1,9},{9,1},{17,25},{25,17},{2,10},{10... | collective-permute-start | bytes 393224 | tf_op jit(solution)/shard_map/ppermute | solution.py:423
  9.9 8.4 %collective-permute-start.3 = (bf16[272,128]{1,0:T(8,128)(2,1)S(1)}, bf16[272,128]{1,0:T(8,128)(2,1)S(1)}, u32[]{:S(2)}, u32[]{:S(2)}) collective-permute-start(bf16[272,128]{1,0:T(8,128)(2,1)S(1)} %get-tuple-element.63), channel_id=1, source_target_pairs={{0,16},{8,24},{16,0},{24,8},{1,17},{9,25},{17,1},{25,9},{2,18},{10... | collective-permute-start | bytes 208904 | tf_op jit(solution)/shard_map/ppermute | solution.py:419
  13.6 6.0 %collective-permute-start.4 = (bf16[272,128]{1,0:T(8,128)(2,1)S(1)}, bf16[272,128]{1,0:T(8,128)(2,1)S(1)}, u32[]{:S(2)}, u32[]{:S(2)}) collective-permute-start(bf16[272,128]{1,0:T(8,128)(2,1)S(1)} %get-tuple-element.66), channel_id=1, source_target_pairs={{0,16},{8,24},{16,0},{24,8},{1,17},{9,25},{17,1},{25,9},{2,18},{10... | collective-permute-start | bytes 208904 | tf_op jit(solution)/shard_map/ppermute | solution.py:419
  20.3 1.2 %collective-permute-start.6 = (f32[2,256]{1,0:T(2,128)S(1)}, f32[2,256]{1,0:T(2,128)S(1)}, u32[]{:S(2)}, u32[]{:S(2)}) collective-permute-start(f32[2,256]{1,0:T(2,128)S(1)} %get-tuple-element.72), channel_id=1, source_target_pairs={{0,2},{2,0},{4,6},{6,4},{1,3},{3,1},{5,7},{7,5},{8,10},{10,8},{12,... | collective-permute-start | bytes 6152 | tf_op jit(solution)/shard_map/ppermute | solution.py:440
  21.5 4.5 %collective-permute-start.8 = (f32[2,256]{1,0:T(2,128)S(1)}, f32[2,256]{1,0:T(2,128)S(1)}, u32[]{:S(2)}, u32[]{:S(2)}) collective-permute-start(f32[2,256]{1,0:T(2,128)S(1)} %add.3.refs_6_), channel_id=1, source_target_pairs={{0,8},{2,6},{4,12},{6,2},{8,0},{10,14},{12,4},{14,10},{16,24},{18,... | collective-permute-start | bytes 6152 | tf_op jit(solution)/shard_map/ppermute | solution.py:448
  24.5 4.5 %collective-permute-start.7 = (f32[2,256]{1,0:T(2,128)S(1)}, f32[2,256]{1,0:T(2,128)S(1)}, u32[]{:S(2)}, u32[]{:S(2)}) collective-permute-start(f32[2,256]{1,0:T(2,128)S(1)} %add.3.refs_6_), channel_id=1, source_target_pairs={{0,12},{2,14},{4,8},{6,10},{8,4},{10,6},{12,0},{14,2},{16,28},{18,... | collective-permute-start | bytes 6152 | tf_op jit(solution)/shard_map/ppermute | solution.py:448
  26.0 2.9 %collective-permute-start.9 = (f32[2,256]{1,0:T(2,128)S(1)}, f32[2,256]{1,0:T(2,128)S(1)}, u32[]{:S(2)}, u32[]{:S(2)}) collective-permute-start(f32[2,256]{1,0:T(2,128)S(1)} %collective-permute-done.8.refs_8_), channel_id=1, source_target_pairs={{0,2},{2,0},{4,6},{6,4},{1,3},{3,1},{5,7},{7,5},{8,10},{10,8},{12,... | collective-permute-start | bytes 6152 | tf_op jit(solution)/shard_map/ppermute | solution.py:440
  29.7 7.8 %collective-permute-start.11 = (bf16[528,128]{1,0:T(8,128)(2,1)S(1)}, bf16[528,128]{1,0:T(8,128)(2,1)S(1)}, u32[]{:S(2)}, u32[]{:S(2)}) collective-permute-start(bf16[528,128]{1,0:T(8,128)(2,1)S(1)} %get-tuple-element.85), channel_id=1, source_target_pairs={{0,16},{8,24},{16,0},{24,8},{1,17},{9,25},{17,1},{25,9},{2,18},{10... | collective-permute-start | bytes 405512 | tf_op jit(solution)/shard_map/ppermute | solution.py:419
  33.5 6.3 %collective-permute-start.10 = (bf16[128,512]{1,0:T(8,128)(2,1)S(1)}, bf16[128,512]{1,0:T(8,128)(2,1)S(1)}, u32[]{:S(2)}, u32[]{:S(2)}) collective-permute-start(bf16[128,512]{1,0:T(8,128)(2,1)S(1)} %get-tuple-element.80), channel_id=1, source_target_pairs={{0,8},{8,0},{16,24},{24,16},{1,9},{9,1},{17,25},{25,17},{2,10},{10... | collective-permute-start | bytes 393224 | tf_op jit(solution)/shard_map/ppermute | solution.py:423
  38.0 5.1 %collective-permute-start.12 = (bf16[128,512]{1,0:T(8,128)(2,1)S(1)}, bf16[128,512]{1,0:T(8,128)(2,1)S(1)}, u32[]{:S(2)}, u32[]{:S(2)}) collective-permute-start(bf16[128,512]{1,0:T(8,128)(2,1)S(1)} %get-tuple-element.86), channel_id=1, source_target_pairs={{0,1},{1,0},{8,9},{9,8},{16,17},{17,16},{24,25},{25,24},{2,3},{3,2... | collective-permute-start | bytes 393224 | tf_op jit(solution)/shard_map/ppermute | solution.py:433
  39.6 5.9 %collective-permute-start.13 = (bf16[128,512]{1,0:T(8,128)(2,1)S(1)}, bf16[128,512]{1,0:T(8,128)(2,1)S(1)}, u32[]{:S(2)}, u32[]{:S(2)}) collective-permute-start(bf16[128,512]{1,0:T(8,128)(2,1)S(1)} %get-tuple-element.87), channel_id=1, source_target_pairs={{0,9},{1,8},{8,1},{9,0},{16,25},{17,24},{24,17},{25,16},{2,11},{3,... | collective-permute-start | bytes 393224 | tf_op jit(solution)/shard_map/ppermute | solution.py:433

commit v10 on v7

--- a/solution.py
+++ b/solution.py
@@ -442,8 +442,8 @@
 
     pair = part + neighbour(part)
     ways = [(1, 0)] + [(flip, k) for k in range(2, count, 2) for flip in (0, 1)]
+    shared = [fetched(pair, *ways[i : i + 2]) for i in range(0, len(ways) - 1, 2)]
     parts = [pair, fetched(pair, ways[-1])]
-    shared = [fetched(pair, *ways[i : i + 2]) for i in range(0, len(ways) - 1, 2)]
     for block in shared:
         parts += [block, neighbour(block)]
     return parts

time: 46.4 us -> 46.4 us (level)
  no operation moved by 1% of the time
where the time goes in v10:
time: 46.4 us; the launch traced here: 46.2 us
  starting transfers between devices  18.6 us (40%)
  waiting for transfers between devices  17.2 us (37%)
  Pallas kernels  9.64 us (21%)
  between operations  0.73 us (2%)
    pallas_call x13, Pallas kernels, call(): pl.pallas_call(kernel, out_shape=outs, in_specs=[pl.BlockSpec(memory_spac...  9.64 us
    ppermute x3, starting transfers between devices, turned(): lax.ppermute(block, axis, [(i, (i + distance) % count) for i in range(cou...  7.43 us
    ppermute x5, starting transfers between devices, swapped(): lax.ppermute(block, 'ctx', [(i, i ^ 1) for i in range(lax.axis_size('ctx'...  5.58 us
    ppermute x3, waiting for transfers between devices, turned(): lax.ppermute(block, axis, [(i, (i + distance) % count) for i in range(cou...  5.07 us
    ppermute x2, waiting for transfers between devices, to_earlier_section(): return lax.ppermute(block, ('ctx', 'pp'), route)  5.01 us
    ppermute x2, starting transfers between devices, fetched(): return lax.ppermute(block, ('ctx', 'tp'), route)  3.86 us
    ppermute x2, waiting for transfers between devices, fetched(): return lax.ppermute(block, ('ctx', 'tp'), route)  3.55 us
    ppermute x5, waiting for transfers between devices, swapped(): lax.ppermute(block, 'ctx', [(i, i ^ 1) for i in range(lax.axis_size('ctx'...  2.39 us
  transfers between devices with their start and end apart: 14, of which 10 were waited for; matrix products, arithmetic and copies ran while one was open for 0% of the time, Pallas kernels for 15%

profile of v10, /device:TPU:0, one launch (start us, length us, event | category | flops | bytes accessed | tf_op | source)
XLA Modules:
  0.0 46.2 jit_solution(11877941206310922365)
XLA Ops:
  0.6 1.0 %shard_map.77 = (bf16[272,256]{1,0:T(8,128)(2,1)S(1)}, bf16[256,256]{1,0:T(8,128)(2,1)S(1)}, f32[8,128]{1,0:T(8,128)S(1)}) custom-call(bf16[1,128,1024]{2,1,0:T(8,128)(2,1)} %k.3, bf16[1,128,1024]{2,1,0:T(8,128)(2,1)} %v.3, f32[1,8,128]{2,1,0:T(8,128)} %bitcast.1), custom_call_target="tpu_custom_call" | custom-call | bytes 802816 | tf_op jit(solution)/shard_map/pallas_call | solution.py:22
  1.6 3.1 %collective-permute-start = (bf16[272,256]{1,0:T(8,128)(2,1)S(1)}, bf16[272,256]{1,0:T(8,128)(2,1)S(1)}, u32[]{:S(2)}, u32[]{:S(2)}) collective-permute-start(bf16[272,256]{1,0:T(8,128)(2,1)S(1)} %get-tuple-element.43), channel_id=1, source_target_pairs={{0,8},{8,0},{16,24},{24,16},{1,9},{9,1},{17,25},{25,17},{2,10},{10... | collective-permute-start | bytes 417800 | tf_op jit(solution)/shard_map/ppermute | solution.py:416
  4.7 0.1 collective-permute-start.1
  4.8 0.0 copy-start
  4.8 1.3 %shard_map.78 = (bf16[128,512]{1,0:T(8,128)(2,1)S(1)}, bf16[128,512]{1,0:T(8,128)(2,1)S(1)}, bf16[512,512]{1,0:T(8,128)(2,1)S(1)}) custom-call(bf16[1,128,1024]{2,1,0:T(8,128)(2,1)} %q.1, bf16[1,128,1024]{2,1,0:T(8,128)(2,1)} %k.3, bf16[1,128,1024]{2,1,0:T(8,128)(2,1)} %v.3, bf16[1,128,1024]{2,1,0:T(8,128)(2,1)} %g.1, bf16[16,256]{1,0:T(8,128)(2,1)S(1)} %slice.3._), custom_call_target="tpu_custom_call" | custom-call | bytes 1843200 | tf_op jit(solution)/shard_map/pallas_call | solution.py:22
  6.1 2.0 %collective-permute-start.2 = (bf16[128,512]{1,0:T(8,128)(2,1)S(1)}, bf16[128,512]{1,0:T(8,128)(2,1)S(1)}, u32[]{:S(2)}, u32[]{:S(2)}) collective-permute-start(bf16[128,512]{1,0:T(8,128)(2,1)S(1)} %get-tuple-element.53), channel_id=1, source_target_pairs={{0,8},{8,0},{16,24},{24,16},{1,9},{9,1},{17,25},{25,17},{2,10},{10... | collective-permute-start | bytes 393224 | tf_op jit(solution)/shard_map/ppermute | solution.py:416
  8.1 0.1 collective-permute-start.5
  8.2 1.1 %collective-permute-done.got = bf16[272,256]{1,0:T(8,128)(2,1)S(1)} collective-permute-done((bf16[272,256]{1,0:T(8,128)(2,1)S(1)}, bf16[272,256]{1,0:T(8,128)(2,1)S(1)}, u32[]{:S(2)}, u32[]{:S(2)}) %collective-permute-start) | collective-permute-done | bytes 139296 | tf_op jit(solution)/shard_map/ppermute | solution.py:416
  9.2 0.0 copy-done
  9.2 0.6 %shard_map.79 = (bf16[256,512]{1,0:T(8,128)(2,1)S(1)}, bf16[256,512]{1,0:T(8,128)(2,1)S(1)}, f32[16,512]{1,0:T(8,128)S(1)}, bf16[256,512]{1,0:T(8,128)(2,1)S(1)}...) custom-call(bf16[272,256]{1,0:T(8,128)(2,1)S(1)} %collective-permute-done.got, ...), custom_call_target="tpu_custom_call" | custom-call | bytes 1581056 | tf_op jit(solution)/shard_map/pallas_call | solution.py:22
  9.9 3.1 %collective-permute-start.3 = (bf16[272,128]{1,0:T(8,128)(2,1)S(1)}, bf16[272,128]{1,0:T(8,128)(2,1)S(1)}, u32[]{:S(2)}, u32[]{:S(2)}) collective-permute-start(bf16[272,128]{1,0:T(8,128)(2,1)S(1)} %get-tuple-element.61), channel_id=1, source_target_pairs={{0,16},{8,24},{16,0},{24,8},{1,17},{9,25},{17,1},{25,9},{2,18},{10... | collective-permute-start | bytes 208904 | tf_op jit(solution)/shard_map/ppermute | solution.py:412
  13.0 0.0 collective-permute-done.1.refs_4_
  13.0 0.6 %shard_map.80 = (bf16[256,512]{1,0:T(8,128)(2,1)S(1)}, bf16[256,512]{1,0:T(8,128)(2,1)S(1)}, f32[16,512]{1,0:T(8,128)S(1)}, bf16[256,512]{1,0:T(8,128)(2,1)S(1)}, bf16[272,128]{1,0:T(8,128)(2,1)S(1)}) custom-call(bf16[256,512]{1,0:T(8,128)(2,1)S(1)} %get-tuple-element.46.refs_0_, ...), custom_call_target="tpu_custom_call", output_to_operand_aliasing={{0}: (0, {}), {1}: (1, {}), {2}: (2, {}), {3}: (3, {})} | custom-call | bytes 2387968 | tf_op jit(solution)/shard_map/pallas_call | solution.py:22
  13.6 2.1 %collective-permute-start.4 = (bf16[272,128]{1,0:T(8,128)(2,1)S(1)}, bf16[272,128]{1,0:T(8,128)(2,1)S(1)}, u32[]{:S(2)}, u32[]{:S(2)}) collective-permute-start(bf16[272,128]{1,0:T(8,128)(2,1)S(1)} %get-tuple-element.64), channel_id=1, source_target_pairs={{0,16},{8,24},{16,0},{24,8},{1,17},{9,25},{17,1},{25,9},{2,18},{10... | collective-permute-start | bytes 208904 | tf_op jit(solution)/shard_map/ppermute | solution.py:412
  15.8 1.3 %collective-permute-done.2.got = bf16[128,512]{1,0:T(8,128)(2,1)S(1)} collective-permute-done((bf16[128,512]{1,0:T(8,128)(2,1)S(1)}, bf16[128,512]{1,0:T(8,128)(2,1)S(1)}, u32[]{:S(2)}, u32[]{:S(2)}) %collective-permute-start.2) | collective-permute-done | bytes 131104 | tf_op jit(solution)/shard_map/ppermute | solution.py:416
  17.1 0.7 %shard_map.81 = (bf16[256,512]{1,0:T(8,128)(2,1)S(1)}, bf16[256,512]{1,0:T(8,128)(2,1)S(1)}, bf16[4,256,256]{2,1,0:T(8,128)(2,1)S(1)}, f32[256,512]{1,0:T(8,128)...) custom-call(bf16[128,512]{1,0:T(8,128)(2,1)S(1)} %collective-permute-done.2.got, ...), custom_call_target="tpu_custom_call" | custom-call | flops 134217728 | bytes 2793472 | tf_op jit(solution)/shard_map/pallas_call | solution.py:22
  17.8 0.5 %collective-permute-done.3.refs_8_.refs_0_ = bf16[272,128]{1,0:T(8,128)(2,1)S(1)} collective-permute-done((bf16[272,128]{1,0:T(8,128)(2,1)S(1)}, bf16[272,128]{1,0:T(8,128)(2,1)S(1)}, u32[]{:S(2)}, u32[]{:S(2)}) %collective-permute-start.3) | collective-permute-done | bytes 69664 | tf_op jit(solution)/shard_map/ppermute | solution.py:412
  18.3 0.4 shard_map.82
  18.7 0.9 %collective-permute-done.4.refs_8_.refs_1_ = bf16[272,128]{1,0:T(8,128)(2,1)S(1)} collective-permute-done((bf16[272,128]{1,0:T(8,128)(2,1)S(1)}, bf16[272,128]{1,0:T(8,128)(2,1)S(1)}, u32[]{:S(2)}, u32[]{:S(2)}) %collective-permute-start.4) | collective-permute-done | bytes 69664 | tf_op jit(solution)/shard_map/ppermute | solution.py:412
  19.6 0.4 shard_map.83
  20.0 0.0 collective-permute-done.5.refs_2_
  20.0 0.2 shard_map.84
  20.3 0.0 collective-permute-start.6
  20.3 1.2 %collective-permute-done.6 = f32[2,256]{1,0:T(2,128)S(1)} collective-permute-done((f32[2,256]{1,0:T(2,128)S(1)}, f32[2,256]{1,0:T(2,128)S(1)}, u32[]{:S(2)}, u32[]{:S(2)}) %collective-permute-start.6) | collective-permute-done | bytes 2080 | tf_op jit(solution)/shard_map/ppermute | solution.py:433
  21.5 2.9 %collective-permute-start.8 = (f32[2,256]{1,0:T(2,128)S(1)}, f32[2,256]{1,0:T(2,128)S(1)}, u32[]{:S(2)}, u32[]{:S(2)}) collective-permute-start(f32[2,256]{1,0:T(2,128)S(1)} %add.3.refs_6_), channel_id=1, source_target_pairs={{0,8},{2,6},{4,12},{6,2},{8,0},{10,14},{12,4},{14,10},{16,24},{18,... | collective-permute-start | bytes 6152 | tf_op jit(solution)/shard_map/ppermute | solution.py:441
  24.5 0.9 %collective-permute-start.7 = (f32[2,256]{1,0:T(2,128)S(1)}, f32[2,256]{1,0:T(2,128)S(1)}, u32[]{:S(2)}, u32[]{:S(2)}) collective-permute-start(f32[2,256]{1,0:T(2,128)S(1)} %add.3.refs_6_), channel_id=1, source_target_pairs={{0,12},{2,14},{4,8},{6,10},{8,4},{10,6},{12,0},{14,2},{16,28},{18,... | collective-permute-start | bytes 6152 | tf_op jit(solution)/shard_map/ppermute | solution.py:441
  25.4 0.6 %collective-permute-done.8.refs_8_ = f32[2,256]{1,0:T(2,128)S(1)} collective-permute-done((f32[2,256]{1,0:T(2,128)S(1)}, f32[2,256]{1,0:T(2,128)S(1)}, u32[]{:S(2)}, u32[]{:S(2)}) %collective-permute-start.8) | collective-permute-done | bytes 2080 | tf_op jit(solution)/shard_map/ppermute | solution.py:441
  26.0 0.0 collective-permute-start.9
  26.0 2.9 %collective-permute-done.7.refs_7_ = f32[2,256]{1,0:T(2,128)S(1)} collective-permute-done((f32[2,256]{1,0:T(2,128)S(1)}, f32[2,256]{1,0:T(2,128)S(1)}, u32[]{:S(2)}, u32[]{:S(2)}) %collective-permute-start.7) | collective-permute-done | bytes 2080 | tf_op jit(solution)/shard_map/ppermute | solution.py:441
  28.9 0.0 collective-permute-done.9.refs_9_
  28.9 0.8 %shard_map.85 = (f32[8,256]{1,0:T(8,128)S(1)}, bf16[256,512]{1,0:T(8,128)(2,1)S(1)}, bf16[528,128]{1,0:T(8,128)(2,1)S(1)}) custom-call(f32[256,512]{1,0:T(8,128)S(1)} %get-tuple-element.65.refs_0_.attended, bf16[256,512]{1,0:T(8,128)(2,1)S(1)} %get-tuple-element.56.refs_2_.refs_1_.q2, bf16[256,512]{1,0:T(8,128)(2,1)S(1)} %get-tuple-element.57.refs_3_.refs_2_, ...), custom_call_target="tpu_custom_call" | custom-call | bytes 1757184 | tf_op jit(solution)/shard_map/pallas_call | solution.py:22
  29.7 2.1 %collective-permute-start.11 = (bf16[528,128]{1,0:T(8,128)(2,1)S(1)}, bf16[528,128]{1,0:T(8,128)(2,1)S(1)}, u32[]{:S(2)}, u32[]{:S(2)}) collective-permute-start(bf16[528,128]{1,0:T(8,128)(2,1)S(1)} %get-tuple-element.81), channel_id=1, source_target_pairs={{0,16},{8,24},{16,0},{24,8},{1,17},{9,25},{17,1},{25,9},{2,18},{10... | collective-permute-start | bytes 405512 | tf_op jit(solution)/shard_map/ppermute | solution.py:412
  31.9 1.6 %shard_map.86 = (bf16[128,512]{1,0:T(8,128)(2,1)S(1)}, bf16[128,512]{1,0:T(8,128)(2,1)S(1)}, f32[256,512]{1,0:T(8,128)S(1)}, f32[256,512]{1,0:T(8,128)S(1)}, bf16[256,512]{1,0:T(8,128)(2,1)S(1)}) custom-call(f32[256,512]{1,0:T(8,128)S(1)} %get-tuple-element.65.refs_0_.attended, f32[8,256]{1,0:T(8,128)S(1)} %get-tuple-element.69.scales, ...), custom_call_target="tpu_custom_call" | custom-call | flops 335544320 | bytes 3842048 | tf_op jit(solution)/shard_map/pallas_call | solution.py:22
  33.5 0.3 collective-permute-start.10
  33.8 3.7 %collective-permute-done.11.refs_4_ = bf16[528,128]{1,0:T(8,128)(2,1)S(1)} collective-permute-done((bf16[528,128]{1,0:T(8,128)(2,1)S(1)}, bf16[528,128]{1,0:T(8,128)(2,1)S(1)}, u32[]{:S(2)}, u32[]{:S(2)}) %collective-permute-start.11) | collective-permute-done | bytes 135200 | tf_op jit(solution)/shard_map/ppermute | solution.py:412
  37.5 0.5 %shard_map.88 = (bf16[128,512]{1,0:T(8,128)(2,1)S(1)}, bf16[128,512]{1,0:T(8,128)(2,1)S(1)}) custom-call(f32[256,512]{1,0:T(8,128)S(1)} %get-tuple-element.77.refs_0_, f32[256,512]{1,0:T(8,128)S(1)} %get-tuple-element.78.refs_1_, bf16[256,512]{1,0:T(8,128)(2,1)S(1)} %get-tuple-element.79.refs_2_, bf16[256,512]{1,0:T(8,128)(2,1)S(1)} %get-tuple-element.80.refs_3_, ...), custom_call_target="tpu_custom_call" | custom-call | bytes 2002944 | tf_op jit(solution)/shard_map/pallas_call | solution.py:22
  38.1 1.6 %collective-permute-start.12 = (bf16[128,512]{1,0:T(8,128)(2,1)S(1)}, bf16[128,512]{1,0:T(8,128)(2,1)S(1)}, u32[]{:S(2)}, u32[]{:S(2)}) collective-permute-start(bf16[128,512]{1,0:T(8,128)(2,1)S(1)} %get-tuple-element.82), channel_id=1, source_target_pairs={{0,1},{1,0},{8,9},{9,8},{16,17},{17,16},{24,25},{25,24},{2,3},{3,2... | collective-permute-start | bytes 393224 | tf_op jit(solution)/shard_map/ppermute | solution.py:426
  39.6 0.1 collective-permute-start.13
  39.8 0.0 collective-permute-done.10.refs_1_
  39.8 0.7 %shard_map.87 = bf16[1,128,1024]{2,1,0:T(8,128)(2,1)} custom-call(bf16[128,512]{1,0:T(8,128)(2,1)S(1)} %get-tuple-element.75.refs_0_, bf16[128,512]{1,0:T(8,128)(2,1)S(1)} %collective-permute-done.10.refs_1_), custom_call_target="tpu_custom_call" | custom-call | bytes 524288 | tf_op jit(solution)/shard_map/pallas_call | solution.py:22
  40.5 2.6 %collective-permute-done.12.refs_0_ = bf16[128,512]{1,0:T(8,128)(2,1)S(1)} collective-permute-done((bf16[128,512]{1,0:T(8,128)(2,1)S(1)}, bf16[128,512]{1,0:T(8,128)(2,1)S(1)}, u32[]{:S(2)}, u32[]{:S(2)}) %collective-permute-start.12) | collective-permute-done | bytes 131104 | tf_op jit(solution)/shard_map/ppermute | solution.py:426
  43.1 2.4 %collective-permute-done.13.refs_1_ = bf16[128,512]{1,0:T(8,128)(2,1)S(1)} collective-permute-done((bf16[128,512]{1,0:T(8,128)(2,1)S(1)}, bf16[128,512]{1,0:T(8,128)(2,1)S(1)}, u32[]{:S(2)}, u32[]{:S(2)}) %collective-permute-start.13) | collective-permute-done | bytes 131104 | tf_op jit(solution)/shard_map/ppermute | solution.py:426
  45.5 0.7 %shard_map.89 = bf16[1,128,1024]{2,1,0:T(8,128)(2,1)} custom-call(bf16[128,512]{1,0:T(8,128)(2,1)S(1)} %collective-permute-done.12.refs_0_, bf16[128,512]{1,0:T(8,128)(2,1)S(1)} %collective-permute-done.13.refs_1_), custom_call_target="tpu_custom_call" | custom-call | bytes 524288 | tf_op jit(solution)/shard_map/pallas_call | solution.py:22
  (3 shorter events, 0.0 us)
Async XLA Ops:
  1.6 7.6 %collective-permute-start = (bf16[272,256]{1,0:T(8,128)(2,1)S(1)}, bf16[272,256]{1,0:T(8,128)(2,1)S(1)}, u32[]{:S(2)}, u32[]{:S(2)}) collective-permute-start(bf16[272,256]{1,0:T(8,128)(2,1)S(1)} %get-tuple-element.43), channel_id=1, source_target_pairs={{0,8},{8,0},{16,24},{24,16},{1,9},{9,1},{17,25},{25,17},{2,10},{10... | collective-permute-start | bytes 417800 | tf_op jit(solution)/shard_map/ppermute | solution.py:416
  4.7 8.3 %collective-permute-start.1 = (bf16[256,256]{1,0:T(8,128)(2,1)S(1)}, bf16[256,256]{1,0:T(8,128)(2,1)S(1)}, u32[]{:S(2)}, u32[]{:S(2)}) collective-permute-start(bf16[256,256]{1,0:T(8,128)(2,1)S(1)} %get-tuple-element.50), channel_id=1, source_target_pairs={{0,8},{8,0},{16,24},{24,16},{1,9},{9,1},{17,25},{25,17},{2,10},{10... | collective-permute-start | bytes 393224 | tf_op jit(solution)/shard_map/ppermute | solution.py:416
  4.8 4.4 %copy-start = (f32[1,4,1024]{2,1,0:T(4,128)S(1)}, f32[1,4,1024]{2,1,0:T(4,128)}, u32[]{:S(2)}) copy-start(f32[1,4,1024]{2,1,0:T(4,128)} %refs_6_.1) | copy-start | bytes 49156
  6.1 11.0 %collective-permute-start.2 = (bf16[128,512]{1,0:T(8,128)(2,1)S(1)}, bf16[128,512]{1,0:T(8,128)(2,1)S(1)}, u32[]{:S(2)}, u32[]{:S(2)}) collective-permute-start(bf16[128,512]{1,0:T(8,128)(2,1)S(1)} %get-tuple-element.53), channel_id=1, source_target_pairs={{0,8},{8,0},{16,24},{24,16},{1,9},{9,1},{17,25},{25,17},{2,10},{10... | collective-permute-start | bytes 393224 | tf_op jit(solution)/shard_map/ppermute | solution.py:416
  8.1 12.0 %collective-permute-start.5 = (bf16[128,512]{1,0:T(8,128)(2,1)S(1)}, bf16[128,512]{1,0:T(8,128)(2,1)S(1)}, u32[]{:S(2)}, u32[]{:S(2)}) collective-permute-start(bf16[128,512]{1,0:T(8,128)(2,1)S(1)} %get-tuple-element.66), channel_id=1, source_target_pairs={{0,8},{8,0},{16,24},{24,16},{1,9},{9,1},{17,25},{25,17},{2,10},{10... | collective-permute-start | bytes 393224 | tf_op jit(solution)/shard_map/ppermute | solution.py:416
  9.9 8.4 %collective-permute-start.3 = (bf16[272,128]{1,0:T(8,128)(2,1)S(1)}, bf16[272,128]{1,0:T(8,128)(2,1)S(1)}, u32[]{:S(2)}, u32[]{:S(2)}) collective-permute-start(bf16[272,128]{1,0:T(8,128)(2,1)S(1)} %get-tuple-element.61), channel_id=1, source_target_pairs={{0,16},{8,24},{16,0},{24,8},{1,17},{9,25},{17,1},{25,9},{2,18},{10... | collective-permute-start | bytes 208904 | tf_op jit(solution)/shard_map/ppermute | solution.py:412
  13.6 6.0 %collective-permute-start.4 = (bf16[272,128]{1,0:T(8,128)(2,1)S(1)}, bf16[272,128]{1,0:T(8,128)(2,1)S(1)}, u32[]{:S(2)}, u32[]{:S(2)}) collective-permute-start(bf16[272,128]{1,0:T(8,128)(2,1)S(1)} %get-tuple-element.64), channel_id=1, source_target_pairs={{0,16},{8,24},{16,0},{24,8},{1,17},{9,25},{17,1},{25,9},{2,18},{10... | collective-permute-start | bytes 208904 | tf_op jit(solution)/shard_map/ppermute | solution.py:412
  20.3 1.2 %collective-permute-start.6 = (f32[2,256]{1,0:T(2,128)S(1)}, f32[2,256]{1,0:T(2,128)S(1)}, u32[]{:S(2)}, u32[]{:S(2)}) collective-permute-start(f32[2,256]{1,0:T(2,128)S(1)} %get-tuple-element.68), channel_id=1, source_target_pairs={{0,2},{2,0},{4,6},{6,4},{1,3},{3,1},{5,7},{7,5},{8,10},{10,8},{12,... | collective-permute-start | bytes 6152 | tf_op jit(solution)/shard_map/ppermute | solution.py:433
  21.5 4.5 %collective-permute-start.8 = (f32[2,256]{1,0:T(2,128)S(1)}, f32[2,256]{1,0:T(2,128)S(1)}, u32[]{:S(2)}, u32[]{:S(2)}) collective-permute-start(f32[2,256]{1,0:T(2,128)S(1)} %add.3.refs_6_), channel_id=1, source_target_pairs={{0,8},{2,6},{4,12},{6,2},{8,0},{10,14},{12,4},{14,10},{16,24},{18,... | collective-permute-start | bytes 6152 | tf_op jit(solution)/shard_map/ppermute | solution.py:441
  24.5 4.5 %collective-permute-start.7 = (f32[2,256]{1,0:T(2,128)S(1)}, f32[2,256]{1,0:T(2,128)S(1)}, u32[]{:S(2)}, u32[]{:S(2)}) collective-permute-start(f32[2,256]{1,0:T(2,128)S(1)} %add.3.refs_6_), channel_id=1, source_target_pairs={{0,12},{2,14},{4,8},{6,10},{8,4},{10,6},{12,0},{14,2},{16,28},{18,... | collective-permute-start | bytes 6152 | tf_op jit(solution)/shard_map/ppermute | solution.py:441
  26.0 2.9 %collective-permute-start.9 = (f32[2,256]{1,0:T(2,128)S(1)}, f32[2,256]{1,0:T(2,128)S(1)}, u32[]{:S(2)}, u32[]{:S(2)}) collective-permute-start(f32[2,256]{1,0:T(2,128)S(1)} %collective-permute-done.8.refs_8_), channel_id=1, source_target_pairs={{0,2},{2,0},{4,6},{6,4},{1,3},{3,1},{5,7},{7,5},{8,10},{10,8},{12,... | collective-permute-start | bytes 6152 | tf_op jit(solution)/shard_map/ppermute | solution.py:433
  29.7 7.8 %collective-permute-start.11 = (bf16[528,128]{1,0:T(8,128)(2,1)S(1)}, bf16[528,128]{1,0:T(8,128)(2,1)S(1)}, u32[]{:S(2)}, u32[]{:S(2)}) collective-permute-start(bf16[528,128]{1,0:T(8,128)(2,1)S(1)} %get-tuple-element.81), channel_id=1, source_target_pairs={{0,16},{8,24},{16,0},{24,8},{1,17},{9,25},{17,1},{25,9},{2,18},{10... | collective-permute-start | bytes 405512 | tf_op jit(solution)/shard_map/ppermute | solution.py:412
  33.5 6.3 %collective-permute-start.10 = (bf16[128,512]{1,0:T(8,128)(2,1)S(1)}, bf16[128,512]{1,0:T(8,128)(2,1)S(1)}, u32[]{:S(2)}, u32[]{:S(2)}) collective-permute-start(bf16[128,512]{1,0:T(8,128)(2,1)S(1)} %get-tuple-element.76), channel_id=1, source_target_pairs={{0,8},{8,0},{16,24},{24,16},{1,9},{9,1},{17,25},{25,17},{2,10},{10... | collective-permute-start | bytes 393224 | tf_op jit(solution)/shard_map/ppermute | solution.py:416
  38.1 5.1 %collective-permute-start.12 = (bf16[128,512]{1,0:T(8,128)(2,1)S(1)}, bf16[128,512]{1,0:T(8,128)(2,1)S(1)}, u32[]{:S(2)}, u32[]{:S(2)}) collective-permute-start(bf16[128,512]{1,0:T(8,128)(2,1)S(1)} %get-tuple-element.82), channel_id=1, source_target_pairs={{0,1},{1,0},{8,9},{9,8},{16,17},{17,16},{24,25},{25,24},{2,3},{3,2... | collective-permute-start | bytes 393224 | tf_op jit(solution)/shard_map/ppermute | solution.py:426
  39.6 5.9 %collective-permute-start.13 = (bf16[128,512]{1,0:T(8,128)(2,1)S(1)}, bf16[128,512]{1,0:T(8,128)(2,1)S(1)}, u32[]{:S(2)}, u32[]{:S(2)}) collective-permute-start(bf16[128,512]{1,0:T(8,128)(2,1)S(1)} %get-tuple-element.83), channel_id=1, source_target_pairs={{0,9},{1,8},{8,1},{9,0},{16,25},{17,24},{24,17},{25,16},{2,11},{3,... | collective-permute-start | bytes 393224 | tf_op jit(solution)/shard_map/ppermute | solution.py:426
